TPU v7x, 32 devices: a whole 2x2x4 slice. The times are simulated.
32 devices in a mesh: xy: 16 (over z, y, core), gz: 2 (over x).
Axes of the slice: x: 2, y: 2, z: 4, core: 2. Of those that a mesh axis runs over, the one named last changes fastest.
Arguments:
- noise: float32 [16, 8, 4, 32], P('xy', 'gz'), may hold values from -3.5 to 3.5
- w_first: bfloat16 [2, 81, 64, 1], replicated, may hold values from -0.625 to 0.625
- b_first: float32 [2, 64], replicated, may hold values from -3 to 3
- w_mid: bfloat16 [2, 81, 64, 64], replicated, may hold values from -0.078125 to 0.078125
- b_mid: float32 [2, 64], replicated, may hold values from -3 to 3
- w_last: bfloat16 [2, 81, 2, 64], replicated, may hold values from -0.078125 to 0.078125
- b_last: float32 [2, 2], replicated, may hold values from -3 to 3
Outputs:
- sample: float32 [16, 8, 4, 32], P('xy', 'gz')
- noise_force: float32 [16, 8, 4, 32], P('xy', 'gz')
- loss: float32 [], replicated
- grad_w_first: float32 [2, 81, 64, 1], replicated
- grad_b_first: float32 [2, 64], replicated
- grad_w_mid: float32 [2, 81, 64, 64], replicated
- grad_b_mid: float32 [2, 64], replicated
- grad_w_last: float32 [2, 81, 2, 64], replicated
- grad_b_last: float32 [2, 2], replicated
All inputs are finite; a program needn't handle non-finite values.
Results may differ from a plain program's by a relative error of at most 0.022.
Values may be sent and summed in bfloat16 or wider, within the bound.
No kernel may reach another device: no remote copies, remote signals or barrier semaphores. Data moves between devices by JAX's collectives and lax.ppermute only.
A program may use at most 320 MiB of HBM per device.

v0:
```python
import jax
import jax.numpy as jnp
from jax import lax
from jax.sharding import PartitionSpec as P

hopping = 0.3
quartic = 0.05


def with_halo(cells, sides, width):
    for axis, dim in sides:
        count = lax.axis_size(axis)
        head = lax.slice_in_dim(cells, 0, width, axis=dim)
        tail = lax.slice_in_dim(cells, cells.shape[dim] - width, cells.shape[dim], axis=dim)
        cells = jnp.concatenate(
            [
                lax.ppermute(tail, axis, [(i, (i + 1) % count) for i in range(count)]),
                cells,
                lax.ppermute(head, axis, [((i + 1) % count, i) for i in range(count)]),
            ],
            axis=dim,
        )
    return cells


def extend_flat(values, period):
    margin = 2 * period
    return jnp.concatenate([values[..., -margin:], values, values[..., :margin]], axis=-1)


def pick_shift(extended, period, length, delta_y, delta_t):
    margin = 2 * period
    base = margin + delta_y * period + delta_t
    main = lax.slice_in_dim(extended, base, base + length, axis=extended.ndim - 1)
    if delta_t == 0:
        return main
    position = lax.broadcasted_iota(jnp.int32, (length,), 0) % period
    if delta_t == 1:
        other = lax.slice_in_dim(
            extended, base - period, base - period + length, axis=extended.ndim - 1
        )
        edge = position == period - 1
    else:
        other = lax.slice_in_dim(
            extended, base + period, base + period + length, axis=extended.ndim - 1
        )
        edge = position == 0
    return jnp.where(edge, other, main)


def unfold(window, sign, period):
    length = window.shape[-1]
    extended = extend_flat(window, period)
    pieces = [
        pick_shift(extended, period, length, -sign * delta_y, -sign * delta_t)
        for delta_y in (-1, 0, 1)
        for delta_t in (-1, 0, 1)
    ]
    return jnp.concatenate(pieces, axis=0).reshape(9 * window.shape[0], -1)


def conv_padded(padded, weight, period):
    channels = padded.shape[0]
    length_first = padded.shape[1] - 2
    length_second = padded.shape[2] - 2
    out_chans = weight.shape[1]
    summed = jnp.zeros((out_chans, length_first * length_second * padded.shape[3]), jnp.float32)
    for step_x in range(3):
        for step_z in range(3):
            weights_group = weight[27 * step_x + 9 * step_z : 27 * step_x + 9 * step_z + 9]
            flattened = weights_group.transpose(1, 0, 2).reshape(out_chans, 9 * channels)
            window = padded[:, step_x : step_x + length_first, step_z : step_z + length_second]
            summed = summed + jnp.dot(
                flattened, unfold(window, -1, period), preferred_element_type=jnp.float32
            )
    return summed.reshape((out_chans, length_first, length_second, padded.shape[3]))


def weights_from_input(grad_out, padded, period):
    out_chans = grad_out.shape[0]
    channels = padded.shape[0]
    length_first = padded.shape[1] - 2
    length_second = padded.shape[2] - 2
    flat_grad = grad_out.reshape(out_chans, -1)
    blocks = []
    for step_x in range(3):
        for step_z in range(3):
            window = padded[:, step_x : step_x + length_first, step_z : step_z + length_second]
            part_sum = lax.dot_general(
                flat_grad,
                unfold(window, -1, period),
                (((1,), (1,)), ((), ())),
                preferred_element_type=jnp.float32,
            )
            blocks.append(part_sum.reshape(out_chans, 9, channels).transpose(1, 0, 2))
    return jnp.concatenate(blocks, axis=0)


def weights_from_output(padded_grad, inputs, period):
    out_chans = padded_grad.shape[0]
    channels = inputs.shape[0]
    length_first = inputs.shape[1]
    length_second = inputs.shape[2]
    flat_inputs = inputs.reshape(channels, -1)
    blocks = []
    for step_x in range(3):
        for step_z in range(3):
            window = padded_grad[
                :, 2 - step_x : 2 - step_x + length_first, 2 - step_z : 2 - step_z + length_second
            ]
            part_sum = lax.dot_general(
                unfold(window, 1, period),
                flat_inputs,
                (((1,), (1,)), ((), ())),
                preferred_element_type=jnp.float32,
            )
            blocks.append(part_sum.reshape(9, out_chans, channels))
    return jnp.concatenate(blocks, axis=0)


def mirrored(weight):
    return weight[::-1].transpose(0, 2, 1)


def expand(bias):
    return bias[:, None, None, None]


def with_rims(values):
    return with_halo(values, (("xy", 1), ("gz", 2)), 1)


def narrow_conv(inputs, weight, period):
    padded = with_halo(inputs, (("xy", 1), ("gz", 2)), 1)
    return conv_padded(padded, weight, period)


def per_device(noise, w_first, b_first, w_mid, b_mid, w_last, b_last):
    shape_in = noise.shape
    period = shape_in[3]
    length = shape_in[2] * shape_in[3]
    field = noise.reshape(shape_in[0], shape_in[1], length)
    extents = field.shape
    volume = float(noise.size * lax.axis_size("xy") * lax.axis_size("gz"))
    flat_pos = lax.broadcasted_iota(jnp.int32, extents, 2)
    coords = lax.broadcasted_iota(jnp.int32, extents, 0) + lax.axis_index("xy") * extents[0]
    coords = (
        coords + lax.broadcasted_iota(jnp.int32, extents, 1) + lax.axis_index("gz") * extents[1]
    )
    coords = coords + flat_pos // period + flat_pos % period
    oddness = (coords % 2).astype(jnp.float32)
    saved = []
    logdet = jnp.zeros((), jnp.float32)
    for layer in range(2):
        frozen = oddness if layer == 0 else 1.0 - oddness
        moving = 1.0 - frozen
        net_input = (frozen * field)[None].astype(jnp.bfloat16)
        input_rims = with_rims(net_input)
        first = jnp.tanh(
            conv_padded(input_rims, w_first[layer], period) + expand(b_first[layer])
        ).astype(jnp.bfloat16)
        first_rims = with_rims(first)
        second = jnp.tanh(
            conv_padded(first_rims, w_mid[layer], period) + expand(b_mid[layer])
        ).astype(jnp.bfloat16)
        output = narrow_conv(second, w_last[layer], period) + expand(b_last[layer])
        growth = jnp.exp(output[0])
        saved.append((field, frozen, input_rims, first_rims, second, growth))
        field = frozen * field + moving * (field * growth + output[1])
        logdet = logdet + jnp.sum(moving * output[0])
    border = with_halo(field, (("xy", 0), ("gz", 1)), 1)
    field_ext = extend_flat(field, period)
    ahead = (
        border[2:, 1:-1]
        + border[1:-1, 2:]
        + pick_shift(field_ext, period, length, 1, 0)
        + pick_shift(field_ext, period, length, 0, 1)
    )
    behind = (
        border[:-2, 1:-1]
        + border[1:-1, :-2]
        + pick_shift(field_ext, period, length, -1, 0)
        + pick_shift(field_ext, period, length, 0, -1)
    )
    squared = field * field
    action = jnp.sum(
        -2.0 * hopping * field * ahead + squared + quartic * (squared - 1.0) * (squared - 1.0)
    )
    local_loss = action - logdet
    loss = lax.psum(local_loss, ("xy", "gz")) / volume
    upstream = (
        -2.0 * hopping * (ahead + behind) + 2.0 * field + 4.0 * quartic * (squared - 1.0) * field
    )
    collected = [None, None]
    for layer in (1, 0):
        field_in, frozen, input_rims, first_rims, second, growth = saved[layer]
        moving = 1.0 - frozen
        grad_scale = upstream * moving * field_in * growth - moving
        grad_shift = upstream * moving
        grad_output = jnp.stack([grad_scale, grad_shift]).astype(jnp.bfloat16)
        output_rims = with_rims(grad_output)
        bias_last = jnp.sum(grad_output.astype(jnp.float32), axis=(1, 2, 3))
        weight_last = weights_from_output(output_rims, second, period)
        second_wide = second.astype(jnp.float32)
        grad_second = (
            conv_padded(output_rims, mirrored(w_last[layer]), period)
            * (1.0 - second_wide * second_wide)
        ).astype(jnp.bfloat16)
        bias_mid = jnp.sum(grad_second.astype(jnp.float32), axis=(1, 2, 3))
        weight_mid = weights_from_input(grad_second, first_rims, period)
        first_wide = first_rims[:, 1:-1, 1:-1].astype(jnp.float32)
        grad_first = (
            conv_padded(with_rims(grad_second), mirrored(w_mid[layer]), period)
            * (1.0 - first_wide * first_wide)
        ).astype(jnp.bfloat16)
        bias_first = jnp.sum(grad_first.astype(jnp.float32), axis=(1, 2, 3))
        weight_first = weights_from_input(grad_first, input_rims, period)
        grad_input = narrow_conv(grad_first, mirrored(w_first[layer]), period)[0]
        upstream = upstream * (frozen + moving * growth) + frozen * grad_input
        collected[layer] = (weight_first, bias_first, weight_mid, bias_mid, weight_last, bias_last)
    first_weights = jnp.stack([collected[0][0], collected[1][0]])
    first_biases = jnp.stack([collected[0][1], collected[1][1]])
    mid_weights = jnp.stack([collected[0][2], collected[1][2]])
    mid_biases = jnp.stack([collected[0][3], collected[1][3]])
    last_weights = jnp.stack([collected[0][4], collected[1][4]])
    last_biases = jnp.stack([collected[0][5], collected[1][5]])
    summed = lax.psum(
        (first_weights, first_biases, mid_weights, mid_biases, last_weights, last_biases),
        ("xy", "gz"),
    )
    return (
        field.reshape(shape_in),
        upstream.reshape(shape_in),
        loss,
        summed[0] / volume,
        summed[1] / volume,
        summed[2] / volume,
        summed[3] / volume,
        summed[4] / volume,
        summed[5] / volume,
    )


def solution(mesh):
    return jax.shard_map(
        per_device,
        mesh=mesh,
        in_specs=(P("xy", "gz", None, None), P(), P(), P(), P(), P(), P()),
        out_specs=(
            P("xy", "gz", None, None),
            P("xy", "gz", None, None),
            P(),
            P(),
            P(),
            P(),
            P(),
            P(),
            P(),
        ),
        check_vma=False,
    )
```

profile of v0, /device:TPU:5, one launch (start us, length us, event | category | flops | bytes accessed | tf_op | source)
XLA Modules:
  0.0 751.3 jit_solution(7435373823705726202)
XLA Ops:
  18.2 18.1 %slice_bitcast_fusion.20 = (bf16[64,9,64]{1,2,0:T(8,128)(2,1)S(1)}, bf16[64,9,64]{1,2,0:T(8,128)(2,1)S(1)}, bf16[64,9,64]{1,2,0:T(8,128)(2,1)S(1)}, bf16[64,9,64...) fusion(bf16[2,81,64,64]{1,3,2,0:T(8,128)(2,1)} %param.10), kind=kLoop, calls=%fused_computation.1176 | loop fusion | bytes 2654208 | tf_op jit(solution)/shard_map/transpose | solution.py:71
  40.1 3.1 copy.175
  46.4 3.1 copy.177
  52.7 3.1 copy.179
  55.8 3.2 copy.180
  59.0 3.1 copy.181
  62.2 3.1 copy.182
  82.6 3.7 copy.207
  86.3 3.2 copy.208
  89.5 3.1 copy.209
  92.6 3.2 copy.210
  98.9 3.1 copy.212
  125.6 4.6 slice_bitcast_fusion.9
  165.5 4.5 slice_bitcast_fusion
  205.9 4.0 collective-permute-start.4
  211.2 3.4 collective-permute-done.5
  280.7 3.4 collective-permute-start.12
  296.6 3.7 collective-permute-start.16
  371.5 3.4 collective-permute-start.24
  376.4 3.5 collective-permute-done.25
  385.9 7.0 collective-permute-start.29
  405.9 3.2 collective-permute-start.33
  428.3 12.5 %concatenate.3030 = f32[81,2,64]{2,0,1:T(8,128)} concatenate(f32[9,2,64]{2,0,1:T(8,128)} %fusion.1058, f32[9,2,64]{2,0,1:T(8,128)} %fusion.1056, f32[9,2,64]{2,0,1:T(8,128)} %fusion.1054, f32[9,2,64]{2,0,1:T(8,128)} %fusion.1052, f32[9,2,64]{2,0,1:T(8,128)} %fusion.1050, f32[9,2,64]{2,0,1:T(8,128)} %fusion.1048, f32[9,2,64]{2,0,1:T(8,128)} %fusion.1046, f32[9,2,64]{2,0,1:T(8,128)} %fusion.1044, ...), dimensions={0} | concatenate | bytes 82944 | tf_op jit(solution)/shard_map/concatenate | solution.py:118
  475.4 10.6 %concatenate.3008 = f32[81,64,1]{1,0,2:T(8,128)} concatenate(f32[9,64,1]{1,0,2:T(8,128)S(1)} %convolution_bitcast_fusion.26, f32[9,64,1]{1,0,2:T(8,128)S(1)} %convolution_bitcast_fusion.25, f32[9,64,1]{1,0,2:T(8,128)S(1)} %convolution_bitcast_fusion.24, f32[9,64,1]{1,0,2:T(8,128)S(1)} %convolution_bitcast_fusion.23, f32[9,64,1]{1,0,2:T(8,128)S(1)} %convolution_bitcast_fusion.22, ...), dimensions={0} | concatenate | bytes 41472 | tf_op jit(solution)/shard_map/concatenate | solution.py:96
  509.3 4.1 collective-permute-start.41
  536.2 5.9 collective-permute-start.45
  554.9 5.7 concatenate.3020
  597.4 5.1 collective-permute-start.49
  603.7 55.0 %all-reduce = (f32[]{:T(128)}, f32[2,81,64,1]{2,1,3,0:T(8,128)S(1)}, f32[2,64]{1,0:T(2,128)S(1)}, f32[2,64]{1,0:T(2,128)S(1)}, f32[2,2]{1,0:T(2,128)S(1)}) all-reduce(f32[]{:T(128)S(6)} %sub.272, f32[2,81,64,1]{2,1,3,0:T(8,128)S(1)} %pad_maximum_fusion.18, ...), channel_id=1, replica_groups=mesh['xy'=16,'gz'=2] {'xy','gz'}, use_global_device_ids=true, to_apply=%region_3.4 | all-reduce | flops 10629 | bytes 85032 | tf_op jit(solution)/shard_map/psum | solution.py:190
  685.4 44.5 %all-reduce.4.cloned.1.call-done = (f32[2,81,64,64]{3,2,1,0:T(8,128)}, f32[2,81,2,64]{3,1,2,0:T(8,128)}) async-done(((f32[2,81,64,64]{3,2,1,0:T(8,128)}, f32[2,81,2,64]{3,1,2,0:T(8,128)}), (f32[2,81,64,64]{3,2,1,0:T(8,128)}, f32[2,81,2,64]{3,1,2,0:T(8,128)})) %all-reduce.4.cloned.1.call-update) | async-done | bytes 2737168 | tf_op jit(solution)/shard_map/psum | solution.py:227
  729.9 5.9 broadcast_multiply_fusion
  735.9 6.4 copy.325
  (1883 shorter events, 477.3 us)
Async XLA Ops:
  7.2 722.8 %all-reduce.4.cloned.1.call-start = ((), (), s32[]{:S(2)}) async-start(), calls=%async_computation | async-start | bytes 10977280 | tf_op jit(solution)/shard_map/psum | solution.py:227
  8.8 186.9 %collective-permute-start = (bf16[1,1,4,128]{3,2,1,0:T(4,128)(2,1)S(1)}, bf16[1,1,4,128]{3,2,1,0:T(4,128)(2,1)S(1)}, u32[]{:S(2)}, u32[]{:S(2)}) collective-permute-start(bf16[1,1,4,128]{3,2,1,0:T(4,128)(2,1)S(1)} %get-tuple-element.183), channel_id=1, source_target_pairs={{0,2},{2,4},{4,6},{6,8},{8,10},{10,12},{12,14},{14,16},{16,18},{18... | collective-permute-start | bytes 3080 | tf_op jit(solution)/shard_map/ppermute | solution.py:17
  10.6 185.1 %collective-permute-start.1 = (bf16[1,1,4,128]{3,2,1,0:T(4,128)(2,1)S(1)}, bf16[1,1,4,128]{3,2,1,0:T(4,128)(2,1)S(1)}, u32[]{:S(2)}, u32[]{:S(2)}) collective-permute-start(bf16[1,1,4,128]{3,2,1,0:T(4,128)(2,1)S(1)} %get-tuple-element.183), channel_id=1, source_target_pairs={{2,0},{4,2},{6,4},{8,6},{10,8},{12,10},{14,12},{16,14},{18,16},{20... | collective-permute-start | bytes 3080 | tf_op jit(solution)/shard_map/ppermute | solution.py:19
  205.9 5.3 collective-permute-start.4
  209.8 4.8 collective-permute-start.5
  215.3 4.3 collective-permute-start.7
  239.4 16.5 %collective-permute-start.8 = (bf16[64,1,4,128]{3,2,0,1:T(4,128)(2,1)S(1)}, bf16[64,1,4,128]{3,2,0,1:T(4,128)(2,1)S(1)}, u32[]{:S(2)}, u32[]{:S(2)}) collective-permute-start(bf16[64,1,4,128]{3,2,0,1:T(4,128)(2,1)S(1)} %tanh_convert_fusion.5), channel_id=1, source_target_pairs={{0,2},{2,4},{4,6},{6,8},{8,10},{10,12},{12,14},{14,16},{16,18},{18... | collective-permute-start | bytes 196616 | tf_op jit(solution)/shard_map/ppermute | solution.py:17
  242.1 13.8 %collective-permute-start.9 = (bf16[64,1,4,128]{3,2,0,1:T(4,128)(2,1)S(1)}, bf16[64,1,4,128]{3,2,0,1:T(4,128)(2,1)S(1)}, u32[]{:S(2)}, u32[]{:S(2)}) collective-permute-start(bf16[64,1,4,128]{3,2,0,1:T(4,128)(2,1)S(1)} %tanh_convert_fusion.5), channel_id=1, source_target_pairs={{2,0},{4,2},{6,4},{8,6},{10,8},{12,10},{14,12},{16,14},{18,16},{20... | collective-permute-start | bytes 196616 | tf_op jit(solution)/shard_map/ppermute | solution.py:19
  256.5 4.7 collective-permute-start.11
  280.7 5.1 collective-permute-start.13
  280.7 5.0 collective-permute-start.12
  296.6 8.3 %collective-permute-start.16 = (bf16[64,1,4,128]{3,2,0,1:T(4,128)(2,1)S(1)}, bf16[64,1,4,128]{3,2,0,1:T(4,128)(2,1)S(1)}, u32[]{:S(2)}, u32[]{:S(2)}) collective-permute-start(bf16[64,1,4,128]{3,2,0,1:T(4,128)(2,1)S(1)} %tanh_convert_fusion.3), channel_id=1, source_target_pairs={{0,2},{2,4},{4,6},{6,8},{8,10},{10,12},{12,14},{14,16},{16,18},{18... | collective-permute-start | bytes 196616 | tf_op jit(solution)/shard_map/ppermute | solution.py:17
  300.3 5.0 collective-permute-start.17
  306.5 4.3 collective-permute-start.19
  332.2 14.7 %collective-permute-start.20 = (bf16[64,1,4,128]{3,2,0,1:T(4,128)(2,1)S(1)}, bf16[64,1,4,128]{3,2,0,1:T(4,128)(2,1)S(1)}, u32[]{:S(2)}, u32[]{:S(2)}) collective-permute-start(bf16[64,1,4,128]{3,2,0,1:T(4,128)(2,1)S(1)} %tanh_convert_fusion.1), channel_id=1, source_target_pairs={{0,2},{2,4},{4,6},{6,8},{8,10},{10,12},{12,14},{14,16},{16,18},{18... | collective-permute-start | bytes 196616 | tf_op jit(solution)/shard_map/ppermute | solution.py:17
  334.3 12.6 %collective-permute-start.21 = (bf16[64,1,4,128]{3,2,0,1:T(4,128)(2,1)S(1)}, bf16[64,1,4,128]{3,2,0,1:T(4,128)(2,1)S(1)}, u32[]{:S(2)}, u32[]{:S(2)}) collective-permute-start(bf16[64,1,4,128]{3,2,0,1:T(4,128)(2,1)S(1)} %tanh_convert_fusion.1), channel_id=1, source_target_pairs={{2,0},{4,2},{6,4},{8,6},{10,8},{12,10},{14,12},{16,14},{18,16},{20... | collective-permute-start | bytes 196616 | tf_op jit(solution)/shard_map/ppermute | solution.py:19
  371.5 4.9 collective-permute-start.24
  374.9 5.0 collective-permute-start.25
  385.3 9.0 %collective-permute-start.28 = (bf16[2,1,4,128]{3,2,1,0:T(4,128)(2,1)S(1)}, bf16[2,1,4,128]{3,2,1,0:T(4,128)(2,1)S(1)}, u32[]{:S(2)}, u32[]{:S(2)}) collective-permute-start(bf16[2,1,4,128]{3,2,1,0:T(4,128)(2,1)S(1)} %pad_maximum_fusion.172), channel_id=1, source_target_pairs={{0,2},{2,4},{4,6},{6,8},{8,10},{10,12},{12,14},{14,16},{16,18},{18... | collective-permute-start | bytes 6152 | tf_op jit(solution)/shard_map/ppermute | solution.py:17
  385.9 8.4 %collective-permute-start.29 = (bf16[2,1,4,128]{3,2,1,0:T(4,128)(2,1)S(1)}, bf16[2,1,4,128]{3,2,1,0:T(4,128)(2,1)S(1)}, u32[]{:S(2)}, u32[]{:S(2)}) collective-permute-start(bf16[2,1,4,128]{3,2,1,0:T(4,128)(2,1)S(1)} %pad_maximum_fusion.172), channel_id=1, source_target_pairs={{2,0},{4,2},{6,4},{8,6},{10,8},{12,10},{14,12},{16,14},{18,16},{20... | collective-permute-start | bytes 6152 | tf_op jit(solution)/shard_map/ppermute | solution.py:19
  405.8 35.0 %collective-permute-start.32 = (bf16[64,1,4,128]{3,2,0,1:T(4,128)(2,1)S(1)}, bf16[64,1,4,128]{3,2,0,1:T(4,128)(2,1)S(1)}, u32[]{:S(2)}, u32[]{:S(2)}) collective-permute-start(bf16[64,1,4,128]{3,2,0,1:T(4,128)(2,1)S(1)} %multiply_convert_fusion.7), channel_id=1, source_target_pairs={{0,2},{2,4},{4,6},{6,8},{8,10},{10,12},{12,14},{14,16},{16,18},{18... | collective-permute-start | bytes 196616 | tf_op jit(solution)/shard_map/ppermute | solution.py:17
  405.9 34.9 %collective-permute-start.33 = (bf16[64,1,4,128]{3,2,0,1:T(4,128)(2,1)S(1)}, bf16[64,1,4,128]{3,2,0,1:T(4,128)(2,1)S(1)}, u32[]{:S(2)}, u32[]{:S(2)}) collective-permute-start(bf16[64,1,4,128]{3,2,0,1:T(4,128)(2,1)S(1)} %multiply_convert_fusion.7), channel_id=1, source_target_pairs={{2,0},{4,2},{6,4},{8,6},{10,8},{12,10},{14,12},{16,14},{18,16},{20... | collective-permute-start | bytes 196616 | tf_op jit(solution)/shard_map/ppermute | solution.py:19
  466.2 19.8 %collective-permute-start.36 = (bf16[64,1,4,128]{3,2,0,1:T(4,128)(2,1)S(1)}, bf16[64,1,4,128]{3,2,0,1:T(4,128)(2,1)S(1)}, u32[]{:S(2)}, u32[]{:S(2)}) collective-permute-start(bf16[64,1,4,128]{3,2,0,1:T(4,128)(2,1)S(1)} %multiply_convert_fusion.5), channel_id=1, source_target_pairs={{0,2},{2,4},{4,6},{6,8},{8,10},{10,12},{12,14},{14,16},{16,18},{18... | collective-permute-start | bytes 196616 | tf_op jit(solution)/shard_map/ppermute | solution.py:17
  466.9 19.1 %collective-permute-start.37 = (bf16[64,1,4,128]{3,2,0,1:T(4,128)(2,1)S(1)}, bf16[64,1,4,128]{3,2,0,1:T(4,128)(2,1)S(1)}, u32[]{:S(2)}, u32[]{:S(2)}) collective-permute-start(bf16[64,1,4,128]{3,2,0,1:T(4,128)(2,1)S(1)} %multiply_convert_fusion.5), channel_id=1, source_target_pairs={{2,0},{4,2},{6,4},{8,6},{10,8},{12,10},{14,12},{16,14},{18,16},{20... | collective-permute-start | bytes 196616 | tf_op jit(solution)/shard_map/ppermute | solution.py:19
  507.7 6.5 collective-permute-start.40
  509.3 4.9 collective-permute-start.41
  535.7 36.2 %collective-permute-start.44 = (bf16[64,1,4,128]{3,2,0,1:T(4,128)(2,1)S(1)}, bf16[64,1,4,128]{3,2,0,1:T(4,128)(2,1)S(1)}, u32[]{:S(2)}, u32[]{:S(2)}) collective-permute-start(bf16[64,1,4,128]{3,2,0,1:T(4,128)(2,1)S(1)} %multiply_convert_fusion.3), channel_id=1, source_target_pairs={{0,2},{2,4},{4,6},{6,8},{8,10},{10,12},{12,14},{14,16},{16,18},{18... | collective-permute-start | bytes 196616 | tf_op jit(solution)/shard_map/ppermute | solution.py:17
  536.2 35.7 %collective-permute-start.45 = (bf16[64,1,4,128]{3,2,0,1:T(4,128)(2,1)S(1)}, bf16[64,1,4,128]{3,2,0,1:T(4,128)(2,1)S(1)}, u32[]{:S(2)}, u32[]{:S(2)}) collective-permute-start(bf16[64,1,4,128]{3,2,0,1:T(4,128)(2,1)S(1)} %multiply_convert_fusion.3), channel_id=1, source_target_pairs={{2,0},{4,2},{6,4},{8,6},{10,8},{12,10},{14,12},{16,14},{18,16},{20... | collective-permute-start | bytes 196616 | tf_op jit(solution)/shard_map/ppermute | solution.py:19
  597.4 65.3 %collective-permute-start.48 = (bf16[64,1,4,128]{3,2,0,1:T(4,128)(2,1)S(1)}, bf16[64,1,4,128]{3,2,0,1:T(4,128)(2,1)S(1)}, u32[]{:S(2)}, u32[]{:S(2)}) collective-permute-start(bf16[64,1,4,128]{3,2,0,1:T(4,128)(2,1)S(1)} %multiply_convert_fusion.1), channel_id=1, source_target_pairs={{0,2},{2,4},{4,6},{6,8},{8,10},{10,12},{12,14},{14,16},{16,18},{18... | collective-permute-start | bytes 196616 | tf_op jit(solution)/shard_map/ppermute | solution.py:17
  597.4 65.2 %collective-permute-start.49 = (bf16[64,1,4,128]{3,2,0,1:T(4,128)(2,1)S(1)}, bf16[64,1,4,128]{3,2,0,1:T(4,128)(2,1)S(1)}, u32[]{:S(2)}, u32[]{:S(2)}) collective-permute-start(bf16[64,1,4,128]{3,2,0,1:T(4,128)(2,1)S(1)} %multiply_convert_fusion.1), channel_id=1, source_target_pairs={{2,0},{4,2},{6,4},{8,6},{10,8},{12,10},{14,12},{16,14},{18,16},{20... | collective-permute-start | bytes 196616 | tf_op jit(solution)/shard_map/ppermute | solution.py:19
  663.0 4.3 collective-permute-start.50
  664.0 4.1 collective-permute-start.51
  (276 other events, 1690.4 us)
Sparse Core Ops, SparseCore 0:
  571.4 158.4 all-reduce.3
where the time goes:
time: 763 us; the launch traced here: 751 us
  local copies, waits for them, and re-layouts  282 us (37%)
  other arithmetic  168 us (22%)
  waiting for transfers between devices  81.4 us (11%)
  starting transfers between devices  74 us (10%)
  matrix products  66.6 us (9%)
  blocking collectives  55 us (7%)
  between operations  24.3 us (3%)
    transpose x78, local copies, waits for them, and re-layouts, conv_padded(): weights_group.transpose(1, 0, 2).reshape(out_chans, 9 * channels)  131 us
    unnamed x383, other arithmetic  110 us
    psum x1, blocking collectives, per_device(): loss = lax.psum(local_loss, ('xy', 'gz')) / volume  55 us
    psum x1, waiting for transfers between devices, per_device(): lax.psum((first_weights, first_biases, mid_weights, mid_biases, last_weig...  44.5 us
    ppermute x26, starting transfers between devices, with_halo(): lax.ppermute(head, axis, [((i + 1) % count, i) for i in range(count)])  42.3 us
    dot_general x108, matrix products, conv_padded(): jnp.dot(flattened, unfold(window, -1, period), preferred_element_type=jnp...  32.4 us
    ppermute x26, starting transfers between devices, with_halo(): lax.ppermute(tail, axis, [(i, (i + 1) % count) for i in range(count)])  31.6 us
    unnamed x735, local copies, waits for them, and re-layouts  25.1 us
  transfers between devices with their start and end apart: 53, of which 31 were waited for; matrix products, arithmetic and copies ran while one was open for 46% of the time, Pallas kernels for 0%

commit v1 on v0

v1 whole, which is shorter than its diff:
```python
import functools

import jax
import jax.numpy as jnp
import numpy as np
from jax import lax
from jax.experimental import pallas as pl
from jax.experimental.pallas import tpu as pltpu
from jax.sharding import PartitionSpec as P

hopping = 0.3
quartic = 0.05

STEPS = (-1, 0, 1)
ROWS = 8
MID = 3
BF = jnp.bfloat16
F32 = jnp.float32
HIGH = lax.Precision.HIGHEST


def ring_order(count):
    if count % 4:
        return list(range(count))
    depth = count // 4
    chips = [(z, 0) for z in range(depth)] + [(z, 1) for z in reversed(range(depth))]
    order = []
    for place, (z, y) in enumerate(chips):
        cores = (0, 1) if place % 2 == 0 else (1, 0)
        order += [z * 4 + y * 2 + core for core in cores]
    return order


def spread_first():
    out = np.zeros((81, 5, 256), np.float32)
    for tap in range(81):
        dx, rest = divmod(tap, 27)
        for dest in range(5):
            out[tap, dest, rest * ROWS + dest + dx] = 1
    return out.reshape(81, 5 * 256)


def spread_last():
    out = np.zeros((216, 54), np.float32)
    for rest in range(27):
        for o in range(2):
            out[rest * 8 + o, rest * 2 + o] = 1
    return out


def spread_last_back():
    out = np.zeros((81, 2, 3, 512), np.float32)
    for tap in range(81):
        dx, rest = divmod(tap, 27)
        for o in range(2):
            for dest in range(3):
                out[tap, o, dest, rest * 16 + o * ROWS + 2 + dest - (dx - 1)] = 1
    return out.reshape(162, 3 * 512)


def spread_first_back():
    out = np.zeros((216, 81), np.float32)
    for tap in range(81):
        dx, rest = divmod(tap, 27)
        out[rest * 8 + dx, tap] = 1
    return out


def z_shift(values, dz):
    length = values.shape[1]
    return values if dz == 0 else pltpu.roll(values, (-dz * 128) % length, 1)


def by_plane(values, fn):
    parts = [fn(values[:, at : at + 128]) for at in range(0, values.shape[1], 128)]
    return parts[0] if len(parts) == 1 else jnp.concatenate(parts, axis=1)


def y_shift(values, dy, period):
    if dy == 0:
        return values
    return by_plane(values, lambda v: pltpu.roll(v, (-dy * period) % 128, 1))


def t_shift(values, dt, period):
    if dt == 0:
        return values

    def one(v):
        place = lax.broadcasted_iota(jnp.int32, v.shape, 1) % period
        main = pltpu.roll(v, (-dt) % 128, 1)
        wrap = pltpu.roll(v, (dt * (period - 1)) % 128, 1)
        return jnp.where(place == (period - 1 if dt == 1 else 0), wrap, main)

    return by_plane(values, one)


def all_shifts(values, sign, period):
    in_t = [t_shift(values, sign * dt, period) for dt in STEPS]
    in_y = [[y_shift(v, sign * dy, period) for v in in_t] for dy in STEPS]
    return [z_shift(in_y[dy][dt], sign * dz) for dz in STEPS for dy in range(3) for dt in range(3)]


def gather_narrow(values, sign, period):
    block = lambda k: values[k * 8 : k * 8 + 8]
    total = None
    for dt in range(3):
        over_y = None
        for dy in range(3):
            over_z = sum(z_shift(block(dz * 9 + dy * 3 + dt), sign * (dz - 1)) for dz in range(3))
            over_z = y_shift(over_z, sign * (dy - 1), period)
            over_y = over_z if over_y is None else over_y + over_z
        over_y = t_shift(over_y, sign * (dt - 1), period)
        total = over_y if total is None else total + over_y
    return total


def gather_wide(values, channels, sign, period):
    block = lambda k: values[k * channels : (k + 1) * channels]
    total = None
    for dt in range(3):
        over_y = None
        for dy in range(3):
            part = y_shift(block(dy * 3 + dt), sign * (dy - 1), period)
            over_y = part if over_y is None else over_y + part
        over_y = t_shift(over_y, sign * (dt - 1), period)
        total = over_y if total is None else total + over_y
    return total


def dot(a, b):
    return jnp.dot(a, b, preferred_element_type=F32)


def dot_nt(a, b):
    return lax.dot_general(a, b, (((1,), (1,)), ((), ())), preferred_element_type=F32)


def stack_planes(stack, planes, channels, order):
    length = stack.shape[1]
    for dx in range(3):
        for dz in range(3):
            plane, step = order(dx, dz)
            rows = pl.ds((dx * 3 + dz) * channels, channels)
            source = planes[plane * channels : (plane + 1) * channels, :]
            if step == 0:
                stack[rows, :] = source
            elif step == 1:
                stack[rows, : length - 128] = source[:, 128:]
                stack[rows, length - 128 :] = source[:, :128]
            else:
                stack[rows, 128:] = source[:, : length - 128]
                stack[rows, :128] = source[:, length - 128 :]


def place_windows(refs, row, target):
    target[...] = jnp.zeros_like(target)
    for r, ref in enumerate(refs):
        target[r : r + 1, :] = ref[row : row + 1, :]


def forward_kernel(
    period, layer, many, *refs
):
    windows, refs = refs[:many], refs[many:]
    (odd, w_first, b_first, w_mid, b_mid, w_last, b_last,
     field_out, state, first_out, second_out, logdet, first, stack, *scratch) = refs
    channels = w_mid.shape[0] // 9
    length = odd.shape[1]
    if many == 1:
        field_out[...] = windows[0][...]
    else:
        growth_out, = scratch
        place_windows(windows, 0, field_out)
        place_windows(windows, 1, growth_out)
    field = field_out[...]
    frozen = odd[...] if layer == 0 else 1.0 - odd[...]
    net = frozen * field
    taps = jnp.concatenate(all_shifts(net, 1, period), axis=0).astype(BF)
    for dest in range(5):
        part = dot(w_first[:, dest * 256 : dest * 256 + 216], taps)
        first[dest * channels : (dest + 1) * channels, :] = jnp.tanh(part + b_first[...]).astype(BF)
    first_out[...] = first[channels : 4 * channels, :]
    for dest in range(3):
        stack_planes(stack, first, channels, lambda dx, dz: (dest + dx, dz - 1))
        for at in range(0, length, 256):
            wide = dot(w_mid[...], stack[:, at : at + 256])
            wide = gather_wide(wide, channels, 1, period)
            second_out[dest * channels : (dest + 1) * channels, at : at + 256] = jnp.tanh(
                wide + b_mid[...]
            ).astype(BF)
    narrow = sum(
        dot(w_last[dx], second_out[dx * channels : (dx + 1) * channels, :]) for dx in range(3)
    )
    narrow = gather_narrow(narrow, 1, period) + b_last[...]
    growth = jnp.exp(narrow[0:1])
    mine = field[MID : MID + 1]
    still = frozen[MID : MID + 1]
    moving = 1.0 - still
    state[0:1, :] = still * mine + moving * (mine * growth + narrow[1:2])
    state[1:2, :] = growth
    flow = moving * narrow[0:1]
    logdet[...] = sum(flow[:, at : at + 128] for at in range(0, length, 128))


def backward_kernel(period, layer, *refs):
    if layer == 1:
        windows, refs = refs[:7], refs[7:]
        (odd, field_in, first_in, second_in, w_last, w_mid, w_first,
         base_out, part_out, action, g_first, gb_first, g_mid, gb_mid, g_last, gb_last,
         field_end, growth, stack, turned) = refs
        place_windows(windows, 0, field_end)
        place_windows(windows, 1, growth)
    else:
        windows, refs = refs[:7], refs[7:]
        (base_in, growth, odd, field_in, first_in, second_in, w_last, w_mid, w_first,
         part_out, g_first, gb_first, g_mid, gb_mid, g_last, gb_last,
         upstream_ref, stack, turned) = refs
    channels = w_mid.shape[0] // 9
    length = odd.shape[1]
    frozen = odd[...] if layer == 0 else 1.0 - odd[...]
    moving = 1.0 - frozen
    place = lax.broadcasted_iota(jnp.int32, (ROWS, length), 0)
    inner = jnp.logical_and(place >= 1, place <= 5)
    if layer == 1:
        field = field_end[...]
        ahead = (
            pltpu.roll(field, ROWS - 1, 0)
            + z_shift(field, 1)
            + y_shift(field, 1, period)
            + t_shift(field, 1, period)
        )
        behind = (
            pltpu.roll(field, 1, 0)
            + z_shift(field, -1)
            + y_shift(field, -1, period)
            + t_shift(field, -1, period)
        )
        squared = field * field
        density = (
            -2.0 * hopping * field * ahead
            + squared
            + quartic * (squared - 1.0) * (squared - 1.0)
        )[MID : MID + 1]
        action[...] = sum(density[:, at : at + 128] for at in range(0, length, 128))
        upstream = (
            -2.0 * hopping * (ahead + behind)
            + 2.0 * field
            + 4.0 * quartic * (squared - 1.0) * field
        )
        upstream = jnp.where(inner, upstream, 0.0)
    else:
        upstream_ref[...] = base_in[...]
        for r in range(1, 6):
            upstream_ref[r : r + 1, :] += (
                windows[r - 1][2:3, :] + windows[r][1:2, :] + windows[r + 1][0:1, :]
            )
        upstream = upstream_ref[...]
    grow = growth[...]
    grad_scale = upstream * moving * field_in[...] * grow - moving
    grad_shift = upstream * moving
    grad_output = jnp.where(
        jnp.concatenate([inner, inner], axis=0),
        jnp.concatenate([grad_scale, grad_shift], axis=0),
        0.0,
    )
    own = jnp.concatenate([grad_output[MID : MID + 1], grad_output[8 + MID : 9 + MID]], axis=0)
    gb_last[...] = jnp.sum(own.astype(BF).astype(F32), axis=1, keepdims=True)
    taps = jnp.concatenate(all_shifts(grad_output, -1, period), axis=0).astype(BF)
    g_last[...] = dot_nt(taps, second_in[channels : 2 * channels, :])
    mids = []
    for dest in range(3):
        part = dot(w_last[:, dest * 512 : dest * 512 + 432], taps)
        wide = second_in[dest * channels : (dest + 1) * channels, :].astype(F32)
        mids.append(part * (1.0 - wide * wide))
    gb_mid[...] = jnp.sum(mids[1].astype(BF).astype(F32), axis=1, keepdims=True)
    rounded = mids[1].astype(BF).astype(F32)
    in_t = [t_shift(rounded, -dt, period) for dt in STEPS]
    for dy in range(3):
        for dt in range(3):
            turned[(dy * 3 + dt) * channels : (dy * 3 + dt + 1) * channels, :] = y_shift(
                in_t[dt], -STEPS[dy], period
            ).astype(BF)
    stack_planes(stack, first_in, channels, lambda dx, dz: (dx, dz - 1))
    g_mid[...] = dot_nt(turned[...], stack[...])
    planes = jnp.concatenate([m.astype(BF) for m in mids], axis=0)
    stack_planes(stack, planes, channels, lambda dx, dz: (2 - dx, 1 - dz))
    firsts = []
    for at in range(0, length, 256):
        wide = dot(w_mid[...], stack[:, at : at + 256])
        wide = gather_wide(wide, channels, -1, period)
        seen = first_in[channels : 2 * channels, at : at + 256].astype(F32)
        firsts.append((wide * (1.0 - seen * seen)).astype(BF))
    grad_first = jnp.concatenate(firsts, axis=1)
    gb_first[...] = jnp.sum(grad_first.astype(F32), axis=1, keepdims=True)
    net = frozen * field_in[...]
    taps = jnp.concatenate(all_shifts(net, 1, period), axis=0).astype(BF)
    g_first[...] = dot_nt(taps, grad_first)
    narrow = gather_narrow(dot(w_first[...], grad_first), -1, period)
    base = upstream * (frozen + moving * grow)
    for d in range(3):
        row = frozen[MID - 1 + d : MID + d] * narrow[d : d + 1]
        if layer == 0 and d == 1:
            row = row + base[MID : MID + 1]
        part_out[d : d + 1, :] = row
    if layer == 1:
        base_out[...] = base


def kernel_call(body, outs, scratch, args, flops):
    vmem = pl.BlockSpec(memory_space=pltpu.VMEM)
    return pl.pallas_call(
        body,
        out_shape=tuple(outs),
        in_specs=[vmem] * len(args),
        out_specs=tuple([vmem] * len(outs)),
        scratch_shapes=scratch,
        compiler_params=pltpu.CompilerParams(vmem_limit_bytes=52 * 2**20),
        cost_estimate=pl.CostEstimate(flops=flops, bytes_accessed=4_000_000, transcendentals=500_000),
    )(*args)


def shape(dims, dtype=F32):
    return jax.ShapeDtypeStruct(dims, dtype)


def forward(period, layer, windows, odd, weights, channels):
    length = odd.shape[1]
    many = len(windows)
    outs = [
        shape((ROWS, length)),
        shape((2, length)),
        shape((3 * channels, length), BF),
        shape((3 * channels, length), BF),
        shape((1, 128)),
    ]
    scratch = [
        pltpu.VMEM((5 * channels, length), BF),
        pltpu.VMEM((9 * channels, length), BF),
    ]
    if many > 1:
        scratch.append(pltpu.VMEM((ROWS, length), F32))
    body = functools.partial(forward_kernel, period, layer, many)
    if many > 1:
        outs.append(shape((ROWS, length)))

        def body(*refs):
            ins = refs[: many + 7]
            field, state, first, second, logdet, growth = refs[many + 7 : many + 13]
            a, b, _ = refs[many + 13 :]
            forward_kernel(
                period, layer, many, *ins, field, state, first, second, logdet, a, b, growth
            )

    return kernel_call(body, outs, scratch, [*windows, odd, *weights], 3 * 2 * 81 * 64 * 64 * length)


def backward(period, layer, windows, extra, odd, field, first, second, weights, channels):
    length = odd.shape[1]
    grads = [
        shape((216, channels)),
        shape((channels, 1)),
        shape((9 * channels, 9 * channels)),
        shape((channels, 1)),
        shape((432, channels)),
        shape((2, 1)),
    ]
    if layer == 1:
        outs = [shape((ROWS, length)), shape((3, length)), shape((1, 128))] + grads
        scratch = [pltpu.VMEM((ROWS, length), F32), pltpu.VMEM((ROWS, length), F32)]
    else:
        outs = [shape((3, length))] + grads
        scratch = [pltpu.VMEM((ROWS, length), F32)]
    scratch += [pltpu.VMEM((9 * channels, length), BF), pltpu.VMEM((9 * channels, length), BF)]
    args = [*windows, *extra, odd, field, first, second, *weights]
    body = functools.partial(backward_kernel, period, layer)
    return kernel_call(body, outs, scratch, args, 2 * 2 * 81 * 64 * 64 * length)


def per_device(noise, w_first, b_first, w_mid, b_mid, w_last, b_last):
    period = noise.shape[3]
    count = lax.axis_size("xy")
    halves = lax.axis_size("gz")
    channels = w_mid.shape[2]
    order = ring_order(count)
    places = np.argsort(np.array(order))
    volume = float(noise.size * count * halves)
    place = jnp.asarray(places, jnp.int32)[lax.axis_index("xy")]
    half = lax.axis_index("gz")

    def step(values, offset):
        return lax.ppermute(
            values, "xy", [(order[(p + offset) % count], order[p]) for p in range(count)]
        )

    flat = noise.reshape(1, -1)
    whole = lax.all_gather(flat, "gz", axis=1, tiled=True)
    length = whole.shape[1]
    near = [
        lax.ppermute(whole, "xy", [((p + d) % count, order[p]) for p in range(count)])
        for d in STEPS
    ]
    near = jnp.concatenate(near, axis=0)
    below = step(near[0:2], -2)
    above = step(near[1:3], 2)
    window = jnp.concatenate([below, near, above, jnp.zeros_like(flat, shape=(1, length))], axis=0)

    lane = lax.broadcasted_iota(jnp.int32, (ROWS, length), 1)
    row = lax.broadcasted_iota(jnp.int32, (ROWS, length), 0)
    within = lane % 128
    odd = ((place + row + 1 + lane // 128 + within // period + within % period) % 2).astype(F32)

    first_spread = jnp.asarray(spread_first(), BF)
    last_spread = jnp.asarray(spread_last(), BF)
    last_back = jnp.asarray(spread_last_back(), BF)
    first_back = jnp.asarray(spread_first_back(), BF)
    ahead_weights, back_weights = [], []
    for layer in range(2):
        wf = w_first[layer, :, :, 0]
        wl = w_last[layer]
        wm = w_mid[layer].reshape(9, 9, channels, channels)
        narrow = jnp.stack(
            [dot(last_spread, wl[27 * dx : 27 * dx + 27].reshape(54, channels)) for dx in range(3)]
        ).astype(BF)
        tail = jnp.zeros((8, 1), F32).at[:2, 0].set(b_last[layer])
        ahead_weights.append((
            lax.dot_general(wf, first_spread, (((0,), (0,)), ((), ())), preferred_element_type=F32).astype(BF),
            b_first[layer][:, None],
            wm.transpose(1, 2, 0, 3).reshape(9 * channels, 9 * channels),
            b_mid[layer][:, None],
            narrow,
            tail,
        ))
        back_weights.append((
            lax.dot_general(
                wl.reshape(162, channels), last_back, (((0,), (0,)), ((), ())),
                preferred_element_type=F32,
            ).astype(BF),
            wm.transpose(1, 3, 0, 2).reshape(9 * channels, 9 * channels),
            dot(first_back, wf).astype(BF),
        ))

    def exchange(values):
        return [values if m == 0 else step(values, m) for m in range(-3, 4)]

    field0, state, first0, second0, logdet0 = forward(
        period, 0, [window], odd, ahead_weights[0], channels
    )
    field1, state, first1, second1, logdet1, growth0 = forward(
        period, 1, exchange(state), odd, ahead_weights[1], channels
    )

    def own_half(values):
        return lax.dynamic_slice_in_dim(values, half * (length // halves), length // halves, axis=1)

    sample = lax.ppermute(
        own_half(state[0:1]), "xy", [(order[p], p) for p in range(count)]
    )
    base, part, action, *grads1 = backward(
        period, 1, exchange(state), [], odd, field1, first1, second1, back_weights[1], channels
    )
    part, *grads0 = backward(
        period, 0, exchange(part), [base, growth0], odd, field0, first0, second0, back_weights[0],
        channels,
    )
    mine = own_half(part)
    force = sum(
        lax.ppermute(mine[d : d + 1], "xy", [(order[p], (p + d - 1) % count) for p in range(count)])
        for d in range(3)
    )
    loss = jnp.sum(action - logdet0 - logdet1)
    pairs = [jnp.stack([a, b]) for a, b in zip(grads0, grads1)]
    loss, pairs = lax.psum((loss, pairs), "xy")
    g_first, gb_first, g_mid, gb_mid, g_last, gb_last = [v / volume for v in pairs]
    g_first = g_first.reshape(2, 27, 8, channels)[:, :, 2:5].transpose(0, 2, 1, 3)
    g_mid = g_mid.reshape(2, 9, channels, 9, channels).transpose(0, 3, 1, 2, 4)
    g_last = g_last.reshape(2, 27, 2, 8, channels)[:, :, :, 4:1:-1].transpose(0, 3, 1, 2, 4)
    return (
        sample.reshape(noise.shape),
        force.reshape(noise.shape),
        loss / volume,
        g_first.reshape(2, 81, channels, 1),
        gb_first[:, :, 0],
        g_mid.reshape(2, 81, channels, channels),
        gb_mid[:, :, 0],
        g_last.reshape(2, 81, 2, channels),
        gb_last[:, :, 0],
    )


def solution(mesh):
    return jax.shard_map(
        per_device,
        mesh=mesh,
        in_specs=(P("xy", "gz", None, None), P(), P(), P(), P(), P(), P()),
        out_specs=(
            P("xy", "gz", None, None),
            P("xy", "gz", None, None),
            P(),
            P(),
            P(),
            P(),
            P(),
            P(),
            P(),
        ),
        check_vma=False,
    )
```

time: 763 us -> 265 us (0.35)
  local copies, waits for them, and re-layouts: 282 us -> 69.3 us
  other arithmetic: 168 us -> 13.2 us
  matrix products: 66.6 us -> 6.45 us
  starting transfers between devices: 74 us -> 44.1 us
  blocking collectives: 55 us -> 28.4 us
  Pallas kernels: 0 us -> 23.2 us
  waiting for transfers between devices: 81.4 us -> 59.5 us
  between operations: 24.3 us -> 16.4 us
    unnamed x383 -> x0, other arithmetic: 110 us -> none
    transpose x78 -> x5, local copies, waits for them, and re-layouts: 131 us -> 21.3 us  [the longest x2 8.67 us: per_device(): wm.transpose(1, 3, 0, 2).reshape(9 * channels, 9 * channels)]
    dot_general x162 -> x12, matrix products: 66.6 us -> 6.45 us  [the longest x8 3.69 us: dot(): return jnp.dot(a, b, preferred_element_type=F32)]
    ppermute x52 -> x27, waiting for transfers between devices: 36.9 us -> 1.89 us  [the longest x1 1.82 us: per_device(): lax.ppermute(own_half(state[0:1]), 'xy', [(order[p], p) for p in range(co...]
    concatenate x54 -> x1, local copies, waits for them, and re-layouts: 34 us -> 0.05 us  [per_device(): jnp.concatenate([below, near, above, jnp.zeros_like(flat, shape=(1, lengt...]
    ppermute x52 -> x27, starting transfers between devices: 73.9 us -> 44.1 us  [the longest x20 17.8 us: step(): lax.ppermute(values, 'xy', [(order[(p + offset) % count], order[p]) for p...]
    psum x1, blocking collectives: 55 us -> 25.2 us  [per_device(): loss, pairs = lax.psum((loss, pairs), 'xy')]
    dot_general x34 -> x0, local copies, waits for them, and re-layouts: 25.9 us -> none  [the longest x16 20.5 us: weights_from_input(): lax.dot_general(flat_grad, unfold(window, -1, period), (((1,), (1,)), (()...]
  transfers between devices with their start and end apart: 53 -> 28, of which waited for: 31 -> 2; matrix products, arithmetic and copies ran while one was open for 46% -> 23% of each run, Pallas kernels for 0% -> 0%
where the time goes in v1:
time: 265 us; the launch traced here: 261 us
  local copies, waits for them, and re-layouts  69.3 us (26%)
  waiting for transfers between devices  59.5 us (22%)
  starting transfers between devices  44.1 us (17%)
  blocking collectives  28.4 us (11%)
  Pallas kernels  23.2 us (9%)
  between operations  16.4 us (6%)
  other arithmetic  13.2 us (5%)
  matrix products  6.45 us (2%)
    psum x1, waiting for transfers between devices, per_device(): loss, pairs = lax.psum((loss, pairs), 'xy')  57.6 us
    psum x1, blocking collectives, per_device(): loss, pairs = lax.psum((loss, pairs), 'xy')  25.2 us
    pallas_call x4, Pallas kernels, kernel_call(): pl.pallas_call(body, out_shape=tuple(outs), in_specs=[vmem] * len(args),...  23.2 us
    ppermute x20, starting transfers between devices, step(): lax.ppermute(values, 'xy', [(order[(p + offset) % count], order[p]) for p...  17.8 us
    unnamed x21, local copies, waits for them, and re-layouts  14.4 us
    ppermute x3, starting transfers between devices, per_device(): lax.ppermute(whole, 'xy', [((p + d) % count, order[p]) for p in range(cou...  12.2 us
    ppermute x3, starting transfers between devices, per_device(): lax.ppermute(mine[d:d + 1], 'xy', [(order[p], (p + d - 1) % count) for p...  10.1 us
    transpose x2, local copies, waits for them, and re-layouts, per_device(): wm.transpose(1, 3, 0, 2).reshape(9 * channels, 9 * channels)  8.67 us
  transfers between devices with their start and end apart: 28, of which 2 were waited for; matrix products, arithmetic and copies ran while one was open for 23% of the time, Pallas kernels for 0%

profile of v1, /device:TPU:5, one launch (start us, length us, event | category | flops | bytes accessed | tf_op | source)
XLA Modules:
  0.0 260.6 jit_solution(533674324712889759)
XLA Ops:
  8.0 3.2 %all_gather.3 = f32[1,1024]{1,0:T(1,128)S(1)} all-gather(f32[1,512]{1,0:T(1,128)S(1)} %reshape.147), channel_id=1, replica_groups=mesh['xy'=16,'gz'=2] {'gz'}, dimensions={1}, use_global_device_ids=true | all-gather | bytes 6144 | tf_op jit(solution)/shard_map/all_gather | solution.py:397
  11.2 3.1 %collective-permute-start.3 = (f32[1,1024]{1,0:T(1,128)S(1)}, f32[1,1024]{1,0:T(1,128)S(1)}, u32[]{:S(2)}, u32[]{:S(2)}) collective-permute-start(f32[1,1024]{1,0:T(1,128)S(1)} %all_gather.3), channel_id=1, source_target_pairs={{2,0},{4,2},{6,10},{8,8},{10,16},{12,18},{14,26},{16,24},{18,28},{... | collective-permute-start | bytes 12296 | tf_op jit(solution)/shard_map/ppermute | solution.py:400
  14.3 2.4 collective-permute-start.1
  16.7 6.7 %collective-permute-start = (f32[1,1024]{1,0:T(1,128)S(1)}, f32[1,1024]{1,0:T(1,128)S(1)}, u32[]{:S(2)}, u32[]{:S(2)}) collective-permute-start(f32[1,1024]{1,0:T(1,128)S(1)} %all_gather.3), channel_id=1, source_target_pairs={{30,0},{0,2},{2,10},{4,8},{6,16},{8,18},{10,26},{12,24},{14,28},{1... | collective-permute-start | bytes 12296 | tf_op jit(solution)/shard_map/ppermute | solution.py:400
  35.2 3.0 %fusion.32 = (bf16[1,81,64,64]{1,3,2,0:T(8,128)(2,1)}, bf16[1,81,64,64]{1,3,2,0:T(8,128)(2,1)}) fusion(bf16[2,81,64,64]{1,3,2,0:T(8,128)(2,1)} %param.19), kind=kLoop, calls=%fused_computation.86 | loop fusion | bytes 2654208 | tf_op jit(solution)/shard_map/slice | solution.py:421
  41.1 3.2 %copy.116 = bf16[1,81,64,64]{3,2,1,0:T(8,128)(2,1)S(1)} copy(bf16[1,81,64,64]{1,3,2,0:T(8,128)(2,1)} %get-tuple-element.113) | data formatting | bytes 1327104
  44.4 2.5 copy.77
  46.9 3.9 %reshape.148.refs_4_ = bf16[576,576]{1,0:T(8,128)(2,1)} reshape(bf16[9,64,9,64]{3,2,1,0:T(8,128)(2,1)} %copy.77) | data formatting | bytes 1327104 | tf_op jit(solution)/shard_map/reshape | solution.py:429
  50.9 5.5 %shard_map.187 = (f32[8,1024]{1,0:T(8,128)S(1)}, f32[2,1024]{1,0:T(2,128)S(1)}, bf16[192,1024]{1,0:T(8,128)(2,1)S(1)}, bf16[192,1024]{1,0:T(8,128)(2,1)S(1)}, f32[1,128]{1,0:T(1,128)S(1)}) custom-call(f32[8,1024]{1,0:T(8,128)S(1)} %concatenate.17.refs_0_, f32[8,1024]{1,0:T(8,128)S(1)} %fusion.13.refs_1_.refs_7_.refs_9_, bf16[64,1280]{1,0:T(8,128)(2,1)S(1)} %fusion.refs_2_, ...), custom_call_target="tpu_custom_call" | custom-call | flops 2038431744 | bytes 4000000 | tf_op jit(solution)/shard_map/pallas_call | solution.py:312
  56.6 2.5 collective-permute-start.9
  62.5 3.2 %copy.117 = bf16[1,81,64,64]{3,2,1,0:T(8,128)(2,1)S(1)} copy(bf16[1,81,64,64]{1,3,2,0:T(8,128)(2,1)} %get-tuple-element.112) | data formatting | bytes 1327104
  65.7 2.5 copy.88
  68.2 3.9 %reshape.153.refs_10_ = bf16[576,576]{1,0:T(8,128)(2,1)} reshape(bf16[9,64,9,64]{3,2,1,0:T(8,128)(2,1)} %copy.88) | data formatting | bytes 1327104 | tf_op jit(solution)/shard_map/reshape | solution.py:429
  72.2 5.6 %shard_map.188 = (f32[8,1024]{1,0:T(8,128)S(1)}, f32[2,1024]{1,0:T(2,128)S(1)}, bf16[192,1024]{1,0:T(8,128)(2,1)S(1)}, bf16[192,1024]{1,0:T(8,128)(2,1)S(1)}, f3...) custom-call(f32[2,1024]{1,0:T(2,128)S(1)} %collective-permute-done.5.refs_0_, f32[2,1024]{1,0:T(2,128)S(1)} %collective-permute-done.6.refs_1_, ...), custom_call_target="tpu_custom_call" | custom-call | flops 2038431744 | bytes 4000000 | tf_op jit(solution)/shard_map/pallas_call | solution.py:312
  83.9 4.3 %copy.99 = bf16[9,64,9,64]{3,2,1,0:T(8,128)(2,1)} copy(bf16[9,64,9,64]{1,3,0,2:T(8,128)(2,1)} %bitcast.108) | data formatting | bytes 1327104 | tf_op jit(solution)/shard_map/transpose | solution.py:439
  88.2 3.9 %reshape.159.refs_12_ = bf16[576,576]{1,0:T(8,128)(2,1)} reshape(bf16[9,64,9,64]{3,2,1,0:T(8,128)(2,1)} %copy.99) | data formatting | bytes 1327104 | tf_op jit(solution)/shard_map/reshape | solution.py:439
  92.2 6.1 %shard_map.189 = (f32[8,1024]{1,0:T(8,128)S(1)}, f32[3,1024]{1,0:T(4,128)S(1)}, f32[1,128]{1,0:T(1,128)S(1)}, f32[216,64]{1,0:T(8,128)S(1)}, f32[64,1]{1,0:T(8,1...) custom-call(f32[2,1024]{1,0:T(2,128)S(1)} %collective-permute-done.12.refs_0_, ...), custom_call_target="tpu_custom_call" | custom-call | flops 1358954496 | bytes 4000000 | tf_op jit(solution)/shard_map/pallas_call | solution.py:312
  104.1 4.3 %copy.102 = bf16[9,64,9,64]{3,2,1,0:T(8,128)(2,1)} copy(bf16[9,64,9,64]{1,3,0,2:T(8,128)(2,1)} %bitcast.106) | data formatting | bytes 1327104 | tf_op jit(solution)/shard_map/transpose | solution.py:439
  108.5 3.9 %reshape.160.refs_14_ = bf16[576,576]{1,0:T(8,128)(2,1)} reshape(bf16[9,64,9,64]{3,2,1,0:T(8,128)(2,1)} %copy.102) | data formatting | bytes 1327104 | tf_op jit(solution)/shard_map/reshape | solution.py:439
  112.4 6.0 %shard_map.190 = (f32[3,1024]{1,0:T(4,128)S(1)}, f32[216,64]{1,0:T(8,128)S(1)}, f32[64,1]{1,0:T(8,128)S(1)}, f32[576,576]{1,0:T(8,128)}, f32[64,1]{1,0:T(8,128)S...) custom-call(f32[3,1024]{1,0:T(4,128)S(1)} %collective-permute-done.18.refs_0_, ...), custom_call_target="tpu_custom_call" | custom-call | flops 1358954496 | bytes 4000000 | tf_op jit(solution)/shard_map/pallas_call | solution.py:312
  120.0 3.2 %pad_maximum_fusion = f32[2,576,576]{2,1,0:T(8,128)} fusion(f32[1,576,576]{2,1,0:T(8,128)S(1)} %bitcast.109, f32[1,576,576]{2,1,0:T(8,128)} %bitcast.110), kind=kLoop, calls=%fused_computation | loop fusion | flops 663552 | bytes 5308416 | tf_op jit(solution)/shard_map/stack | solution.py:472
  123.2 4.0 %collective-permute-start.11 = (f32[1,512]{1,0:T(1,128)S(1)}, f32[1,512]{1,0:T(1,128)S(1)}, u32[]{:S(2)}, u32[]{:S(2)}) collective-permute-start(f32[1,512]{1,0:T(1,128)S(1)} %constant_dynamic-slice_fusion.1), channel_id=1, source_target_pairs={{0,0},{2,2},{10,4},{8,6},{16,8},{18,10},{26,12},{24,14},{28,16},{3... | collective-permute-start | bytes 6152 | tf_op jit(solution)/shard_map/ppermute | solution.py:456
  127.2 1.8 collective-permute-done.11
  132.3 4.9 %collective-permute-start.25 = (f32[1,512]{1,0:T(1,128)S(1)}, f32[1,512]{1,0:T(1,128)S(1)}, u32[]{:S(2)}, u32[]{:S(2)}) collective-permute-start(f32[1,512]{1,0:T(1,128)S(1)} %get-tuple-element.122), channel_id=1, source_target_pairs={{0,0},{2,2},{10,4},{8,6},{16,8},{18,10},{26,12},{24,14},{28,16},{3... | collective-permute-start | bytes 6152 | tf_op jit(solution)/shard_map/ppermute | solution.py:468
  137.1 3.3 %collective-permute-start.24 = (f32[1,512]{1,0:T(1,128)S(1)}, f32[1,512]{1,0:T(1,128)S(1)}, u32[]{:S(2)}, u32[]{:S(2)}) collective-permute-start(f32[1,512]{1,0:T(1,128)S(1)} %get-tuple-element.123), channel_id=1, source_target_pairs={{0,30},{2,0},{10,2},{8,4},{16,6},{18,8},{26,10},{24,12},{28,14},{3... | collective-permute-start | bytes 6152 | tf_op jit(solution)/shard_map/ppermute | solution.py:468
  140.5 1.9 collective-permute-start.26
  142.4 25.2 %all-reduce.2 = (f32[]{:T(128)}, f32[2,64,1]{1,2,0:T(1,128)S(1)}, f32[2,64,1]{1,2,0:T(1,128)S(1)}, f32[2,2,1]{1,2,0:T(1,128)S(1)}) all-reduce(f32[]{:T(128)} %subtract_reduce_fusion, f32[2,64,1]{1,2,0:T(1,128)S(1)} %pad_maximum_fusion.7, f32[2,64,1]{1,2,0:T(1,128)S(1)} %pad_maximum_fusion.8, ...), channel_id=1, replica_groups=mesh['xy'=16,'gz'=2] {'xy'}, use_global_device_ids=true, to_apply=%region_1.2 | all-reduce | flops 261 | bytes 2088 | tf_op jit(solution)/shard_map/psum | solution.py:473
  170.7 57.6 %all-reduce.6.cloned.1.call-done = (f32[2,216,64]{2,1,0:T(8,128)}, f32[2,576,576]{2,1,0:T(8,128)}, f32[2,432,64]{2,1,0:T(8,128)}) async-done(((f32[2,216,64]{2,1,0:T(8,128)}, f32[2,576,576]{2,1,0:T(8,128)}, f32[2,432,64]{2,1,0:T(8,128)}), (f32[2,216,64]{2,1,0:T(8,128)}, f32[2,576,576]{2,1,0:T(8,128)}, f32[2,432,64]{2,1,0:T(8,128)})) %all-reduce.6.cloned.1.call-update) | async-done | bytes 2986000 | tf_op jit(solution)/shard_map/psum | solution.py:473
  232.1 2.0 broadcast_multiply_fusion
  234.1 4.4 %reshape.164 = f32[2,9,64,9,64]{4,3,2,1,0:T(8,128)} reshape(f32[2,576,576]{2,1,0:T(8,128)S(1)} %broadcast_multiply_fusion) | data formatting | bytes 5308416 | tf_op jit(solution)/shard_map/reshape | solution.py:476
  238.5 7.7 %copy.105 = f32[2,9,9,64,64]{4,3,2,1,0:T(8,128)} copy(f32[2,9,9,64,64]{4,1,3,2,0:T(8,128)} %bitcast.103) | data formatting | bytes 5308416 | tf_op jit(solution)/shard_map/transpose | solution.py:476
  246.2 6.4 %copy.108 = f32[2,81,64,64]{1,3,2,0:T(8,128)} copy(f32[2,81,64,64]{3,2,1,0:T(8,128)} %bitcast.104) | data formatting | bytes 5308416
  (148 shorter events, 41.8 us)
Async XLA Ops:
  7.2 221.2 %all-reduce.6.cloned.1.call-start = ((), (), s32[]{:S(2)}) async-start(), calls=%async_computation | async-start | bytes 7225344 | tf_op jit(solution)/shard_map/psum | solution.py:473
  11.2 27.5 %collective-permute-start.3 = (f32[1,1024]{1,0:T(1,128)S(1)}, f32[1,1024]{1,0:T(1,128)S(1)}, u32[]{:S(2)}, u32[]{:S(2)}) collective-permute-start(f32[1,1024]{1,0:T(1,128)S(1)} %all_gather.3), channel_id=1, source_target_pairs={{2,0},{4,2},{6,10},{8,8},{10,16},{12,18},{14,26},{16,24},{18,28},{... | collective-permute-start | bytes 12296 | tf_op jit(solution)/shard_map/ppermute | solution.py:400
  14.3 24.4 %collective-permute-start.1 = (f32[1,1024]{1,0:T(1,128)S(1)}, f32[1,1024]{1,0:T(1,128)S(1)}, u32[]{:S(2)}, u32[]{:S(2)}) collective-permute-start(f32[1,1024]{1,0:T(1,128)S(1)} %all_gather.3), channel_id=1, source_target_pairs={{0,0},{2,2},{4,10},{6,8},{8,16},{10,18},{12,26},{14,24},{16,28},{1... | collective-permute-start | bytes 12296 | tf_op jit(solution)/shard_map/ppermute | solution.py:400
  16.7 22.0 %collective-permute-start = (f32[1,1024]{1,0:T(1,128)S(1)}, f32[1,1024]{1,0:T(1,128)S(1)}, u32[]{:S(2)}, u32[]{:S(2)}) collective-permute-start(f32[1,1024]{1,0:T(1,128)S(1)} %all_gather.3), channel_id=1, source_target_pairs={{30,0},{0,2},{2,10},{4,8},{6,16},{8,18},{10,26},{12,24},{14,28},{1... | collective-permute-start | bytes 12296 | tf_op jit(solution)/shard_map/ppermute | solution.py:400
  25.7 12.7 %copy-start.3 = (bf16[216,54]{1,0:T(8,128)(2,1)S(1)}, bf16[216,54]{1,0:T(8,128)(2,1)}, u32[]{:S(2)}) copy-start(bf16[216,54]{1,0:T(8,128)(2,1)} %constant.154.clone) | copy-start | bytes 69988
  38.8 12.1 %collective-permute-start.4 = (f32[2,1024]{1,0:T(2,128)S(1)}, f32[2,1024]{1,0:T(2,128)S(1)}, u32[]{:S(2)}, u32[]{:S(2)}) collective-permute-start(f32[2,1024]{1,0:T(2,128)S(1)} %get-tuple-element.125), channel_id=1, source_target_pairs={{10,0},{8,2},{16,10},{18,8},{26,16},{24,18},{28,26},{30,24},{22,28... | collective-permute-start | bytes 24584 | tf_op jit(solution)/shard_map/ppermute | solution.py:392
  39.3 11.6 %collective-permute-start.2 = (f32[2,1024]{1,0:T(2,128)S(1)}, f32[2,1024]{1,0:T(2,128)S(1)}, u32[]{:S(2)}, u32[]{:S(2)}) collective-permute-start(f32[2,1024]{1,0:T(2,128)S(1)} %get-tuple-element.126), channel_id=1, source_target_pairs={{6,0},{4,2},{0,10},{2,8},{10,16},{8,18},{16,26},{18,24},{26,28},{2... | collective-permute-start | bytes 24584 | tf_op jit(solution)/shard_map/ppermute | solution.py:392
  56.4 3.8 %collective-permute-start.10 = (f32[2,1024]{1,0:T(2,128)S(1)}, f32[2,1024]{1,0:T(2,128)S(1)}, u32[]{:S(2)}, u32[]{:S(2)}) collective-permute-start(f32[2,1024]{1,0:T(2,128)S(1)} %get-tuple-element.60.refs_3_), channel_id=1, source_target_pairs={{8,0},{16,2},{18,10},{26,8},{24,16},{28,18},{30,26},{22,24},{20,28... | collective-permute-start | bytes 24584 | tf_op jit(solution)/shard_map/ppermute | solution.py:392
  56.6 15.5 %collective-permute-start.9 = (f32[2,1024]{1,0:T(2,128)S(1)}, f32[2,1024]{1,0:T(2,128)S(1)}, u32[]{:S(2)}, u32[]{:S(2)}) collective-permute-start(f32[2,1024]{1,0:T(2,128)S(1)} %get-tuple-element.60.refs_3_), channel_id=1, source_target_pairs={{10,0},{8,2},{16,10},{18,8},{26,16},{24,18},{28,26},{30,24},{22,28... | collective-permute-start | bytes 24584 | tf_op jit(solution)/shard_map/ppermute | solution.py:392
  59.2 12.9 %collective-permute-start.8 = (f32[2,1024]{1,0:T(2,128)S(1)}, f32[2,1024]{1,0:T(2,128)S(1)}, u32[]{:S(2)}, u32[]{:S(2)}) collective-permute-start(f32[2,1024]{1,0:T(2,128)S(1)} %get-tuple-element.60.refs_3_), channel_id=1, source_target_pairs={{2,0},{10,2},{8,10},{16,8},{18,16},{26,18},{24,26},{28,24},{30,28}... | collective-permute-start | bytes 24584 | tf_op jit(solution)/shard_map/ppermute | solution.py:392
  59.2 13.0 %collective-permute-start.7 = (f32[2,1024]{1,0:T(2,128)S(1)}, f32[2,1024]{1,0:T(2,128)S(1)}, u32[]{:S(2)}, u32[]{:S(2)}) collective-permute-start(f32[2,1024]{1,0:T(2,128)S(1)} %get-tuple-element.60.refs_3_), channel_id=1, source_target_pairs={{4,0},{0,2},{2,10},{10,8},{8,16},{16,18},{18,26},{26,24},{24,28},{... | collective-permute-start | bytes 24584 | tf_op jit(solution)/shard_map/ppermute | solution.py:392
  59.7 12.5 %collective-permute-start.6 = (f32[2,1024]{1,0:T(2,128)S(1)}, f32[2,1024]{1,0:T(2,128)S(1)}, u32[]{:S(2)}, u32[]{:S(2)}) collective-permute-start(f32[2,1024]{1,0:T(2,128)S(1)} %get-tuple-element.60.refs_3_), channel_id=1, source_target_pairs={{6,0},{4,2},{0,10},{2,8},{10,16},{8,18},{16,26},{18,24},{26,28},{2... | collective-permute-start | bytes 24584 | tf_op jit(solution)/shard_map/ppermute | solution.py:392
  60.2 11.9 %collective-permute-start.5 = (f32[2,1024]{1,0:T(2,128)S(1)}, f32[2,1024]{1,0:T(2,128)S(1)}, u32[]{:S(2)}, u32[]{:S(2)}) collective-permute-start(f32[2,1024]{1,0:T(2,128)S(1)} %get-tuple-element.60.refs_3_), channel_id=1, source_target_pairs={{14,0},{6,2},{4,10},{0,8},{2,16},{10,18},{8,26},{16,24},{18,28},{2... | collective-permute-start | bytes 24584 | tf_op jit(solution)/shard_map/ppermute | solution.py:392
  72.1 11.3 %copy-start.5 = (bf16[216,81]{1,0:T(8,128)(2,1)S(1)}, bf16[216,81]{1,0:T(8,128)(2,1)}, u32[]{:S(2)}) copy-start(bf16[216,81]{1,0:T(8,128)(2,1)} %constant.156.clone) | copy-start | bytes 104980
  72.1 11.3 %copy-start.6 = (bf16[2,81,64,1]{1,2,3,0:T(8,128)(2,1)S(1)}, bf16[2,81,64,1]{1,2,3,0:T(8,128)(2,1)}, u32[]{:S(2)}) copy-start(bf16[2,81,64,1]{1,2,3,0:T(8,128)(2,1)} %param.17) | copy-start | bytes 62212
  77.7 3.9 %collective-permute-start.17 = (f32[2,1024]{1,0:T(2,128)S(1)}, f32[2,1024]{1,0:T(2,128)S(1)}, u32[]{:S(2)}, u32[]{:S(2)}) collective-permute-start(f32[2,1024]{1,0:T(2,128)S(1)} %get-tuple-element.61.refs_3_), channel_id=1, source_target_pairs={{8,0},{16,2},{18,10},{26,8},{24,16},{28,18},{30,26},{22,24},{20,28... | collective-permute-start | bytes 24584 | tf_op jit(solution)/shard_map/ppermute | solution.py:392
  79.0 13.1 %collective-permute-start.16 = (f32[2,1024]{1,0:T(2,128)S(1)}, f32[2,1024]{1,0:T(2,128)S(1)}, u32[]{:S(2)}, u32[]{:S(2)}) collective-permute-start(f32[2,1024]{1,0:T(2,128)S(1)} %get-tuple-element.61.refs_3_), channel_id=1, source_target_pairs={{10,0},{8,2},{16,10},{18,8},{26,16},{24,18},{28,26},{30,24},{22,28... | collective-permute-start | bytes 24584 | tf_op jit(solution)/shard_map/ppermute | solution.py:392
  80.4 11.8 %collective-permute-start.15 = (f32[2,1024]{1,0:T(2,128)S(1)}, f32[2,1024]{1,0:T(2,128)S(1)}, u32[]{:S(2)}, u32[]{:S(2)}) collective-permute-start(f32[2,1024]{1,0:T(2,128)S(1)} %get-tuple-element.61.refs_3_), channel_id=1, source_target_pairs={{2,0},{10,2},{8,10},{16,8},{18,16},{26,18},{24,26},{28,24},{30,28}... | collective-permute-start | bytes 24584 | tf_op jit(solution)/shard_map/ppermute | solution.py:392
  81.0 11.1 %collective-permute-start.14 = (f32[2,1024]{1,0:T(2,128)S(1)}, f32[2,1024]{1,0:T(2,128)S(1)}, u32[]{:S(2)}, u32[]{:S(2)}) collective-permute-start(f32[2,1024]{1,0:T(2,128)S(1)} %get-tuple-element.61.refs_3_), channel_id=1, source_target_pairs={{4,0},{0,2},{2,10},{10,8},{8,16},{16,18},{18,26},{26,24},{24,28},{... | collective-permute-start | bytes 24584 | tf_op jit(solution)/shard_map/ppermute | solution.py:392
  81.0 11.1 %collective-permute-start.13 = (f32[2,1024]{1,0:T(2,128)S(1)}, f32[2,1024]{1,0:T(2,128)S(1)}, u32[]{:S(2)}, u32[]{:S(2)}) collective-permute-start(f32[2,1024]{1,0:T(2,128)S(1)} %get-tuple-element.61.refs_3_), channel_id=1, source_target_pairs={{6,0},{4,2},{0,10},{2,8},{10,16},{8,18},{16,26},{18,24},{26,28},{2... | collective-permute-start | bytes 24584 | tf_op jit(solution)/shard_map/ppermute | solution.py:392
  81.7 10.5 %collective-permute-start.12 = (f32[2,1024]{1,0:T(2,128)S(1)}, f32[2,1024]{1,0:T(2,128)S(1)}, u32[]{:S(2)}, u32[]{:S(2)}) collective-permute-start(f32[2,1024]{1,0:T(2,128)S(1)} %get-tuple-element.61.refs_3_), channel_id=1, source_target_pairs={{14,0},{6,2},{4,10},{0,8},{2,16},{10,18},{8,26},{16,24},{18,28},{2... | collective-permute-start | bytes 24584 | tf_op jit(solution)/shard_map/ppermute | solution.py:392
  98.3 3.9 %collective-permute-start.23 = (f32[3,1024]{1,0:T(4,128)S(1)}, f32[3,1024]{1,0:T(4,128)S(1)}, u32[]{:S(2)}, u32[]{:S(2)}) collective-permute-start(f32[3,1024]{1,0:T(4,128)S(1)} %get-tuple-element.65.refs_3_), channel_id=1, source_target_pairs={{8,0},{16,2},{18,10},{26,8},{24,16},{28,18},{30,26},{22,24},{20,28... | collective-permute-start | bytes 36872 | tf_op jit(solution)/shard_map/ppermute | solution.py:392
  99.5 12.9 %collective-permute-start.22 = (f32[3,1024]{1,0:T(4,128)S(1)}, f32[3,1024]{1,0:T(4,128)S(1)}, u32[]{:S(2)}, u32[]{:S(2)}) collective-permute-start(f32[3,1024]{1,0:T(4,128)S(1)} %get-tuple-element.65.refs_3_), channel_id=1, source_target_pairs={{10,0},{8,2},{16,10},{18,8},{26,16},{24,18},{28,26},{30,24},{22,28... | collective-permute-start | bytes 36872 | tf_op jit(solution)/shard_map/ppermute | solution.py:392
  100.8 11.6 %collective-permute-start.21 = (f32[3,1024]{1,0:T(4,128)S(1)}, f32[3,1024]{1,0:T(4,128)S(1)}, u32[]{:S(2)}, u32[]{:S(2)}) collective-permute-start(f32[3,1024]{1,0:T(4,128)S(1)} %get-tuple-element.65.refs_3_), channel_id=1, source_target_pairs={{2,0},{10,2},{8,10},{16,8},{18,16},{26,18},{24,26},{28,24},{30,28}... | collective-permute-start | bytes 36872 | tf_op jit(solution)/shard_map/ppermute | solution.py:392
  101.5 10.9 %collective-permute-start.20 = (f32[3,1024]{1,0:T(4,128)S(1)}, f32[3,1024]{1,0:T(4,128)S(1)}, u32[]{:S(2)}, u32[]{:S(2)}) collective-permute-start(f32[3,1024]{1,0:T(4,128)S(1)} %get-tuple-element.65.refs_3_), channel_id=1, source_target_pairs={{4,0},{0,2},{2,10},{10,8},{8,16},{16,18},{18,26},{26,24},{24,28},{... | collective-permute-start | bytes 36872 | tf_op jit(solution)/shard_map/ppermute | solution.py:392
  101.5 10.9 %collective-permute-start.19 = (f32[3,1024]{1,0:T(4,128)S(1)}, f32[3,1024]{1,0:T(4,128)S(1)}, u32[]{:S(2)}, u32[]{:S(2)}) collective-permute-start(f32[3,1024]{1,0:T(4,128)S(1)} %get-tuple-element.65.refs_3_), channel_id=1, source_target_pairs={{6,0},{4,2},{0,10},{2,8},{10,16},{8,18},{16,26},{18,24},{26,28},{2... | collective-permute-start | bytes 36872 | tf_op jit(solution)/shard_map/ppermute | solution.py:392
  102.2 10.3 %collective-permute-start.18 = (f32[3,1024]{1,0:T(4,128)S(1)}, f32[3,1024]{1,0:T(4,128)S(1)}, u32[]{:S(2)}, u32[]{:S(2)}) collective-permute-start(f32[3,1024]{1,0:T(4,128)S(1)} %get-tuple-element.65.refs_3_), channel_id=1, source_target_pairs={{14,0},{6,2},{4,10},{0,8},{2,16},{10,18},{8,26},{16,24},{18,28},{2... | collective-permute-start | bytes 36872 | tf_op jit(solution)/shard_map/ppermute | solution.py:392
  112.4 7.6 %copy-start.4 = (f32[576,576]{1,0:T(8,128)S(1)}, f32[576,576]{1,0:T(8,128)}, u32[]{:S(2)}) copy-start(f32[576,576]{1,0:T(8,128)} %get-tuple-element.80) | copy-start | bytes 3981316
  123.2 5.8 %collective-permute-start.11 = (f32[1,512]{1,0:T(1,128)S(1)}, f32[1,512]{1,0:T(1,128)S(1)}, u32[]{:S(2)}, u32[]{:S(2)}) collective-permute-start(f32[1,512]{1,0:T(1,128)S(1)} %constant_dynamic-slice_fusion.1), channel_id=1, source_target_pairs={{0,0},{2,2},{10,4},{8,6},{16,8},{18,10},{26,12},{24,14},{28,16},{3... | collective-permute-start | bytes 6152 | tf_op jit(solution)/shard_map/ppermute | solution.py:456
  132.3 37.8 %collective-permute-start.25 = (f32[1,512]{1,0:T(1,128)S(1)}, f32[1,512]{1,0:T(1,128)S(1)}, u32[]{:S(2)}, u32[]{:S(2)}) collective-permute-start(f32[1,512]{1,0:T(1,128)S(1)} %get-tuple-element.122), channel_id=1, source_target_pairs={{0,0},{2,2},{10,4},{8,6},{16,8},{18,10},{26,12},{24,14},{28,16},{3... | collective-permute-start | bytes 6152 | tf_op jit(solution)/shard_map/ppermute | solution.py:468
  137.1 32.9 %collective-permute-start.24 = (f32[1,512]{1,0:T(1,128)S(1)}, f32[1,512]{1,0:T(1,128)S(1)}, u32[]{:S(2)}, u32[]{:S(2)}) collective-permute-start(f32[1,512]{1,0:T(1,128)S(1)} %get-tuple-element.123), channel_id=1, source_target_pairs={{0,30},{2,0},{10,2},{8,4},{16,6},{18,8},{26,10},{24,12},{28,14},{3... | collective-permute-start | bytes 6152 | tf_op jit(solution)/shard_map/ppermute | solution.py:468
  140.5 29.5 %collective-permute-start.26 = (f32[1,512]{1,0:T(1,128)S(1)}, f32[1,512]{1,0:T(1,128)S(1)}, u32[]{:S(2)}, u32[]{:S(2)}) collective-permute-start(f32[1,512]{1,0:T(1,128)S(1)} %get-tuple-element.124), channel_id=1, source_target_pairs={{0,2},{2,4},{10,6},{8,8},{16,10},{18,12},{26,14},{24,16},{28,18},{... | collective-permute-start | bytes 6152 | tf_op jit(solution)/shard_map/ppermute | solution.py:468
  (3 other events, 19.6 us)
Sparse Core Ops, SparseCore 0:
  123.3 104.9 all-reduce.5

commit v2 on v1

v2 whole, which is shorter than its diff:
```python
import functools

import jax
import jax.numpy as jnp
import numpy as np
from jax import lax
from jax.experimental import pallas as pl
from jax.experimental.pallas import tpu as pltpu
from jax.sharding import PartitionSpec as P

hopping = 0.3
quartic = 0.05

STEPS = (-1, 0, 1)
ROWS = 8
MID = 3
BF = jnp.bfloat16
F32 = jnp.float32
TAPS = 81


def ring_order(count):
    if count % 4:
        return list(range(count))
    depth = count // 4
    chips = [(z, 0) for z in range(depth)] + [(z, 1) for z in reversed(range(depth))]
    order = []
    for place, (z, y) in enumerate(chips):
        cores = (0, 1) if place % 2 == 0 else (1, 0)
        order += [z * 4 + y * 2 + core for core in cores]
    return order


def spread_first():
    out = np.zeros((81, 5, 256), np.float32)
    for tap in range(81):
        dx, rest = divmod(tap, 27)
        for dest in range(5):
            out[tap, dest, rest * ROWS + dest + dx] = 1
    return out.reshape(81, 5 * 256)


def spread_last():
    out = np.zeros((3, 2, 216, 81), np.float32)
    for tap in range(81):
        dx, rest = divmod(tap, 27)
        for o in range(2):
            out[dx, o, rest * 8 + o, tap] = 1
    return out


def spread_last_back():
    out = np.zeros((2, 81, 3, 512), np.float32)
    for tap in range(81):
        dx, rest = divmod(tap, 27)
        for o in range(2):
            for dest in range(3):
                out[o, tap, dest, rest * 16 + o * ROWS + 2 + dest - (dx - 1)] = 1
    return out.reshape(2, 81, 3 * 512)


def spread_first_back():
    out = np.zeros((216, 81), np.float32)
    for tap in range(81):
        dx, rest = divmod(tap, 27)
        out[rest * 8 + dx, tap] = 1
    return out


def pick_last():
    out = np.zeros((432, 2, 128), np.float32)
    for tap in range(81):
        dx, rest = divmod(tap, 27)
        for o in range(2):
            out[rest * 16 + o * ROWS + MID - (dx - 1), o, tap] = 1
    return out.reshape(432, 256)


def pick_first():
    out = np.zeros((216, 128), np.float32)
    for tap in range(81):
        dx, rest = divmod(tap, 27)
        out[rest * ROWS + MID + dx - 1, tap] = 1
    return out


def z_shift(values, dz):
    length = values.shape[1]
    return values if dz == 0 else pltpu.roll(values, (-dz * 128) % length, 1)


def by_plane(values, fn):
    parts = [fn(values[:, at : at + 128]) for at in range(0, values.shape[1], 128)]
    return parts[0] if len(parts) == 1 else jnp.concatenate(parts, axis=1)


def y_shift(values, dy, period):
    if dy == 0:
        return values
    return by_plane(values, lambda v: pltpu.roll(v, (-dy * period) % 128, 1))


def t_shift(values, dt, period):
    if dt == 0:
        return values

    def one(v):
        place = lax.broadcasted_iota(jnp.int32, v.shape, 1) % period
        main = pltpu.roll(v, (-dt) % 128, 1)
        wrap = pltpu.roll(v, (dt * (period - 1)) % 128, 1)
        return jnp.where(place == (period - 1 if dt == 1 else 0), wrap, main)

    return by_plane(values, one)


def all_shifts(values, sign, period):
    in_t = [t_shift(values, sign * dt, period) for dt in STEPS]
    in_y = [[y_shift(v, sign * dy, period) for v in in_t] for dy in STEPS]
    return [z_shift(in_y[dy][dt], sign * dz) for dz in STEPS for dy in range(3) for dt in range(3)]


def gather_narrow(values, sign, period):
    block = lambda k: values[k * 8 : k * 8 + 8]
    total = None
    for dt in range(3):
        over_y = None
        for dy in range(3):
            over_z = sum(z_shift(block(dz * 9 + dy * 3 + dt), sign * (dz - 1)) for dz in range(3))
            over_z = y_shift(over_z, sign * (dy - 1), period)
            over_y = over_z if over_y is None else over_y + over_z
        over_y = t_shift(over_y, sign * (dt - 1), period)
        total = over_y if total is None else total + over_y
    return total


def gather_wide(values, channels, sign, period):
    block = lambda k: values[k * channels : (k + 1) * channels]
    total = None
    for dt in range(3):
        over_y = None
        for dy in range(3):
            part = y_shift(block(dy * 3 + dt), sign * (dy - 1), period)
            over_y = part if over_y is None else over_y + part
        over_y = t_shift(over_y, sign * (dt - 1), period)
        total = over_y if total is None else total + over_y
    return total


def dot(a, b):
    return jnp.dot(a, b, preferred_element_type=F32)


def dot_nt(a, b):
    return lax.dot_general(a, b, (((1,), (1,)), ((), ())), preferred_element_type=F32)


def stack_planes(stack, planes, channels, order):
    length = stack.shape[1]
    for dx in range(3):
        for dz in range(3):
            plane, step = order(dx, dz)
            rows = pl.ds((dx * 3 + dz) * channels, channels)
            source = planes[plane * channels : (plane + 1) * channels, :]
            if step == 0:
                stack[rows, :] = source
            elif step == 1:
                stack[rows, : length - 128] = source[:, 128:]
                stack[rows, length - 128 :] = source[:, :128]
            else:
                stack[rows, 128:] = source[:, : length - 128]
                stack[rows, :128] = source[:, length - 128 :]


def pack_kernel(w_mid, w_first, w_last, pick_f, pick_l, pick_lb, pick_fb,
                matrix, first, narrow, last_back, first_back, taps):
    channels = w_mid.shape[1]
    for o in range(0, channels, 2):
        pair = w_mid[0, o : o + 2].reshape(2 * channels, TAPS).astype(F32).T
        taps[pl.ds(o, TAPS, stride=channels), :] = pair[:, :channels]
        taps[pl.ds(o + 1, TAPS, stride=channels), :] = pair[:, channels:]
    block = lambda tap: taps[tap * channels : (tap + 1) * channels, :]
    for inner in range(9):
        rows = pl.ds(inner * channels, channels)
        for outer in range(0, 9, 2):
            if outer < 8:
                both = jnp.concatenate([block(outer * 9 + inner), block(outer * 9 + 9 + inner)], axis=1)
                matrix[rows, outer * channels : (outer + 2) * channels] = both.astype(BF)
            else:
                matrix[rows, outer * channels :] = block(outer * 9 + inner).astype(BF)
    wf = w_first[0]
    first[...] = dot(wf, pick_f[...]).astype(BF)
    first_back[...] = dot_nt(pick_fb[...], wf).astype(BF)
    for dx in range(3):
        narrow[dx] = sum(dot_nt(pick_l[dx, o], w_last[0, o]) for o in range(2)).astype(BF)
    last_back[...] = sum(dot(w_last[0, o], pick_lb[o]) for o in range(2)).astype(BF)


def turn_kernel(matrix, turned):
    channels = matrix.shape[0] // 9
    for inner in range(9):
        rows = pl.ds(inner * channels, channels)
        for outer in range(0, 9, 2):
            if outer < 8:
                block = matrix[rows, outer * channels : (outer + 2) * channels].astype(F32).T
                both = jnp.concatenate([block[:channels], block[channels:]], axis=1)
                turned[rows, outer * channels : (outer + 2) * channels] = both.astype(BF)
            else:
                block = matrix[rows, outer * channels :].astype(F32).T
                turned[rows, outer * channels :] = block.astype(BF)


def unpack_kernel(layout, volume, coords, mine, other, *refs):
    g_mid, g_last, g_first, bulk, taps = refs[-5:]
    channels = g_mid.shape[1]
    halves, depth, chunk = layout
    g, c, y, z = (coords[i] for i in range(1, 5))
    for from_core, ref in ((c, mine), (1 - c, other)):
        at = 0
        for rg in range(halves):
            for ry in range(2):
                for rz in range(depth):
                    to = (((lax.rem(g + rg, halves) * 2 + from_core) * 2 + (1 - y if ry else y)) * depth
                          + lax.rem(z + rz, depth)) * chunk
                    bulk[pl.ds(pl.multiple_of(to, 16), chunk), :] = ref[at : at + chunk, :]
                    at += chunk
    rows = 9 * channels
    for tap in range(TAPS):
        outer, inner = divmod(tap, 9)
        start = (outer // 2) * rows + inner * channels
        low = (outer % 2) * channels
        taps[tap * channels : (tap + 1) * channels, :] = (
            bulk[start : start + channels, low : low + channels].astype(F32) * (1.0 / volume)
        )
    for o in range(0, channels, 2):
        pair = jnp.concatenate(
            [taps[pl.ds(o, TAPS, stride=channels), :], taps[pl.ds(o + 1, TAPS, stride=channels), :]],
            axis=1,
        )
        g_mid[0, o : o + 2] = pair.T.reshape(2, channels, TAPS)
    rest = bulk[5 * rows : 5 * rows + 3 * channels, :].astype(F32) * (1.0 / volume)
    for o in range(2):
        g_last[0, o] = rest[o * channels : (o + 1) * channels, :TAPS]
    g_first[0] = rest[2 * channels : 3 * channels, :TAPS]


def place_windows(refs, row, target):
    target[...] = jnp.zeros_like(target)
    for r, ref in enumerate(refs):
        target[r : r + 1, :] = ref[row : row + 1, :]


def oddness(shape, place, period):
    lane = lax.broadcasted_iota(jnp.int32, shape, 1)
    row = lax.broadcasted_iota(jnp.int32, shape, 0)
    within = lane % 128
    return ((place + row + 1 + lane // 128 + within // period + within % period) % 2).astype(F32)


def forward_kernel(period, layer, halves, *refs):
    if layer == 0:
        (coords, below, near, above, w_first, b_first, w_mid, b_mid, w_last, b_last,
         field_out, state, own_out, first_out, second_out, logdet, first, stack) = refs
        field_out[...] = jnp.zeros_like(field_out)
        piece = field_out.shape[1] // halves
        for rel in range(halves):
            to = pl.multiple_of(lax.rem(coords[1] + rel, halves) * piece, 128)
            lanes = slice(rel * piece, (rel + 1) * piece)
            field_out[0:2, pl.ds(to, piece)] = below[0:2, lanes]
            field_out[2:5, pl.ds(to, piece)] = near[0:3, lanes]
            field_out[5:7, pl.ds(to, piece)] = above[1:3, lanes]
    else:
        windows, refs = refs[:7], refs[7:]
        (coords, w_first, b_first, w_mid, b_mid, w_last, b_last,
         field_out, state, own_out, first_out, second_out, logdet, growth_out, first, stack) = refs
        place_windows(windows, 0, field_out)
        place_windows(windows, 1, growth_out)
    channels = w_mid.shape[0] // 9
    field = field_out[...]
    length = field.shape[1]
    frozen = oddness(field.shape, coords[0], period)
    if layer == 1:
        frozen = 1.0 - frozen
    net = frozen * field
    taps = jnp.concatenate(all_shifts(net, 1, period), axis=0).astype(BF)
    for dest in range(5):
        part = dot(w_first[:, dest * 256 : dest * 256 + 216], taps)
        first[dest * channels : (dest + 1) * channels, :] = jnp.tanh(part + b_first[...]).astype(BF)
    first_out[...] = first[channels : 4 * channels, :]
    for dest in range(3):
        stack_planes(stack, first, channels, lambda dx, dz: (dest + dx, dz - 1))
        for at in range(0, length, 256):
            wide = dot(w_mid[...], stack[:, at : at + 256])
            wide = gather_wide(wide, channels, 1, period)
            second_out[dest * channels : (dest + 1) * channels, at : at + 256] = jnp.tanh(
                wide + b_mid[...]
            ).astype(BF)
    narrow = sum(
        dot(w_last[dx], second_out[dx * channels : (dx + 1) * channels, :]) for dx in range(3)
    )
    narrow = gather_narrow(narrow, 1, period) + b_last[...]
    growth = jnp.exp(narrow[0:1])
    mine = field[MID : MID + 1]
    still = frozen[MID : MID + 1]
    moving = 1.0 - still
    state[0:1, :] = still * mine + moving * (mine * growth + narrow[1:2])
    state[1:2, :] = growth
    piece = own_out.shape[1]
    own_out[...] = state[0:1, pl.ds(pl.multiple_of(coords[1] * piece, 128), piece)]
    flow = moving * narrow[0:1]
    logdet[...] = sum(flow[:, at : at + 128] for at in range(0, length, 128))


def backward_kernel(period, layer, layout, *refs):
    windows, refs = refs[:7], refs[7:]
    if layer == 1:
        (logdet0, logdet1, coords, field_in, first_in, second_in, w_last, w_mid, w_first, pick_l, pick_f,
         base_out, part_out, small, send, keep,
         field_end, growth, stack, turned, bulk) = refs
        place_windows(windows, 0, field_end)
        place_windows(windows, 1, growth)
    else:
        (base_in, growth, small_in, coords, field_in, first_in, second_in, w_last, w_mid, w_first,
         pick_l, pick_f,
         part_low, part_mid, part_high, small, send, keep,
         upstream_ref, part_out, stack, turned, bulk) = refs
    channels = w_mid.shape[0] // 9
    length = field_in.shape[1]
    frozen = oddness(field_in.shape, coords[0], period)
    if layer == 1:
        frozen = 1.0 - frozen
    moving = 1.0 - frozen
    place = lax.broadcasted_iota(jnp.int32, (ROWS, length), 0)
    inner = jnp.logical_and(place >= 1, place <= 5)
    if layer == 1:
        field = field_end[...]
        ahead = (
            pltpu.roll(field, ROWS - 1, 0)
            + z_shift(field, 1)
            + y_shift(field, 1, period)
            + t_shift(field, 1, period)
        )
        behind = (
            pltpu.roll(field, 1, 0)
            + z_shift(field, -1)
            + y_shift(field, -1, period)
            + t_shift(field, -1, period)
        )
        squared = field * field
        density = (
            -2.0 * hopping * field * ahead
            + squared
            + quartic * (squared - 1.0) * (squared - 1.0)
        )[MID : MID + 1]
        action = sum(density[:, at : at + 128] for at in range(0, length, 128))
        upstream = (
            -2.0 * hopping * (ahead + behind)
            + 2.0 * field
            + 4.0 * quartic * (squared - 1.0) * field
        )
        upstream = jnp.where(inner, upstream, 0.0)
        small[...] = jnp.zeros_like(small)
        small[3:4, :] = action - logdet0[...] - logdet1[...]
    else:
        upstream_ref[...] = base_in[...]
        for r in range(1, 6):
            upstream_ref[r : r + 1, :] += (
                windows[r - 1][2:3, :] + windows[r][1:2, :] + windows[r + 1][0:1, :]
            )
        upstream = upstream_ref[...]
        small[0:8, :] = jnp.zeros((8, 128), F32)
        small[8:16, :] = small_in[...]
    grow = growth[...]
    grad_scale = upstream * moving * field_in[...] * grow - moving
    grad_shift = upstream * moving
    grad_output = jnp.where(
        jnp.concatenate([inner, inner], axis=0),
        jnp.concatenate([grad_scale, grad_shift], axis=0),
        0.0,
    )
    ones = jnp.ones((8, length), BF)
    sums = dot_nt(ones, grad_output.astype(BF))
    small[2:3, 0:1] = sums[0:1, MID : MID + 1]
    small[2:3, 1:2] = sums[0:1, 8 + MID : 9 + MID]
    taps = jnp.concatenate(all_shifts(grad_output, -1, period), axis=0).astype(BF)
    rows = 9 * channels
    if bulk.shape[0] > 5 * rows + 3 * channels:
        bulk[5 * rows + 3 * channels :, :] = jnp.zeros(
            (bulk.shape[0] - 5 * rows - 3 * channels, 128), BF
        )
    g_last = dot_nt(second_in[channels : 2 * channels, :], taps).astype(BF)
    g_last = dot(g_last, pick_l[...]).astype(BF)
    for o in range(2):
        bulk[5 * rows + o * channels : 5 * rows + (o + 1) * channels, :] = g_last[
            :, o * 128 : (o + 1) * 128
        ]
    mids = []
    for dest in range(3):
        part = dot(w_last[:, dest * 512 : dest * 512 + 432], taps)
        wide = second_in[dest * channels : (dest + 1) * channels, :].astype(F32)
        mids.append((part * (1.0 - wide * wide)).astype(BF))
    small[1:2, 0:channels] = dot_nt(ones, mids[1])[0:1]
    rounded = mids[1].astype(F32)
    in_t = [t_shift(rounded, -dt, period) for dt in STEPS]
    for dy in range(3):
        for dt in range(3):
            turned[(dy * 3 + dt) * channels : (dy * 3 + dt + 1) * channels, :] = y_shift(
                in_t[dt], -STEPS[dy], period
            ).astype(BF)
    stack_planes(stack, first_in, channels, lambda dx, dz: (dx, dz - 1))
    g_mid = dot_nt(turned[...], stack[...]).astype(BF)
    for b in range(5):
        part = g_mid[:, b * 128 : (b + 1) * 128]
        if part.shape[1] < 128:
            part = jnp.concatenate([part, jnp.zeros((rows, 128 - part.shape[1]), BF)], axis=1)
        bulk[b * rows : (b + 1) * rows, :] = part
    planes = jnp.concatenate(mids, axis=0)
    stack_planes(stack, planes, channels, lambda dx, dz: (2 - dx, 1 - dz))
    firsts = []
    for at in range(0, length, 256):
        wide = dot(w_mid[...], stack[:, at : at + 256])
        wide = gather_wide(wide, channels, -1, period)
        seen = first_in[channels : 2 * channels, at : at + 256].astype(F32)
        firsts.append((wide * (1.0 - seen * seen)).astype(BF))
    grad_first = jnp.concatenate(firsts, axis=1)
    small[0:1, 0:channels] = dot_nt(ones, grad_first)[0:1]
    net = frozen * field_in[...]
    taps = jnp.concatenate(all_shifts(net, 1, period), axis=0).astype(BF)
    g_first = dot_nt(grad_first, taps).astype(BF)
    bulk[5 * rows + 2 * channels : 5 * rows + 3 * channels, :] = dot(g_first, pick_f[...]).astype(BF)
    narrow = gather_narrow(dot(w_first[...], grad_first), -1, period)
    base = upstream * (frozen + moving * grow)
    for d in range(3):
        row = frozen[MID - 1 + d : MID + d] * narrow[d : d + 1]
        if layer == 0 and d == 1:
            row = row + base[MID : MID + 1]
        part_out[d : d + 1, :] = row
    if layer == 1:
        base_out[...] = base
    else:
        piece = part_low.shape[1]
        lanes = pl.ds(pl.multiple_of(coords[1] * piece, 128), piece)
        for d, ref in enumerate((part_low, part_mid, part_high)):
            ref[...] = part_out[d : d + 1, lanes]
    halves, depth, chunk = layout
    g, c, y, z = (coords[i] for i in range(1, 5))
    for core, ref in ((c, keep), (1 - c, send)):
        at = 0
        for ry in range(2):
            for rz in range(depth):
                source = (((g * 2 + core) * 2 + (1 - y if ry else y)) * depth
                          + lax.rem(z + rz, depth)) * chunk
                ref[at : at + chunk, :] = bulk[pl.ds(pl.multiple_of(source, 16), chunk), :]
                at += chunk


SMEM = pl.BlockSpec(memory_space=pltpu.SMEM)
VMEM = pl.BlockSpec(memory_space=pltpu.VMEM)


def kernel_call(body, outs, scratch, args, flops, small=None):
    return pl.pallas_call(
        body,
        out_shape=tuple(outs),
        in_specs=[SMEM if a is small else VMEM for a in args],
        out_specs=tuple([VMEM] * len(outs)),
        scratch_shapes=scratch,
        compiler_params=pltpu.CompilerParams(vmem_limit_bytes=52 * 2**20),
        cost_estimate=pl.CostEstimate(flops=flops, bytes_accessed=4_000_000, transcendentals=500_000),
    )(*args)


def shape(dims, dtype=F32):
    return jax.ShapeDtypeStruct(dims, dtype)


def forward(period, layer, windows, coords, weights, channels, halves):
    length = windows[0].shape[1]
    outs = [
        shape((ROWS, length)),
        shape((2, length)),
        shape((1, length // halves)),
        shape((3 * channels, length), BF),
        shape((3 * channels, length), BF),
        shape((1, 128)),
    ]
    scratch = [
        pltpu.VMEM((5 * channels, length), BF),
        pltpu.VMEM((9 * channels, length), BF),
    ]
    if layer == 1:
        outs.append(shape((ROWS, length)))
        args = [*windows, coords, *weights]
    else:
        args = [coords, *windows, *weights]
    body = functools.partial(forward_kernel, period, layer, halves)
    return kernel_call(body, outs, scratch, args, 3 * 2 * 81 * 64 * 64 * length, coords)


def backward(period, layer, layout, windows, extra, coords, field, first, second, weights, channels):
    length = field.shape[1]
    halves, depth, chunk = layout
    part = 2 * depth * chunk
    if layer == 1:
        outs = [shape((ROWS, length)), shape((3, length)), shape((8, 128))]
        scratch = [pltpu.VMEM((ROWS, length), F32), pltpu.VMEM((ROWS, length), F32)]
    else:
        outs = [shape((1, length // halves))] * 3 + [shape((16, 128))]
        scratch = [pltpu.VMEM((ROWS, length), F32), pltpu.VMEM((ROWS, length), F32)]
    outs += [shape((part, 128), BF)] * 2
    scratch += [
        pltpu.VMEM((9 * channels, length), BF),
        pltpu.VMEM((9 * channels, length), BF),
        pltpu.VMEM((part * 2 * halves, 128), BF),
    ]
    args = [*windows, *extra, coords, field, first, second, *weights]
    body = functools.partial(backward_kernel, period, layer, layout)
    return kernel_call(body, outs, scratch, args, 2 * 2 * 81 * 64 * 64 * length, coords)


def pack(layer, w_mid, w_first, w_last, picks):
    channels = w_mid.shape[1]
    whole = lambda a: pl.BlockSpec(a.shape, lambda i: (0,) * len(a.shape))
    one = lambda a: pl.BlockSpec((1,) + a.shape[1:], lambda i: (layer,) + (0,) * (len(a.shape) - 1))
    outs = (
        shape((9 * channels, 9 * channels), BF),
        shape((channels, 5 * 256), BF),
        shape((3, 216, channels), BF),
        shape((channels, 3 * 512), BF),
        shape((216, channels), BF),
    )
    return pl.pallas_call(
        pack_kernel,
        grid=(1,),
        out_shape=outs,
        in_specs=[one(w_mid), one(w_first), one(w_last)] + [whole(a) for a in picks],
        out_specs=tuple(whole(a) for a in outs),
        scratch_shapes=[pltpu.VMEM((TAPS * channels, channels), F32)],
        compiler_params=pltpu.CompilerParams(vmem_limit_bytes=40 * 2**20),
        cost_estimate=pl.CostEstimate(flops=2_000_000_000, bytes_accessed=8_000_000, transcendentals=0),
    )(w_mid, w_first, w_last, *picks)


def unpack(layer, layout, volume, coords, mine, other, channels, before):
    halves, depth, chunk = layout
    rows = 4 * halves * depth * chunk
    outs = (
        shape((2, channels, channels, TAPS)),
        shape((2, 2, channels, TAPS)),
        shape((2, channels, TAPS)),
    )
    block = lambda a: pl.BlockSpec(
        (1,) + a.shape[1:], lambda i: (layer,) + (0,) * (len(a.shape) - 1)
    )
    whole = lambda a: pl.BlockSpec(a.shape, lambda i: (0,) * len(a.shape))
    return pl.pallas_call(
        functools.partial(unpack_kernel, layout, volume),
        grid=(1,),
        out_shape=outs,
        in_specs=[SMEM, whole(mine), whole(other)] + [pl.BlockSpec(memory_space=pl.ANY)] * len(before),
        out_specs=tuple(block(a) for a in outs),
        scratch_shapes=[pltpu.VMEM((rows, 128), BF), pltpu.VMEM((TAPS * channels, channels), F32)],
        input_output_aliases={3 + i: i for i in range(len(before))},
        compiler_params=pltpu.CompilerParams(vmem_limit_bytes=40 * 2**20),
        cost_estimate=pl.CostEstimate(flops=2_000_000_000, bytes_accessed=8_000_000, transcendentals=0),
    )(coords, mine, other, *before)


def add(*parts):
    return sum(p.astype(F32) for p in parts).astype(BF)


def sum_gradients(send, keep, layout, count):
    halves, depth, chunk = layout
    xy = lambda fn: [(fn(a), a) for a in range(count)]
    core = xy(lambda a: a ^ 1)
    got = lax.ppermute(send, "xy", core)
    half = depth * chunk
    away = add(keep[half:], got[half:])
    stay = add(keep[:half], got[:half])
    got = lax.ppermute(away, "xy", xy(lambda a: a ^ 2))
    pieces = [
        add(stay[s * chunk : (s + 1) * chunk], got[s * chunk : (s + 1) * chunk]) for s in range(depth)
    ]
    got = [
        lax.ppermute(pieces[s], "xy", xy(lambda a, s=s: (a - 4 * s) % count)) for s in range(1, depth)
    ]
    total = add(pieces[0], *got)
    line = [total] + [
        lax.ppermute(total, "xy", xy(lambda a, s=s: (a + 4 * s) % count)) for s in range(1, depth)
    ]
    line = jnp.concatenate(line, axis=0)
    square = []
    for rg in range(halves):
        for ry in range(2):
            if rg == 0 and ry == 0:
                square.append(line)
                continue
            pairs = [
                ((a ^ (2 * ry)) * halves + (j + rg) % halves, a * halves + j)
                for a in range(count)
                for j in range(halves)
            ]
            square.append(lax.ppermute(line, ("xy", "gz"), pairs))
    square = jnp.concatenate(square, axis=0)
    return square, lax.ppermute(square, "xy", core)


def per_device(noise, w_first, b_first, w_mid, b_mid, w_last, b_last):
    period = noise.shape[3]
    count = lax.axis_size("xy")
    halves = lax.axis_size("gz")
    channels = w_mid.shape[2]
    order = ring_order(count)
    places = np.argsort(np.array(order))
    volume = float(noise.size * count * halves)
    index = lax.axis_index("xy")
    depth = count // 4
    coords = jnp.stack(
        [
            jnp.asarray(places, jnp.int32)[index],
            lax.axis_index("gz"),
            index % 2,
            index // 2 % 2,
            index // 4,
        ]
    ).astype(jnp.int32)
    need = 45 * channels + 3 * channels
    chunk = -(-need // (4 * halves * depth * 16)) * 16
    layout = (halves, depth, chunk)

    def step(values, offset):
        return lax.ppermute(
            values, "xy", [(order[(p + offset) % count], order[p]) for p in range(count)]
        )

    flat = noise.reshape(1, -1)
    near = []
    for d in STEPS:
        parts = []
        for rel in range(halves):
            pairs = [
                ((p + d) % count * halves + (j + rel) % halves, order[p] * halves + j)
                for p in range(count)
                for j in range(halves)
            ]
            parts.append(lax.ppermute(flat, ("xy", "gz"), pairs))
        near.append(jnp.concatenate(parts, axis=1))
    near = jnp.concatenate(near, axis=0)
    noises = [step(near, -2), near, step(near, 2)]

    mid = w_mid.transpose(0, 2, 3, 1)
    firsts = w_first.transpose(0, 2, 3, 1).reshape(2, channels, TAPS)
    lasts = w_last.transpose(0, 2, 3, 1)
    picks = [
        jnp.asarray(fn(), BF) for fn in (spread_first, spread_last, spread_last_back, spread_first_back)
    ]
    pick_l, pick_f = jnp.asarray(pick_last(), BF), jnp.asarray(pick_first(), BF)
    ahead_weights, back_weights = [], []
    for layer in range(2):
        matrix, first, narrow, last_back, first_back = pack(layer, mid, firsts, lasts, picks)
        (turned,) = kernel_call(
            turn_kernel, [shape(matrix.shape, BF)], [], [matrix], 1_000_000_000
        )
        tail = jnp.pad(b_last[layer][:, None], ((0, 6), (0, 0)))
        ahead_weights.append(
            (first, b_first[layer][:, None], matrix, b_mid[layer][:, None], narrow, tail)
        )
        back_weights.append((last_back, turned, first_back, pick_l, pick_f))

    def exchange(values):
        return [values if m == 0 else step(values, m) for m in range(-3, 4)]

    field0, state, _, first0, second0, logdet0 = forward(
        period, 0, noises, coords, ahead_weights[0], channels, halves
    )
    field1, state, own, first1, second1, logdet1, growth0 = forward(
        period, 1, exchange(state), coords, ahead_weights[1], channels, halves
    )
    sample = lax.ppermute(own, "xy", [(order[p], p) for p in range(count)])
    base, part, small, send1, keep1 = backward(
        period, 1, layout, exchange(state), [logdet0, logdet1], coords, field1, first1, second1,
        back_weights[1], channels,
    )
    *mine, small, send0, keep0 = backward(
        period, 0, layout, exchange(part), [base, growth0, small], coords, field0, first0, second0,
        back_weights[0], channels,
    )
    force = sum(
        lax.ppermute(mine[d], "xy", [(order[p], (p + d - 1) % count) for p in range(count)])
        for d in range(3)
    )
    outs = unpack(1, layout, volume, coords, *sum_gradients(send1, keep1, layout, count), channels, [])
    jump = 1
    while jump < count:
        small = small + lax.ppermute(small, "xy", [(a ^ jump, a) for a in range(count)])
        jump *= 2
    g_mid, g_last, g_first = unpack(
        0, layout, volume, coords, *sum_gradients(send0, keep0, layout, count), channels, list(outs)
    )
    small = small.reshape(2, 8, 128) / volume
    return (
        sample.reshape(noise.shape),
        force.reshape(noise.shape),
        jnp.sum(small[1, 3]),
        g_first.reshape(2, channels, 1, TAPS).transpose(0, 3, 1, 2),
        small[:, 0, :channels],
        g_mid.transpose(0, 3, 1, 2),
        small[:, 1, :channels],
        g_last.transpose(0, 3, 1, 2),
        small[:, 2, :2],
    )


def solution(mesh):
    return jax.shard_map(
        per_device,
        mesh=mesh,
        in_specs=(P("xy", "gz", None, None), P(), P(), P(), P(), P(), P()),
        out_specs=(
            P("xy", "gz", None, None),
            P("xy", "gz", None, None),
            P(),
            P(),
            P(),
            P(),
            P(),
            P(),
            P(),
        ),
        check_vma=False,
    )
```

time: 265 us -> 166 us (0.63); the launches traced: 261 us -> 165 us
  waiting for transfers between devices: 59.5 us -> 6.96 us
  starting transfers between devices: 44.1 us -> 91.8 us
  local copies, waits for them, and re-layouts: 69.3 us -> 26.4 us
  blocking collectives: 28.4 us -> 0 us
  between operations: 16.4 us -> 1.27 us
  Pallas kernels: 23.2 us -> 36.9 us
  other arithmetic: 13.2 us -> 1.53 us
  matrix products: 6.45 us -> 0 us
    psum x1 -> x0, waiting for transfers between devices: 57.6 us -> none  [per_device(): loss, pairs = lax.psum((loss, pairs), 'xy')]
    ppermute x7 -> x38, starting transfers between devices: 26.3 us -> 71.4 us  [the longest x6 17.7 us: per_device(): parts.append(lax.ppermute(flat, ('xy', 'gz'), pairs))]
    psum x1 -> x0, blocking collectives: 25.2 us -> none  [per_device(): loss, pairs = lax.psum((loss, pairs), 'xy')]
    transpose x5 -> x0, local copies, waits for them, and re-layouts: 21.3 us -> none  [the longest x2 8.67 us: per_device(): wm.transpose(1, 3, 0, 2).reshape(9 * channels, 9 * channels)]
    reshape x11 -> x0, local copies, waits for them, and re-layouts: 20.3 us -> none  [the longest x2 7.86 us: per_device(): wm.transpose(1, 3, 0, 2).reshape(9 * channels, 9 * channels)]
    pallas_call x4 -> x10, Pallas kernels: 23.2 us -> 36.9 us  [the longest x6 24 us: kernel_call(): pl.pallas_call(body, out_shape=tuple(outs), in_specs=[SMEM if a is small...]
    dot_general x12 -> x0, matrix products: 6.45 us -> none  [the longest x8 3.69 us: dot(): return jnp.dot(a, b, preferred_element_type=F32)]
    div x6 -> x1, other arithmetic: 4.76 us -> 0.01 us  [per_device(): small = small.reshape(2, 8, 128) / volume]
  transfers between devices with their start and end apart: 28 -> 58, of which waited for: 2 -> 10; matrix products, arithmetic and copies ran while one was open for 23% -> 5% of each run, Pallas kernels for 0% -> 6%
where the time goes in v2:
time: 166 us; the launch traced here: 165 us
  starting transfers between devices  91.8 us (55%)
  Pallas kernels  36.9 us (22%)
  local copies, waits for them, and re-layouts  26.4 us (16%)
  waiting for transfers between devices  6.96 us (4%)
    pallas_call x6, Pallas kernels, kernel_call(): pl.pallas_call(body, out_shape=tuple(outs), in_specs=[SMEM if a is small...  24 us
    ppermute x20, starting transfers between devices, step(): lax.ppermute(values, 'xy', [(order[(p + offset) % count], order[p]) for p...  20.4 us
    unnamed x90, local copies, waits for them, and re-layouts  18.4 us
    ppermute x6, starting transfers between devices, per_device(): parts.append(lax.ppermute(flat, ('xy', 'gz'), pairs))  17.7 us
    ppermute x2, starting transfers between devices, sum_gradients(): return (square, lax.ppermute(square, 'xy', core))  12 us
    ppermute x6, starting transfers between devices, sum_gradients(): lax.ppermute(pieces[s], 'xy', xy(lambda a, s=s: (a - 4 * s) % count))  8.11 us
    pallas_call x2, Pallas kernels, unpack(): pl.pallas_call(functools.partial(unpack_kernel, layout, volume), grid=(1,...  8.1 us
    ppermute x3, starting transfers between devices, per_device(): lax.ppermute(mine[d], 'xy', [(order[p], (p + d - 1) % count) for p in ran...  7.88 us
  transfers between devices with their start and end apart: 58, of which 10 were waited for; matrix products, arithmetic and copies ran while one was open for 5% of the time, Pallas kernels for 6%

profile of v2, /device:TPU:5, one launch (start us, length us, event | category | flops | bytes accessed | tf_op | source)
XLA Modules:
  0.0 164.8 jit_solution(12297370090525151182)
XLA Ops:
  1.4 4.7 %collective-permute-start = (f32[1,512]{1,0:T(1,128)S(1)}, f32[1,512]{1,0:T(1,128)S(1)}, u32[]{:S(2)}, u32[]{:S(2)}) collective-permute-start(f32[1,512]{1,0:T(1,128)S(1)} %reshape.36), channel_id=1, source_target_pairs={{30,0},{31,1},{0,2},{1,3},{2,10},{3,11},{4,8},{5,9},{6,16},{7,17},... | collective-permute-start | bytes 6152 | tf_op jit(solution)/shard_map/ppermute | solution.py:646
  6.2 3.0 %collective-permute-start.1 = (f32[1,512]{1,0:T(1,128)S(1)}, f32[1,512]{1,0:T(1,128)S(1)}, u32[]{:S(2)}, u32[]{:S(2)}) collective-permute-start(f32[1,512]{1,0:T(1,128)S(1)} %reshape.36), channel_id=1, source_target_pairs={{31,0},{30,1},{1,2},{0,3},{3,10},{2,11},{5,8},{4,9},{7,16},{6,17},... | collective-permute-start | bytes 6152 | tf_op jit(solution)/shard_map/ppermute | solution.py:646
  9.1 1.9 %collective-permute-start.2 = (f32[1,512]{1,0:T(1,128)S(1)}, f32[1,512]{1,0:T(1,128)S(1)}, u32[]{:S(2)}, u32[]{:S(2)}) collective-permute-start(f32[1,512]{1,0:T(1,128)S(1)} %reshape.36), channel_id=1, source_target_pairs={{0,0},{1,1},{2,2},{3,3},{4,10},{5,11},{6,8},{7,9},{8,16},{9,17},{1... | collective-permute-start | bytes 6152 | tf_op jit(solution)/shard_map/ppermute | solution.py:646
  11.7 1.9 %collective-permute-start.4 = (f32[1,512]{1,0:T(1,128)S(1)}, f32[1,512]{1,0:T(1,128)S(1)}, u32[]{:S(2)}, u32[]{:S(2)}) collective-permute-start(f32[1,512]{1,0:T(1,128)S(1)} %reshape.36), channel_id=1, source_target_pairs={{2,0},{3,1},{4,2},{5,3},{6,10},{7,11},{8,8},{9,9},{10,16},{11,17},... | collective-permute-start | bytes 6152 | tf_op jit(solution)/shard_map/ppermute | solution.py:646
  15.1 5.6 %collective-permute-start.5 = (f32[1,512]{1,0:T(1,128)S(1)}, f32[1,512]{1,0:T(1,128)S(1)}, u32[]{:S(2)}, u32[]{:S(2)}) collective-permute-start(f32[1,512]{1,0:T(1,128)S(1)} %reshape.36), channel_id=1, source_target_pairs={{3,0},{2,1},{5,2},{4,3},{7,10},{6,11},{9,8},{8,9},{11,16},{10,17},... | collective-permute-start | bytes 6152 | tf_op jit(solution)/shard_map/ppermute | solution.py:646
  21.6 2.1 %collective-permute-start.7 = (f32[3,1024]{1,0:T(4,128)S(1)}, f32[3,1024]{1,0:T(4,128)S(1)}, u32[]{:S(2)}, u32[]{:S(2)}) collective-permute-start(f32[3,1024]{1,0:T(4,128)S(1)} %maximum_maximum_fusion.refs_2_), channel_id=1, source_target_pairs={{10,0},{8,2},{16,10},{18,8},{26,16},{24,18},{28,26},{30,24},{22,28... | collective-permute-start | bytes 36872 | tf_op jit(solution)/shard_map/ppermute | solution.py:632
  23.6 1.6 copy-done
  30.6 2.4 %shard_map.205 = (bf16[576,576]{1,0:T(8,128)(2,1)S(1)}, bf16[64,1280]{1,0:T(8,128)(2,1)S(1)}, bf16[3,216,64]{2,1,0:T(8,128)(2,1)S(1)}, bf16[64,1536]{1,0:T(8,128)(2,1)S(1)}, bf16[216,64]{1,0:T(8,128)(2,1)S(1)}) custom-call(bf16[2,64,64,81]{3,2,1,0:T(8,128)(2,1)S(1)} %bitcast.41, bf16[2,64,81]{2,1,0:T(8,128)(2,1)S(1)} %bitcast.45, ...), custom_call_target="tpu_custom_call" | custom-call | flops 2000000000 | bytes 8000000 | tf_op jit(solution)/shard_map/pallas_call | solution.py:531
  39.6 5.5 %shard_map.206 = (f32[8,1024]{1,0:T(8,128)S(1)}, f32[2,1024]{1,0:T(2,128)S(1)}, f32[1,512]{1,0:T(1,128)}, bf16[192,1024]{1,0:T(8,128)(2,1)S(1)}, bf16[192,1024]{1,0:T(8,128)(2,1)S(1)}, /*index=5*/f32[1,128]{1,0:T(1,128)S(1)}) custom-call(s32[5]{0:T(128)S(1)} %stack.19.refs_0_.refs_7_.refs_9_.refs_10_.coords, f32[3,1024]{1,0:T(4,128)S(1)} %collective-permute-done.6.refs_1_, ...), custom_call_target="tpu_custom_call" | custom-call | flops 2038431744 | bytes 4000000 | tf_op jit(solution)/shard_map/pallas_call | solution.py:461
  45.7 2.4 %collective-permute-start.10 = (f32[2,1024]{1,0:T(2,128)S(1)}, f32[2,1024]{1,0:T(2,128)S(1)}, u32[]{:S(2)}, u32[]{:S(2)}) collective-permute-start(f32[2,1024]{1,0:T(2,128)S(1)} %get-tuple-element.51.refs_3_), channel_id=1, source_target_pairs={{4,0},{0,2},{2,10},{10,8},{8,16},{16,18},{18,26},{26,24},{24,28},{... | collective-permute-start | bytes 24584 | tf_op jit(solution)/shard_map/ppermute | solution.py:632
  51.2 1.9 %collective-permute-start.9 = (f32[2,1024]{1,0:T(2,128)S(1)}, f32[2,1024]{1,0:T(2,128)S(1)}, u32[]{:S(2)}, u32[]{:S(2)}) collective-permute-start(f32[2,1024]{1,0:T(2,128)S(1)} %get-tuple-element.51.refs_3_), channel_id=1, source_target_pairs={{6,0},{4,2},{0,10},{2,8},{10,16},{8,18},{16,26},{18,24},{26,28},{2... | collective-permute-start | bytes 24584 | tf_op jit(solution)/shard_map/ppermute | solution.py:632
  54.1 2.4 %shard_map.207 = (bf16[576,576]{1,0:T(8,128)(2,1)S(1)}, bf16[64,1280]{1,0:T(8,128)(2,1)S(1)}, bf16[3,216,64]{2,1,0:T(8,128)(2,1)S(1)}, bf16[64,1536]{1,0:T(8,128)(2,1)S(1)}, bf16[216,64]{1,0:T(8,128)(2,1)S(1)}) custom-call(bf16[2,64,64,81]{3,2,1,0:T(8,128)(2,1)S(1)} %bitcast.42, bf16[2,64,81]{2,1,0:T(8,128)(2,1)S(1)} %bitcast.46, ...), custom_call_target="tpu_custom_call" | custom-call | flops 2000000000 | bytes 8000000 | tf_op jit(solution)/shard_map/pallas_call | solution.py:531
  60.0 5.6 %shard_map.208 = (f32[8,1024]{1,0:T(8,128)S(1)}, f32[2,1024]{1,0:T(2,128)S(1)}, f32[1,512]{1,0:T(1,128)S(1)}, bf16[192,1024]{1,0:T(8,128)(2,1)S(1)}, bf16[192,10...) custom-call(f32[2,1024]{1,0:T(2,128)S(1)} %collective-permute-done.8.refs_0_, ...), custom_call_target="tpu_custom_call" | custom-call | flops 2038431744 | bytes 4000000 | tf_op jit(solution)/shard_map/pallas_call | solution.py:461
  72.5 5.8 %shard_map.210 = (f32[8,1024]{1,0:T(8,128)S(1)}, f32[3,1024]{1,0:T(4,128)S(1)}, f32[8,128]{1,0:T(8,128)S(1)}, bf16[768,128]{1,0:T(8,128)(2,1)S(1)}, bf16[768,128]{1,0:T(8,128)(2,1)S(1)}) custom-call(f32[2,1024]{1,0:T(2,128)S(1)} %collective-permute-done.15.refs_0_, f32[2,1024]{1,0:T(2,128)S(1)} %collective-permute-done.16.refs_1_, ...), custom_call_target="tpu_custom_call" | custom-call | flops 1358954496 | bytes 4000000 | tf_op jit(solution)/shard_map/pallas_call | solution.py:461
  79.5 1.5 collective-permute-start.22
  86.2 5.7 %shard_map.212 = (f32[1,512]{1,0:T(1,128)S(1)}, f32[1,512]{1,0:T(1,128)S(1)}, f32[1,512]{1,0:T(1,128)S(1)}, f32[16,128]{1,0:T(8,128)S(1)}, bf16[768,128]{1,0:T(8,128)(2,1)S(1)}, /*index=5*/bf16[768,128]{1,0:T(8,128)(2,1)S(1)}) custom-call(f32[3,1024]{1,0:T(4,128)S(1)} %collective-permute-done.21.refs_0_, f32[3,1024]{1,0:T(4,128)S(1)} %collective-permute-done.22.refs_1_, ...), custom_call_target="tpu_custom_call" | custom-call | flops 1358954496 | bytes 4000000 | tf_op jit(solution)/shard_map/pallas_call | solution.py:461
  97.0 5.4 %collective-permute-start.14 = (f32[1,512]{1,0:T(1,128)S(1)}, f32[1,512]{1,0:T(1,128)S(1)}, u32[]{:S(2)}, u32[]{:S(2)}) collective-permute-start(f32[1,512]{1,0:T(1,128)S(1)} %get-tuple-element.55), channel_id=1, source_target_pairs={{0,0},{2,2},{10,4},{8,6},{16,8},{18,10},{26,12},{24,14},{28,16},{3... | collective-permute-start | bytes 6152 | tf_op jit(solution)/shard_map/ppermute | solution.py:679
  102.4 3.6 %collective-permute-start.27 = (f32[1,512]{1,0:T(1,128)S(1)}, f32[1,512]{1,0:T(1,128)S(1)}, u32[]{:S(2)}, u32[]{:S(2)}) collective-permute-start(f32[1,512]{1,0:T(1,128)S(1)} %get-tuple-element.73), channel_id=1, source_target_pairs={{0,30},{2,0},{10,2},{8,4},{16,6},{18,8},{26,10},{24,12},{28,14},{3... | collective-permute-start | bytes 6152 | tf_op jit(solution)/shard_map/ppermute | solution.py:689
  106.0 1.9 %collective-permute-start.28 = (f32[1,512]{1,0:T(1,128)S(1)}, f32[1,512]{1,0:T(1,128)S(1)}, u32[]{:S(2)}, u32[]{:S(2)}) collective-permute-start(f32[1,512]{1,0:T(1,128)S(1)} %get-tuple-element.74), channel_id=1, source_target_pairs={{0,0},{2,2},{10,4},{8,6},{16,8},{18,10},{26,12},{24,14},{28,16},{3... | collective-permute-start | bytes 6152 | tf_op jit(solution)/shard_map/ppermute | solution.py:689
  107.9 2.4 %collective-permute-start.29 = (f32[1,512]{1,0:T(1,128)S(1)}, f32[1,512]{1,0:T(1,128)S(1)}, u32[]{:S(2)}, u32[]{:S(2)}) collective-permute-start(f32[1,512]{1,0:T(1,128)S(1)} %get-tuple-element.75), channel_id=1, source_target_pairs={{0,2},{2,4},{10,6},{8,8},{16,10},{18,12},{26,14},{24,16},{28,18},{... | collective-permute-start | bytes 6152 | tf_op jit(solution)/shard_map/ppermute | solution.py:689
  112.7 2.6 %collective-permute-start.33 = (f32[16,128]{1,0:T(8,128)S(1)}, f32[16,128]{1,0:T(8,128)S(1)}, u32[]{:S(2)}, u32[]{:S(2)}) collective-permute-start(f32[16,128]{1,0:T(8,128)S(1)} %add.95), channel_id=1, source_target_pairs={{16,0},{18,2},{20,4},{22,6},{24,8},{26,10},{28,12},{30,14},{0,16},... | collective-permute-start | bytes 24584 | tf_op jit(solution)/shard_map/ppermute | solution.py:695
  117.6 2.7 %collective-permute-start.47 = (bf16[384,128]{1,0:T(8,128)(2,1)S(1)}, bf16[384,128]{1,0:T(8,128)(2,1)S(1)}, u32[]{:S(2)}, u32[]{:S(2)}) collective-permute-start(bf16[384,128]{1,0:T(8,128)(2,1)S(1)} %get-tuple-element.101), channel_id=1, source_target_pairs={{4,0},{6,2},{0,4},{2,6},{12,8},{14,10},{8,12},{10,14},{20,16},{22,... | collective-permute-start | bytes 294920 | tf_op jit(solution)/shard_map/ppermute | solution.py:580
  120.5 1.9 %collective-permute-done.47 = bf16[384,128]{1,0:T(8,128)(2,1)S(1)} collective-permute-done((bf16[384,128]{1,0:T(8,128)(2,1)S(1)}, bf16[384,128]{1,0:T(8,128)(2,1)S(1)}, u32[]{:S(2)}, u32[]{:S(2)}) %collective-permute-start.47) | collective-permute-done | bytes 98336 | tf_op jit(solution)/shard_map/ppermute | solution.py:580
  122.4 1.8 %collective-permute-start.48 = (bf16[96,128]{1,0:T(8,128)(2,1)S(1)}, bf16[96,128]{1,0:T(8,128)(2,1)S(1)}, u32[]{:S(2)}, u32[]{:S(2)}) collective-permute-start(bf16[96,128]{1,0:T(8,128)(2,1)S(1)} %get-tuple-element.104), channel_id=1, source_target_pairs={{24,0},{26,2},{28,4},{30,6},{0,8},{2,10},{4,12},{6,14},{8,16},{10,... | collective-permute-start | bytes 73736 | tf_op jit(solution)/shard_map/ppermute | solution.py:585
  124.9 2.3 %collective-permute-start.50 = (bf16[96,128]{1,0:T(8,128)(2,1)S(1)}, bf16[96,128]{1,0:T(8,128)(2,1)S(1)}, u32[]{:S(2)}, u32[]{:S(2)}) collective-permute-start(bf16[96,128]{1,0:T(8,128)(2,1)S(1)} %get-tuple-element.105), channel_id=1, source_target_pairs={{8,0},{10,2},{12,4},{14,6},{16,8},{18,10},{20,12},{22,14},{24,16},... | collective-permute-start | bytes 73736 | tf_op jit(solution)/shard_map/ppermute | solution.py:585
  128.0 2.5 %collective-permute-start.38 = (bf16[96,128]{1,0:T(8,128)(2,1)S(1)}, bf16[96,128]{1,0:T(8,128)(2,1)S(1)}, u32[]{:S(2)}, u32[]{:S(2)}) collective-permute-start(bf16[96,128]{1,0:T(8,128)(2,1)S(1)} %get-tuple-element.108), channel_id=1, source_target_pairs={{8,0},{10,2},{12,4},{14,6},{16,8},{18,10},{20,12},{22,14},{24,16},... | collective-permute-start | bytes 73736 | tf_op jit(solution)/shard_map/ppermute | solution.py:585
  133.6 1.9 %collective-permute-start.39 = (bf16[96,128]{1,0:T(8,128)(2,1)S(1)}, bf16[96,128]{1,0:T(8,128)(2,1)S(1)}, u32[]{:S(2)}, u32[]{:S(2)}) collective-permute-start(bf16[96,128]{1,0:T(8,128)(2,1)S(1)} %get-tuple-element.99), channel_id=1, source_target_pairs={{8,0},{10,2},{12,4},{14,6},{16,8},{18,10},{20,12},{22,14},{24,16},... | collective-permute-start | bytes 73736 | tf_op jit(solution)/shard_map/ppermute | solution.py:589
  140.2 1.8 %collective-permute-start.42 = (bf16[384,128]{1,0:T(8,128)(2,1)S(1)}, bf16[384,128]{1,0:T(8,128)(2,1)S(1)}, u32[]{:S(2)}, u32[]{:S(2)}) collective-permute-start(bf16[384,128]{1,0:T(8,128)(2,1)S(1)} %pad_maximum_fusion), channel_id=1, source_target_pairs={{4,0},{5,1},{6,2},{7,3},{0,4},{1,5},{2,6},{3,7},{12,8},{13,9},{14,... | collective-permute-start | bytes 294920 | tf_op jit(solution)/shard_map/ppermute | solution.py:603
  144.1 7.5 %collective-permute-start.57 = (bf16[1536,128]{1,0:T(8,128)(2,1)S(1)}, bf16[1536,128]{1,0:T(8,128)(2,1)S(1)}, u32[]{:S(2)}, u32[]{:S(2)}) collective-permute-start(bf16[1536,128]{1,0:T(8,128)(2,1)S(1)} %constant_dynamic-update-slice_fusion.7.mine), channel_id=1, source_target_pairs={{2,0},{0,2},{6,4},{4,6},{10,8},{8,10},{14,12},{12,14},{18,16},{16,... | collective-permute-start | bytes 1179656 | tf_op jit(solution)/shard_map/ppermute | solution.py:605
  151.7 4.5 %collective-permute-start.45 = (bf16[1536,128]{1,0:T(8,128)(2,1)S(1)}, bf16[1536,128]{1,0:T(8,128)(2,1)S(1)}, u32[]{:S(2)}, u32[]{:S(2)}) collective-permute-start(bf16[1536,128]{1,0:T(8,128)(2,1)S(1)} %constant_dynamic-update-slice_fusion.mine), channel_id=1, source_target_pairs={{2,0},{0,2},{6,4},{4,6},{10,8},{8,10},{14,12},{12,14},{18,16},{16,... | collective-permute-start | bytes 1179656 | tf_op jit(solution)/shard_map/ppermute | solution.py:605
  156.7 4.0 %shard_map.213 = (f32[2,64,64,81]{3,2,1,0:T(8,128)}, f32[2,2,64,81]{3,2,1,0:T(8,128)}, f32[2,64,81]{2,1,0:T(8,128)}) custom-call(s32[5]{0:T(128)S(1)} %stack.19.refs_0_.refs_7_.refs_9_.refs_10_.coords, bf16[1536,128]{1,0:T(8,128)(2,1)S(1)} %constant_dynamic-update-slice_fusion.7.mine, bf16[1536,128]{1,0:T(8,128)(2,1)S(1)} %collective-permute-done.57.other), custom_call_target="tpu_custom_call" | custom-call | flops 2000000000 | bytes 8000000 | tf_op jit(solution)/shard_map/pallas_call | solution.py:555
  160.8 4.0 %shard_map.214 = (f32[2,64,64,81]{3,2,1,0:T(8,128)}, f32[2,2,64,81]{3,2,1,0:T(8,128)}, f32[2,64,81]{2,1,0:T(8,128)}) custom-call(s32[5]{0:T(128)S(1)} %stack.19.refs_0_.refs_7_.refs_9_.refs_10_.coords, bf16[1536,128]{1,0:T(8,128)(2,1)S(1)} %constant_dynamic-update-slice_fusion.mine, ...), custom_call_target="tpu_custom_call", output_to_operand_aliasing={{0}: (3, {}), {1}: (4, {}), {2}: (5, {})} | custom-call | flops 2000000000 | bytes 8000000 | tf_op jit(solution)/shard_map/pallas_call | solution.py:555
  (221 shorter events, 58.9 us)
Async XLA Ops:
  1.4 13.7 %collective-permute-start = (f32[1,512]{1,0:T(1,128)S(1)}, f32[1,512]{1,0:T(1,128)S(1)}, u32[]{:S(2)}, u32[]{:S(2)}) collective-permute-start(f32[1,512]{1,0:T(1,128)S(1)} %reshape.36), channel_id=1, source_target_pairs={{30,0},{31,1},{0,2},{1,3},{2,10},{3,11},{4,8},{5,9},{6,16},{7,17},... | collective-permute-start | bytes 6152 | tf_op jit(solution)/shard_map/ppermute | solution.py:646
  6.2 15.3 %collective-permute-start.1 = (f32[1,512]{1,0:T(1,128)S(1)}, f32[1,512]{1,0:T(1,128)S(1)}, u32[]{:S(2)}, u32[]{:S(2)}) collective-permute-start(f32[1,512]{1,0:T(1,128)S(1)} %reshape.36), channel_id=1, source_target_pairs={{31,0},{30,1},{1,2},{0,3},{3,10},{2,11},{5,8},{4,9},{7,16},{6,17},... | collective-permute-start | bytes 6152 | tf_op jit(solution)/shard_map/ppermute | solution.py:646
  9.1 12.3 %collective-permute-start.2 = (f32[1,512]{1,0:T(1,128)S(1)}, f32[1,512]{1,0:T(1,128)S(1)}, u32[]{:S(2)}, u32[]{:S(2)}) collective-permute-start(f32[1,512]{1,0:T(1,128)S(1)} %reshape.36), channel_id=1, source_target_pairs={{0,0},{1,1},{2,2},{3,3},{4,10},{5,11},{6,8},{7,9},{8,16},{9,17},{1... | collective-permute-start | bytes 6152 | tf_op jit(solution)/shard_map/ppermute | solution.py:646
  11.0 10.4 %collective-permute-start.3 = (f32[1,512]{1,0:T(1,128)S(1)}, f32[1,512]{1,0:T(1,128)S(1)}, u32[]{:S(2)}, u32[]{:S(2)}) collective-permute-start(f32[1,512]{1,0:T(1,128)S(1)} %reshape.36), channel_id=1, source_target_pairs={{1,0},{0,1},{3,2},{2,3},{5,10},{4,11},{7,8},{6,9},{9,16},{8,17},{1... | collective-permute-start | bytes 6152 | tf_op jit(solution)/shard_map/ppermute | solution.py:646
  11.7 9.8 %collective-permute-start.4 = (f32[1,512]{1,0:T(1,128)S(1)}, f32[1,512]{1,0:T(1,128)S(1)}, u32[]{:S(2)}, u32[]{:S(2)}) collective-permute-start(f32[1,512]{1,0:T(1,128)S(1)} %reshape.36), channel_id=1, source_target_pairs={{2,0},{3,1},{4,2},{5,3},{6,10},{7,11},{8,8},{9,9},{10,16},{11,17},... | collective-permute-start | bytes 6152 | tf_op jit(solution)/shard_map/ppermute | solution.py:646
  15.1 6.4 %collective-permute-start.5 = (f32[1,512]{1,0:T(1,128)S(1)}, f32[1,512]{1,0:T(1,128)S(1)}, u32[]{:S(2)}, u32[]{:S(2)}) collective-permute-start(f32[1,512]{1,0:T(1,128)S(1)} %reshape.36), channel_id=1, source_target_pairs={{3,0},{2,1},{5,2},{4,3},{7,10},{6,11},{9,8},{8,9},{11,16},{10,17},... | collective-permute-start | bytes 6152 | tf_op jit(solution)/shard_map/ppermute | solution.py:646
  21.5 16.0 %collective-permute-start.6 = (f32[3,1024]{1,0:T(4,128)S(1)}, f32[3,1024]{1,0:T(4,128)S(1)}, u32[]{:S(2)}, u32[]{:S(2)}) collective-permute-start(f32[3,1024]{1,0:T(4,128)S(1)} %maximum_maximum_fusion.refs_2_), channel_id=1, source_target_pairs={{6,0},{4,2},{0,10},{2,8},{10,16},{8,18},{16,26},{18,24},{26,28},{2... | collective-permute-start | bytes 36872 | tf_op jit(solution)/shard_map/ppermute | solution.py:632
  21.6 15.9 %collective-permute-start.7 = (f32[3,1024]{1,0:T(4,128)S(1)}, f32[3,1024]{1,0:T(4,128)S(1)}, u32[]{:S(2)}, u32[]{:S(2)}) collective-permute-start(f32[3,1024]{1,0:T(4,128)S(1)} %maximum_maximum_fusion.refs_2_), channel_id=1, source_target_pairs={{10,0},{8,2},{16,10},{18,8},{26,16},{24,18},{28,26},{30,24},{22,28... | collective-permute-start | bytes 36872 | tf_op jit(solution)/shard_map/ppermute | solution.py:632
  48.0 11.0 %collective-permute-start.11 = (f32[2,1024]{1,0:T(2,128)S(1)}, f32[2,1024]{1,0:T(2,128)S(1)}, u32[]{:S(2)}, u32[]{:S(2)}) collective-permute-start(f32[2,1024]{1,0:T(2,128)S(1)} %get-tuple-element.51.refs_3_), channel_id=1, source_target_pairs={{2,0},{10,2},{8,10},{16,8},{18,16},{26,18},{24,26},{28,24},{30,28}... | collective-permute-start | bytes 24584 | tf_op jit(solution)/shard_map/ppermute | solution.py:632
  49.3 9.7 %collective-permute-start.12 = (f32[2,1024]{1,0:T(2,128)S(1)}, f32[2,1024]{1,0:T(2,128)S(1)}, u32[]{:S(2)}, u32[]{:S(2)}) collective-permute-start(f32[2,1024]{1,0:T(2,128)S(1)} %get-tuple-element.51.refs_3_), channel_id=1, source_target_pairs={{10,0},{8,2},{16,10},{18,8},{26,16},{24,18},{28,26},{30,24},{22,28... | collective-permute-start | bytes 24584 | tf_op jit(solution)/shard_map/ppermute | solution.py:632
  49.7 9.3 %collective-permute-start.13 = (f32[2,1024]{1,0:T(2,128)S(1)}, f32[2,1024]{1,0:T(2,128)S(1)}, u32[]{:S(2)}, u32[]{:S(2)}) collective-permute-start(f32[2,1024]{1,0:T(2,128)S(1)} %get-tuple-element.51.refs_3_), channel_id=1, source_target_pairs={{8,0},{16,2},{18,10},{26,8},{24,16},{28,18},{30,26},{22,24},{20,28... | collective-permute-start | bytes 24584 | tf_op jit(solution)/shard_map/ppermute | solution.py:632
  50.1 9.0 %collective-permute-start.8 = (f32[2,1024]{1,0:T(2,128)S(1)}, f32[2,1024]{1,0:T(2,128)S(1)}, u32[]{:S(2)}, u32[]{:S(2)}) collective-permute-start(f32[2,1024]{1,0:T(2,128)S(1)} %get-tuple-element.51.refs_3_), channel_id=1, source_target_pairs={{14,0},{6,2},{4,10},{0,8},{2,16},{10,18},{8,26},{16,24},{18,28},{2... | collective-permute-start | bytes 24584 | tf_op jit(solution)/shard_map/ppermute | solution.py:632
  51.2 7.9 %collective-permute-start.9 = (f32[2,1024]{1,0:T(2,128)S(1)}, f32[2,1024]{1,0:T(2,128)S(1)}, u32[]{:S(2)}, u32[]{:S(2)}) collective-permute-start(f32[2,1024]{1,0:T(2,128)S(1)} %get-tuple-element.51.refs_3_), channel_id=1, source_target_pairs={{6,0},{4,2},{0,10},{2,8},{10,16},{8,18},{16,26},{18,24},{26,28},{2... | collective-permute-start | bytes 24584 | tf_op jit(solution)/shard_map/ppermute | solution.py:632
  65.7 6.5 %collective-permute-start.16 = (f32[2,1024]{1,0:T(2,128)S(1)}, f32[2,1024]{1,0:T(2,128)S(1)}, u32[]{:S(2)}, u32[]{:S(2)}) collective-permute-start(f32[2,1024]{1,0:T(2,128)S(1)} %get-tuple-element.56.refs_3_), channel_id=1, source_target_pairs={{6,0},{4,2},{0,10},{2,8},{10,16},{8,18},{16,26},{18,24},{26,28},{2... | collective-permute-start | bytes 24584 | tf_op jit(solution)/shard_map/ppermute | solution.py:632
  79.5 6.5 %collective-permute-start.22 = (f32[3,1024]{1,0:T(4,128)S(1)}, f32[3,1024]{1,0:T(4,128)S(1)}, u32[]{:S(2)}, u32[]{:S(2)}) collective-permute-start(f32[3,1024]{1,0:T(4,128)S(1)} %get-tuple-element.64.refs_3_), channel_id=1, source_target_pairs={{6,0},{4,2},{0,10},{2,8},{10,16},{8,18},{16,26},{18,24},{26,28},{2... | collective-permute-start | bytes 36872 | tf_op jit(solution)/shard_map/ppermute | solution.py:632
  96.1 16.5 %collective-permute-start.32 = (f32[16,128]{1,0:T(8,128)S(1)}, f32[16,128]{1,0:T(8,128)S(1)}, u32[]{:S(2)}, u32[]{:S(2)}) collective-permute-start(f32[16,128]{1,0:T(8,128)S(1)} %add.94), channel_id=1, source_target_pairs={{8,0},{10,2},{12,4},{14,6},{0,8},{2,10},{4,12},{6,14},{24,16},{26,... | collective-permute-start | bytes 24584 | tf_op jit(solution)/shard_map/ppermute | solution.py:695
  97.0 13.3 %collective-permute-start.14 = (f32[1,512]{1,0:T(1,128)S(1)}, f32[1,512]{1,0:T(1,128)S(1)}, u32[]{:S(2)}, u32[]{:S(2)}) collective-permute-start(f32[1,512]{1,0:T(1,128)S(1)} %get-tuple-element.55), channel_id=1, source_target_pairs={{0,0},{2,2},{10,4},{8,6},{16,8},{18,10},{26,12},{24,14},{28,16},{3... | collective-permute-start | bytes 6152 | tf_op jit(solution)/shard_map/ppermute | solution.py:679
  102.4 10.3 %collective-permute-start.27 = (f32[1,512]{1,0:T(1,128)S(1)}, f32[1,512]{1,0:T(1,128)S(1)}, u32[]{:S(2)}, u32[]{:S(2)}) collective-permute-start(f32[1,512]{1,0:T(1,128)S(1)} %get-tuple-element.73), channel_id=1, source_target_pairs={{0,30},{2,0},{10,2},{8,4},{16,6},{18,8},{26,10},{24,12},{28,14},{3... | collective-permute-start | bytes 6152 | tf_op jit(solution)/shard_map/ppermute | solution.py:689
  106.0 9.3 %collective-permute-start.28 = (f32[1,512]{1,0:T(1,128)S(1)}, f32[1,512]{1,0:T(1,128)S(1)}, u32[]{:S(2)}, u32[]{:S(2)}) collective-permute-start(f32[1,512]{1,0:T(1,128)S(1)} %get-tuple-element.74), channel_id=1, source_target_pairs={{0,0},{2,2},{10,4},{8,6},{16,8},{18,10},{26,12},{24,14},{28,16},{3... | collective-permute-start | bytes 6152 | tf_op jit(solution)/shard_map/ppermute | solution.py:689
  107.9 7.4 %collective-permute-start.29 = (f32[1,512]{1,0:T(1,128)S(1)}, f32[1,512]{1,0:T(1,128)S(1)}, u32[]{:S(2)}, u32[]{:S(2)}) collective-permute-start(f32[1,512]{1,0:T(1,128)S(1)} %get-tuple-element.75), channel_id=1, source_target_pairs={{0,2},{2,4},{10,6},{8,8},{16,10},{18,12},{26,14},{24,16},{28,18},{... | collective-permute-start | bytes 6152 | tf_op jit(solution)/shard_map/ppermute | solution.py:689
  112.6 7.7 %collective-permute-start.34 = (bf16[768,128]{1,0:T(8,128)(2,1)S(1)}, bf16[768,128]{1,0:T(8,128)(2,1)S(1)}, u32[]{:S(2)}, u32[]{:S(2)}) collective-permute-start(bf16[768,128]{1,0:T(8,128)(2,1)S(1)} %get-tuple-element.78), channel_id=1, source_target_pairs={{2,0},{0,2},{6,4},{4,6},{10,8},{8,10},{14,12},{12,14},{18,16},{16,... | collective-permute-start | bytes 589832 | tf_op jit(solution)/shard_map/ppermute | solution.py:576
  120.4 6.8 %collective-permute-start.35 = (bf16[384,128]{1,0:T(8,128)(2,1)S(1)}, bf16[384,128]{1,0:T(8,128)(2,1)S(1)}, u32[]{:S(2)}, u32[]{:S(2)}) collective-permute-start(bf16[384,128]{1,0:T(8,128)(2,1)S(1)} %get-tuple-element.103), channel_id=1, source_target_pairs={{4,0},{6,2},{0,4},{2,6},{12,8},{14,10},{8,12},{10,14},{20,16},{22,... | collective-permute-start | bytes 294920 | tf_op jit(solution)/shard_map/ppermute | solution.py:580
  122.4 5.7 %collective-permute-start.48 = (bf16[96,128]{1,0:T(8,128)(2,1)S(1)}, bf16[96,128]{1,0:T(8,128)(2,1)S(1)}, u32[]{:S(2)}, u32[]{:S(2)}) collective-permute-start(bf16[96,128]{1,0:T(8,128)(2,1)S(1)} %get-tuple-element.104), channel_id=1, source_target_pairs={{24,0},{26,2},{28,4},{30,6},{0,8},{2,10},{4,12},{6,14},{8,16},{10,... | collective-permute-start | bytes 73736 | tf_op jit(solution)/shard_map/ppermute | solution.py:585
  124.1 6.4 %collective-permute-start.49 = (bf16[96,128]{1,0:T(8,128)(2,1)S(1)}, bf16[96,128]{1,0:T(8,128)(2,1)S(1)}, u32[]{:S(2)}, u32[]{:S(2)}) collective-permute-start(bf16[96,128]{1,0:T(8,128)(2,1)S(1)} %get-tuple-element.106), channel_id=1, source_target_pairs={{16,0},{18,2},{20,4},{22,6},{24,8},{26,10},{28,12},{30,14},{0,16},... | collective-permute-start | bytes 73736 | tf_op jit(solution)/shard_map/ppermute | solution.py:585
  127.2 6.3 %collective-permute-start.37 = (bf16[96,128]{1,0:T(8,128)(2,1)S(1)}, bf16[96,128]{1,0:T(8,128)(2,1)S(1)}, u32[]{:S(2)}, u32[]{:S(2)}) collective-permute-start(bf16[96,128]{1,0:T(8,128)(2,1)S(1)} %get-tuple-element.109), channel_id=1, source_target_pairs={{16,0},{18,2},{20,4},{22,6},{24,8},{26,10},{28,12},{30,14},{0,16},... | collective-permute-start | bytes 73736 | tf_op jit(solution)/shard_map/ppermute | solution.py:585
  133.6 5.9 %collective-permute-start.39 = (bf16[96,128]{1,0:T(8,128)(2,1)S(1)}, bf16[96,128]{1,0:T(8,128)(2,1)S(1)}, u32[]{:S(2)}, u32[]{:S(2)}) collective-permute-start(bf16[96,128]{1,0:T(8,128)(2,1)S(1)} %get-tuple-element.99), channel_id=1, source_target_pairs={{8,0},{10,2},{12,4},{14,6},{16,8},{18,10},{20,12},{22,14},{24,16},... | collective-permute-start | bytes 73736 | tf_op jit(solution)/shard_map/ppermute | solution.py:589
  136.9 6.3 %collective-permute-start.54 = (bf16[384,128]{1,0:T(8,128)(2,1)S(1)}, bf16[384,128]{1,0:T(8,128)(2,1)S(1)}, u32[]{:S(2)}, u32[]{:S(2)}) collective-permute-start(bf16[384,128]{1,0:T(8,128)(2,1)S(1)} %pad_maximum_fusion.1), channel_id=1, source_target_pairs={{4,0},{5,1},{6,2},{7,3},{0,4},{1,5},{2,6},{3,7},{12,8},{13,9},{14,... | collective-permute-start | bytes 294920 | tf_op jit(solution)/shard_map/ppermute | solution.py:603
  140.2 11.4 %collective-permute-start.42 = (bf16[384,128]{1,0:T(8,128)(2,1)S(1)}, bf16[384,128]{1,0:T(8,128)(2,1)S(1)}, u32[]{:S(2)}, u32[]{:S(2)}) collective-permute-start(bf16[384,128]{1,0:T(8,128)(2,1)S(1)} %pad_maximum_fusion), channel_id=1, source_target_pairs={{4,0},{5,1},{6,2},{7,3},{0,4},{1,5},{2,6},{3,7},{12,8},{13,9},{14,... | collective-permute-start | bytes 294920 | tf_op jit(solution)/shard_map/ppermute | solution.py:603
  141.9 9.6 %collective-permute-start.43 = (bf16[384,128]{1,0:T(8,128)(2,1)S(1)}, bf16[384,128]{1,0:T(8,128)(2,1)S(1)}, u32[]{:S(2)}, u32[]{:S(2)}) collective-permute-start(bf16[384,128]{1,0:T(8,128)(2,1)S(1)} %pad_maximum_fusion), channel_id=1, source_target_pairs={{1,0},{0,1},{3,2},{2,3},{5,4},{4,5},{7,6},{6,7},{9,8},{8,9},{11,10... | collective-permute-start | bytes 294920 | tf_op jit(solution)/shard_map/ppermute | solution.py:603
  143.2 8.4 %collective-permute-start.44 = (bf16[384,128]{1,0:T(8,128)(2,1)S(1)}, bf16[384,128]{1,0:T(8,128)(2,1)S(1)}, u32[]{:S(2)}, u32[]{:S(2)}) collective-permute-start(bf16[384,128]{1,0:T(8,128)(2,1)S(1)} %pad_maximum_fusion), channel_id=1, source_target_pairs={{5,0},{4,1},{7,2},{6,3},{1,4},{0,5},{3,6},{2,7},{13,8},{12,9},{15,... | collective-permute-start | bytes 294920 | tf_op jit(solution)/shard_map/ppermute | solution.py:603
  144.1 12.7 %collective-permute-start.57 = (bf16[1536,128]{1,0:T(8,128)(2,1)S(1)}, bf16[1536,128]{1,0:T(8,128)(2,1)S(1)}, u32[]{:S(2)}, u32[]{:S(2)}) collective-permute-start(bf16[1536,128]{1,0:T(8,128)(2,1)S(1)} %constant_dynamic-update-slice_fusion.7.mine), channel_id=1, source_target_pairs={{2,0},{0,2},{6,4},{4,6},{10,8},{8,10},{14,12},{12,14},{18,16},{16,... | collective-permute-start | bytes 1179656 | tf_op jit(solution)/shard_map/ppermute | solution.py:605
  151.7 9.1 %collective-permute-start.45 = (bf16[1536,128]{1,0:T(8,128)(2,1)S(1)}, bf16[1536,128]{1,0:T(8,128)(2,1)S(1)}, u32[]{:S(2)}, u32[]{:S(2)}) collective-permute-start(bf16[1536,128]{1,0:T(8,128)(2,1)S(1)} %constant_dynamic-update-slice_fusion.mine), channel_id=1, source_target_pairs={{2,0},{0,2},{6,4},{4,6},{10,8},{8,10},{14,12},{12,14},{18,16},{16,... | collective-permute-start | bytes 1179656 | tf_op jit(solution)/shard_map/ppermute | solution.py:605
  (66 other events, 428.6 us)

commit v3 on v1

v3 whole, which is shorter than its diff:
```python
import functools

import jax
import jax.numpy as jnp
import numpy as np
from jax import lax
from jax.experimental import pallas as pl
from jax.experimental.pallas import tpu as pltpu
from jax.sharding import PartitionSpec as P

hopping = 0.3
quartic = 0.05

STEPS = (-1, 0, 1)
ROWS = 8
MID = 3
BF = jnp.bfloat16
F32 = jnp.float32
TAPS = 81
VMEM_MB = 20


def ring_order(count):
    if count % 4:
        return list(range(count))
    depth = count // 4
    chips = [(z, 0) for z in range(depth)] + [(z, 1) for z in reversed(range(depth))]
    order = []
    for place, (z, y) in enumerate(chips):
        cores = (0, 1) if place % 2 == 0 else (1, 0)
        order += [z * 4 + y * 2 + core for core in cores]
    return order


def spread_first():
    out = np.zeros((81, 5, 256), np.float32)
    for tap in range(81):
        dx, rest = divmod(tap, 27)
        for dest in range(5):
            out[tap, dest, rest * ROWS + dest + dx] = 1
    return out.reshape(81, 5 * 256)


def spread_last():
    out = np.zeros((3, 2, 216, 81), np.float32)
    for tap in range(81):
        dx, rest = divmod(tap, 27)
        for o in range(2):
            out[dx, o, rest * 8 + o, tap] = 1
    return out


def spread_last_back():
    out = np.zeros((2, 81, 3, 512), np.float32)
    for tap in range(81):
        dx, rest = divmod(tap, 27)
        for o in range(2):
            for dest in range(3):
                out[o, tap, dest, rest * 16 + o * ROWS + 2 + dest - (dx - 1)] = 1
    return out.reshape(2, 81, 3 * 512)


def spread_first_back():
    out = np.zeros((216, 81), np.float32)
    for tap in range(81):
        dx, rest = divmod(tap, 27)
        out[rest * 8 + dx, tap] = 1
    return out


def pick_last():
    out = np.zeros((432, 2, 128), np.float32)
    for tap in range(81):
        dx, rest = divmod(tap, 27)
        for o in range(2):
            out[rest * 16 + o * ROWS + MID - (dx - 1), o, tap] = 1
    return out.reshape(432, 256)


def pick_first():
    out = np.zeros((216, 128), np.float32)
    for tap in range(81):
        dx, rest = divmod(tap, 27)
        out[rest * ROWS + MID + dx - 1, tap] = 1
    return out


def z_shift(values, dz):
    length = values.shape[1]
    return values if dz == 0 else pltpu.roll(values, (-dz * 128) % length, 1)


def by_plane(values, fn):
    parts = [fn(values[:, at : at + 128]) for at in range(0, values.shape[1], 128)]
    return parts[0] if len(parts) == 1 else jnp.concatenate(parts, axis=1)


def y_shift(values, dy, period):
    if dy == 0:
        return values
    return by_plane(values, lambda v: pltpu.roll(v, (-dy * period) % 128, 1))


def t_shift(values, dt, period):
    if dt == 0:
        return values

    def one(v):
        place = lax.broadcasted_iota(jnp.int32, v.shape, 1) % period
        main = pltpu.roll(v, (-dt) % 128, 1)
        wrap = pltpu.roll(v, (dt * (period - 1)) % 128, 1)
        return jnp.where(place == (period - 1 if dt == 1 else 0), wrap, main)

    return by_plane(values, one)


def all_shifts(values, sign, period):
    in_t = [t_shift(values, sign * dt, period) for dt in STEPS]
    in_y = [[y_shift(v, sign * dy, period) for v in in_t] for dy in STEPS]
    return [z_shift(in_y[dy][dt], sign * dz) for dz in STEPS for dy in range(3) for dt in range(3)]


def gather_narrow(values, sign, period):
    block = lambda k: values[k * 8 : k * 8 + 8]
    total = None
    for dt in range(3):
        over_y = None
        for dy in range(3):
            over_z = sum(z_shift(block(dz * 9 + dy * 3 + dt), sign * (dz - 1)) for dz in range(3))
            over_z = y_shift(over_z, sign * (dy - 1), period)
            over_y = over_z if over_y is None else over_y + over_z
        over_y = t_shift(over_y, sign * (dt - 1), period)
        total = over_y if total is None else total + over_y
    return total


def gather_wide(values, channels, sign, period):
    block = lambda k: values[k * channels : (k + 1) * channels]
    total = None
    for dt in range(3):
        over_y = None
        for dy in range(3):
            part = y_shift(block(dy * 3 + dt), sign * (dy - 1), period)
            over_y = part if over_y is None else over_y + part
        over_y = t_shift(over_y, sign * (dt - 1), period)
        total = over_y if total is None else total + over_y
    return total


def dot(a, b):
    return jnp.dot(a, b, preferred_element_type=F32)


def dot_nt(a, b):
    return lax.dot_general(a, b, (((1,), (1,)), ((), ())), preferred_element_type=F32)


def stack_planes(stack, planes, channels, order):
    length = stack.shape[1]
    for dx in range(3):
        for dz in range(3):
            plane, step = order(dx, dz)
            rows = pl.ds((dx * 3 + dz) * channels, channels)
            source = planes[plane * channels : (plane + 1) * channels, :]
            if step == 0:
                stack[rows, :] = source
            elif step == 1:
                stack[rows, : length - 128] = source[:, 128:]
                stack[rows, length - 128 :] = source[:, :128]
            else:
                stack[rows, 128:] = source[:, : length - 128]
                stack[rows, :128] = source[:, length - 128 :]


def pack_kernel(layer, ready, w_mid, w_first, w_last, b_first, b_mid, b_last, lanes, rows_81,
                matrix, first, narrow, last_back, first_back, turned, columns, taps, rows):
    channels = w_mid.shape[1]
    for o in range(0, channels, 2):
        pair = w_mid[layer, o : o + 2].reshape(2 * channels, TAPS).astype(F32).T
        taps[pl.ds(o, TAPS, stride=channels), :] = pair[:, :channels]
        taps[pl.ds(o + 1, TAPS, stride=channels), :] = pair[:, channels:]
    block = lambda tap: taps[tap * channels : (tap + 1) * channels, :]
    for inner in range(9):
        at = pl.ds(inner * channels, channels)
        for outer in range(0, 9, 2):
            low = block(outer * 9 + inner)
            if outer < 8:
                high = block(outer * 9 + 9 + inner)
                wide = slice(outer * channels, (outer + 2) * channels)
                matrix[at, wide] = jnp.concatenate([low, high], axis=1).astype(BF)
            else:
                matrix[at, outer * channels :] = low.astype(BF)
    for inner in range(9):
        at = pl.ds(inner * channels, channels)
        for outer in range(0, 9, 2):
            if outer < 8:
                wide = slice(outer * channels, (outer + 2) * channels)
                both = matrix[at, wide].astype(F32).T
                turned[at, wide] = jnp.concatenate([both[:channels], both[channels:]], axis=1).astype(BF)
            else:
                turned[at, outer * channels :] = matrix[at, outer * channels :].astype(F32).T.astype(BF)
    wf = w_first[layer]
    first[...] = dot(wf, lanes[:, : 5 * 256]).astype(BF)
    first_back[...] = dot_nt(rows_81[6 * 216 : 7 * 216, :TAPS], wf).astype(BF)
    for dx in range(3):
        narrow[dx] = sum(
            dot_nt(rows_81[(dx * 2 + o) * 216 : (dx * 2 + o + 1) * 216, :TAPS], w_last[layer, o])
            for o in range(2)
        ).astype(BF)
    last_back[...] = sum(
        dot(w_last[layer, o], lanes[:, 5 * 256 + o * 1536 : 5 * 256 + (o + 1) * 1536]) for o in range(2)
    ).astype(BF)
    rows[...] = jnp.zeros_like(rows)
    rows[0:1, :channels] = b_first[layer : layer + 1, :]
    rows[1:2, :channels] = b_mid[layer : layer + 1, :]
    rows[2:3, :2] = b_last[layer : layer + 1, :]
    columns[...] = rows[...].T


def unpack_kernel(layout, volume, last, ready, coords, pieces, *refs):
    if last:
        refs = refs[3:]
        g_mid, g_last, g_first, gb_first, gb_mid, gb_last, loss = refs[:7]
        bulk, taps, mid, lasts, firsts, sems = refs[7:]
    else:
        g_mid, g_last, g_first = refs[:3]
        bulk, taps, mid, lasts, firsts, sems = refs[3:]
    channels = g_mid.shape[2]
    few = channels // 2
    halves, depth, chunk = layout
    g, y, z = coords[1], coords[3], coords[4]
    core = 1 - coords[2] if last else coords[2]
    per_layer = 2 * halves * depth * chunk
    at = 0
    for rg in range(halves):
        for ry in range(2):
            for rz in range(depth):
                to = ((lax.rem(g + rg, halves) * 2 + (1 - y if ry else y)) * depth
                      + lax.rem(z + rz, depth)) * chunk
                for layer in range(2):
                    bulk[layer, pl.ds(pl.multiple_of(to, 16), chunk), :] = pieces[at : at + chunk, :]
                    at += chunk
    rows = 9 * few
    copies = []
    for layer in range(2):
        for tap in range(TAPS):
            outer, inner = divmod(tap, 9)
            start = (outer // 2) * rows + inner * few
            low = (outer % 2) * channels
            taps[tap * few : (tap + 1) * few, :] = (
                bulk[layer, start : start + few, low : low + channels].astype(F32) * (1.0 / volume)
            )
        for o in range(0, few, 2):
            pair = jnp.concatenate(
                [taps[pl.ds(o, TAPS, stride=few), :], taps[pl.ds(o + 1, TAPS, stride=few), :]],
                axis=1,
            )
            mid[layer, o : o + 2] = pair.T.reshape(2, channels, TAPS)
        rest = bulk[layer, 5 * rows : 5 * rows + channels + few, :].astype(F32) * (1.0 / volume)
        lasts[layer] = rest[:channels, :TAPS]
        firsts[layer] = rest[channels:, :TAPS]
        if last:
            small = bulk[layer, 4 * rows : 4 * rows + 16, channels:].astype(F32) * (1.0 / volume)
            gb_first[layer : layer + 1, :] = small[0:1]
            gb_mid[layer : layer + 1, :] = small[1:2]
            gb_last[layer : layer + 1, :] = small[2:3, :2]
            if layer == 1:
                loss[...] = jnp.sum(
                    jnp.sum(small[3:6], axis=0, keepdims=True), axis=1, keepdims=True
                )
        copies += [
            pltpu.make_async_copy(
                mid.at[layer], g_mid.at[layer, pl.ds(core * few, few)], sems.at[layer * 3]
            ),
            pltpu.make_async_copy(lasts.at[layer], g_last.at[layer, core], sems.at[layer * 3 + 1]),
            pltpu.make_async_copy(
                firsts.at[layer],
                g_first.at[layer, pl.ds(pl.multiple_of(core * few, few), few)],
                sems.at[layer * 3 + 2],
            ),
        ]
        for copy in copies[-3:]:
            copy.start()
    for copy in copies:
        copy.wait()


def place_windows(refs, row, target):
    target[...] = jnp.zeros_like(target)
    for r, ref in enumerate(refs):
        target[r : r + 1, :] = ref[row : row + 1, :]


def oddness(shape, place, period):
    lane = lax.broadcasted_iota(jnp.int32, shape, 1)
    row = lax.broadcasted_iota(jnp.int32, shape, 0)
    within = lane % 128
    return ((place + row + 1 + lane // 128 + within // period + within % period) % 2).astype(F32)


def forward_kernel(period, layer, halves, ready, *refs):
    windows, refs = refs[:7], refs[7:]
    if layer == 0:
        (coords, w_first, w_mid, w_last, columns,
         field_out, state, own_out, logdet, first_out, second_out, first, stack) = refs
        field_out[...] = jnp.zeros_like(field_out)
        piece = field_out.shape[1] // halves
        for rel in range(halves):
            to = pl.multiple_of(lax.rem(coords[1] + rel, halves) * piece, 128)
            for r, ref in enumerate(windows):
                field_out[r : r + 1, pl.ds(to, piece)] = ref[:, rel * piece : (rel + 1) * piece]
    else:
        (coords, w_first, w_mid, w_last, columns,
         field_out, state, own_out, logdet, growth_out, first_out, second_out,
         first, stack) = refs
        place_windows(windows, 0, field_out)
        place_windows(windows, 1, growth_out)
    channels = w_mid.shape[0] // 9
    field = field_out[...]
    length = field.shape[1]
    frozen = oddness(field.shape, coords[0], period)
    if layer == 1:
        frozen = 1.0 - frozen
    net = frozen * field
    taps = jnp.concatenate(all_shifts(net, 1, period), axis=0).astype(BF)
    ready(w_first, columns)
    bias_first, bias_mid = columns[:channels, 0:1], columns[:channels, 1:2]
    for dest in range(5):
        part = dot(w_first[:, dest * 256 : dest * 256 + 216], taps)
        first[dest * channels : (dest + 1) * channels, :] = jnp.tanh(part + bias_first).astype(BF)
    first_out[...] = first[channels : 4 * channels, :]
    ready(w_mid)
    for dest in range(3):
        stack_planes(stack, first, channels, lambda dx, dz: (dest + dx, dz - 1))
        for at in range(0, length, 256):
            wide = dot(w_mid[...], stack[:, at : at + 256])
            wide = gather_wide(wide, channels, 1, period)
            second_out[dest * channels : (dest + 1) * channels, at : at + 256] = jnp.tanh(
                wide + bias_mid
            ).astype(BF)
    ready(w_last)
    narrow = sum(
        dot(w_last[dx], second_out[dx * channels : (dx + 1) * channels, :]) for dx in range(3)
    )
    narrow = gather_narrow(narrow, 1, period) + columns[:8, 2:3]
    growth = jnp.exp(narrow[0:1])
    mine = field[MID : MID + 1]
    still = frozen[MID : MID + 1]
    moving = 1.0 - still
    state[0:1, :] = still * mine + moving * (mine * growth + narrow[1:2])
    state[1:2, :] = growth
    own_out[...] = state[0:1, :]
    flow = moving * narrow[0:1]
    logdet[...] = sum(flow[:, at : at + 128] for at in range(0, length, 128))


def put_chunks(layout, coords, bulks, send, keep):
    halves, depth, chunk = layout
    per_core = bulks[0].shape[0] // 2
    g, c, y, z = (coords[i] for i in range(1, 5))
    for core, ref in ((c, keep), (1 - c, send)):
        at = 0
        for ry in range(2):
            for rz in range(depth):
                source = core * per_core + (
                    (g * 2 + (1 - y if ry else y)) * depth + lax.rem(z + rz, depth)
                ) * chunk
                for bulk in bulks:
                    ref[at : at + chunk, :] = bulk[pl.ds(pl.multiple_of(source, 16), chunk), :]
                    at += chunk


def output_taps(grad_output, period):
    return jnp.concatenate(all_shifts(grad_output, -1, period), axis=0).astype(BF)


def output_gradient(upstream, moving, field, grow):
    place = lax.broadcasted_iota(jnp.int32, (2 * ROWS, field.shape[1]), 0) % ROWS
    grad_scale = upstream * moving * field * grow - moving
    grad_shift = upstream * moving
    both = jnp.concatenate([grad_scale, grad_shift], axis=0)
    return jnp.where(jnp.logical_and(place >= 1, place <= 5), both, 0.0)


def second_gradient(w_last, second, taps, mids):
    channels = mids.shape[0] // 3
    for dest in range(3):
        part = dot(w_last[:, dest * 512 : dest * 512 + 432], taps)
        rows = slice(dest * channels, (dest + 1) * channels)
        wide = second[rows, :].astype(F32)
        mids[rows, :] = (part * (1.0 - wide * wide)).astype(BF)


def first_gradient(period, mids, first, w_mid, stack, grad_first):
    channels = mids.shape[0] // 3
    stack_planes(stack, mids, channels, lambda dx, dz: (2 - dx, 1 - dz))
    for at in range(0, stack.shape[1], 256):
        wide = dot(w_mid[...], stack[:, at : at + 256])
        wide = gather_wide(wide, channels, -1, period)
        seen = first[channels : 2 * channels, at : at + 256].astype(F32)
        grad_first[:, at : at + 256] = (wide * (1.0 - seen * seen)).astype(BF)


def first_weights(period, net, grad_first, pick_f):
    taps = jnp.concatenate(all_shifts(net, 1, period), axis=0).astype(BF)
    g_first = dot_nt(grad_first, taps).astype(BF)
    return dot(g_first, pick_f)


def fill_bulk(period, mids, first, second, taps, pick_l, g_first, small, stack, turned, bulk):
    channels = mids.shape[0] // 3
    few = channels // 2
    own = slice(channels, 2 * channels)
    rounded = mids[own, :].astype(F32)
    in_t = [t_shift(rounded, -dt, period) for dt in STEPS]
    for dy in range(3):
        for dt in range(3):
            turned[(dy * 3 + dt) * channels : (dy * 3 + dt + 1) * channels, :] = y_shift(
                in_t[dt], -STEPS[dy], period
            ).astype(BF)
    stack_planes(stack, first, channels, lambda dx, dz: (dx, dz - 1))
    g_mid = dot_nt(turned[...], stack[...]).astype(BF)
    per_core = bulk.shape[0] // 2
    rows = 9 * few
    g_last = dot_nt(second[own, :], taps).astype(BF)
    g_last = dot(g_last, pick_l).astype(BF)
    for core in range(2):
        base = core * per_core
        for b in range(5):
            for inner in range(9):
                at = inner * channels + core * few
                part = g_mid[at : at + few, b * 128 : (b + 1) * 128]
                if part.shape[1] < 128:
                    part = jnp.concatenate([part, jnp.zeros((few, 128 - part.shape[1]), BF)], axis=1)
                to = base + b * rows + inner * few
                bulk[to : to + few, :] = part
        at = base + 4 * rows
        bulk[at : at + 16, channels:] = small.astype(BF)
        at = base + 5 * rows
        bulk[at : at + channels, :] = g_last[:, core * 128 : (core + 1) * 128]
        bulk[at + channels : at + channels + few, :] = g_first[core * few : (core + 1) * few, :].astype(BF)
        at += channels + few
        if at < base + per_core:
            bulk[at : base + per_core, :] = jnp.zeros((base + per_core - at, 128), BF)


def bias_rows(small, grad_output, mids, grad_first):
    channels = mids.shape[0] // 3
    ones = jnp.ones((8, mids.shape[1]), BF)
    small[0:1, :] = dot_nt(ones, grad_first)[0:1]
    small[1:2, :] = dot_nt(ones, mids[channels : 2 * channels, :])[0:1]
    sums = dot_nt(ones, grad_output.astype(BF))
    small[2:3, 0:1] = sums[0:1, MID : MID + 1]
    small[2:3, 1:2] = sums[0:1, 8 + MID : 9 + MID]


def back_one_kernel(period, ready, *refs):
    windows, refs = refs[:7], refs[7:]
    (logdet0, logdet1, coords, field_in, first_in, second_in, w_last, w_mid, w_first,
     base_out, part_out, small, grad_out, mids, grad_first, field_end, growth, stack) = refs
    place_windows(windows, 0, field_end)
    place_windows(windows, 1, growth)
    frozen = 1.0 - oddness(field_in.shape, coords[0], period)
    moving = 1.0 - frozen
    field = field_end[...]
    ahead = (
        pltpu.roll(field, ROWS - 1, 0)
        + z_shift(field, 1)
        + y_shift(field, 1, period)
        + t_shift(field, 1, period)
    )
    behind = (
        pltpu.roll(field, 1, 0)
        + z_shift(field, -1)
        + y_shift(field, -1, period)
        + t_shift(field, -1, period)
    )
    squared = field * field
    density = (
        -2.0 * hopping * field * ahead + squared + quartic * (squared - 1.0) * (squared - 1.0)
    )[MID : MID + 1]
    action = sum(density[:, at : at + 128] for at in range(0, field.shape[1], 128))
    loss = jnp.sum(action - logdet0[...] - logdet1[...], axis=1, keepdims=True)
    small[...] = jnp.zeros_like(small)
    slot = lax.broadcasted_iota(jnp.int32, (1, small.shape[1]), 1) == coords[0]
    for part in range(3):
        top = loss.astype(BF).astype(F32)
        small[3 + part : 4 + part, :] = jnp.where(slot, top, 0.0)
        loss = loss - top
    place = lax.broadcasted_iota(jnp.int32, field.shape, 0)
    upstream = (
        -2.0 * hopping * (ahead + behind) + 2.0 * field + 4.0 * quartic * (squared - 1.0) * field
    )
    upstream = jnp.where(jnp.logical_and(place >= 1, place <= 5), upstream, 0.0)
    grow = growth[...]
    grad_out[...] = output_gradient(upstream, moving, field_in[...], grow)
    base_out[...] = upstream * (frozen + moving * grow)
    taps = output_taps(grad_out[...], period)
    ready(w_last, second_in)
    second_gradient(w_last, second_in, taps, mids)
    ready(w_mid, first_in)
    first_gradient(period, mids, first_in, w_mid, stack, grad_first)
    bias_rows(small, grad_out[...], mids, grad_first[...])
    ready(w_first)
    narrow = gather_narrow(dot(w_first[...], grad_first[...]), -1, period)
    for d in range(3):
        part_out[d : d + 1, :] = frozen[MID - 1 + d : MID + d] * narrow[d : d + 1]


def weights_one_kernel(period, ready, coords, field_in, first_in, second_in, grad_out, mids, grad_first, small,
                       pick_l, pick_f, bulk, stack, turned):
    taps = output_taps(grad_out[...], period)
    frozen = 1.0 - oddness(field_in.shape, coords[0], period)
    ready(first_in, second_in, pick_l, pick_f)
    g_first = first_weights(period, frozen * field_in[...], grad_first[...], pick_f[...])
    fill_bulk(
        period, mids, first_in, second_in, taps, pick_l[...], g_first, small[...], stack, turned, bulk
    )


def back_zero_kernel(period, layout, ready, *refs):
    windows, refs = refs[:7], refs[7:]
    (base_in, growth, own_in, coords, field_in, bulk_one, first_in, second_in, w_last, w_mid, w_first,
     pick_l, pick_f,
     part_low, part_mid, part_high, send, keep,
     upstream_ref, mids, stack, turned, bulk, grad_first, small) = refs
    frozen = oddness(field_in.shape, coords[0], period)
    upstream_ref[...] = base_in[...]
    for r in range(1, 6):
        upstream_ref[r : r + 1, :] += (
            windows[r - 1][2:3, :] + windows[r][1:2, :] + windows[r + 1][0:1, :]
        )
    grad_output = output_gradient(upstream_ref[...], 1.0 - frozen, field_in[...], growth[...])
    taps = output_taps(grad_output, period)
    ready(w_last, second_in)
    second_gradient(w_last, second_in, taps, mids)
    ready(w_mid, first_in)
    first_gradient(period, mids, first_in, w_mid, stack, grad_first)
    small[...] = jnp.zeros_like(small)
    bias_rows(small, grad_output, mids, grad_first[...])
    ready(w_first, pick_f, pick_l)
    g_first = first_weights(period, frozen * field_in[...], grad_first[...], pick_f[...])
    fill_bulk(
        period, mids, first_in, second_in, taps, pick_l[...], g_first, small[...], stack, turned, bulk
    )
    ready(bulk_one)
    put_chunks(layout, coords, (bulk, bulk_one), send, keep)
    narrow = gather_narrow(dot(w_first[...], grad_first[...]), -1, period)
    base = upstream_ref[...] * (frozen + (1.0 - frozen) * growth[...])
    for d in range(3):
        row = frozen[MID - 1 + d : MID + d] * narrow[d : d + 1]
        if d == 1:
            row = row + base[MID : MID + 1]
        if d == 1:
            part_mid[0:1, :] = row
        else:
            (part_low if d == 0 else part_high)[...] = row
    part_mid[1:2, :] = own_in[...]


def force_kernel(ready, coords, above, middle, below, out):
    piece = out.shape[1]
    lanes = pl.ds(pl.multiple_of(coords[1] * piece, 128), piece)
    out[0:1, :] = above[:, lanes] + middle[0:1, lanes] + below[:, lanes]
    out[1:2, :] = middle[1:2, lanes]


def stage(jobs, after=()):
    arrays, outs, plan = [], [], []
    for kind, parts, group in jobs:
        first = len(arrays)
        arrays += group
        rows = group[0].shape[0]
        if kind == "split":
            sizes = [rows // parts] * parts
        elif kind == "sum":
            sizes = [rows]
        else:
            sizes = [sum(a.shape[0] for a in group)]
        plan.append((kind, first, len(group), len(outs), sizes))
        outs += [shape((n, 128), BF) for n in sizes]
    waits = len(after)

    def body(_, *refs):
        ins, results = refs[: len(arrays)], refs[len(arrays) + waits :]
        for kind, first, many, out, sizes in plan:
            group = ins[first : first + many]
            if kind == "join":
                at = 0
                for ref in group:
                    results[out][at : at + ref.shape[0], :] = ref[...]
                    at += ref.shape[0]
                continue
            at = 0
            for i, n in enumerate(sizes):
                results[out + i][...] = sum(ref[at : at + n, :].astype(F32) for ref in group).astype(BF)
                at += n

    got = kernel_call(body, outs, [], [*arrays, *after], 1_000_000, loose=after, vmem=12, bytes_moved=500_000)
    groups, at = [], 0
    for _, _, _, _, sizes in plan:
        groups.append(list(got[at : at + len(sizes)]))
        at += len(sizes)
    return groups


SMEM = pl.BlockSpec(memory_space=pltpu.SMEM)
VMEM = pl.BlockSpec(memory_space=pltpu.VMEM)
HBM = pl.BlockSpec(memory_space=pltpu.HBM)


def kernel_call(body, outs, scratch, args, flops, small=None, late=(), loose=(), hbm_outs=0, aliases=None,
                vmem=VMEM_MB, bytes_moved=4_000_000):
    late = [id(a) for a in late]
    loose = [id(a) for a in loose]
    spec = lambda a: SMEM if a is small else HBM if id(a) in late or id(a) in loose else VMEM
    where = [i for i, a in enumerate(args) if id(a) in late]
    many, extra = len(args), len(where)

    def whole(*refs):
        refs = list(refs)
        ins, rest = refs[:many], refs[many:]
        if extra:
            held, sems = rest[len(rest) - extra - 1 : -1], rest[-1]
            rest = rest[: len(rest) - extra - 1]
        waits = {}
        for n, i in enumerate(where):
            copy = pltpu.make_async_copy(ins[i], held[n], sems.at[n])
            copy.start()
            waits[id(held[n])] = copy
            ins[i] = held[n]

        def ready(*wanted):
            for ref in wanted:
                copy = waits.pop(id(ref), None)
                if copy is not None:
                    copy.wait()

        body(ready, *ins, *rest)
        for copy in waits.values():
            copy.wait()

    held = [pltpu.VMEM(args[i].shape, args[i].dtype) for i in where]
    if extra:
        held.append(pltpu.SemaphoreType.DMA((extra,)))
    return pl.pallas_call(
        whole,
        out_shape=tuple(outs),
        in_specs=[spec(a) for a in args],
        out_specs=tuple([VMEM] * (len(outs) - hbm_outs) + [HBM] * hbm_outs),
        scratch_shapes=[*scratch, *held],
        input_output_aliases=aliases or {},
        compiler_params=pltpu.CompilerParams(vmem_limit_bytes=vmem * 2**20),
        cost_estimate=pl.CostEstimate(flops=flops, bytes_accessed=bytes_moved, transcendentals=0),
    )(*args)


def shape(dims, dtype=F32):
    return jax.ShapeDtypeStruct(dims, dtype)


def forward(period, layer, windows, coords, weights, channels, halves):
    length = windows[0].shape[1]
    outs = [
        shape((ROWS, length)),
        shape((2, length)),
        shape((1, length)),
        shape((1, 128)),
    ]
    if layer == 1:
        outs.append(shape((ROWS, length)))
    args = [*windows, coords, *weights]
    outs += [shape((3 * channels, length), BF)] * 2
    scratch = [
        pltpu.VMEM((5 * channels, length), BF),
        pltpu.VMEM((9 * channels, length), BF),
    ]
    body = functools.partial(forward_kernel, period, layer, halves)
    flops = 3 * 2 * TAPS * channels * channels * length
    return kernel_call(body, outs, scratch, args, flops, coords)


def pack(params, picks):
    channels = params[0].shape[1]
    outs = [
        shape((9 * channels, 9 * channels), BF),
        shape((channels, 5 * 256), BF),
        shape((3, 216, channels), BF),
        shape((channels, 3 * 512), BF),
        shape((216, channels), BF),
        shape((9 * channels, 9 * channels), BF),
        shape((128, 8)),
    ]
    many = len(outs)

    def body(ready, *refs):
        ins, rest = refs[:8], refs[8:]
        for layer in range(2):
            pack_kernel(layer, ready, *ins, *rest[layer * many : (layer + 1) * many], *rest[2 * many :])

    scratch = [pltpu.VMEM((TAPS * channels, channels), F32), pltpu.VMEM((8, 128), F32)]
    args = [*params, *picks]
    got = kernel_call(body, outs * 2, scratch, args, 1_000_000_000)
    return got[:many], got[many:]


def unpack(last, layout, volume, coords, pieces, channels, before):
    halves, depth, chunk = layout
    few = channels // 2
    arrays = [
        shape((2, channels, channels, TAPS)),
        shape((2, 2, channels, TAPS)),
        shape((2, channels, TAPS)),
    ]
    scratch = [
        pltpu.VMEM((2, 2 * halves * depth * chunk, 128), BF),
        pltpu.VMEM((TAPS * few, channels), F32),
        pltpu.VMEM((2, few, channels, TAPS), F32),
        pltpu.VMEM((2, channels, TAPS), F32),
        pltpu.VMEM((2, few, TAPS), F32),
        pltpu.SemaphoreType.DMA((6,)),
    ]
    body = functools.partial(unpack_kernel, layout, volume, last)
    if not last:
        return kernel_call(
            body, arrays, scratch, [coords, pieces], 1_000_000_000, coords, hbm_outs=3
        )
    extra = [shape((2, channels)), shape((2, channels)), shape((2, 2)), shape((1, 1))]

    def reordered(ready, coords, pieces, *refs):
        before, outs, rest = refs[:3], refs[3:10], refs[10:]
        body(ready, coords, pieces, *before, *outs[4:], *outs[:4], *rest)

    got = kernel_call(
        reordered, extra + arrays, scratch, [coords, pieces, *before], 1_000_000_000, coords,
        loose=before, hbm_outs=3, aliases={2: 4, 3: 5, 4: 6},
    )
    return [*got[4:], *got[:4]]


def permuters(count, halves, depth):
    xy = lambda fn: [(fn(a), a) for a in range(count)]

    def core(v):
        return lax.ppermute(v, "xy", xy(lambda a: a ^ 1))

    def y(v):
        return lax.ppermute(v, "xy", xy(lambda a: a ^ 2))

    def scatter(pieces):
        return [
            lax.ppermute(pieces[s], "xy", xy(lambda a, s=s: (a - 4 * s) % count))
            for s in range(1, depth)
        ]

    def gather(v):
        return [lax.ppermute(v, "xy", xy(lambda a, s=s: (a + 4 * s) % count)) for s in range(1, depth)]

    def square(v):
        out = []
        for rg in range(halves):
            for ry in range(2):
                if rg or ry:
                    pairs = [
                        ((a ^ (2 * ry)) * halves + (j + rg) % halves, a * halves + j)
                        for a in range(count)
                        for j in range(halves)
                    ]
                    out.append(lax.ppermute(v, ("xy", "gz"), pairs))
        return out

    return core, y, scatter, gather, square


def per_device(noise, w_first, b_first, w_mid, b_mid, w_last, b_last):
    period = noise.shape[3]
    count = lax.axis_size("xy")
    halves = lax.axis_size("gz")
    channels = w_mid.shape[2]
    order = ring_order(count)
    places = np.argsort(np.array(order))
    volume = float(noise.size * count * halves)
    index = lax.axis_index("xy")
    depth = count // 4
    coords = jnp.stack(
        [
            jnp.asarray(places, jnp.int32)[index],
            lax.axis_index("gz"),
            index % 2,
            index // 2 % 2,
            index // 4,
        ]
    ).astype(jnp.int32)
    need = 45 * channels // 2 + channels + channels // 2
    chunk = -(-need // (2 * halves * depth * 16)) * 16
    layout = (halves, depth, chunk)

    def step(values, offset):
        return lax.ppermute(
            values, "xy", [(order[(p + offset) % count], order[p]) for p in range(count)]
        )

    flat = noise.reshape(1, -1)
    whole = [
        lax.ppermute(
            flat,
            ("xy", "gz"),
            [
                (p * halves + (j + rel) % halves, order[p] * halves + j)
                for p in range(count)
                for j in range(halves)
            ],
        )
        for rel in range(halves)
    ]
    whole = jnp.concatenate(whole, axis=1)

    params = [
        w_mid.transpose(0, 2, 3, 1),
        w_first.transpose(0, 2, 3, 1).reshape(2, channels, TAPS),
        w_last.transpose(0, 2, 3, 1),
        b_first,
        b_mid,
        b_last,
    ]
    back = spread_last_back()
    tall = np.concatenate([spread_last().reshape(6 * 216, TAPS), spread_first_back()], axis=0)
    picks = [
        jnp.asarray(np.concatenate([spread_first(), back[0], back[1]], axis=1), BF),
        jnp.asarray(np.pad(tall, ((0, 0), (0, 128 - TAPS))), BF),
    ]
    pick_l, pick_f = jnp.asarray(pick_last(), BF), jnp.asarray(pick_first(), BF)
    packed = pack(params, picks)
    ahead_weights = [(p[1], p[0], p[2], p[6]) for p in packed]
    back_weights = [(p[3], p[5], p[4]) for p in packed]

    def exchange(values):
        return [values if m == 0 else step(values, m) for m in range(-3, 4)]

    field0, state, _, logdet0, first0, second0 = forward(
        period, 0, exchange(whole), coords, ahead_weights[0], channels, halves
    )
    field1, state, own, logdet1, growth0, first1, second1 = forward(
        period, 1, exchange(state), coords, ahead_weights[1], channels, halves
    )
    core, cross, scatter, gather, square = permuters(count, halves, depth)
    length = field0.shape[1]
    full = shape((ROWS, length))
    planes = shape((3 * channels, length), BF)
    wide = pltpu.VMEM((9 * channels, length), BF)
    bulk = (4 * halves * depth * chunk, 128)
    part = 4 * depth * chunk
    flops = 2 * TAPS * channels * channels * length

    weights = back_weights[1]
    base, parts, small, grad_out, mids, grad_first = kernel_call(
        functools.partial(back_one_kernel, period),
        [full, shape((3, length)), shape((16, channels)), shape((2 * ROWS, length)), planes,
         shape((channels, length), BF)],
        [pltpu.VMEM((ROWS, length), F32), pltpu.VMEM((ROWS, length), F32), wide],
        [*exchange(state), logdet0, logdet1, coords, field1, first1, second1, *weights],
        flops, coords,
    )
    (bulk1,) = kernel_call(
        functools.partial(weights_one_kernel, period),
        [shape(bulk, BF)], [wide, wide],
        [coords, field1, first1, second1, grad_out, mids, grad_first, small, pick_l, pick_f],
        flops, coords,
    )

    weights = back_weights[0]
    low, middle, high, send, keep = kernel_call(
        functools.partial(back_zero_kernel, period, layout),
        [shape((1, length)), shape((2, length)), shape((1, length))]
        + [shape((part, 128), BF)] * 2,
        [pltpu.VMEM((ROWS, length), F32), pltpu.VMEM((3 * channels, length), BF), wide, wide,
         pltpu.VMEM(bulk, BF), pltpu.VMEM((channels, length), BF),
         pltpu.VMEM((16, channels), F32)],
        [*exchange(parts), base, growth0, own, coords, field0, bulk1, first0, second0, *weights,
         pick_l, pick_f],
        2 * flops, coords,
    )

    ((stay, away),) = stage([("split", 2, [keep, core(send)])])
    crossed = cross(away)
    (force,) = kernel_call(
        force_kernel, [shape((2, length // halves))], [],
        [coords, step(low, 1), middle, step(high, -1)], 1000, coords, bytes_moved=1000,
    )
    (pieces,) = stage([("split", depth, [stay, crossed])], after=(force,))
    force = lax.ppermute(force, "xy", [(order[p], p) for p in range(count)])
    ((total,),) = stage([("sum", 1, [pieces[0], *scatter(pieces)])], after=(force,))
    ((line,),) = stage([("join", 1, [total, *gather(total)])])
    ((mine,),) = stage([("join", 1, [line, *square(line)])])
    other = core(mine)
    outs = unpack(False, layout, volume, coords, mine, channels, [])
    g_mid, g_last, g_first, gb_first, gb_mid, gb_last, loss = unpack(
        True, layout, volume, coords, other, channels, list(outs)
    )

    return (
        force[1:2].reshape(noise.shape),
        force[0:1].reshape(noise.shape),
        loss.reshape(()),
        g_first.reshape(2, channels, 1, TAPS).transpose(0, 3, 1, 2),
        gb_first,
        g_mid.transpose(0, 3, 1, 2),
        gb_mid,
        g_last.transpose(0, 3, 1, 2),
        gb_last,
    )


def solution(mesh):
    return jax.shard_map(
        per_device,
        mesh=mesh,
        in_specs=(P("xy", "gz", None, None), P(), P(), P(), P(), P(), P()),
        out_specs=(
            P("xy", "gz", None, None),
            P("xy", "gz", None, None),
            P(),
            P(),
            P(),
            P(),
            P(),
            P(),
            P(),
        ),
        check_vma=False,
    )
```

time: 265 us -> 127 us (0.48); the launches traced: 261 us -> 126 us
  local copies, waits for them, and re-layouts: 69.3 us -> 14.1 us
  waiting for transfers between devices: 59.5 us -> 25.4 us
  blocking collectives: 28.4 us -> 0 us
  between operations: 16.4 us -> 1.04 us
  Pallas kernels: 23.2 us -> 36.6 us
  other arithmetic: 13.2 us -> 0 us
  matrix products: 6.45 us -> 0 us
  starting transfers between devices: 44.1 us -> 48.6 us
    psum x1 -> x0, waiting for transfers between devices: 57.6 us -> none  [per_device(): loss, pairs = lax.psum((loss, pairs), 'xy')]
    psum x1 -> x0, blocking collectives: 25.2 us -> none  [per_device(): loss, pairs = lax.psum((loss, pairs), 'xy')]
    transpose x5 -> x0, local copies, waits for them, and re-layouts: 21.3 us -> none  [the longest x2 8.67 us: per_device(): wm.transpose(1, 3, 0, 2).reshape(9 * channels, 9 * channels)]
    reshape x13 -> x2, local copies, waits for them, and re-layouts: 21.7 us -> 1.36 us  [the longest x1 0.68 us: per_device(): force[1:2].reshape(noise.shape)]
    ppermute x7 -> x15, waiting for transfers between devices: 1.84 us -> 17.4 us  [the longest x3 5.26 us: square(): out.append(lax.ppermute(v, ('xy', 'gz'), pairs))]
    pallas_call x4 -> x14, Pallas kernels: 23.2 us -> 36.6 us  [kernel_call(): pl.pallas_call(whole, out_shape=tuple(outs), in_specs=[spec(a) for a in a...]
    ppermute x20 -> x26, waiting for transfers between devices: 0.05 us -> 7.93 us  [step(): lax.ppermute(values, 'xy', [(order[(p + offset) % count], order[p]) for p...]
    dot_general x12 -> x0, matrix products: 6.45 us -> none  [the longest x8 3.69 us: dot(): return jnp.dot(a, b, preferred_element_type=F32)]
  transfers between devices with their start and end apart: 28 -> 41, of which waited for: 2 -> 18; matrix products, arithmetic and copies ran while one was open for 23% -> 3% of each run, Pallas kernels for 0% -> 11%
where the time goes in v3:
time: 127 us; the launch traced here: 126 us
  starting transfers between devices  48.6 us (38%)
  Pallas kernels  36.6 us (29%)
  waiting for transfers between devices  25.4 us (20%)
  local copies, waits for them, and re-layouts  14.1 us (11%)
    pallas_call x14, Pallas kernels, kernel_call(): pl.pallas_call(whole, out_shape=tuple(outs), in_specs=[spec(a) for a in a...  36.6 us
    ppermute x26, starting transfers between devices, step(): lax.ppermute(values, 'xy', [(order[(p + offset) % count], order[p]) for p...  22.4 us
    unnamed x29, local copies, waits for them, and re-layouts  9.94 us
    ppermute x26, waiting for transfers between devices, step(): lax.ppermute(values, 'xy', [(order[(p + offset) % count], order[p]) for p...  7.93 us
    ppermute x2, starting transfers between devices, per_device(): lax.ppermute(flat, ('xy', 'gz'), [(p * halves + (j + rel) % halves, order...  6.25 us
    ppermute x2, starting transfers between devices, core(): return lax.ppermute(v, 'xy', xy(lambda a: a ^ 1))  5.44 us
    ppermute x3, waiting for transfers between devices, square(): out.append(lax.ppermute(v, ('xy', 'gz'), pairs))  5.26 us
    ppermute x3, waiting for transfers between devices, gather(): lax.ppermute(v, 'xy', xy(lambda a, s=s: (a + 4 * s) % count))  4.57 us
  transfers between devices with their start and end apart: 41, of which 18 were waited for; matrix products, arithmetic and copies ran while one was open for 3% of the time, Pallas kernels for 11%

profile of v3, /device:TPU:5, one launch (start us, length us, event | category | flops | bytes accessed | tf_op | source)
XLA Modules:
  0.0 125.6 jit_solution(7257451794478755915)
XLA Ops:
  1.4 3.7 %collective-permute-start = (f32[1,512]{1,0:T(1,128)S(1)}, f32[1,512]{1,0:T(1,128)S(1)}, u32[]{:S(2)}, u32[]{:S(2)}) collective-permute-start(f32[1,512]{1,0:T(1,128)S(1)} %reshape.36), channel_id=1, source_target_pairs={{0,0},{1,1},{2,2},{3,3},{4,10},{5,11},{6,8},{7,9},{8,16},{9,17},{1... | collective-permute-start | bytes 6152 | tf_op jit(solution)/shard_map/ppermute | solution.py:805
  5.1 2.6 %collective-permute-start.1 = (f32[1,512]{1,0:T(1,128)S(1)}, f32[1,512]{1,0:T(1,128)S(1)}, u32[]{:S(2)}, u32[]{:S(2)}) collective-permute-start(f32[1,512]{1,0:T(1,128)S(1)} %reshape.36), channel_id=1, source_target_pairs={{1,0},{0,1},{3,2},{2,3},{5,10},{4,11},{7,8},{6,9},{9,16},{8,17},{1... | collective-permute-start | bytes 6152 | tf_op jit(solution)/shard_map/ppermute | solution.py:805
  8.5 2.4 %collective-permute-done.1 = f32[1,512]{1,0:T(1,128)S(1)} collective-permute-done((f32[1,512]{1,0:T(1,128)S(1)}, f32[1,512]{1,0:T(1,128)S(1)}, u32[]{:S(2)}, u32[]{:S(2)}) %collective-permute-start.1) | collective-permute-done | bytes 2080 | tf_op jit(solution)/shard_map/ppermute | solution.py:805
  12.1 1.8 %collective-permute-start.4 = (f32[1,1024]{1,0:T(1,128)S(1)}, f32[1,1024]{1,0:T(1,128)S(1)}, u32[]{:S(2)}, u32[]{:S(2)}) collective-permute-start(f32[1,1024]{1,0:T(1,128)S(1)} %constant_dynamic-update-slice_fusion.refs_3_), channel_id=1, source_target_pairs={{4,0},{0,2},{2,10},{10,8},{8,16},{16,18},{18,26},{26,24},{24,28},{... | collective-permute-start | bytes 12296 | tf_op jit(solution)/shard_map/ppermute | solution.py:799
  13.9 1.7 %collective-permute-start.6 = (f32[1,1024]{1,0:T(1,128)S(1)}, f32[1,1024]{1,0:T(1,128)S(1)}, u32[]{:S(2)}, u32[]{:S(2)}) collective-permute-start(f32[1,1024]{1,0:T(1,128)S(1)} %constant_dynamic-update-slice_fusion.refs_3_), channel_id=1, source_target_pairs={{10,0},{8,2},{16,10},{18,8},{26,16},{24,18},{28,26},{30,24},{22,28... | collective-permute-start | bytes 12296 | tf_op jit(solution)/shard_map/ppermute | solution.py:799
  16.7 1.6 %copy-done = bf16[2,81,64,64]{1,3,2,0:T(8,128)(2,1)S(1)} copy-done((bf16[2,81,64,64]{1,3,2,0:T(8,128)(2,1)S(1)}, bf16[2,81,64,64]{1,3,2,0:T(8,128)(2,1)}, u32[]{:S(2)}) %copy-start) | copy-done | bytes 1327128
  24.0 6.0 %shard_map.187 = (bf16[576,576]{1,0:T(8,128)(2,1)S(1)}, bf16[64,1280]{1,0:T(8,128)(2,1)S(1)}, bf16[3,216,64]{2,1,0:T(8,128)(2,1)S(1)}, bf16[64,1536]{1,0:T(8,128...) custom-call(bf16[2,64,64,81]{3,2,1,0:T(8,128)(2,1)S(1)} %bitcast.19,, ...), custom_call_target="tpu_custom_call" | custom-call | flops 1000000000 | bytes 4000000 | tf_op jit(solution)/shard_map/pallas_call | solution.py:646
  34.6 5.5 %shard_map.188 = (f32[8,1024]{1,0:T(8,128)S(1)}, f32[2,1024]{1,0:T(2,128)S(1)}, f32[1,1024]{1,0:T(1,128)}, f32[1,128]{1,0:T(1,128)S(1)}, bf16[192,1024]{1,0:T(8,128)(2,1)S(1)}, /*index=5*/bf16[192,1024]{1,0:T(8,128)(2,1)S(1)}) custom-call(f32[1,1024]{1,0:T(1,128)S(1)} %collective-permute-done.2.refs_0_, f32[1,1024]{1,0:T(1,128)S(1)} %collective-permute-done.3.refs_1_, ...), custom_call_target="tpu_custom_call" | custom-call | flops 2038431744 | bytes 4000000 | tf_op jit(solution)/shard_map/pallas_call | solution.py:646
  41.6 2.2 %collective-permute-start.12 = (f32[2,1024]{1,0:T(2,128)S(1)}, f32[2,1024]{1,0:T(2,128)S(1)}, u32[]{:S(2)}, u32[]{:S(2)}) collective-permute-start(f32[2,1024]{1,0:T(2,128)S(1)} %get-tuple-element.66.refs_3_), channel_id=1, source_target_pairs={{10,0},{8,2},{16,10},{18,8},{26,16},{24,18},{28,26},{30,24},{22,28... | collective-permute-start | bytes 24584 | tf_op jit(solution)/shard_map/ppermute | solution.py:799
  43.9 1.5 %collective-permute-start.8 = (f32[2,1024]{1,0:T(2,128)S(1)}, f32[2,1024]{1,0:T(2,128)S(1)}, u32[]{:S(2)}, u32[]{:S(2)}) collective-permute-start(f32[2,1024]{1,0:T(2,128)S(1)} %get-tuple-element.66.refs_3_), channel_id=1, source_target_pairs={{14,0},{6,2},{4,10},{0,8},{2,16},{10,18},{8,26},{16,24},{18,28},{2... | collective-permute-start | bytes 24584 | tf_op jit(solution)/shard_map/ppermute | solution.py:799
  46.4 1.5 %collective-permute-done.8.refs_0_ = f32[2,1024]{1,0:T(2,128)S(1)} collective-permute-done((f32[2,1024]{1,0:T(2,128)S(1)}, f32[2,1024]{1,0:T(2,128)S(1)}, u32[]{:S(2)}, u32[]{:S(2)}) %collective-permute-start.8) | collective-permute-done | bytes 8224 | tf_op jit(solution)/shard_map/ppermute | solution.py:799
  48.4 5.0 %shard_map.189 = (f32[8,1024]{1,0:T(8,128)S(1)}, f32[2,1024]{1,0:T(2,128)S(1)}, f32[1,1024]{1,0:T(1,128)S(1)}, f32[1,128]{1,0:T(1,128)S(1)}, f32[8,1024]{1,0:T(8...) custom-call(f32[2,1024]{1,0:T(2,128)S(1)} %collective-permute-done.8.refs_0_, ...), custom_call_target="tpu_custom_call" | custom-call | flops 2038431744 | bytes 4000000 | tf_op jit(solution)/shard_map/pallas_call | solution.py:646
  55.8 1.9 %collective-permute-start.18 = (f32[2,1024]{1,0:T(2,128)S(1)}, f32[2,1024]{1,0:T(2,128)S(1)}, u32[]{:S(2)}, u32[]{:S(2)}) collective-permute-start(f32[2,1024]{1,0:T(2,128)S(1)} %get-tuple-element.71.refs_3_), channel_id=1, source_target_pairs={{10,0},{8,2},{16,10},{18,8},{26,16},{24,18},{28,26},{30,24},{22,28... | collective-permute-start | bytes 24584 | tf_op jit(solution)/shard_map/ppermute | solution.py:799
  58.9 1.7 %collective-permute-done.19.refs_6_ = f32[2,1024]{1,0:T(2,128)S(1)} collective-permute-done((f32[2,1024]{1,0:T(2,128)S(1)}, f32[2,1024]{1,0:T(2,128)S(1)}, u32[]{:S(2)}, u32[]{:S(2)}) %collective-permute-start.19) | collective-permute-done | bytes 8224 | tf_op jit(solution)/shard_map/ppermute | solution.py:799
  60.6 3.1 %shard_map.190 = (f32[8,1024]{1,0:T(8,128)S(1)}, f32[3,1024]{1,0:T(4,128)S(1)}, f32[16,64]{1,0:T(8,128)S(1)}, f32[16,1024]{1,0:T(8,128)S(1)}, bf16[192,1024]{1,0...) custom-call(f32[2,1024]{1,0:T(2,128)S(1)} %collective-permute-done.14.refs_0_, f32[2,1024]{1,0:T(2,128)S(1)} %collective-permute-done.15.refs_1_, ...), custom_call_target="tpu_custom_call" | custom-call | flops 679477248 | bytes 4000000 | tf_op jit(solution)/shard_map/pallas_call | solution.py:646
  66.9 1.4 %collective-permute-start.24 = (f32[3,1024]{1,0:T(4,128)S(1)}, f32[3,1024]{1,0:T(4,128)S(1)}, u32[]{:S(2)}, u32[]{:S(2)}) collective-permute-start(f32[3,1024]{1,0:T(4,128)S(1)} %get-tuple-element.80.refs_3_), channel_id=1, source_target_pairs={{10,0},{8,2},{16,10},{18,8},{26,16},{24,18},{28,26},{30,24},{22,28... | collective-permute-start | bytes 36872 | tf_op jit(solution)/shard_map/ppermute | solution.py:799
  69.4 2.6 %shard_map.191.refs_12_ = bf16[3072,128]{1,0:T(8,128)(2,1)S(1)} custom-call(s32[5]{0:T(128)S(1)} %stack.19.refs_7_.refs_9_.refs_0_.refs_10_, f32[8,1024]{1,0:T(8,128)S(1)} %get-tuple-element.74.refs_10_.refs_1_, bf16[192,1024]{1,0:T(8,128)(2,1)S(1)} %get-tuple-element.75.refs_11_.refs_2_, bf16[192,1024]{1,0:T(8,128)(2,1)S(1)} %get-tuple-element.76.refs_12_.refs_3_, ...), custom_call_target="tpu_custom_call" | custom-call | flops 679477248 | bytes 4000000 | tf_op jit(solution)/shard_map/pallas_call | solution.py:646
  72.0 4.7 %shard_map.192 = (f32[1,1024]{1,0:T(1,128)S(1)}, f32[2,1024]{1,0:T(2,128)S(1)}, f32[1,1024]{1,0:T(1,128)S(1)}, bf16[1536,128]{1,0:T(8,128)(2,1)S(1)}, bf16[1536,128]{1,0:T(8,128)(2,1)S(1)}) custom-call(f32[3,1024]{1,0:T(4,128)S(1)} %collective-permute-done.20.refs_0_, f32[3,1024]{1,0:T(4,128)S(1)} %collective-permute-done.21.refs_1_, ...), custom_call_target="tpu_custom_call" | custom-call | flops 1358954496 | bytes 4000000 | tf_op jit(solution)/shard_map/pallas_call | solution.py:646
  77.0 1.5 %collective-permute-done.29.refs_1_ = bf16[1536,128]{1,0:T(8,128)(2,1)S(1)} collective-permute-done((bf16[1536,128]{1,0:T(8,128)(2,1)S(1)}, bf16[1536,128]{1,0:T(8,128)(2,1)S(1)}, u32[]{:S(2)}, u32[]{:S(2)}) %collective-permute-start.29) | collective-permute-done | bytes 393248 | tf_op jit(solution)/shard_map/ppermute | solution.py:745
  80.8 2.0 %collective-permute-done.27.refs_3_ = f32[1,1024]{1,0:T(1,128)S(1)} collective-permute-done((f32[1,1024]{1,0:T(1,128)S(1)}, f32[1,1024]{1,0:T(1,128)S(1)}, u32[]{:S(2)}, u32[]{:S(2)}) %collective-permute-start.27) | collective-permute-done | bytes 4128 | tf_op jit(solution)/shard_map/ppermute | solution.py:799
  83.4 1.5 %collective-permute-done.30.refs_1_ = bf16[768,128]{1,0:T(8,128)(2,1)S(1)} collective-permute-done((bf16[768,128]{1,0:T(8,128)(2,1)S(1)}, bf16[768,128]{1,0:T(8,128)(2,1)S(1)}, u32[]{:S(2)}, u32[]{:S(2)}) %collective-permute-start.30) | collective-permute-done | bytes 196640 | tf_op jit(solution)/shard_map/ppermute | solution.py:748
  85.7 1.5 %collective-permute-start.32 = (bf16[192,128]{1,0:T(8,128)(2,1)S(1)}, bf16[192,128]{1,0:T(8,128)(2,1)S(1)}, u32[]{:S(2)}, u32[]{:S(2)}) collective-permute-start(bf16[192,128]{1,0:T(8,128)(2,1)S(1)} %get-tuple-element.103), channel_id=1, source_target_pairs={{16,0},{18,2},{20,4},{22,6},{24,8},{26,10},{28,12},{30,14},{0,16},... | collective-permute-start | bytes 147464 | tf_op jit(solution)/shard_map/ppermute | solution.py:752
  87.2 1.4 %collective-permute-start.33 = (bf16[192,128]{1,0:T(8,128)(2,1)S(1)}, bf16[192,128]{1,0:T(8,128)(2,1)S(1)}, u32[]{:S(2)}, u32[]{:S(2)}) collective-permute-start(bf16[192,128]{1,0:T(8,128)(2,1)S(1)} %get-tuple-element.104), channel_id=1, source_target_pairs={{8,0},{10,2},{12,4},{14,6},{16,8},{18,10},{20,12},{22,14},{24,16},... | collective-permute-start | bytes 147464 | tf_op jit(solution)/shard_map/ppermute | solution.py:752
  88.6 4.4 %collective-permute-start.28 = (f32[2,512]{1,0:T(2,128)S(1)}, f32[2,512]{1,0:T(2,128)S(1)}, u32[]{:S(2)}, u32[]{:S(2)}) collective-permute-start(f32[2,512]{1,0:T(2,128)S(1)} %shard_map.193.refs_2_), channel_id=1, source_target_pairs={{0,0},{2,2},{10,4},{8,6},{16,8},{18,10},{26,12},{24,14},{28,16},{3... | collective-permute-start | bytes 12296 | tf_op jit(solution)/shard_map/ppermute | solution.py:891
  93.0 1.4 %collective-permute-done.28.refs_4_ = f32[2,512]{1,0:T(2,128)S(1)} collective-permute-done((f32[2,512]{1,0:T(2,128)S(1)}, f32[2,512]{1,0:T(2,128)S(1)}, u32[]{:S(2)}, u32[]{:S(2)}) %collective-permute-start.28) | collective-permute-done | bytes 4128 | tf_op jit(solution)/shard_map/ppermute | solution.py:891
  94.5 2.6 %collective-permute-start.34 = (bf16[192,128]{1,0:T(8,128)(2,1)S(1)}, bf16[192,128]{1,0:T(8,128)(2,1)S(1)}, u32[]{:S(2)}, u32[]{:S(2)}) collective-permute-start(bf16[192,128]{1,0:T(8,128)(2,1)S(1)} %shard_map.196.refs_0_), channel_id=1, source_target_pairs={{8,0},{10,2},{12,4},{14,6},{16,8},{18,10},{20,12},{22,14},{24,16},... | collective-permute-start | bytes 147464 | tf_op jit(solution)/shard_map/ppermute | solution.py:757
  98.3 2.9 %collective-permute-done.35.refs_2_ = bf16[192,128]{1,0:T(8,128)(2,1)S(1)} collective-permute-done((bf16[192,128]{1,0:T(8,128)(2,1)S(1)}, bf16[192,128]{1,0:T(8,128)(2,1)S(1)}, u32[]{:S(2)}, u32[]{:S(2)}) %collective-permute-start.35) | collective-permute-done | bytes 49184 | tf_op jit(solution)/shard_map/ppermute | solution.py:757
  104.8 1.9 %collective-permute-done.37.refs_1_ = bf16[768,128]{1,0:T(8,128)(2,1)S(1)} collective-permute-done((bf16[768,128]{1,0:T(8,128)(2,1)S(1)}, bf16[768,128]{1,0:T(8,128)(2,1)S(1)}, u32[]{:S(2)}, u32[]{:S(2)}) %collective-permute-start.37) | collective-permute-done | bytes 196640 | tf_op jit(solution)/shard_map/ppermute | solution.py:769
  106.7 3.3 %collective-permute-done.39.refs_3_ = bf16[768,128]{1,0:T(8,128)(2,1)S(1)} collective-permute-done((bf16[768,128]{1,0:T(8,128)(2,1)S(1)}, bf16[768,128]{1,0:T(8,128)(2,1)S(1)}, u32[]{:S(2)}, u32[]{:S(2)}) %collective-permute-start.39) | collective-permute-done | bytes 196640 | tf_op jit(solution)/shard_map/ppermute | solution.py:769
  110.1 5.1 %collective-permute-start.40 = (bf16[3072,128]{1,0:T(8,128)(2,1)S(1)}, bf16[3072,128]{1,0:T(8,128)(2,1)S(1)}, u32[]{:S(2)}, u32[]{:S(2)}) collective-permute-start(bf16[3072,128]{1,0:T(8,128)(2,1)S(1)} %shard_map.198.refs_1_), channel_id=1, source_target_pairs={{2,0},{0,2},{6,4},{4,6},{10,8},{8,10},{14,12},{12,14},{18,16},{16,... | collective-permute-start | bytes 2359304 | tf_op jit(solution)/shard_map/ppermute | solution.py:745
  116.6 4.1 %shard_map.199 = (f32[2,64,64,81]{3,2,1,0:T(8,128)}, f32[2,2,64,81]{3,2,1,0:T(8,128)}, f32[2,64,81]{2,1,0:T(8,128)}) custom-call(s32[5]{0:T(128)S(1)} %stack.19.refs_7_.refs_9_.refs_0_.refs_10_, bf16[3072,128]{1,0:T(8,128)(2,1)S(1)} %shard_map.198.refs_1_), custom_call_target="tpu_custom_call" | custom-call | flops 1000000000 | bytes 4000000 | tf_op jit(solution)/shard_map/pallas_call | solution.py:646
  120.7 4.7 %shard_map.200 = (f32[2,64]{1,0:T(2,128)}, f32[2,64]{1,0:T(2,128)}, f32[2,2]{1,0:T(2,128)}, f32[1,1]{1,0:T(1,128)}, f32[2,64,64,81]{3,2,1,0:T(8,128)}, /*index=5*/f32[2,2,64,81]{3,2,1,0:T(8,128)}, f32[2,64,81]{2,1,0:T(8,128)}) custom-call(s32[5]{0:T(128)S(1)} %stack.19.refs_7_.refs_9_.refs_0_.refs_10_, ...), custom_call_target="tpu_custom_call", output_to_operand_aliasing={{4}: (2, {}), {5}: (3, {}), {6}: (4, {})} | custom-call | flops 1000000000 | bytes 4000000 | tf_op jit(solution)/shard_map/pallas_call | solution.py:646
  (100 shorter events, 35.5 us)
Async XLA Ops:
  1.4 7.0 %collective-permute-start = (f32[1,512]{1,0:T(1,128)S(1)}, f32[1,512]{1,0:T(1,128)S(1)}, u32[]{:S(2)}, u32[]{:S(2)}) collective-permute-start(f32[1,512]{1,0:T(1,128)S(1)} %reshape.36), channel_id=1, source_target_pairs={{0,0},{1,1},{2,2},{3,3},{4,10},{5,11},{6,8},{7,9},{8,16},{9,17},{1... | collective-permute-start | bytes 6152 | tf_op jit(solution)/shard_map/ppermute | solution.py:805
  5.1 5.8 %collective-permute-start.1 = (f32[1,512]{1,0:T(1,128)S(1)}, f32[1,512]{1,0:T(1,128)S(1)}, u32[]{:S(2)}, u32[]{:S(2)}) collective-permute-start(f32[1,512]{1,0:T(1,128)S(1)} %reshape.36), channel_id=1, source_target_pairs={{1,0},{0,1},{3,2},{2,3},{5,10},{4,11},{7,8},{6,9},{9,16},{8,17},{1... | collective-permute-start | bytes 6152 | tf_op jit(solution)/shard_map/ppermute | solution.py:805
  10.9 4.7 %collective-permute-start.2 = (f32[1,1024]{1,0:T(1,128)S(1)}, f32[1,1024]{1,0:T(1,128)S(1)}, u32[]{:S(2)}, u32[]{:S(2)}) collective-permute-start(f32[1,1024]{1,0:T(1,128)S(1)} %constant_dynamic-update-slice_fusion.refs_3_), channel_id=1, source_target_pairs={{14,0},{6,2},{4,10},{0,8},{2,16},{10,18},{8,26},{16,24},{18,28},{2... | collective-permute-start | bytes 12296 | tf_op jit(solution)/shard_map/ppermute | solution.py:799
  10.9 22.5 %collective-permute-start.3 = (f32[1,1024]{1,0:T(1,128)S(1)}, f32[1,1024]{1,0:T(1,128)S(1)}, u32[]{:S(2)}, u32[]{:S(2)}) collective-permute-start(f32[1,1024]{1,0:T(1,128)S(1)} %constant_dynamic-update-slice_fusion.refs_3_), channel_id=1, source_target_pairs={{6,0},{4,2},{0,10},{2,8},{10,16},{8,18},{16,26},{18,24},{26,28},{2... | collective-permute-start | bytes 12296 | tf_op jit(solution)/shard_map/ppermute | solution.py:799
  12.1 21.3 %collective-permute-start.4 = (f32[1,1024]{1,0:T(1,128)S(1)}, f32[1,1024]{1,0:T(1,128)S(1)}, u32[]{:S(2)}, u32[]{:S(2)}) collective-permute-start(f32[1,1024]{1,0:T(1,128)S(1)} %constant_dynamic-update-slice_fusion.refs_3_), channel_id=1, source_target_pairs={{4,0},{0,2},{2,10},{10,8},{8,16},{16,18},{18,26},{26,24},{24,28},{... | collective-permute-start | bytes 12296 | tf_op jit(solution)/shard_map/ppermute | solution.py:799
  13.9 19.5 %collective-permute-start.5 = (f32[1,1024]{1,0:T(1,128)S(1)}, f32[1,1024]{1,0:T(1,128)S(1)}, u32[]{:S(2)}, u32[]{:S(2)}) collective-permute-start(f32[1,1024]{1,0:T(1,128)S(1)} %constant_dynamic-update-slice_fusion.refs_3_), channel_id=1, source_target_pairs={{2,0},{10,2},{8,10},{16,8},{18,16},{26,18},{24,26},{28,24},{30,28}... | collective-permute-start | bytes 12296 | tf_op jit(solution)/shard_map/ppermute | solution.py:799
  13.9 19.5 %collective-permute-start.6 = (f32[1,1024]{1,0:T(1,128)S(1)}, f32[1,1024]{1,0:T(1,128)S(1)}, u32[]{:S(2)}, u32[]{:S(2)}) collective-permute-start(f32[1,1024]{1,0:T(1,128)S(1)} %constant_dynamic-update-slice_fusion.refs_3_), channel_id=1, source_target_pairs={{10,0},{8,2},{16,10},{18,8},{26,16},{24,18},{28,26},{30,24},{22,28... | collective-permute-start | bytes 12296 | tf_op jit(solution)/shard_map/ppermute | solution.py:799
  15.6 17.9 %collective-permute-start.7 = (f32[1,1024]{1,0:T(1,128)S(1)}, f32[1,1024]{1,0:T(1,128)S(1)}, u32[]{:S(2)}, u32[]{:S(2)}) collective-permute-start(f32[1,1024]{1,0:T(1,128)S(1)} %constant_dynamic-update-slice_fusion.refs_3_), channel_id=1, source_target_pairs={{8,0},{16,2},{18,10},{26,8},{24,16},{28,18},{30,26},{22,24},{20,28... | collective-permute-start | bytes 12296 | tf_op jit(solution)/shard_map/ppermute | solution.py:799
  40.1 5.2 %collective-permute-start.10 = (f32[2,1024]{1,0:T(2,128)S(1)}, f32[2,1024]{1,0:T(2,128)S(1)}, u32[]{:S(2)}, u32[]{:S(2)}) collective-permute-start(f32[2,1024]{1,0:T(2,128)S(1)} %get-tuple-element.66.refs_3_), channel_id=1, source_target_pairs={{4,0},{0,2},{2,10},{10,8},{8,16},{16,18},{18,26},{26,24},{24,28},{... | collective-permute-start | bytes 24584 | tf_op jit(solution)/shard_map/ppermute | solution.py:799
  41.3 4.1 %collective-permute-start.11 = (f32[2,1024]{1,0:T(2,128)S(1)}, f32[2,1024]{1,0:T(2,128)S(1)}, u32[]{:S(2)}, u32[]{:S(2)}) collective-permute-start(f32[2,1024]{1,0:T(2,128)S(1)} %get-tuple-element.66.refs_3_), channel_id=1, source_target_pairs={{2,0},{10,2},{8,10},{16,8},{18,16},{26,18},{24,26},{28,24},{30,28}... | collective-permute-start | bytes 24584 | tf_op jit(solution)/shard_map/ppermute | solution.py:799
  41.6 3.8 %collective-permute-start.12 = (f32[2,1024]{1,0:T(2,128)S(1)}, f32[2,1024]{1,0:T(2,128)S(1)}, u32[]{:S(2)}, u32[]{:S(2)}) collective-permute-start(f32[2,1024]{1,0:T(2,128)S(1)} %get-tuple-element.66.refs_3_), channel_id=1, source_target_pairs={{10,0},{8,2},{16,10},{18,8},{26,16},{24,18},{28,26},{30,24},{22,28... | collective-permute-start | bytes 24584 | tf_op jit(solution)/shard_map/ppermute | solution.py:799
  43.9 4.0 %collective-permute-start.8 = (f32[2,1024]{1,0:T(2,128)S(1)}, f32[2,1024]{1,0:T(2,128)S(1)}, u32[]{:S(2)}, u32[]{:S(2)}) collective-permute-start(f32[2,1024]{1,0:T(2,128)S(1)} %get-tuple-element.66.refs_3_), channel_id=1, source_target_pairs={{14,0},{6,2},{4,10},{0,8},{2,16},{10,18},{8,26},{16,24},{18,28},{2... | collective-permute-start | bytes 24584 | tf_op jit(solution)/shard_map/ppermute | solution.py:799
  53.5 4.3 %collective-permute-start.14 = (f32[2,1024]{1,0:T(2,128)S(1)}, f32[2,1024]{1,0:T(2,128)S(1)}, u32[]{:S(2)}, u32[]{:S(2)}) collective-permute-start(f32[2,1024]{1,0:T(2,128)S(1)} %get-tuple-element.71.refs_3_), channel_id=1, source_target_pairs={{14,0},{6,2},{4,10},{0,8},{2,16},{10,18},{8,26},{16,24},{18,28},{2... | collective-permute-start | bytes 24584 | tf_op jit(solution)/shard_map/ppermute | solution.py:799
  54.0 4.4 %collective-permute-start.15 = (f32[2,1024]{1,0:T(2,128)S(1)}, f32[2,1024]{1,0:T(2,128)S(1)}, u32[]{:S(2)}, u32[]{:S(2)}) collective-permute-start(f32[2,1024]{1,0:T(2,128)S(1)} %get-tuple-element.71.refs_3_), channel_id=1, source_target_pairs={{6,0},{4,2},{0,10},{2,8},{10,16},{8,18},{16,26},{18,24},{26,28},{2... | collective-permute-start | bytes 24584 | tf_op jit(solution)/shard_map/ppermute | solution.py:799
  54.4 4.1 %collective-permute-start.16 = (f32[2,1024]{1,0:T(2,128)S(1)}, f32[2,1024]{1,0:T(2,128)S(1)}, u32[]{:S(2)}, u32[]{:S(2)}) collective-permute-start(f32[2,1024]{1,0:T(2,128)S(1)} %get-tuple-element.71.refs_3_), channel_id=1, source_target_pairs={{4,0},{0,2},{2,10},{10,8},{8,16},{16,18},{18,26},{26,24},{24,28},{... | collective-permute-start | bytes 24584 | tf_op jit(solution)/shard_map/ppermute | solution.py:799
  63.7 4.6 %collective-permute-start.20 = (f32[3,1024]{1,0:T(4,128)S(1)}, f32[3,1024]{1,0:T(4,128)S(1)}, u32[]{:S(2)}, u32[]{:S(2)}) collective-permute-start(f32[3,1024]{1,0:T(4,128)S(1)} %get-tuple-element.80.refs_3_), channel_id=1, source_target_pairs={{14,0},{6,2},{4,10},{0,8},{2,16},{10,18},{8,26},{16,24},{18,28},{2... | collective-permute-start | bytes 36872 | tf_op jit(solution)/shard_map/ppermute | solution.py:799
  64.4 7.6 %collective-permute-start.21 = (f32[3,1024]{1,0:T(4,128)S(1)}, f32[3,1024]{1,0:T(4,128)S(1)}, u32[]{:S(2)}, u32[]{:S(2)}) collective-permute-start(f32[3,1024]{1,0:T(4,128)S(1)} %get-tuple-element.80.refs_3_), channel_id=1, source_target_pairs={{6,0},{4,2},{0,10},{2,8},{10,16},{8,18},{16,26},{18,24},{26,28},{2... | collective-permute-start | bytes 36872 | tf_op jit(solution)/shard_map/ppermute | solution.py:799
  65.4 6.6 %collective-permute-start.22 = (f32[3,1024]{1,0:T(4,128)S(1)}, f32[3,1024]{1,0:T(4,128)S(1)}, u32[]{:S(2)}, u32[]{:S(2)}) collective-permute-start(f32[3,1024]{1,0:T(4,128)S(1)} %get-tuple-element.80.refs_3_), channel_id=1, source_target_pairs={{4,0},{0,2},{2,10},{10,8},{8,16},{16,18},{18,26},{26,24},{24,28},{... | collective-permute-start | bytes 36872 | tf_op jit(solution)/shard_map/ppermute | solution.py:799
  66.4 5.6 %collective-permute-start.23 = (f32[3,1024]{1,0:T(4,128)S(1)}, f32[3,1024]{1,0:T(4,128)S(1)}, u32[]{:S(2)}, u32[]{:S(2)}) collective-permute-start(f32[3,1024]{1,0:T(4,128)S(1)} %get-tuple-element.80.refs_3_), channel_id=1, source_target_pairs={{2,0},{10,2},{8,10},{16,8},{18,16},{26,18},{24,26},{28,24},{30,28}... | collective-permute-start | bytes 36872 | tf_op jit(solution)/shard_map/ppermute | solution.py:799
  66.9 5.1 %collective-permute-start.24 = (f32[3,1024]{1,0:T(4,128)S(1)}, f32[3,1024]{1,0:T(4,128)S(1)}, u32[]{:S(2)}, u32[]{:S(2)}) collective-permute-start(f32[3,1024]{1,0:T(4,128)S(1)} %get-tuple-element.80.refs_3_), channel_id=1, source_target_pairs={{10,0},{8,2},{16,10},{18,8},{26,16},{24,18},{28,26},{30,24},{22,28... | collective-permute-start | bytes 36872 | tf_op jit(solution)/shard_map/ppermute | solution.py:799
  78.6 6.3 %collective-permute-start.30 = (bf16[768,128]{1,0:T(8,128)(2,1)S(1)}, bf16[768,128]{1,0:T(8,128)(2,1)S(1)}, u32[]{:S(2)}, u32[]{:S(2)}) collective-permute-start(bf16[768,128]{1,0:T(8,128)(2,1)S(1)} %get-tuple-element.100), channel_id=1, source_target_pairs={{4,0},{6,2},{0,4},{2,6},{12,8},{14,10},{8,12},{10,14},{20,16},{22,... | collective-permute-start | bytes 589832 | tf_op jit(solution)/shard_map/ppermute | solution.py:748
  85.0 9.5 %collective-permute-start.31 = (bf16[192,128]{1,0:T(8,128)(2,1)S(1)}, bf16[192,128]{1,0:T(8,128)(2,1)S(1)}, u32[]{:S(2)}, u32[]{:S(2)}) collective-permute-start(bf16[192,128]{1,0:T(8,128)(2,1)S(1)} %get-tuple-element.102), channel_id=1, source_target_pairs={{24,0},{26,2},{28,4},{30,6},{0,8},{2,10},{4,12},{6,14},{8,16},{10,... | collective-permute-start | bytes 147464 | tf_op jit(solution)/shard_map/ppermute | solution.py:752
  85.7 8.7 %collective-permute-start.32 = (bf16[192,128]{1,0:T(8,128)(2,1)S(1)}, bf16[192,128]{1,0:T(8,128)(2,1)S(1)}, u32[]{:S(2)}, u32[]{:S(2)}) collective-permute-start(bf16[192,128]{1,0:T(8,128)(2,1)S(1)} %get-tuple-element.103), channel_id=1, source_target_pairs={{16,0},{18,2},{20,4},{22,6},{24,8},{26,10},{28,12},{30,14},{0,16},... | collective-permute-start | bytes 147464 | tf_op jit(solution)/shard_map/ppermute | solution.py:752
  87.2 7.2 %collective-permute-start.33 = (bf16[192,128]{1,0:T(8,128)(2,1)S(1)}, bf16[192,128]{1,0:T(8,128)(2,1)S(1)}, u32[]{:S(2)}, u32[]{:S(2)}) collective-permute-start(bf16[192,128]{1,0:T(8,128)(2,1)S(1)} %get-tuple-element.104), channel_id=1, source_target_pairs={{8,0},{10,2},{12,4},{14,6},{16,8},{18,10},{20,12},{22,14},{24,16},... | collective-permute-start | bytes 147464 | tf_op jit(solution)/shard_map/ppermute | solution.py:752
  88.6 5.8 %collective-permute-start.28 = (f32[2,512]{1,0:T(2,128)S(1)}, f32[2,512]{1,0:T(2,128)S(1)}, u32[]{:S(2)}, u32[]{:S(2)}) collective-permute-start(f32[2,512]{1,0:T(2,128)S(1)} %shard_map.193.refs_2_), channel_id=1, source_target_pairs={{0,0},{2,2},{10,4},{8,6},{16,8},{18,10},{26,12},{24,14},{28,16},{3... | collective-permute-start | bytes 12296 | tf_op jit(solution)/shard_map/ppermute | solution.py:891
  94.5 3.8 %collective-permute-start.34 = (bf16[192,128]{1,0:T(8,128)(2,1)S(1)}, bf16[192,128]{1,0:T(8,128)(2,1)S(1)}, u32[]{:S(2)}, u32[]{:S(2)}) collective-permute-start(bf16[192,128]{1,0:T(8,128)(2,1)S(1)} %shard_map.196.refs_0_), channel_id=1, source_target_pairs={{8,0},{10,2},{12,4},{14,6},{16,8},{18,10},{20,12},{22,14},{24,16},... | collective-permute-start | bytes 147464 | tf_op jit(solution)/shard_map/ppermute | solution.py:757
  97.1 4.1 %collective-permute-start.35 = (bf16[192,128]{1,0:T(8,128)(2,1)S(1)}, bf16[192,128]{1,0:T(8,128)(2,1)S(1)}, u32[]{:S(2)}, u32[]{:S(2)}) collective-permute-start(bf16[192,128]{1,0:T(8,128)(2,1)S(1)} %shard_map.196.refs_0_), channel_id=1, source_target_pairs={{16,0},{18,2},{20,4},{22,6},{24,8},{26,10},{28,12},{30,14},{0,16},... | collective-permute-start | bytes 147464 | tf_op jit(solution)/shard_map/ppermute | solution.py:757
  97.1 4.9 %collective-permute-start.36 = (bf16[192,128]{1,0:T(8,128)(2,1)S(1)}, bf16[192,128]{1,0:T(8,128)(2,1)S(1)}, u32[]{:S(2)}, u32[]{:S(2)}) collective-permute-start(bf16[192,128]{1,0:T(8,128)(2,1)S(1)} %shard_map.196.refs_0_), channel_id=1, source_target_pairs={{24,0},{26,2},{28,4},{30,6},{0,8},{2,10},{4,12},{6,14},{8,16},{10,... | collective-permute-start | bytes 147464 | tf_op jit(solution)/shard_map/ppermute | solution.py:757
  102.0 4.6 %collective-permute-start.37 = (bf16[768,128]{1,0:T(8,128)(2,1)S(1)}, bf16[768,128]{1,0:T(8,128)(2,1)S(1)}, u32[]{:S(2)}, u32[]{:S(2)}) collective-permute-start(bf16[768,128]{1,0:T(8,128)(2,1)S(1)} %shard_map.197.refs_0_), channel_id=1, source_target_pairs={{4,0},{5,1},{6,2},{7,3},{0,4},{1,5},{2,6},{3,7},{12,8},{13,9},{14,... | collective-permute-start | bytes 589832 | tf_op jit(solution)/shard_map/ppermute | solution.py:769
  102.1 4.6 %collective-permute-start.38 = (bf16[768,128]{1,0:T(8,128)(2,1)S(1)}, bf16[768,128]{1,0:T(8,128)(2,1)S(1)}, u32[]{:S(2)}, u32[]{:S(2)}) collective-permute-start(bf16[768,128]{1,0:T(8,128)(2,1)S(1)} %shard_map.197.refs_0_), channel_id=1, source_target_pairs={{1,0},{0,1},{3,2},{2,3},{5,4},{4,5},{7,6},{6,7},{9,8},{8,9},{11,10... | collective-permute-start | bytes 589832 | tf_op jit(solution)/shard_map/ppermute | solution.py:769
  103.4 6.6 %collective-permute-start.39 = (bf16[768,128]{1,0:T(8,128)(2,1)S(1)}, bf16[768,128]{1,0:T(8,128)(2,1)S(1)}, u32[]{:S(2)}, u32[]{:S(2)}) collective-permute-start(bf16[768,128]{1,0:T(8,128)(2,1)S(1)} %shard_map.197.refs_0_), channel_id=1, source_target_pairs={{5,0},{4,1},{7,2},{6,3},{1,4},{0,5},{3,6},{2,7},{13,8},{12,9},{15,... | collective-permute-start | bytes 589832 | tf_op jit(solution)/shard_map/ppermute | solution.py:769
  110.1 10.6 %collective-permute-start.40 = (bf16[3072,128]{1,0:T(8,128)(2,1)S(1)}, bf16[3072,128]{1,0:T(8,128)(2,1)S(1)}, u32[]{:S(2)}, u32[]{:S(2)}) collective-permute-start(bf16[3072,128]{1,0:T(8,128)(2,1)S(1)} %shard_map.198.refs_1_), channel_id=1, source_target_pairs={{2,0},{0,2},{6,4},{4,6},{10,8},{8,10},{14,12},{12,14},{18,16},{16,... | collective-permute-start | bytes 2359304 | tf_op jit(solution)/shard_map/ppermute | solution.py:745
  (23 other events, 96.6 us)

commit v4 on v3

--- a/solution.py
+++ b/solution.py
@@ -172,14 +172,23 @@
                 stack[rows, :128] = source[:, length - 128 :]
 
 
-def pack_kernel(layer, ready, w_mid, w_first, w_last, b_first, b_mid, b_last, lanes, rows_81,
+def identity(n):
+    row = lax.broadcasted_iota(jnp.int32, (n, n), 0)
+    return (row == lax.broadcasted_iota(jnp.int32, (n, n), 1)).astype(F32).astype(BF)
+
+
+def pack_kernel(layer, ready, w_mid, w_first, w_last, biases, lanes, rows_81,
                 matrix, first, narrow, last_back, first_back, turned, columns, taps, rows):
     channels = w_mid.shape[1]
-    for o in range(0, channels, 2):
-        pair = w_mid[layer, o : o + 2].reshape(2 * channels, TAPS).astype(F32).T
-        taps[pl.ds(o, TAPS, stride=channels), :] = pair[:, :channels]
-        taps[pl.ds(o + 1, TAPS, stride=channels), :] = pair[:, channels:]
-    block = lambda tap: taps[tap * channels : (tap + 1) * channels, :]
+    few = channels // 2
+    for o in range(few):
+        pair = jnp.concatenate([w_mid[layer, o], w_mid[layer, o + few]], axis=0)
+        taps[pl.ds(o, TAPS, stride=few), :] = dot_nt(identity(TAPS), pair)
+
+    def block(tap):
+        both = taps[tap * few : (tap + 1) * few, :]
+        return jnp.concatenate([both[:, :channels], both[:, channels:]], axis=0)
+
     for inner in range(9):
         at = pl.ds(inner * channels, channels)
         for outer in range(0, 9, 2):
@@ -195,10 +204,12 @@
         for outer in range(0, 9, 2):
             if outer < 8:
                 wide = slice(outer * channels, (outer + 2) * channels)
-                both = matrix[at, wide].astype(F32).T
+                both = dot_nt(identity(2 * channels), matrix[at, wide])
                 turned[at, wide] = jnp.concatenate([both[:channels], both[channels:]], axis=1).astype(BF)
             else:
-                turned[at, outer * channels :] = matrix[at, outer * channels :].astype(F32).T.astype(BF)
+                turned[at, outer * channels :] = dot_nt(
+                    identity(channels), matrix[at, outer * channels :]
+                ).astype(BF)
     wf = w_first[layer]
     first[...] = dot(wf, lanes[:, : 5 * 256]).astype(BF)
     first_back[...] = dot_nt(rows_81[6 * 216 : 7 * 216, :TAPS], wf).astype(BF)
@@ -211,9 +222,7 @@
         dot(w_last[layer, o], lanes[:, 5 * 256 + o * 1536 : 5 * 256 + (o + 1) * 1536]) for o in range(2)
     ).astype(BF)
     rows[...] = jnp.zeros_like(rows)
-    rows[0:1, :channels] = b_first[layer : layer + 1, :]
-    rows[1:2, :channels] = b_mid[layer : layer + 1, :]
-    rows[2:3, :2] = b_last[layer : layer + 1, :]
+    rows[0:3, :channels] = biases[3 * layer : 3 * layer + 3, :]
     columns[...] = rows[...].T
 
 
@@ -240,22 +249,21 @@
                 for layer in range(2):
                     bulk[layer, pl.ds(pl.multiple_of(to, 16), chunk), :] = pieces[at : at + chunk, :]
                     at += chunk
-    rows = 9 * few
+    rows, pairs = 9 * few, few // 2
     copies = []
     for layer in range(2):
         for tap in range(TAPS):
             outer, inner = divmod(tap, 9)
             start = (outer // 2) * rows + inner * few
             low = (outer % 2) * channels
-            taps[tap * few : (tap + 1) * few, :] = (
-                bulk[layer, start : start + few, low : low + channels].astype(F32) * (1.0 / volume)
-            )
-        for o in range(0, few, 2):
-            pair = jnp.concatenate(
-                [taps[pl.ds(o, TAPS, stride=few), :], taps[pl.ds(o + 1, TAPS, stride=few), :]],
-                axis=1,
-            )
-            mid[layer, o : o + 2] = pair.T.reshape(2, channels, TAPS)
+            both = bulk[layer, start : start + few, low : low + channels].astype(F32)
+            taps[tap * pairs : (tap + 1) * pairs, :channels] = both[:pairs]
+            taps[tap * pairs : (tap + 1) * pairs, channels:] = both[pairs:]
+        for o in range(pairs):
+            pair = taps[pl.ds(o, TAPS, stride=pairs), :].astype(BF)
+            pair = dot_nt(identity(2 * channels), pair) * (1.0 / volume)
+            mid[layer, o] = pair[:channels]
+            mid[layer, o + pairs] = pair[channels:]
         rest = bulk[layer, 5 * rows : 5 * rows + channels + few, :].astype(F32) * (1.0 / volume)
         lasts[layer] = rest[:channels, :TAPS]
         firsts[layer] = rest[channels:, :TAPS]
@@ -609,11 +617,25 @@
 HBM = pl.BlockSpec(memory_space=pltpu.HBM)
 
 
-def kernel_call(body, outs, scratch, args, flops, small=None, late=(), loose=(), hbm_outs=0, aliases=None,
+HERE = "here"
+
+
+def locate():
+    index = lax.axis_index("xy")
+    depth = lax.axis_size("xy") // 4
+    core, y, z = index % 2, index // 2 % 2, index // 4
+    chip = jnp.where(y == 0, z, 2 * depth - 1 - z)
+    place = 2 * chip + jnp.where(chip % 2 == 0, core, 1 - core)
+    return place, lax.axis_index("gz"), core, y, z
+
+
+def kernel_call(body, outs, scratch, args, flops, late=(), loose=(), hbm_outs=0, aliases=None,
                 vmem=VMEM_MB, bytes_moved=4_000_000):
+    here = next((i for i, a in enumerate(args) if a is HERE), None)
+    args = [a for a in args if a is not HERE]
     late = [id(a) for a in late]
     loose = [id(a) for a in loose]
-    spec = lambda a: SMEM if a is small else HBM if id(a) in late or id(a) in loose else VMEM
+    spec = lambda a: HBM if id(a) in late or id(a) in loose else VMEM
     where = [i for i, a in enumerate(args) if id(a) in late]
     many, extra = len(args), len(where)
 
@@ -636,6 +658,8 @@
                 if copy is not None:
                     copy.wait()
 
+        if here is not None:
+            ins.insert(here, locate())
         body(ready, *ins, *rest)
         for copy in waits.values():
             copy.wait()
@@ -677,7 +701,7 @@
     ]
     body = functools.partial(forward_kernel, period, layer, halves)
     flops = 3 * 2 * TAPS * channels * channels * length
-    return kernel_call(body, outs, scratch, args, flops, coords)
+    return kernel_call(body, outs, scratch, args, flops)
 
 
 def pack(params, picks):
@@ -694,11 +718,11 @@
     many = len(outs)
 
     def body(ready, *refs):
-        ins, rest = refs[:8], refs[8:]
+        ins, rest = refs[:6], refs[6:]
         for layer in range(2):
             pack_kernel(layer, ready, *ins, *rest[layer * many : (layer + 1) * many], *rest[2 * many :])
 
-    scratch = [pltpu.VMEM((TAPS * channels, channels), F32), pltpu.VMEM((8, 128), F32)]
+    scratch = [pltpu.VMEM((TAPS * channels // 2, 2 * channels), F32), pltpu.VMEM((8, 128), F32)]
     args = [*params, *picks]
     got = kernel_call(body, outs * 2, scratch, args, 1_000_000_000)
     return got[:many], got[many:]
@@ -714,7 +738,7 @@
     ]
     scratch = [
         pltpu.VMEM((2, 2 * halves * depth * chunk, 128), BF),
-        pltpu.VMEM((TAPS * few, channels), F32),
+        pltpu.VMEM((TAPS * few // 2, 2 * channels), F32),
         pltpu.VMEM((2, few, channels, TAPS), F32),
         pltpu.VMEM((2, channels, TAPS), F32),
         pltpu.VMEM((2, few, TAPS), F32),
@@ -723,7 +747,7 @@
     body = functools.partial(unpack_kernel, layout, volume, last)
     if not last:
         return kernel_call(
-            body, arrays, scratch, [coords, pieces], 1_000_000_000, coords, hbm_outs=3
+            body, arrays, scratch, [coords, pieces], 1_000_000_000, hbm_outs=3
         )
     extra = [shape((2, channels)), shape((2, channels)), shape((2, 2)), shape((1, 1))]
 
@@ -732,8 +756,8 @@
         body(ready, coords, pieces, *before, *outs[4:], *outs[:4], *rest)
 
     got = kernel_call(
-        reordered, extra + arrays, scratch, [coords, pieces, *before], 1_000_000_000, coords,
-        loose=before, hbm_outs=3, aliases={2: 4, 3: 5, 4: 6},
+        reordered, extra + arrays, scratch, [coords, pieces, *before], 1_000_000_000,
+        loose=before, hbm_outs=3, aliases={1: 4, 2: 5, 3: 6},
     )
     return [*got[4:], *got[:4]]
 
@@ -778,19 +802,9 @@
     halves = lax.axis_size("gz")
     channels = w_mid.shape[2]
     order = ring_order(count)
-    places = np.argsort(np.array(order))
     volume = float(noise.size * count * halves)
-    index = lax.axis_index("xy")
     depth = count // 4
-    coords = jnp.stack(
-        [
-            jnp.asarray(places, jnp.int32)[index],
-            lax.axis_index("gz"),
-            index % 2,
-            index // 2 % 2,
-            index // 4,
-        ]
-    ).astype(jnp.int32)
+    coords = HERE
     need = 45 * channels // 2 + channels + channels // 2
     chunk = -(-need // (2 * halves * depth * 16)) * 16
     layout = (halves, depth, chunk)
@@ -813,15 +827,11 @@
         )
         for rel in range(halves)
     ]
-    whole = jnp.concatenate(whole, axis=1)
-
     params = [
         w_mid.transpose(0, 2, 3, 1),
         w_first.transpose(0, 2, 3, 1).reshape(2, channels, TAPS),
         w_last.transpose(0, 2, 3, 1),
-        b_first,
-        b_mid,
-        b_last,
+        jnp.stack([b_first, b_mid, jnp.pad(b_last, ((0, 0), (0, channels - 2)))], axis=1).reshape(6, channels),
     ]
     back = spread_last_back()
     tall = np.concatenate([spread_last().reshape(6 * 216, TAPS), spread_first_back()], axis=0)
@@ -834,6 +844,16 @@
     ahead_weights = [(p[1], p[0], p[2], p[6]) for p in packed]
     back_weights = [(p[3], p[5], p[4]) for p in packed]
 
+    def join(ready, *refs):
+        piece = refs[0].shape[1]
+        for rel in range(halves):
+            refs[-1][:, rel * piece : (rel + 1) * piece] = refs[rel][...]
+
+    waits = (packed[1][5],)
+    (whole,) = kernel_call(
+        join, [shape((1, flat.shape[1] * halves))], [], [*whole, *waits], 1000, loose=waits, bytes_moved=1000
+    )
+
     def exchange(values):
         return [values if m == 0 else step(values, m) for m in range(-3, 4)]
 
@@ -859,13 +879,13 @@
          shape((channels, length), BF)],
         [pltpu.VMEM((ROWS, length), F32), pltpu.VMEM((ROWS, length), F32), wide],
         [*exchange(state), logdet0, logdet1, coords, field1, first1, second1, *weights],
-        flops, coords,
+        flops,
     )
     (bulk1,) = kernel_call(
         functools.partial(weights_one_kernel, period),
         [shape(bulk, BF)], [wide, wide],
         [coords, field1, first1, second1, grad_out, mids, grad_first, small, pick_l, pick_f],
-        flops, coords,
+        flops,
     )
 
     weights = back_weights[0]
@@ -878,21 +898,21 @@
          pltpu.VMEM((16, channels), F32)],
         [*exchange(parts), base, growth0, own, coords, field0, bulk1, first0, second0, *weights,
          pick_l, pick_f],
-        2 * flops, coords,
+        2 * flops,
     )
 
     ((stay, away),) = stage([("split", 2, [keep, core(send)])])
     crossed = cross(away)
     (force,) = kernel_call(
         force_kernel, [shape((2, length // halves))], [],
-        [coords, step(low, 1), middle, step(high, -1)], 1000, coords, bytes_moved=1000,
+        [coords, step(low, 1), middle, step(high, -1)], 1000, bytes_moved=1000,
     )
     (pieces,) = stage([("split", depth, [stay, crossed])], after=(force,))
-    force = lax.ppermute(force, "xy", [(order[p], p) for p in range(count)])
-    ((total,),) = stage([("sum", 1, [pieces[0], *scatter(pieces)])], after=(force,))
+    ((total,),) = stage([("sum", 1, [pieces[0], *scatter(pieces)])])
     ((line,),) = stage([("join", 1, [total, *gather(total)])])
     ((mine,),) = stage([("join", 1, [line, *square(line)])])
     other = core(mine)
+    force = lax.ppermute(force, "xy", [(order[p], p) for p in range(count)])
     outs = unpack(False, layout, volume, coords, mine, channels, [])
     g_mid, g_last, g_first, gb_first, gb_mid, gb_last, loss = unpack(
         True, layout, volume, coords, other, channels, list(outs)

time: 127 us -> 116 us (0.913)
  Pallas kernels: 36.6 us -> 28.4 us
  local copies, waits for them, and re-layouts: 14.1 us -> 8.17 us
  waiting for transfers between devices: 25.4 us -> 29.1 us
    pallas_call x14 -> x15, Pallas kernels: 36.6 us -> 28.4 us  [kernel_call(): pl.pallas_call(whole, out_shape=tuple(outs), in_specs=[spec(a) for a in a...]
    unnamed x29 -> x14, local copies, waits for them, and re-layouts: 9.94 us -> 5.31 us
    ppermute x2, waiting for transfers between devices: 3.2 us -> 0.01 us  [per_device(): lax.ppermute(flat, ('xy', 'gz'), [(p * halves + (j + rel) % halves, order...]
    ppermute x1, starting transfers between devices: 4.38 us -> 1.92 us  [per_device(): force = lax.ppermute(force, 'xy', [(order[p], p) for p in range(count)])]
    ppermute x1, waiting for transfers between devices: 1.42 us -> 3.89 us  [per_device(): force = lax.ppermute(force, 'xy', [(order[p], p) for p in range(count)])]
    ppermute x3, waiting for transfers between devices: 0.01 us -> 2.27 us  [scatter(): lax.ppermute(pieces[s], 'xy', xy(lambda a, s=s: (a - 4 * s) % count))]
    ppermute x26, waiting for transfers between devices: 7.93 us -> 9.8 us  [step(): lax.ppermute(values, 'xy', [(order[(p + offset) % count], order[p]) for p...]
  transfers between devices with their start and end apart: 41 -> 41, of which waited for: 18 -> 20; matrix products, arithmetic and copies ran while one was open for 3% -> 2% of each run, Pallas kernels for 11% -> 8%
where the time goes in v4:
time: 116 us; the launch traced here: 115 us
  starting transfers between devices  47.9 us (41%)
  waiting for transfers between devices  29.1 us (25%)
  Pallas kernels  28.4 us (24%)
  local copies, waits for them, and re-layouts  8.17 us (7%)
    pallas_call x15, Pallas kernels, kernel_call(): pl.pallas_call(whole, out_shape=tuple(outs), in_specs=[spec(a) for a in a...  28.4 us
    ppermute x26, starting transfers between devices, step(): lax.ppermute(values, 'xy', [(order[(p + offset) % count], order[p]) for p...  23.3 us
    ppermute x26, waiting for transfers between devices, step(): lax.ppermute(values, 'xy', [(order[(p + offset) % count], order[p]) for p...  9.8 us
    ppermute x2, starting transfers between devices, per_device(): lax.ppermute(flat, ('xy', 'gz'), [(p * halves + (j + rel) % halves, order...  6.25 us
    ppermute x2, starting transfers between devices, core(): return lax.ppermute(v, 'xy', xy(lambda a: a ^ 1))  5.35 us
    unnamed x14, local copies, waits for them, and re-layouts  5.31 us
    ppermute x3, waiting for transfers between devices, square(): out.append(lax.ppermute(v, ('xy', 'gz'), pairs))  5.27 us
    ppermute x3, waiting for transfers between devices, gather(): lax.ppermute(v, 'xy', xy(lambda a, s=s: (a + 4 * s) % count))  4.73 us
  transfers between devices with their start and end apart: 41, of which 20 were waited for; matrix products, arithmetic and copies ran while one was open for 2% of the time, Pallas kernels for 8%

profile of v4, /device:TPU:5, one launch (start us, length us, event | category | flops | bytes accessed | tf_op | source)
XLA Modules:
  0.0 115.3 jit_solution(7313193071995049049)
XLA Ops:
  1.4 3.7 %collective-permute-start = (f32[1,512]{1,0:T(1,128)S(1)}, f32[1,512]{1,0:T(1,128)S(1)}, u32[]{:S(2)}, u32[]{:S(2)}) collective-permute-start(f32[1,512]{1,0:T(1,128)S(1)} %reshape.39), channel_id=1, source_target_pairs={{0,0},{1,1},{2,2},{3,3},{4,10},{5,11},{6,8},{7,9},{8,16},{9,17},{1... | collective-permute-start | bytes 6152 | tf_op jit(solution)/shard_map/ppermute | solution.py:819
  5.1 2.6 %collective-permute-start.1 = (f32[1,512]{1,0:T(1,128)S(1)}, f32[1,512]{1,0:T(1,128)S(1)}, u32[]{:S(2)}, u32[]{:S(2)}) collective-permute-start(f32[1,512]{1,0:T(1,128)S(1)} %reshape.39), channel_id=1, source_target_pairs={{1,0},{0,1},{3,2},{2,3},{5,10},{4,11},{7,8},{6,9},{9,16},{8,17},{1... | collective-permute-start | bytes 6152 | tf_op jit(solution)/shard_map/ppermute | solution.py:819
  9.1 1.6 %copy-done = bf16[2,81,64,64]{1,3,2,0:T(8,128)(2,1)S(1)} copy-done((bf16[2,81,64,64]{1,3,2,0:T(8,128)(2,1)S(1)}, bf16[2,81,64,64]{1,3,2,0:T(8,128)(2,1)}, u32[]{:S(2)}) %copy-start) | copy-done | bytes 1327128
  14.4 5.0 %shard_map.178 = (bf16[576,576]{1,0:T(8,128)(2,1)S(1)}, bf16[64,1280]{1,0:T(8,128)(2,1)S(1)}, bf16[3,216,64]{2,1,0:T(8,128)(2,1)S(1)}, bf16[64,1536]{1,0:T(8,128...) custom-call(bf16[2,64,64,81]{3,2,1,0:T(8,128)(2,1)S(1)} %bitcast.19,, ...), custom_call_target="tpu_custom_call" | custom-call | flops 1000000000 | bytes 4000000 | tf_op jit(solution)/shard_map/pallas_call | solution.py:670
  19.5 3.1 %collective-permute-start.3 = (f32[1,1024]{1,0:T(1,128)S(1)}, f32[1,1024]{1,0:T(1,128)S(1)}, u32[]{:S(2)}, u32[]{:S(2)}) collective-permute-start(f32[1,1024]{1,0:T(1,128)S(1)} %shard_map.179.refs_3_), channel_id=1, source_target_pairs={{6,0},{4,2},{0,10},{2,8},{10,16},{8,18},{16,26},{18,24},{26,28},{2... | collective-permute-start | bytes 12296 | tf_op jit(solution)/shard_map/ppermute | solution.py:813
  22.6 1.5 %collective-permute-start.5 = (f32[1,1024]{1,0:T(1,128)S(1)}, f32[1,1024]{1,0:T(1,128)S(1)}, u32[]{:S(2)}, u32[]{:S(2)}) collective-permute-start(f32[1,1024]{1,0:T(1,128)S(1)} %shard_map.179.refs_3_), channel_id=1, source_target_pairs={{2,0},{10,2},{8,10},{16,8},{18,16},{26,18},{24,26},{28,24},{30,28}... | collective-permute-start | bytes 12296 | tf_op jit(solution)/shard_map/ppermute | solution.py:813
  25.1 2.0 %collective-permute-done.6.refs_5_ = f32[1,1024]{1,0:T(1,128)S(1)} collective-permute-done((f32[1,1024]{1,0:T(1,128)S(1)}, f32[1,1024]{1,0:T(1,128)S(1)}, u32[]{:S(2)}, u32[]{:S(2)}) %collective-permute-start.6) | collective-permute-done | bytes 4128 | tf_op jit(solution)/shard_map/ppermute | solution.py:813
  27.1 5.0 %shard_map.180 = (f32[8,1024]{1,0:T(8,128)S(1)}, f32[2,1024]{1,0:T(2,128)S(1)}, f32[1,1024]{1,0:T(1,128)}, f32[1,128]{1,0:T(1,128)S(1)}, bf16[192,1024]{1,0:T(8,128)(2,1)S(1)}, /*index=5*/bf16[192,1024]{1,0:T(8,128)(2,1)S(1)}) custom-call(f32[1,1024]{1,0:T(1,128)S(1)} %collective-permute-done.2.refs_0_, f32[1,1024]{1,0:T(1,128)S(1)} %collective-permute-done.3.refs_1_, ...), custom_call_target="tpu_custom_call" | custom-call | flops 2038431744 | bytes 4000000 | tf_op jit(solution)/shard_map/pallas_call | solution.py:670
  33.6 2.0 %collective-permute-start.12 = (f32[2,1024]{1,0:T(2,128)S(1)}, f32[2,1024]{1,0:T(2,128)S(1)}, u32[]{:S(2)}, u32[]{:S(2)}) collective-permute-start(f32[2,1024]{1,0:T(2,128)S(1)} %get-tuple-element.67.refs_3_), channel_id=1, source_target_pairs={{10,0},{8,2},{16,10},{18,8},{26,16},{24,18},{28,26},{30,24},{22,28... | collective-permute-start | bytes 24584 | tf_op jit(solution)/shard_map/ppermute | solution.py:813
  37.0 1.5 %collective-permute-start.9 = (f32[2,1024]{1,0:T(2,128)S(1)}, f32[2,1024]{1,0:T(2,128)S(1)}, u32[]{:S(2)}, u32[]{:S(2)}) collective-permute-start(f32[2,1024]{1,0:T(2,128)S(1)} %get-tuple-element.67.refs_3_), channel_id=1, source_target_pairs={{6,0},{4,2},{0,10},{2,8},{10,16},{8,18},{16,26},{18,24},{26,28},{2... | collective-permute-start | bytes 24584 | tf_op jit(solution)/shard_map/ppermute | solution.py:813
  38.6 1.4 %collective-permute-done.8.refs_0_ = f32[2,1024]{1,0:T(2,128)S(1)} collective-permute-done((f32[2,1024]{1,0:T(2,128)S(1)}, f32[2,1024]{1,0:T(2,128)S(1)}, u32[]{:S(2)}, u32[]{:S(2)}) %collective-permute-start.8) | collective-permute-done | bytes 8224 | tf_op jit(solution)/shard_map/ppermute | solution.py:813
  40.1 4.4 %shard_map.181 = (f32[8,1024]{1,0:T(8,128)S(1)}, f32[2,1024]{1,0:T(2,128)S(1)}, f32[1,1024]{1,0:T(1,128)S(1)}, f32[1,128]{1,0:T(1,128)S(1)}, f32[8,1024]{1,0:T(8...) custom-call(f32[2,1024]{1,0:T(2,128)S(1)} %collective-permute-done.8.refs_0_, ...), custom_call_target="tpu_custom_call" | custom-call | flops 2038431744 | bytes 4000000 | tf_op jit(solution)/shard_map/pallas_call | solution.py:670
  44.5 1.9 %collective-permute-start.14 = (f32[2,1024]{1,0:T(2,128)S(1)}, f32[2,1024]{1,0:T(2,128)S(1)}, u32[]{:S(2)}, u32[]{:S(2)}) collective-permute-start(f32[2,1024]{1,0:T(2,128)S(1)} %get-tuple-element.72.refs_3_), channel_id=1, source_target_pairs={{14,0},{6,2},{4,10},{0,8},{2,16},{10,18},{8,26},{16,24},{18,28},{2... | collective-permute-start | bytes 24584 | tf_op jit(solution)/shard_map/ppermute | solution.py:813
  50.2 1.9 %collective-permute-done.18.refs_5_ = f32[2,1024]{1,0:T(2,128)S(1)} collective-permute-done((f32[2,1024]{1,0:T(2,128)S(1)}, f32[2,1024]{1,0:T(2,128)S(1)}, u32[]{:S(2)}, u32[]{:S(2)}) %collective-permute-start.18) | collective-permute-done | bytes 8224 | tf_op jit(solution)/shard_map/ppermute | solution.py:813
  53.0 2.6 %shard_map.182 = (f32[8,1024]{1,0:T(8,128)S(1)}, f32[3,1024]{1,0:T(4,128)S(1)}, f32[16,64]{1,0:T(8,128)S(1)}, f32[16,1024]{1,0:T(8,128)S(1)}, bf16[192,1024]{1,0...) custom-call(f32[2,1024]{1,0:T(2,128)S(1)} %collective-permute-done.14.refs_0_, f32[2,1024]{1,0:T(2,128)S(1)} %collective-permute-done.15.refs_1_, ...), custom_call_target="tpu_custom_call" | custom-call | flops 679477248 | bytes 4000000 | tf_op jit(solution)/shard_map/pallas_call | solution.py:670
  60.8 2.1 %shard_map.183.refs_11_ = bf16[3072,128]{1,0:T(8,128)(2,1)S(1)} custom-call(f32[8,1024]{1,0:T(8,128)S(1)} %get-tuple-element.75.refs_9_.refs_0_, bf16[192,1024]{1,0:T(8,128)(2,1)S(1)} %get-tuple-element.76.refs_10_.refs_1_, bf16[192,1024]{1,0:T(8,128)(2,1)S(1)} %get-tuple-element.77.refs_11_.refs_2_, f32[16,1024]{1,0:T(8,128)S(1)} %get-tuple-element.85.refs_3_, ...), custom_call_target="tpu_custom_call" | custom-call | flops 679477248 | bytes 4000000 | tf_op jit(solution)/shard_map/pallas_call | solution.py:670
  63.6 4.1 %shard_map.184 = (f32[1,1024]{1,0:T(1,128)S(1)}, f32[2,1024]{1,0:T(2,128)S(1)}, f32[1,1024]{1,0:T(1,128)S(1)}, bf16[1536,128]{1,0:T(8,128)(2,1)S(1)}, bf16[1536,128]{1,0:T(8,128)(2,1)S(1)}) custom-call(f32[3,1024]{1,0:T(4,128)S(1)} %collective-permute-done.20.refs_0_, f32[3,1024]{1,0:T(4,128)S(1)} %collective-permute-done.21.refs_1_, ...), custom_call_target="tpu_custom_call" | custom-call | flops 1358954496 | bytes 4000000 | tf_op jit(solution)/shard_map/pallas_call | solution.py:670
  68.2 1.3 %collective-permute-done.29.refs_1_ = bf16[1536,128]{1,0:T(8,128)(2,1)S(1)} collective-permute-done((bf16[1536,128]{1,0:T(8,128)(2,1)S(1)}, bf16[1536,128]{1,0:T(8,128)(2,1)S(1)}, u32[]{:S(2)}, u32[]{:S(2)}) %collective-permute-start.29) | collective-permute-done | bytes 393248 | tf_op jit(solution)/shard_map/ppermute | solution.py:769
  72.2 1.9 %collective-permute-done.27.refs_2_ = f32[1,1024]{1,0:T(1,128)S(1)} collective-permute-done((f32[1,1024]{1,0:T(1,128)S(1)}, f32[1,1024]{1,0:T(1,128)S(1)}, u32[]{:S(2)}, u32[]{:S(2)}) %collective-permute-start.27) | collective-permute-done | bytes 4128 | tf_op jit(solution)/shard_map/ppermute | solution.py:813
  74.0 1.8 %collective-permute-done.30.refs_1_ = bf16[768,128]{1,0:T(8,128)(2,1)S(1)} collective-permute-done((bf16[768,128]{1,0:T(8,128)(2,1)S(1)}, bf16[768,128]{1,0:T(8,128)(2,1)S(1)}, u32[]{:S(2)}, u32[]{:S(2)}) %collective-permute-start.30) | collective-permute-done | bytes 196640 | tf_op jit(solution)/shard_map/ppermute | solution.py:772
  81.7 2.5 %collective-permute-start.34 = (bf16[192,128]{1,0:T(8,128)(2,1)S(1)}, bf16[192,128]{1,0:T(8,128)(2,1)S(1)}, u32[]{:S(2)}, u32[]{:S(2)}) collective-permute-start(bf16[192,128]{1,0:T(8,128)(2,1)S(1)} %shard_map.188.refs_0_), channel_id=1, source_target_pairs={{8,0},{10,2},{12,4},{14,6},{16,8},{18,10},{20,12},{22,14},{24,16},... | collective-permute-start | bytes 147464 | tf_op jit(solution)/shard_map/ppermute | solution.py:781
  85.4 2.8 %collective-permute-done.35.refs_2_ = bf16[192,128]{1,0:T(8,128)(2,1)S(1)} collective-permute-done((bf16[192,128]{1,0:T(8,128)(2,1)S(1)}, bf16[192,128]{1,0:T(8,128)(2,1)S(1)}, u32[]{:S(2)}, u32[]{:S(2)}) %collective-permute-start.35) | collective-permute-done | bytes 49184 | tf_op jit(solution)/shard_map/ppermute | solution.py:781
  88.2 1.6 %collective-permute-done.36.refs_3_ = bf16[192,128]{1,0:T(8,128)(2,1)S(1)} collective-permute-done((bf16[192,128]{1,0:T(8,128)(2,1)S(1)}, bf16[192,128]{1,0:T(8,128)(2,1)S(1)}, u32[]{:S(2)}, u32[]{:S(2)}) %collective-permute-start.36) | collective-permute-done | bytes 49184 | tf_op jit(solution)/shard_map/ppermute | solution.py:781
  89.8 1.7 %collective-permute-start.37 = (bf16[768,128]{1,0:T(8,128)(2,1)S(1)}, bf16[768,128]{1,0:T(8,128)(2,1)S(1)}, u32[]{:S(2)}, u32[]{:S(2)}) collective-permute-start(bf16[768,128]{1,0:T(8,128)(2,1)S(1)} %shard_map.189.refs_0_), channel_id=1, source_target_pairs={{4,0},{5,1},{6,2},{7,3},{0,4},{1,5},{2,6},{3,7},{12,8},{13,9},{14,... | collective-permute-start | bytes 589832 | tf_op jit(solution)/shard_map/ppermute | solution.py:793
  92.8 1.8 %collective-permute-done.37.refs_1_ = bf16[768,128]{1,0:T(8,128)(2,1)S(1)} collective-permute-done((bf16[768,128]{1,0:T(8,128)(2,1)S(1)}, bf16[768,128]{1,0:T(8,128)(2,1)S(1)}, u32[]{:S(2)}, u32[]{:S(2)}) %collective-permute-start.37) | collective-permute-done | bytes 196640 | tf_op jit(solution)/shard_map/ppermute | solution.py:793
  94.6 1.5 %collective-permute-done.38.refs_2_ = bf16[768,128]{1,0:T(8,128)(2,1)S(1)} collective-permute-done((bf16[768,128]{1,0:T(8,128)(2,1)S(1)}, bf16[768,128]{1,0:T(8,128)(2,1)S(1)}, u32[]{:S(2)}, u32[]{:S(2)}) %collective-permute-start.38) | collective-permute-done | bytes 196640 | tf_op jit(solution)/shard_map/ppermute | solution.py:793
  96.0 2.0 %collective-permute-done.39.refs_3_ = bf16[768,128]{1,0:T(8,128)(2,1)S(1)} collective-permute-done((bf16[768,128]{1,0:T(8,128)(2,1)S(1)}, bf16[768,128]{1,0:T(8,128)(2,1)S(1)}, u32[]{:S(2)}, u32[]{:S(2)}) %collective-permute-start.39) | collective-permute-done | bytes 196640 | tf_op jit(solution)/shard_map/ppermute | solution.py:793
  98.1 4.9 %collective-permute-start.40 = (bf16[3072,128]{1,0:T(8,128)(2,1)S(1)}, bf16[3072,128]{1,0:T(8,128)(2,1)S(1)}, u32[]{:S(2)}, u32[]{:S(2)}) collective-permute-start(bf16[3072,128]{1,0:T(8,128)(2,1)S(1)} %shard_map.190.refs_0_), channel_id=1, source_target_pairs={{2,0},{0,2},{6,4},{4,6},{10,8},{8,10},{14,12},{12,14},{18,16},{16,... | collective-permute-start | bytes 2359304 | tf_op jit(solution)/shard_map/ppermute | solution.py:769
  103.0 1.9 %collective-permute-start.28 = (f32[2,512]{1,0:T(2,128)S(1)}, f32[2,512]{1,0:T(2,128)S(1)}, u32[]{:S(2)}, u32[]{:S(2)}) collective-permute-start(f32[2,512]{1,0:T(2,128)S(1)} %shard_map.185.refs_2_), channel_id=1, source_target_pairs={{0,0},{2,2},{10,4},{8,6},{16,8},{18,10},{26,12},{24,14},{28,16},{3... | collective-permute-start | bytes 12296 | tf_op jit(solution)/shard_map/ppermute | solution.py:915
  104.9 3.9 %collective-permute-done.28 = f32[2,512]{1,0:T(2,128)S(1)} collective-permute-done((f32[2,512]{1,0:T(2,128)S(1)}, f32[2,512]{1,0:T(2,128)S(1)}, u32[]{:S(2)}, u32[]{:S(2)}) %collective-permute-start.28) | collective-permute-done | bytes 4128 | tf_op jit(solution)/shard_map/ppermute | solution.py:915
  110.2 2.2 %shard_map.191 = (f32[2,64,64,81]{3,2,1,0:T(8,128)}, f32[2,2,64,81]{3,2,1,0:T(8,128)}, f32[2,64,81]{2,1,0:T(8,128)}) custom-call(bf16[3072,128]{1,0:T(8,128)(2,1)S(1)} %shard_map.190.refs_0_), custom_call_target="tpu_custom_call" | custom-call | flops 1000000000 | bytes 4000000 | tf_op jit(solution)/shard_map/pallas_call | solution.py:670
  112.3 2.7 %shard_map.192 = (f32[2,64]{1,0:T(2,128)}, f32[2,64]{1,0:T(2,128)}, f32[2,2]{1,0:T(2,128)}, f32[1,1]{1,0:T(1,128)}, f32[2,64,64,81]{3,2,1,0:T(8,128)}, /*index=5*/f32[2,2,64,81]{3,2,1,0:T(8,128)}, f32[2,64,81]{2,1,0:T(8,128)}) custom-call(bf16[3072,128]{1,0:T(8,128)(2,1)S(1)} %collective-permute-done.40.re, ...), custom_call_target="tpu_custom_call", output_to_operand_aliasing={{4}: (1, {}), {5}: (2, {}), {6}: (3, {})} | custom-call | flops 1000000000 | bytes 4000000 | tf_op jit(solution)/shard_map/pallas_call | solution.py:670
  (87 shorter events, 33.5 us)
Async XLA Ops:
  1.4 18.0 %collective-permute-start = (f32[1,512]{1,0:T(1,128)S(1)}, f32[1,512]{1,0:T(1,128)S(1)}, u32[]{:S(2)}, u32[]{:S(2)}) collective-permute-start(f32[1,512]{1,0:T(1,128)S(1)} %reshape.39), channel_id=1, source_target_pairs={{0,0},{1,1},{2,2},{3,3},{4,10},{5,11},{6,8},{7,9},{8,16},{9,17},{1... | collective-permute-start | bytes 6152 | tf_op jit(solution)/shard_map/ppermute | solution.py:819
  5.1 14.3 %collective-permute-start.1 = (f32[1,512]{1,0:T(1,128)S(1)}, f32[1,512]{1,0:T(1,128)S(1)}, u32[]{:S(2)}, u32[]{:S(2)}) collective-permute-start(f32[1,512]{1,0:T(1,128)S(1)} %reshape.39), channel_id=1, source_target_pairs={{1,0},{0,1},{3,2},{2,3},{5,10},{4,11},{7,8},{6,9},{9,16},{8,17},{1... | collective-permute-start | bytes 6152 | tf_op jit(solution)/shard_map/ppermute | solution.py:819
  19.4 4.6 %collective-permute-start.2 = (f32[1,1024]{1,0:T(1,128)S(1)}, f32[1,1024]{1,0:T(1,128)S(1)}, u32[]{:S(2)}, u32[]{:S(2)}) collective-permute-start(f32[1,1024]{1,0:T(1,128)S(1)} %shard_map.179.refs_3_), channel_id=1, source_target_pairs={{14,0},{6,2},{4,10},{0,8},{2,16},{10,18},{8,26},{16,24},{18,28},{2... | collective-permute-start | bytes 12296 | tf_op jit(solution)/shard_map/ppermute | solution.py:813
  19.5 5.3 %collective-permute-start.3 = (f32[1,1024]{1,0:T(1,128)S(1)}, f32[1,1024]{1,0:T(1,128)S(1)}, u32[]{:S(2)}, u32[]{:S(2)}) collective-permute-start(f32[1,1024]{1,0:T(1,128)S(1)} %shard_map.179.refs_3_), channel_id=1, source_target_pairs={{6,0},{4,2},{0,10},{2,8},{10,16},{8,18},{16,26},{18,24},{26,28},{2... | collective-permute-start | bytes 12296 | tf_op jit(solution)/shard_map/ppermute | solution.py:813
  24.1 3.0 %collective-permute-start.6 = (f32[1,1024]{1,0:T(1,128)S(1)}, f32[1,1024]{1,0:T(1,128)S(1)}, u32[]{:S(2)}, u32[]{:S(2)}) collective-permute-start(f32[1,1024]{1,0:T(1,128)S(1)} %shard_map.179.refs_3_), channel_id=1, source_target_pairs={{10,0},{8,2},{16,10},{18,8},{26,16},{24,18},{28,26},{30,24},{22,28... | collective-permute-start | bytes 12296 | tf_op jit(solution)/shard_map/ppermute | solution.py:813
  24.1 3.0 %collective-permute-start.7 = (f32[1,1024]{1,0:T(1,128)S(1)}, f32[1,1024]{1,0:T(1,128)S(1)}, u32[]{:S(2)}, u32[]{:S(2)}) collective-permute-start(f32[1,1024]{1,0:T(1,128)S(1)} %shard_map.179.refs_3_), channel_id=1, source_target_pairs={{8,0},{16,2},{18,10},{26,8},{24,16},{28,18},{30,26},{22,24},{20,28... | collective-permute-start | bytes 12296 | tf_op jit(solution)/shard_map/ppermute | solution.py:813
  32.1 4.9 %collective-permute-start.10 = (f32[2,1024]{1,0:T(2,128)S(1)}, f32[2,1024]{1,0:T(2,128)S(1)}, u32[]{:S(2)}, u32[]{:S(2)}) collective-permute-start(f32[2,1024]{1,0:T(2,128)S(1)} %get-tuple-element.67.refs_3_), channel_id=1, source_target_pairs={{4,0},{0,2},{2,10},{10,8},{8,16},{16,18},{18,26},{26,24},{24,28},{... | collective-permute-start | bytes 24584 | tf_op jit(solution)/shard_map/ppermute | solution.py:813
  33.5 5.1 %collective-permute-start.11 = (f32[2,1024]{1,0:T(2,128)S(1)}, f32[2,1024]{1,0:T(2,128)S(1)}, u32[]{:S(2)}, u32[]{:S(2)}) collective-permute-start(f32[2,1024]{1,0:T(2,128)S(1)} %get-tuple-element.67.refs_3_), channel_id=1, source_target_pairs={{2,0},{10,2},{8,10},{16,8},{18,16},{26,18},{24,26},{28,24},{30,28}... | collective-permute-start | bytes 24584 | tf_op jit(solution)/shard_map/ppermute | solution.py:813
  33.6 5.0 %collective-permute-start.12 = (f32[2,1024]{1,0:T(2,128)S(1)}, f32[2,1024]{1,0:T(2,128)S(1)}, u32[]{:S(2)}, u32[]{:S(2)}) collective-permute-start(f32[2,1024]{1,0:T(2,128)S(1)} %get-tuple-element.67.refs_3_), channel_id=1, source_target_pairs={{10,0},{8,2},{16,10},{18,8},{26,16},{24,18},{28,26},{30,24},{22,28... | collective-permute-start | bytes 24584 | tf_op jit(solution)/shard_map/ppermute | solution.py:813
  35.6 3.0 %collective-permute-start.13 = (f32[2,1024]{1,0:T(2,128)S(1)}, f32[2,1024]{1,0:T(2,128)S(1)}, u32[]{:S(2)}, u32[]{:S(2)}) collective-permute-start(f32[2,1024]{1,0:T(2,128)S(1)} %get-tuple-element.67.refs_3_), channel_id=1, source_target_pairs={{8,0},{16,2},{18,10},{26,8},{24,16},{28,18},{30,26},{22,24},{20,28... | collective-permute-start | bytes 24584 | tf_op jit(solution)/shard_map/ppermute | solution.py:813
  36.0 4.0 %collective-permute-start.8 = (f32[2,1024]{1,0:T(2,128)S(1)}, f32[2,1024]{1,0:T(2,128)S(1)}, u32[]{:S(2)}, u32[]{:S(2)}) collective-permute-start(f32[2,1024]{1,0:T(2,128)S(1)} %get-tuple-element.67.refs_3_), channel_id=1, source_target_pairs={{14,0},{6,2},{4,10},{0,8},{2,16},{10,18},{8,26},{16,24},{18,28},{2... | collective-permute-start | bytes 24584 | tf_op jit(solution)/shard_map/ppermute | solution.py:813
  37.0 3.1 %collective-permute-start.9 = (f32[2,1024]{1,0:T(2,128)S(1)}, f32[2,1024]{1,0:T(2,128)S(1)}, u32[]{:S(2)}, u32[]{:S(2)}) collective-permute-start(f32[2,1024]{1,0:T(2,128)S(1)} %get-tuple-element.67.refs_3_), channel_id=1, source_target_pairs={{6,0},{4,2},{0,10},{2,8},{10,16},{8,18},{16,26},{18,24},{26,28},{2... | collective-permute-start | bytes 24584 | tf_op jit(solution)/shard_map/ppermute | solution.py:813
  44.5 5.7 %collective-permute-start.14 = (f32[2,1024]{1,0:T(2,128)S(1)}, f32[2,1024]{1,0:T(2,128)S(1)}, u32[]{:S(2)}, u32[]{:S(2)}) collective-permute-start(f32[2,1024]{1,0:T(2,128)S(1)} %get-tuple-element.72.refs_3_), channel_id=1, source_target_pairs={{14,0},{6,2},{4,10},{0,8},{2,16},{10,18},{8,26},{16,24},{18,28},{2... | collective-permute-start | bytes 24584 | tf_op jit(solution)/shard_map/ppermute | solution.py:813
  46.4 3.8 %collective-permute-start.15 = (f32[2,1024]{1,0:T(2,128)S(1)}, f32[2,1024]{1,0:T(2,128)S(1)}, u32[]{:S(2)}, u32[]{:S(2)}) collective-permute-start(f32[2,1024]{1,0:T(2,128)S(1)} %get-tuple-element.72.refs_3_), channel_id=1, source_target_pairs={{6,0},{4,2},{0,10},{2,8},{10,16},{8,18},{16,26},{18,24},{26,28},{2... | collective-permute-start | bytes 24584 | tf_op jit(solution)/shard_map/ppermute | solution.py:813
  49.0 3.1 %collective-permute-start.18 = (f32[2,1024]{1,0:T(2,128)S(1)}, f32[2,1024]{1,0:T(2,128)S(1)}, u32[]{:S(2)}, u32[]{:S(2)}) collective-permute-start(f32[2,1024]{1,0:T(2,128)S(1)} %get-tuple-element.72.refs_3_), channel_id=1, source_target_pairs={{10,0},{8,2},{16,10},{18,8},{26,16},{24,18},{28,26},{30,24},{22,28... | collective-permute-start | bytes 24584 | tf_op jit(solution)/shard_map/ppermute | solution.py:813
  55.6 5.1 %collective-permute-start.20 = (f32[3,1024]{1,0:T(4,128)S(1)}, f32[3,1024]{1,0:T(4,128)S(1)}, u32[]{:S(2)}, u32[]{:S(2)}) collective-permute-start(f32[3,1024]{1,0:T(4,128)S(1)} %get-tuple-element.80.refs_3_), channel_id=1, source_target_pairs={{14,0},{6,2},{4,10},{0,8},{2,16},{10,18},{8,26},{16,24},{18,28},{2... | collective-permute-start | bytes 36872 | tf_op jit(solution)/shard_map/ppermute | solution.py:813
  56.9 5.9 %collective-permute-start.21 = (f32[3,1024]{1,0:T(4,128)S(1)}, f32[3,1024]{1,0:T(4,128)S(1)}, u32[]{:S(2)}, u32[]{:S(2)}) collective-permute-start(f32[3,1024]{1,0:T(4,128)S(1)} %get-tuple-element.80.refs_3_), channel_id=1, source_target_pairs={{6,0},{4,2},{0,10},{2,8},{10,16},{8,18},{16,26},{18,24},{26,28},{2... | collective-permute-start | bytes 36872 | tf_op jit(solution)/shard_map/ppermute | solution.py:813
  57.9 5.0 %collective-permute-start.22 = (f32[3,1024]{1,0:T(4,128)S(1)}, f32[3,1024]{1,0:T(4,128)S(1)}, u32[]{:S(2)}, u32[]{:S(2)}) collective-permute-start(f32[3,1024]{1,0:T(4,128)S(1)} %get-tuple-element.80.refs_3_), channel_id=1, source_target_pairs={{4,0},{0,2},{2,10},{10,8},{8,16},{16,18},{18,26},{26,24},{24,28},{... | collective-permute-start | bytes 36872 | tf_op jit(solution)/shard_map/ppermute | solution.py:813
  58.4 4.5 %collective-permute-start.23 = (f32[3,1024]{1,0:T(4,128)S(1)}, f32[3,1024]{1,0:T(4,128)S(1)}, u32[]{:S(2)}, u32[]{:S(2)}) collective-permute-start(f32[3,1024]{1,0:T(4,128)S(1)} %get-tuple-element.80.refs_3_), channel_id=1, source_target_pairs={{2,0},{10,2},{8,10},{16,8},{18,16},{26,18},{24,26},{28,24},{30,28}... | collective-permute-start | bytes 36872 | tf_op jit(solution)/shard_map/ppermute | solution.py:813
  59.4 3.5 %collective-permute-start.24 = (f32[3,1024]{1,0:T(4,128)S(1)}, f32[3,1024]{1,0:T(4,128)S(1)}, u32[]{:S(2)}, u32[]{:S(2)}) collective-permute-start(f32[3,1024]{1,0:T(4,128)S(1)} %get-tuple-element.80.refs_3_), channel_id=1, source_target_pairs={{10,0},{8,2},{16,10},{18,8},{26,16},{24,18},{28,26},{30,24},{22,28... | collective-permute-start | bytes 36872 | tf_op jit(solution)/shard_map/ppermute | solution.py:813
  69.6 6.2 %collective-permute-start.30 = (bf16[768,128]{1,0:T(8,128)(2,1)S(1)}, bf16[768,128]{1,0:T(8,128)(2,1)S(1)}, u32[]{:S(2)}, u32[]{:S(2)}) collective-permute-start(bf16[768,128]{1,0:T(8,128)(2,1)S(1)} %get-tuple-element.100), channel_id=1, source_target_pairs={{4,0},{6,2},{0,4},{2,6},{12,8},{14,10},{8,12},{10,14},{20,16},{22,... | collective-permute-start | bytes 589832 | tf_op jit(solution)/shard_map/ppermute | solution.py:772
  75.9 4.8 %collective-permute-start.31 = (bf16[192,128]{1,0:T(8,128)(2,1)S(1)}, bf16[192,128]{1,0:T(8,128)(2,1)S(1)}, u32[]{:S(2)}, u32[]{:S(2)}) collective-permute-start(bf16[192,128]{1,0:T(8,128)(2,1)S(1)} %get-tuple-element.102), channel_id=1, source_target_pairs={{24,0},{26,2},{28,4},{30,6},{0,8},{2,10},{4,12},{6,14},{8,16},{10,... | collective-permute-start | bytes 147464 | tf_op jit(solution)/shard_map/ppermute | solution.py:776
  76.9 4.8 %collective-permute-start.32 = (bf16[192,128]{1,0:T(8,128)(2,1)S(1)}, bf16[192,128]{1,0:T(8,128)(2,1)S(1)}, u32[]{:S(2)}, u32[]{:S(2)}) collective-permute-start(bf16[192,128]{1,0:T(8,128)(2,1)S(1)} %get-tuple-element.103), channel_id=1, source_target_pairs={{16,0},{18,2},{20,4},{22,6},{24,8},{26,10},{28,12},{30,14},{0,16},... | collective-permute-start | bytes 147464 | tf_op jit(solution)/shard_map/ppermute | solution.py:776
  78.1 3.6 %collective-permute-start.33 = (bf16[192,128]{1,0:T(8,128)(2,1)S(1)}, bf16[192,128]{1,0:T(8,128)(2,1)S(1)}, u32[]{:S(2)}, u32[]{:S(2)}) collective-permute-start(bf16[192,128]{1,0:T(8,128)(2,1)S(1)} %get-tuple-element.104), channel_id=1, source_target_pairs={{8,0},{10,2},{12,4},{14,6},{16,8},{18,10},{20,12},{22,14},{24,16},... | collective-permute-start | bytes 147464 | tf_op jit(solution)/shard_map/ppermute | solution.py:776
  81.7 3.7 %collective-permute-start.34 = (bf16[192,128]{1,0:T(8,128)(2,1)S(1)}, bf16[192,128]{1,0:T(8,128)(2,1)S(1)}, u32[]{:S(2)}, u32[]{:S(2)}) collective-permute-start(bf16[192,128]{1,0:T(8,128)(2,1)S(1)} %shard_map.188.refs_0_), channel_id=1, source_target_pairs={{8,0},{10,2},{12,4},{14,6},{16,8},{18,10},{20,12},{22,14},{24,16},... | collective-permute-start | bytes 147464 | tf_op jit(solution)/shard_map/ppermute | solution.py:781
  84.3 4.0 %collective-permute-start.35 = (bf16[192,128]{1,0:T(8,128)(2,1)S(1)}, bf16[192,128]{1,0:T(8,128)(2,1)S(1)}, u32[]{:S(2)}, u32[]{:S(2)}) collective-permute-start(bf16[192,128]{1,0:T(8,128)(2,1)S(1)} %shard_map.188.refs_0_), channel_id=1, source_target_pairs={{16,0},{18,2},{20,4},{22,6},{24,8},{26,10},{28,12},{30,14},{0,16},... | collective-permute-start | bytes 147464 | tf_op jit(solution)/shard_map/ppermute | solution.py:781
  85.0 4.7 %collective-permute-start.36 = (bf16[192,128]{1,0:T(8,128)(2,1)S(1)}, bf16[192,128]{1,0:T(8,128)(2,1)S(1)}, u32[]{:S(2)}, u32[]{:S(2)}) collective-permute-start(bf16[192,128]{1,0:T(8,128)(2,1)S(1)} %shard_map.188.refs_0_), channel_id=1, source_target_pairs={{24,0},{26,2},{28,4},{30,6},{0,8},{2,10},{4,12},{6,14},{8,16},{10,... | collective-permute-start | bytes 147464 | tf_op jit(solution)/shard_map/ppermute | solution.py:781
  89.8 4.8 %collective-permute-start.37 = (bf16[768,128]{1,0:T(8,128)(2,1)S(1)}, bf16[768,128]{1,0:T(8,128)(2,1)S(1)}, u32[]{:S(2)}, u32[]{:S(2)}) collective-permute-start(bf16[768,128]{1,0:T(8,128)(2,1)S(1)} %shard_map.189.refs_0_), channel_id=1, source_target_pairs={{4,0},{5,1},{6,2},{7,3},{0,4},{1,5},{2,6},{3,7},{12,8},{13,9},{14,... | collective-permute-start | bytes 589832 | tf_op jit(solution)/shard_map/ppermute | solution.py:793
  91.5 4.5 %collective-permute-start.38 = (bf16[768,128]{1,0:T(8,128)(2,1)S(1)}, bf16[768,128]{1,0:T(8,128)(2,1)S(1)}, u32[]{:S(2)}, u32[]{:S(2)}) collective-permute-start(bf16[768,128]{1,0:T(8,128)(2,1)S(1)} %shard_map.189.refs_0_), channel_id=1, source_target_pairs={{1,0},{0,1},{3,2},{2,3},{5,4},{4,5},{7,6},{6,7},{9,8},{8,9},{11,10... | collective-permute-start | bytes 589832 | tf_op jit(solution)/shard_map/ppermute | solution.py:793
  91.8 6.3 %collective-permute-start.39 = (bf16[768,128]{1,0:T(8,128)(2,1)S(1)}, bf16[768,128]{1,0:T(8,128)(2,1)S(1)}, u32[]{:S(2)}, u32[]{:S(2)}) collective-permute-start(bf16[768,128]{1,0:T(8,128)(2,1)S(1)} %shard_map.189.refs_0_), channel_id=1, source_target_pairs={{5,0},{4,1},{7,2},{6,3},{1,4},{0,5},{3,6},{2,7},{13,8},{12,9},{15,... | collective-permute-start | bytes 589832 | tf_op jit(solution)/shard_map/ppermute | solution.py:793
  98.1 14.2 %collective-permute-start.40 = (bf16[3072,128]{1,0:T(8,128)(2,1)S(1)}, bf16[3072,128]{1,0:T(8,128)(2,1)S(1)}, u32[]{:S(2)}, u32[]{:S(2)}) collective-permute-start(bf16[3072,128]{1,0:T(8,128)(2,1)S(1)} %shard_map.190.refs_0_), channel_id=1, source_target_pairs={{2,0},{0,2},{6,4},{4,6},{10,8},{8,10},{14,12},{12,14},{18,16},{16,... | collective-permute-start | bytes 2359304 | tf_op jit(solution)/shard_map/ppermute | solution.py:769
  103.0 5.8 %collective-permute-start.28 = (f32[2,512]{1,0:T(2,128)S(1)}, f32[2,512]{1,0:T(2,128)S(1)}, u32[]{:S(2)}, u32[]{:S(2)}) collective-permute-start(f32[2,512]{1,0:T(2,128)S(1)} %shard_map.185.refs_2_), channel_id=1, source_target_pairs={{0,0},{2,2},{10,4},{8,6},{16,8},{18,10},{26,12},{24,14},{28,16},{3... | collective-permute-start | bytes 12296 | tf_op jit(solution)/shard_map/ppermute | solution.py:915
  (16 other events, 68.1 us)

commit v5 on v4

--- a/solution.py
+++ b/solution.py
@@ -177,8 +177,8 @@
     return (row == lax.broadcasted_iota(jnp.int32, (n, n), 1)).astype(F32).astype(BF)
 
 
-def pack_kernel(layer, ready, w_mid, w_first, w_last, biases, lanes, rows_81,
-                matrix, first, narrow, last_back, first_back, turned, columns, taps, rows):
+def pack_ahead_kernel(layer, ready, w_mid, w_first, w_last, biases, lanes, spread_rows, *refs):
+    matrix, first, narrow, columns, taps, rows = refs[-6:]
     channels = w_mid.shape[1]
     few = channels // 2
     for o in range(few):
@@ -199,38 +199,47 @@
                 matrix[at, wide] = jnp.concatenate([low, high], axis=1).astype(BF)
             else:
                 matrix[at, outer * channels :] = low.astype(BF)
-    for inner in range(9):
-        at = pl.ds(inner * channels, channels)
-        for outer in range(0, 9, 2):
-            if outer < 8:
-                wide = slice(outer * channels, (outer + 2) * channels)
-                both = dot_nt(identity(2 * channels), matrix[at, wide])
-                turned[at, wide] = jnp.concatenate([both[:channels], both[channels:]], axis=1).astype(BF)
-            else:
-                turned[at, outer * channels :] = dot_nt(
-                    identity(channels), matrix[at, outer * channels :]
-                ).astype(BF)
-    wf = w_first[layer]
-    first[...] = dot(wf, lanes[:, : 5 * 256]).astype(BF)
-    first_back[...] = dot_nt(rows_81[6 * 216 : 7 * 216, :TAPS], wf).astype(BF)
+    first[...] = dot(w_first[layer], lanes[...]).astype(BF)
     for dx in range(3):
         narrow[dx] = sum(
-            dot_nt(rows_81[(dx * 2 + o) * 216 : (dx * 2 + o + 1) * 216, :TAPS], w_last[layer, o])
+            dot_nt(spread_rows[(dx * 2 + o) * 216 : (dx * 2 + o + 1) * 216, :TAPS], w_last[layer, o])
             for o in range(2)
         ).astype(BF)
-    last_back[...] = sum(
-        dot(w_last[layer, o], lanes[:, 5 * 256 + o * 1536 : 5 * 256 + (o + 1) * 1536]) for o in range(2)
-    ).astype(BF)
     rows[...] = jnp.zeros_like(rows)
     rows[0:3, :channels] = biases[3 * layer : 3 * layer + 3, :]
     columns[...] = rows[...].T
 
 
+def pack_back_kernel(ready, matrix_zero, matrix_one, w_first, w_last, lanes, spread_rows, *refs):
+    outs = refs[-6:]
+    channels = w_first.shape[1]
+    for layer, matrix in ((0, matrix_zero), (1, matrix_one)):
+        last_back, turned, first_back = outs[3 * layer : 3 * layer + 3]
+        for inner in range(9):
+            at = pl.ds(inner * channels, channels)
+            for outer in range(0, 9, 2):
+                end = min(outer + 2, 9) * channels
+                both = dot_nt(identity(end - outer * channels), matrix[at, outer * channels : end])
+                if outer < 8:
+                    both = jnp.concatenate([both[:channels], both[channels:]], axis=1)
+                turned[at, outer * channels : end] = both.astype(BF)
+        first_back[...] = dot_nt(spread_rows[:, :TAPS], w_first[layer]).astype(BF)
+        last_back[...] = sum(
+            dot(w_last[layer, o], lanes[:, o * 1536 : (o + 1) * 1536]) for o in range(2)
+        ).astype(BF)
+
+
 def unpack_kernel(layout, volume, last, ready, coords, pieces, *refs):
     if last:
-        refs = refs[3:]
-        g_mid, g_last, g_first, gb_first, gb_mid, gb_last, loss = refs[:7]
-        bulk, taps, mid, lasts, firsts, sems = refs[7:]
+        force_in, refs = refs[0], refs[4:]
+        g_mid, g_last, g_first, gb_first, gb_mid, gb_last, loss, sample, force = refs[:9]
+        bulk, taps, mid, lasts, firsts, sems = refs[9:]
+        period = force.shape[3]
+        for row, target in ((0, force), (1, sample)):
+            for k in range(target.shape[1] * target.shape[2]):
+                target[0, k // target.shape[2], k % target.shape[2] : k % target.shape[2] + 1, :] = (
+                    force_in[row : row + 1, k * period : (k + 1) * period]
+                )
     else:
         g_mid, g_last, g_first = refs[:3]
         bulk, taps, mid, lasts, firsts, sems = refs[3:]
@@ -245,7 +254,7 @@
         for ry in range(2):
             for rz in range(depth):
                 to = ((lax.rem(g + rg, halves) * 2 + (1 - y if ry else y)) * depth
-                      + lax.rem(z + rz, depth)) * chunk
+                      + (z ^ rz)) * chunk
                 for layer in range(2):
                     bulk[layer, pl.ds(pl.multiple_of(to, 16), chunk), :] = pieces[at : at + chunk, :]
                     at += chunk
@@ -371,7 +380,7 @@
         for ry in range(2):
             for rz in range(depth):
                 source = core * per_core + (
-                    (g * 2 + (1 - y if ry else y)) * depth + lax.rem(z + rz, depth)
+                    (g * 2 + (1 - y if ry else y)) * depth + (z ^ rz)
                 ) * chunk
                 for bulk in bulks:
                     ref[at : at + chunk, :] = bulk[pl.ds(pl.multiple_of(source, 16), chunk), :]
@@ -704,31 +713,33 @@
     return kernel_call(body, outs, scratch, args, flops)
 
 
-def pack(params, picks):
+def pack_ahead(layer, params, picks, after=()):
     channels = params[0].shape[1]
     outs = [
         shape((9 * channels, 9 * channels), BF),
         shape((channels, 5 * 256), BF),
         shape((3, 216, channels), BF),
-        shape((channels, 3 * 512), BF),
-        shape((216, channels), BF),
-        shape((9 * channels, 9 * channels), BF),
         shape((128, 8)),
     ]
-    many = len(outs)
-
-    def body(ready, *refs):
-        ins, rest = refs[:6], refs[6:]
-        for layer in range(2):
-            pack_kernel(layer, ready, *ins, *rest[layer * many : (layer + 1) * many], *rest[2 * many :])
-
     scratch = [pltpu.VMEM((TAPS * channels // 2, 2 * channels), F32), pltpu.VMEM((8, 128), F32)]
-    args = [*params, *picks]
-    got = kernel_call(body, outs * 2, scratch, args, 1_000_000_000)
-    return got[:many], got[many:]
-
-
-def unpack(last, layout, volume, coords, pieces, channels, before):
+    body = functools.partial(pack_ahead_kernel, layer)
+    return kernel_call(body, outs, scratch, [*params, *picks, *after], 1_000_000_000, loose=after)
+
+
+def pack_back(matrices, narrow, picks, after):
+    channels = narrow[0].shape[1]
+    outs = [
+        shape((channels, 3 * 512), BF),
+        shape((9 * channels, 9 * channels), BF),
+        shape((216, channels), BF),
+    ]
+    got = kernel_call(
+        pack_back_kernel, outs * 2, [], [*matrices, *narrow, *picks, *after], 1_000_000_000, loose=after
+    )
+    return got[:3], got[3:]
+
+
+def unpack(last, layout, volume, coords, pieces, channels, before, force=None, block=None):
     halves, depth, chunk = layout
     few = channels // 2
     arrays = [
@@ -749,17 +760,18 @@
         return kernel_call(
             body, arrays, scratch, [coords, pieces], 1_000_000_000, hbm_outs=3
         )
-    extra = [shape((2, channels)), shape((2, channels)), shape((2, 2)), shape((1, 1))]
+    extra = [shape((2, channels)), shape((2, channels)), shape((2, 2)), shape((1, 1)), shape(block), shape(block)]
+    new = len(extra)
 
     def reordered(ready, coords, pieces, *refs):
-        before, outs, rest = refs[:3], refs[3:10], refs[10:]
-        body(ready, coords, pieces, *before, *outs[4:], *outs[:4], *rest)
+        ins, outs, rest = refs[:4], refs[4 : 7 + new], refs[7 + new :]
+        body(ready, coords, pieces, *ins, *outs[new:], *outs[:new], *rest)
 
     got = kernel_call(
-        reordered, extra + arrays, scratch, [coords, pieces, *before], 1_000_000_000,
-        loose=before, hbm_outs=3, aliases={1: 4, 2: 5, 3: 6},
-    )
-    return [*got[4:], *got[:4]]
+        reordered, extra + arrays, scratch, [coords, pieces, force, *before], 1_000_000_000,
+        loose=before, hbm_outs=3, aliases={2 + i: new + i for i in range(3)},
+    )
+    return [*got[new:], *got[:new]]
 
 
 def permuters(count, halves, depth):
@@ -772,13 +784,10 @@
         return lax.ppermute(v, "xy", xy(lambda a: a ^ 2))
 
     def scatter(pieces):
-        return [
-            lax.ppermute(pieces[s], "xy", xy(lambda a, s=s: (a - 4 * s) % count))
-            for s in range(1, depth)
-        ]
+        return [lax.ppermute(pieces[s], "xy", xy(lambda a, s=s: a ^ (4 * s))) for s in range(1, depth)]
 
     def gather(v):
-        return [lax.ppermute(v, "xy", xy(lambda a, s=s: (a + 4 * s) % count)) for s in range(1, depth)]
+        return [lax.ppermute(v, "xy", xy(lambda a, s=s: a ^ (4 * s))) for s in range(1, depth)]
 
     def square(v):
         out = []
@@ -814,10 +823,9 @@
             values, "xy", [(order[(p + offset) % count], order[p]) for p in range(count)]
         )
 
-    flat = noise.reshape(1, -1)
     whole = [
         lax.ppermute(
-            flat,
+            noise,
             ("xy", "gz"),
             [
                 (p * halves + (j + rel) % halves, order[p] * halves + j)
@@ -834,35 +842,43 @@
         jnp.stack([b_first, b_mid, jnp.pad(b_last, ((0, 0), (0, channels - 2)))], axis=1).reshape(6, channels),
     ]
     back = spread_last_back()
-    tall = np.concatenate([spread_last().reshape(6 * 216, TAPS), spread_first_back()], axis=0)
+    pad = ((0, 0), (0, 128 - TAPS))
     picks = [
-        jnp.asarray(np.concatenate([spread_first(), back[0], back[1]], axis=1), BF),
-        jnp.asarray(np.pad(tall, ((0, 0), (0, 128 - TAPS))), BF),
+        jnp.asarray(spread_first(), BF),
+        jnp.asarray(np.pad(spread_last().reshape(6 * 216, TAPS), pad), BF),
+    ]
+    back_picks = [
+        jnp.asarray(np.concatenate([back[0], back[1]], axis=1), BF),
+        jnp.asarray(np.pad(spread_first_back(), pad), BF),
     ]
     pick_l, pick_f = jnp.asarray(pick_last(), BF), jnp.asarray(pick_first(), BF)
-    packed = pack(params, picks)
-    ahead_weights = [(p[1], p[0], p[2], p[6]) for p in packed]
-    back_weights = [(p[3], p[5], p[4]) for p in packed]
+    packed = [pack_ahead(0, params, picks)]
 
     def join(ready, *refs):
-        piece = refs[0].shape[1]
+        rows = noise.shape[1] * noise.shape[2]
         for rel in range(halves):
-            refs[-1][:, rel * piece : (rel + 1) * piece] = refs[rel][...]
-
-    waits = (packed[1][5],)
+            for k in range(rows):
+                at = (rel * rows + k) * period
+                y = k % noise.shape[2]
+                refs[-1][:, at : at + period] = refs[rel][0, k // noise.shape[2], y : y + 1, :]
+
+    waits = (packed[0][0],)
     (whole,) = kernel_call(
-        join, [shape((1, flat.shape[1] * halves))], [], [*whole, *waits], 1000, loose=waits, bytes_moved=1000
+        join, [shape((1, noise.size * halves))], [], [*whole, *waits], 1000, loose=waits, bytes_moved=1000
     )
 
     def exchange(values):
         return [values if m == 0 else step(values, m) for m in range(-3, 4)]
 
+    order_weights = lambda p: (p[1], p[0], p[2], p[3])
     field0, state, _, logdet0, first0, second0 = forward(
-        period, 0, exchange(whole), coords, ahead_weights[0], channels, halves
-    )
+        period, 0, exchange(whole), coords, order_weights(packed[0]), channels, halves
+    )
+    packed.append(pack_ahead(1, params, picks, (logdet0,)))
     field1, state, own, logdet1, growth0, first1, second1 = forward(
-        period, 1, exchange(state), coords, ahead_weights[1], channels, halves
-    )
+        period, 1, exchange(state), coords, order_weights(packed[1]), channels, halves
+    )
+    back_weights = pack_back([p[0] for p in packed], params[1:3], back_picks, (logdet1,))
     core, cross, scatter, gather, square = permuters(count, halves, depth)
     length = field0.shape[1]
     full = shape((ROWS, length))
@@ -914,13 +930,13 @@
     other = core(mine)
     force = lax.ppermute(force, "xy", [(order[p], p) for p in range(count)])
     outs = unpack(False, layout, volume, coords, mine, channels, [])
-    g_mid, g_last, g_first, gb_first, gb_mid, gb_last, loss = unpack(
-        True, layout, volume, coords, other, channels, list(outs)
+    g_mid, g_last, g_first, gb_first, gb_mid, gb_last, loss, sample, force = unpack(
+        True, layout, volume, coords, other, channels, list(outs), force, noise.shape
     )
 
     return (
-        force[1:2].reshape(noise.shape),
-        force[0:1].reshape(noise.shape),
+        sample,
+        force,
         loss.reshape(()),
         g_first.reshape(2, channels, 1, TAPS).transpose(0, 3, 1, 2),
         gb_first,

time: 116 us -> 107 us (0.922)
  waiting for transfers between devices: 29.1 us -> 22.1 us
  local copies, waits for them, and re-layouts: 8.17 us -> 5.84 us
    ppermute x1, waiting for transfers between devices: 3.89 us -> 0.04 us  [per_device(): force = lax.ppermute(force, 'xy', [(order[p], p) for p in range(count)])]
    reshape x3 -> x0, local copies, waits for them, and re-layouts: 2.15 us -> none  [the longest x1 0.78 us: per_device(): flat = noise.reshape(1, -1)]
    ppermute x1, starting transfers between devices: 1.92 us -> 3.6 us  [per_device(): force = lax.ppermute(force, 'xy', [(order[p], p) for p in range(count)])]
    ppermute x26, waiting for transfers between devices: 9.8 us -> 8.28 us  [step(): lax.ppermute(values, 'xy', [(order[(p + offset) % count], order[p]) for p...]
    ppermute x8, waiting for transfers between devices: 7.01 us -> 5.51 us  [the longest x3 2.81 us: gather(): lax.ppermute(v, 'xy', xy(lambda a, s=s: a ^ 4 * s))]
    pallas_call x15 -> x17, Pallas kernels: 28.4 us -> 28.2 us  [kernel_call(): pl.pallas_call(whole, out_shape=tuple(outs), in_specs=[spec(a) for a in a...]
    unnamed x14 -> x24, local copies, waits for them, and re-layouts: 5.31 us -> 5.14 us
  transfers between devices with their start and end apart: 41 -> 41, of which waited for: 20 -> 16; matrix products, arithmetic and copies ran while one was open for 2% -> 1% of each run, Pallas kernels for 8% -> 8%
where the time goes in v5:
time: 107 us
  starting transfers between devices  48.7 us (46%)
  Pallas kernels  28.2 us (26%)
  waiting for transfers between devices  22.1 us (21%)
  local copies, waits for them, and re-layouts  5.84 us (5%)
  between operations  1.1 us (1%)
    pallas_call x17, Pallas kernels, kernel_call(): pl.pallas_call(whole, out_shape=tuple(outs), in_specs=[spec(a) for a in a...  28.2 us
    ppermute x26, starting transfers between devices, step(): lax.ppermute(values, 'xy', [(order[(p + offset) % count], order[p]) for p...  22.6 us
    ppermute x26, waiting for transfers between devices, step(): lax.ppermute(values, 'xy', [(order[(p + offset) % count], order[p]) for p...  8.28 us
    ppermute x2, starting transfers between devices, per_device(): lax.ppermute(noise, ('xy', 'gz'), [(p * halves + (j + rel) % halves, orde...  6.25 us
    ppermute x2, starting transfers between devices, core(): return lax.ppermute(v, 'xy', xy(lambda a: a ^ 1))  5.85 us
    unnamed x24, local copies, waits for them, and re-layouts  5.14 us
    ppermute x3, waiting for transfers between devices, square(): out.append(lax.ppermute(v, ('xy', 'gz'), pairs))  4.88 us
    ppermute x3, starting transfers between devices, gather(): lax.ppermute(v, 'xy', xy(lambda a, s=s: a ^ 4 * s))  3.61 us
  transfers between devices with their start and end apart: 41, of which 16 were waited for; matrix products, arithmetic and copies ran while one was open for 1% of the time, Pallas kernels for 8%

profile of v5, /device:TPU:5, one launch (start us, length us, event | category | flops | bytes accessed | tf_op | source)
XLA Modules:
  0.0 106.6 jit_solution(15236055643768881424)
XLA Ops:
  0.6 2.8 %collective-permute-start.1 = (f32[1,4,4,32]{3,2,1,0:T(4,128)}, f32[1,4,4,32]{3,2,1,0:T(4,128)S(1)}, u32[]{:S(2)}, u32[]{:S(2)}) collective-permute-start(f32[1,4,4,32]{3,2,1,0:T(4,128)} %param.13), channel_id=1, source_target_pairs={{1,0},{0,1},{3,2},{2,3},{5,10},{4,11},{7,8},{6,9},{9,16},{8,17},{1... | collective-permute-start | bytes 6152 | tf_op jit(solution)/shard_map/ppermute | solution.py:827
  3.4 3.5 %collective-permute-start = (f32[1,4,4,32]{3,2,1,0:T(4,128)}, f32[1,4,4,32]{3,2,1,0:T(4,128)S(1)}, u32[]{:S(2)}, u32[]{:S(2)}) collective-permute-start(f32[1,4,4,32]{3,2,1,0:T(4,128)} %param.13), channel_id=1, source_target_pairs={{0,0},{1,1},{2,2},{3,3},{4,10},{5,11},{6,8},{7,9},{8,16},{9,17},{1... | collective-permute-start | bytes 6152 | tf_op jit(solution)/shard_map/ppermute | solution.py:827
  8.3 1.6 %copy-done = bf16[2,81,64,64]{1,3,2,0:T(8,128)(2,1)S(1)} copy-done((bf16[2,81,64,64]{1,3,2,0:T(8,128)(2,1)S(1)}, bf16[2,81,64,64]{1,3,2,0:T(8,128)(2,1)}, u32[]{:S(2)}) %copy-start) | copy-done | bytes 1327128
  13.4 1.7 %shard_map.196 = (bf16[576,576]{1,0:T(8,128)(2,1)S(1)}, bf16[64,1280]{1,0:T(8,128)(2,1)S(1)}, bf16[3,216,64]{2,1,0:T(8,128)(2,1)S(1)}, f32[128,8]{1,0:T(8,128)S(1)}) custom-call(bf16[2,64,64,81]{3,2,1,0:T(8,128)(2,1)S(1)} %bitcast.19, bf16[2,64,81]{2,1,0:T(8,128)(2,1)S(1)} %bitcast.24, bf16[2,2,64,81]{3,2,1,0:T(8,128)(2,1)S(1)} %bitcast.21, ...), custom_call_target="tpu_custom_call" | custom-call | flops 1000000000 | bytes 4000000 | tf_op jit(solution)/shard_map/pallas_call | solution.py:679
  15.4 1.8 %collective-permute-start.6 = (f32[1,1024]{1,0:T(1,128)S(1)}, f32[1,1024]{1,0:T(1,128)S(1)}, u32[]{:S(2)}, u32[]{:S(2)}) collective-permute-start(f32[1,1024]{1,0:T(1,128)S(1)} %shard_map.197.refs_3_), channel_id=1, source_target_pairs={{10,0},{8,2},{16,10},{18,8},{26,16},{24,18},{28,26},{30,24},{22,28... | collective-permute-start | bytes 12296 | tf_op jit(solution)/shard_map/ppermute | solution.py:822
  21.7 1.7 %collective-permute-done.2.refs_0_ = f32[1,1024]{1,0:T(1,128)S(1)} collective-permute-done((f32[1,1024]{1,0:T(1,128)S(1)}, f32[1,1024]{1,0:T(1,128)S(1)}, u32[]{:S(2)}, u32[]{:S(2)}) %collective-permute-start.2) | collective-permute-done | bytes 4128 | tf_op jit(solution)/shard_map/ppermute | solution.py:822
  23.3 5.0 %shard_map.198 = (f32[8,1024]{1,0:T(8,128)S(1)}, f32[2,1024]{1,0:T(2,128)S(1)}, f32[1,1024]{1,0:T(1,128)}, f32[1,128]{1,0:T(1,128)S(1)}, bf16[192,1024]{1,0:T(8,128)(2,1)S(1)}, /*index=5*/bf16[192,1024]{1,0:T(8,128)(2,1)S(1)}) custom-call(f32[1,1024]{1,0:T(1,128)S(1)} %collective-permute-done.2.refs_0_, f32[1,1024]{1,0:T(1,128)S(1)} %collective-permute-done.3.refs_1_, ...), custom_call_target="tpu_custom_call" | custom-call | flops 2038431744 | bytes 4000000 | tf_op jit(solution)/shard_map/pallas_call | solution.py:679
  28.4 2.2 %collective-permute-start.13 = (f32[2,1024]{1,0:T(2,128)S(1)}, f32[2,1024]{1,0:T(2,128)S(1)}, u32[]{:S(2)}, u32[]{:S(2)}) collective-permute-start(f32[2,1024]{1,0:T(2,128)S(1)} %get-tuple-element.68.refs_3_), channel_id=1, source_target_pairs={{8,0},{16,2},{18,10},{26,8},{24,16},{28,18},{30,26},{22,24},{20,28... | collective-permute-start | bytes 24584 | tf_op jit(solution)/shard_map/ppermute | solution.py:822
  33.8 1.7 %shard_map.199 = (bf16[576,576]{1,0:T(8,128)(2,1)S(1)}, bf16[64,1280]{1,0:T(8,128)(2,1)S(1)}, bf16[3,216,64]{2,1,0:T(8,128)(2,1)S(1)}, f32[128,8]{1,0:T(8,128)S(1)}) custom-call(bf16[2,64,64,81]{3,2,1,0:T(8,128)(2,1)S(1)} %bitcast.20, bf16[2,64,81]{2,1,0:T(8,128)(2,1)S(1)} %bitcast.25, bf16[2,2,64,81]{3,2,1,0:T(8,128)(2,1)S(1)} %bitcast.22, ...), custom_call_target="tpu_custom_call" | custom-call | flops 1000000000 | bytes 4000000 | tf_op jit(solution)/shard_map/pallas_call | solution.py:679
  35.6 1.4 %collective-permute-done.8.refs_0_ = f32[2,1024]{1,0:T(2,128)S(1)} collective-permute-done((f32[2,1024]{1,0:T(2,128)S(1)}, f32[2,1024]{1,0:T(2,128)S(1)}, u32[]{:S(2)}, u32[]{:S(2)}) %collective-permute-start.8) | collective-permute-done | bytes 8224 | tf_op jit(solution)/shard_map/ppermute | solution.py:822
  37.0 4.5 %shard_map.200 = (f32[8,1024]{1,0:T(8,128)S(1)}, f32[2,1024]{1,0:T(2,128)S(1)}, f32[1,1024]{1,0:T(1,128)S(1)}, f32[1,128]{1,0:T(1,128)S(1)}, f32[8,1024]{1,0:T(8...) custom-call(f32[2,1024]{1,0:T(2,128)S(1)} %collective-permute-done.8.refs_0_, ...), custom_call_target="tpu_custom_call" | custom-call | flops 2038431744 | bytes 4000000 | tf_op jit(solution)/shard_map/pallas_call | solution.py:679
  41.5 1.5 %collective-permute-start.19 = (f32[2,1024]{1,0:T(2,128)S(1)}, f32[2,1024]{1,0:T(2,128)S(1)}, u32[]{:S(2)}, u32[]{:S(2)}) collective-permute-start(f32[2,1024]{1,0:T(2,128)S(1)} %get-tuple-element.74.refs_3_), channel_id=1, source_target_pairs={{8,0},{16,2},{18,10},{26,8},{24,16},{28,18},{30,26},{22,24},{20,28... | collective-permute-start | bytes 24584 | tf_op jit(solution)/shard_map/ppermute | solution.py:822
  43.6 1.6 %collective-permute-start.15 = (f32[2,1024]{1,0:T(2,128)S(1)}, f32[2,1024]{1,0:T(2,128)S(1)}, u32[]{:S(2)}, u32[]{:S(2)}) collective-permute-start(f32[2,1024]{1,0:T(2,128)S(1)} %get-tuple-element.74.refs_3_), channel_id=1, source_target_pairs={{6,0},{4,2},{0,10},{2,8},{10,16},{8,18},{16,26},{18,24},{26,28},{2... | collective-permute-start | bytes 24584 | tf_op jit(solution)/shard_map/ppermute | solution.py:822
  45.2 1.7 %collective-permute-start.14 = (f32[2,1024]{1,0:T(2,128)S(1)}, f32[2,1024]{1,0:T(2,128)S(1)}, u32[]{:S(2)}, u32[]{:S(2)}) collective-permute-start(f32[2,1024]{1,0:T(2,128)S(1)} %get-tuple-element.74.refs_3_), channel_id=1, source_target_pairs={{14,0},{6,2},{4,10},{0,8},{2,16},{10,18},{8,26},{16,24},{18,28},{2... | collective-permute-start | bytes 24584 | tf_op jit(solution)/shard_map/ppermute | solution.py:822
  49.2 2.6 %shard_map.202 = (f32[8,1024]{1,0:T(8,128)S(1)}, f32[3,1024]{1,0:T(4,128)S(1)}, f32[16,64]{1,0:T(8,128)S(1)}, f32[16,1024]{1,0:T(8,128)S(1)}, bf16[192,1024]{1,0...) custom-call(f32[2,1024]{1,0:T(2,128)S(1)} %collective-permute-done.14.refs_0_, f32[2,1024]{1,0:T(2,128)S(1)} %collective-permute-done.15.refs_1_, ...), custom_call_target="tpu_custom_call" | custom-call | flops 679477248 | bytes 4000000 | tf_op jit(solution)/shard_map/pallas_call | solution.py:679
  51.8 1.5 %collective-permute-start.25 = (f32[3,1024]{1,0:T(4,128)S(1)}, f32[3,1024]{1,0:T(4,128)S(1)}, u32[]{:S(2)}, u32[]{:S(2)}) collective-permute-start(f32[3,1024]{1,0:T(4,128)S(1)} %get-tuple-element.82.refs_3_), channel_id=1, source_target_pairs={{8,0},{16,2},{18,10},{26,8},{24,16},{28,18},{30,26},{22,24},{20,28... | collective-permute-start | bytes 36872 | tf_op jit(solution)/shard_map/ppermute | solution.py:822
  54.2 1.4 %collective-permute-start.21 = (f32[3,1024]{1,0:T(4,128)S(1)}, f32[3,1024]{1,0:T(4,128)S(1)}, u32[]{:S(2)}, u32[]{:S(2)}) collective-permute-start(f32[3,1024]{1,0:T(4,128)S(1)} %get-tuple-element.82.refs_3_), channel_id=1, source_target_pairs={{6,0},{4,2},{0,10},{2,8},{10,16},{8,18},{16,26},{18,24},{26,28},{2... | collective-permute-start | bytes 36872 | tf_op jit(solution)/shard_map/ppermute | solution.py:822
  55.6 1.5 %collective-permute-start.20 = (f32[3,1024]{1,0:T(4,128)S(1)}, f32[3,1024]{1,0:T(4,128)S(1)}, u32[]{:S(2)}, u32[]{:S(2)}) collective-permute-start(f32[3,1024]{1,0:T(4,128)S(1)} %get-tuple-element.82.refs_3_), channel_id=1, source_target_pairs={{14,0},{6,2},{4,10},{0,8},{2,16},{10,18},{8,26},{16,24},{18,28},{2... | collective-permute-start | bytes 36872 | tf_op jit(solution)/shard_map/ppermute | solution.py:822
  57.1 2.1 %shard_map.203.refs_11_ = bf16[3072,128]{1,0:T(8,128)(2,1)S(1)} custom-call(f32[8,1024]{1,0:T(8,128)S(1)} %get-tuple-element.76.refs_9_.refs_0_, bf16[192,1024]{1,0:T(8,128)(2,1)S(1)} %get-tuple-element.77.refs_10_.refs_1_, bf16[192,1024]{1,0:T(8,128)(2,1)S(1)} %get-tuple-element.78.refs_11_.refs_2_, f32[16,1024]{1,0:T(8,128)S(1)} %get-tuple-element.87.refs_3_, ...), custom_call_target="tpu_custom_call" | custom-call | flops 679477248 | bytes 4000000 | tf_op jit(solution)/shard_map/pallas_call | solution.py:679
  59.7 4.1 %shard_map.204 = (f32[1,1024]{1,0:T(1,128)S(1)}, f32[2,1024]{1,0:T(2,128)S(1)}, f32[1,1024]{1,0:T(1,128)S(1)}, bf16[1536,128]{1,0:T(8,128)(2,1)S(1)}, bf16[1536,128]{1,0:T(8,128)(2,1)S(1)}) custom-call(f32[3,1024]{1,0:T(4,128)S(1)} %collective-permute-done.20.refs_0_, f32[3,1024]{1,0:T(4,128)S(1)} %collective-permute-done.21.refs_1_, ...), custom_call_target="tpu_custom_call" | custom-call | flops 1358954496 | bytes 4000000 | tf_op jit(solution)/shard_map/pallas_call | solution.py:679
  68.0 2.0 %collective-permute-done.29.refs_2_ = f32[1,1024]{1,0:T(1,128)S(1)} collective-permute-done((f32[1,1024]{1,0:T(1,128)S(1)}, f32[1,1024]{1,0:T(1,128)S(1)}, u32[]{:S(2)}, u32[]{:S(2)}) %collective-permute-start.29) | collective-permute-done | bytes 4128 | tf_op jit(solution)/shard_map/ppermute | solution.py:822
  70.0 2.0 %collective-permute-done.27.refs_1_ = bf16[768,128]{1,0:T(8,128)(2,1)S(1)} collective-permute-done((bf16[768,128]{1,0:T(8,128)(2,1)S(1)}, bf16[768,128]{1,0:T(8,128)(2,1)S(1)}, u32[]{:S(2)}, u32[]{:S(2)}) %collective-permute-start.27) | collective-permute-done | bytes 196640 | tf_op jit(solution)/shard_map/ppermute | solution.py:784
  73.7 2.1 %collective-permute-start.32 = (bf16[192,128]{1,0:T(8,128)(2,1)S(1)}, bf16[192,128]{1,0:T(8,128)(2,1)S(1)}, u32[]{:S(2)}, u32[]{:S(2)}) collective-permute-start(bf16[192,128]{1,0:T(8,128)(2,1)S(1)} %get-tuple-element.106), channel_id=1, source_target_pairs={{24,0},{26,2},{28,4},{30,6},{16,8},{18,10},{20,12},{22,14},{8,16},... | collective-permute-start | bytes 147464 | tf_op jit(solution)/shard_map/ppermute | solution.py:787
  76.7 1.7 %collective-permute-done.32.refs_3_ = bf16[192,128]{1,0:T(8,128)(2,1)S(1)} collective-permute-done((bf16[192,128]{1,0:T(8,128)(2,1)S(1)}, bf16[192,128]{1,0:T(8,128)(2,1)S(1)}, u32[]{:S(2)}, u32[]{:S(2)}) %collective-permute-start.32) | collective-permute-done | bytes 49184 | tf_op jit(solution)/shard_map/ppermute | solution.py:787
  78.5 2.6 %collective-permute-start.35 = (bf16[192,128]{1,0:T(8,128)(2,1)S(1)}, bf16[192,128]{1,0:T(8,128)(2,1)S(1)}, u32[]{:S(2)}, u32[]{:S(2)}) collective-permute-start(bf16[192,128]{1,0:T(8,128)(2,1)S(1)} %shard_map.208.refs_0_), channel_id=1, source_target_pairs={{24,0},{26,2},{28,4},{30,6},{16,8},{18,10},{20,12},{22,14},{8,16},... | collective-permute-start | bytes 147464 | tf_op jit(solution)/shard_map/ppermute | solution.py:790
  83.3 1.6 %collective-permute-done.34.refs_2_ = bf16[192,128]{1,0:T(8,128)(2,1)S(1)} collective-permute-done((bf16[192,128]{1,0:T(8,128)(2,1)S(1)}, bf16[192,128]{1,0:T(8,128)(2,1)S(1)}, u32[]{:S(2)}, u32[]{:S(2)}) %collective-permute-start.34) | collective-permute-done | bytes 49184 | tf_op jit(solution)/shard_map/ppermute | solution.py:790
  87.6 2.8 %collective-permute-done.38.refs_3_ = bf16[768,128]{1,0:T(8,128)(2,1)S(1)} collective-permute-done((bf16[768,128]{1,0:T(8,128)(2,1)S(1)}, bf16[768,128]{1,0:T(8,128)(2,1)S(1)}, u32[]{:S(2)}, u32[]{:S(2)}) %collective-permute-start.38) | collective-permute-done | bytes 196640 | tf_op jit(solution)/shard_map/ppermute | solution.py:802
  90.5 2.0 %collective-permute-done.37.refs_2_ = bf16[768,128]{1,0:T(8,128)(2,1)S(1)} collective-permute-done((bf16[768,128]{1,0:T(8,128)(2,1)S(1)}, bf16[768,128]{1,0:T(8,128)(2,1)S(1)}, u32[]{:S(2)}, u32[]{:S(2)}) %collective-permute-start.37) | collective-permute-done | bytes 196640 | tf_op jit(solution)/shard_map/ppermute | solution.py:802
  92.6 5.3 %collective-permute-start.39 = (bf16[3072,128]{1,0:T(8,128)(2,1)S(1)}, bf16[3072,128]{1,0:T(8,128)(2,1)S(1)}, u32[]{:S(2)}, u32[]{:S(2)}) collective-permute-start(bf16[3072,128]{1,0:T(8,128)(2,1)S(1)} %shard_map.210.refs_0_), channel_id=1, source_target_pairs={{2,0},{0,2},{6,4},{4,6},{10,8},{8,10},{14,12},{12,14},{18,16},{16,... | collective-permute-start | bytes 2359304 | tf_op jit(solution)/shard_map/ppermute | solution.py:781
  97.8 3.6 %collective-permute-start.40 = (f32[2,512]{1,0:T(2,128)S(1)}, f32[2,512]{1,0:T(2,128)S(1)}, u32[]{:S(2)}, u32[]{:S(2)}) collective-permute-start(f32[2,512]{1,0:T(2,128)S(1)} %shard_map.206.refs_2_), channel_id=1, source_target_pairs={{0,0},{2,2},{10,4},{8,6},{16,8},{18,10},{26,12},{24,14},{28,16},{3... | collective-permute-start | bytes 12296 | tf_op jit(solution)/shard_map/ppermute | solution.py:931
  101.4 2.2 %shard_map.211 = (f32[2,64,64,81]{3,2,1,0:T(8,128)}, f32[2,2,64,81]{3,2,1,0:T(8,128)}, f32[2,64,81]{2,1,0:T(8,128)}) custom-call(bf16[3072,128]{1,0:T(8,128)(2,1)S(1)} %shard_map.210.refs_0_), custom_call_target="tpu_custom_call" | custom-call | flops 1000000000 | bytes 4000000 | tf_op jit(solution)/shard_map/pallas_call | solution.py:679
  103.6 2.8 %shard_map.212 = (f32[2,64]{1,0:T(2,128)}, f32[2,64]{1,0:T(2,128)}, f32[2,2]{1,0:T(2,128)}, f32[1,1]{1,0:T(1,128)}, f32[1,4,4,32]{3,2,1,0:T(4,128)}, /*index=5*/...) custom-call(bf16[3072,128]{1,0:T(8,128)(2,1)S(1)} %collective-permut, ...), custom_call_target="tpu_custom_call", output_to_operand_aliasing={{6}: (2, {}), {7}: (3, {}), {8}: (4, {})} | custom-call | flops 1000000000 | bytes 4000000 | tf_op jit(solution)/shard_map/pallas_call | solution.py:679
  (95 shorter events, 29.1 us)
Async XLA Ops:
  0.6 14.4 %collective-permute-start.1 = (f32[1,4,4,32]{3,2,1,0:T(4,128)}, f32[1,4,4,32]{3,2,1,0:T(4,128)S(1)}, u32[]{:S(2)}, u32[]{:S(2)}) collective-permute-start(f32[1,4,4,32]{3,2,1,0:T(4,128)} %param.13), channel_id=1, source_target_pairs={{1,0},{0,1},{3,2},{2,3},{5,10},{4,11},{7,8},{6,9},{9,16},{8,17},{1... | collective-permute-start | bytes 6152 | tf_op jit(solution)/shard_map/ppermute | solution.py:827
  3.4 11.7 %collective-permute-start = (f32[1,4,4,32]{3,2,1,0:T(4,128)}, f32[1,4,4,32]{3,2,1,0:T(4,128)S(1)}, u32[]{:S(2)}, u32[]{:S(2)}) collective-permute-start(f32[1,4,4,32]{3,2,1,0:T(4,128)} %param.13), channel_id=1, source_target_pairs={{0,0},{1,1},{2,2},{3,3},{4,10},{5,11},{6,8},{7,9},{8,16},{9,17},{1... | collective-permute-start | bytes 6152 | tf_op jit(solution)/shard_map/ppermute | solution.py:827
  15.2 4.2 %collective-permute-start.7 = (f32[1,1024]{1,0:T(1,128)S(1)}, f32[1,1024]{1,0:T(1,128)S(1)}, u32[]{:S(2)}, u32[]{:S(2)}) collective-permute-start(f32[1,1024]{1,0:T(1,128)S(1)} %shard_map.197.refs_3_), channel_id=1, source_target_pairs={{8,0},{16,2},{18,10},{26,8},{24,16},{28,18},{30,26},{22,24},{20,28... | collective-permute-start | bytes 12296 | tf_op jit(solution)/shard_map/ppermute | solution.py:822
  15.4 5.2 %collective-permute-start.6 = (f32[1,1024]{1,0:T(1,128)S(1)}, f32[1,1024]{1,0:T(1,128)S(1)}, u32[]{:S(2)}, u32[]{:S(2)}) collective-permute-start(f32[1,1024]{1,0:T(1,128)S(1)} %shard_map.197.refs_3_), channel_id=1, source_target_pairs={{10,0},{8,2},{16,10},{18,8},{26,16},{24,18},{28,26},{30,24},{22,28... | collective-permute-start | bytes 12296 | tf_op jit(solution)/shard_map/ppermute | solution.py:822
  19.4 3.9 %collective-permute-start.2 = (f32[1,1024]{1,0:T(1,128)S(1)}, f32[1,1024]{1,0:T(1,128)S(1)}, u32[]{:S(2)}, u32[]{:S(2)}) collective-permute-start(f32[1,1024]{1,0:T(1,128)S(1)} %shard_map.197.refs_3_), channel_id=1, source_target_pairs={{14,0},{6,2},{4,10},{0,8},{2,16},{10,18},{8,26},{16,24},{18,28},{2... | collective-permute-start | bytes 12296 | tf_op jit(solution)/shard_map/ppermute | solution.py:822
  28.4 4.5 %collective-permute-start.13 = (f32[2,1024]{1,0:T(2,128)S(1)}, f32[2,1024]{1,0:T(2,128)S(1)}, u32[]{:S(2)}, u32[]{:S(2)}) collective-permute-start(f32[2,1024]{1,0:T(2,128)S(1)} %get-tuple-element.68.refs_3_), channel_id=1, source_target_pairs={{8,0},{16,2},{18,10},{26,8},{24,16},{28,18},{30,26},{22,24},{20,28... | collective-permute-start | bytes 24584 | tf_op jit(solution)/shard_map/ppermute | solution.py:822
  30.5 5.0 %collective-permute-start.12 = (f32[2,1024]{1,0:T(2,128)S(1)}, f32[2,1024]{1,0:T(2,128)S(1)}, u32[]{:S(2)}, u32[]{:S(2)}) collective-permute-start(f32[2,1024]{1,0:T(2,128)S(1)} %get-tuple-element.68.refs_3_), channel_id=1, source_target_pairs={{10,0},{8,2},{16,10},{18,8},{26,16},{24,18},{28,26},{30,24},{22,28... | collective-permute-start | bytes 24584 | tf_op jit(solution)/shard_map/ppermute | solution.py:822
  31.1 4.5 %collective-permute-start.11 = (f32[2,1024]{1,0:T(2,128)S(1)}, f32[2,1024]{1,0:T(2,128)S(1)}, u32[]{:S(2)}, u32[]{:S(2)}) collective-permute-start(f32[2,1024]{1,0:T(2,128)S(1)} %get-tuple-element.68.refs_3_), channel_id=1, source_target_pairs={{2,0},{10,2},{8,10},{16,8},{18,16},{26,18},{24,26},{28,24},{30,28}... | collective-permute-start | bytes 24584 | tf_op jit(solution)/shard_map/ppermute | solution.py:822
  31.2 4.3 %collective-permute-start.10 = (f32[2,1024]{1,0:T(2,128)S(1)}, f32[2,1024]{1,0:T(2,128)S(1)}, u32[]{:S(2)}, u32[]{:S(2)}) collective-permute-start(f32[2,1024]{1,0:T(2,128)S(1)} %get-tuple-element.68.refs_3_), channel_id=1, source_target_pairs={{4,0},{0,2},{2,10},{10,8},{8,16},{16,18},{18,26},{26,24},{24,28},{... | collective-permute-start | bytes 24584 | tf_op jit(solution)/shard_map/ppermute | solution.py:822
  31.6 4.0 %collective-permute-start.9 = (f32[2,1024]{1,0:T(2,128)S(1)}, f32[2,1024]{1,0:T(2,128)S(1)}, u32[]{:S(2)}, u32[]{:S(2)}) collective-permute-start(f32[2,1024]{1,0:T(2,128)S(1)} %get-tuple-element.68.refs_3_), channel_id=1, source_target_pairs={{6,0},{4,2},{0,10},{2,8},{10,16},{8,18},{16,26},{18,24},{26,28},{2... | collective-permute-start | bytes 24584 | tf_op jit(solution)/shard_map/ppermute | solution.py:822
  32.9 4.1 %collective-permute-start.8 = (f32[2,1024]{1,0:T(2,128)S(1)}, f32[2,1024]{1,0:T(2,128)S(1)}, u32[]{:S(2)}, u32[]{:S(2)}) collective-permute-start(f32[2,1024]{1,0:T(2,128)S(1)} %get-tuple-element.68.refs_3_), channel_id=1, source_target_pairs={{14,0},{6,2},{4,10},{0,8},{2,16},{10,18},{8,26},{16,24},{18,28},{2... | collective-permute-start | bytes 24584 | tf_op jit(solution)/shard_map/ppermute | solution.py:822
  43.0 5.3 %collective-permute-start.18 = (f32[2,1024]{1,0:T(2,128)S(1)}, f32[2,1024]{1,0:T(2,128)S(1)}, u32[]{:S(2)}, u32[]{:S(2)}) collective-permute-start(f32[2,1024]{1,0:T(2,128)S(1)} %get-tuple-element.74.refs_3_), channel_id=1, source_target_pairs={{10,0},{8,2},{16,10},{18,8},{26,16},{24,18},{28,26},{30,24},{22,28... | collective-permute-start | bytes 24584 | tf_op jit(solution)/shard_map/ppermute | solution.py:822
  43.0 5.2 %collective-permute-start.17 = (f32[2,1024]{1,0:T(2,128)S(1)}, f32[2,1024]{1,0:T(2,128)S(1)}, u32[]{:S(2)}, u32[]{:S(2)}) collective-permute-start(f32[2,1024]{1,0:T(2,128)S(1)} %get-tuple-element.74.refs_3_), channel_id=1, source_target_pairs={{2,0},{10,2},{8,10},{16,8},{18,16},{26,18},{24,26},{28,24},{30,28}... | collective-permute-start | bytes 24584 | tf_op jit(solution)/shard_map/ppermute | solution.py:822
  43.6 4.7 %collective-permute-start.16 = (f32[2,1024]{1,0:T(2,128)S(1)}, f32[2,1024]{1,0:T(2,128)S(1)}, u32[]{:S(2)}, u32[]{:S(2)}) collective-permute-start(f32[2,1024]{1,0:T(2,128)S(1)} %get-tuple-element.74.refs_3_), channel_id=1, source_target_pairs={{4,0},{0,2},{2,10},{10,8},{8,16},{16,18},{18,26},{26,24},{24,28},{... | collective-permute-start | bytes 24584 | tf_op jit(solution)/shard_map/ppermute | solution.py:822
  43.6 4.7 %collective-permute-start.15 = (f32[2,1024]{1,0:T(2,128)S(1)}, f32[2,1024]{1,0:T(2,128)S(1)}, u32[]{:S(2)}, u32[]{:S(2)}) collective-permute-start(f32[2,1024]{1,0:T(2,128)S(1)} %get-tuple-element.74.refs_3_), channel_id=1, source_target_pairs={{6,0},{4,2},{0,10},{2,8},{10,16},{8,18},{16,26},{18,24},{26,28},{2... | collective-permute-start | bytes 24584 | tf_op jit(solution)/shard_map/ppermute | solution.py:822
  45.2 4.0 %collective-permute-start.14 = (f32[2,1024]{1,0:T(2,128)S(1)}, f32[2,1024]{1,0:T(2,128)S(1)}, u32[]{:S(2)}, u32[]{:S(2)}) collective-permute-start(f32[2,1024]{1,0:T(2,128)S(1)} %get-tuple-element.74.refs_3_), channel_id=1, source_target_pairs={{14,0},{6,2},{4,10},{0,8},{2,16},{10,18},{8,26},{16,24},{18,28},{2... | collective-permute-start | bytes 24584 | tf_op jit(solution)/shard_map/ppermute | solution.py:822
  53.3 5.9 %collective-permute-start.24 = (f32[3,1024]{1,0:T(4,128)S(1)}, f32[3,1024]{1,0:T(4,128)S(1)}, u32[]{:S(2)}, u32[]{:S(2)}) collective-permute-start(f32[3,1024]{1,0:T(4,128)S(1)} %get-tuple-element.82.refs_3_), channel_id=1, source_target_pairs={{10,0},{8,2},{16,10},{18,8},{26,16},{24,18},{28,26},{30,24},{22,28... | collective-permute-start | bytes 36872 | tf_op jit(solution)/shard_map/ppermute | solution.py:822
  53.5 5.7 %collective-permute-start.23 = (f32[3,1024]{1,0:T(4,128)S(1)}, f32[3,1024]{1,0:T(4,128)S(1)}, u32[]{:S(2)}, u32[]{:S(2)}) collective-permute-start(f32[3,1024]{1,0:T(4,128)S(1)} %get-tuple-element.82.refs_3_), channel_id=1, source_target_pairs={{2,0},{10,2},{8,10},{16,8},{18,16},{26,18},{24,26},{28,24},{30,28}... | collective-permute-start | bytes 36872 | tf_op jit(solution)/shard_map/ppermute | solution.py:822
  54.2 5.1 %collective-permute-start.22 = (f32[3,1024]{1,0:T(4,128)S(1)}, f32[3,1024]{1,0:T(4,128)S(1)}, u32[]{:S(2)}, u32[]{:S(2)}) collective-permute-start(f32[3,1024]{1,0:T(4,128)S(1)} %get-tuple-element.82.refs_3_), channel_id=1, source_target_pairs={{4,0},{0,2},{2,10},{10,8},{8,16},{16,18},{18,26},{26,24},{24,28},{... | collective-permute-start | bytes 36872 | tf_op jit(solution)/shard_map/ppermute | solution.py:822
  54.2 5.1 %collective-permute-start.21 = (f32[3,1024]{1,0:T(4,128)S(1)}, f32[3,1024]{1,0:T(4,128)S(1)}, u32[]{:S(2)}, u32[]{:S(2)}) collective-permute-start(f32[3,1024]{1,0:T(4,128)S(1)} %get-tuple-element.82.refs_3_), channel_id=1, source_target_pairs={{6,0},{4,2},{0,10},{2,8},{10,16},{8,18},{16,26},{18,24},{26,28},{2... | collective-permute-start | bytes 36872 | tf_op jit(solution)/shard_map/ppermute | solution.py:822
  55.6 4.1 %collective-permute-start.20 = (f32[3,1024]{1,0:T(4,128)S(1)}, f32[3,1024]{1,0:T(4,128)S(1)}, u32[]{:S(2)}, u32[]{:S(2)}) collective-permute-start(f32[3,1024]{1,0:T(4,128)S(1)} %get-tuple-element.82.refs_3_), channel_id=1, source_target_pairs={{14,0},{6,2},{4,10},{0,8},{2,16},{10,18},{8,26},{16,24},{18,28},{2... | collective-permute-start | bytes 36872 | tf_op jit(solution)/shard_map/ppermute | solution.py:822
  65.9 6.2 %collective-permute-start.27 = (bf16[768,128]{1,0:T(8,128)(2,1)S(1)}, bf16[768,128]{1,0:T(8,128)(2,1)S(1)}, u32[]{:S(2)}, u32[]{:S(2)}) collective-permute-start(bf16[768,128]{1,0:T(8,128)(2,1)S(1)} %get-tuple-element.99), channel_id=1, source_target_pairs={{4,0},{6,2},{0,4},{2,6},{12,8},{14,10},{8,12},{10,14},{20,16},{22,... | collective-permute-start | bytes 589832 | tf_op jit(solution)/shard_map/ppermute | solution.py:784
  72.9 3.9 %collective-permute-start.31 = (bf16[192,128]{1,0:T(8,128)(2,1)S(1)}, bf16[192,128]{1,0:T(8,128)(2,1)S(1)}, u32[]{:S(2)}, u32[]{:S(2)}) collective-permute-start(bf16[192,128]{1,0:T(8,128)(2,1)S(1)} %get-tuple-element.105), channel_id=1, source_target_pairs={{16,0},{18,2},{20,4},{22,6},{24,8},{26,10},{28,12},{30,14},{0,16},... | collective-permute-start | bytes 147464 | tf_op jit(solution)/shard_map/ppermute | solution.py:787
  73.7 4.8 %collective-permute-start.32 = (bf16[192,128]{1,0:T(8,128)(2,1)S(1)}, bf16[192,128]{1,0:T(8,128)(2,1)S(1)}, u32[]{:S(2)}, u32[]{:S(2)}) collective-permute-start(bf16[192,128]{1,0:T(8,128)(2,1)S(1)} %get-tuple-element.106), channel_id=1, source_target_pairs={{24,0},{26,2},{28,4},{30,6},{16,8},{18,10},{20,12},{22,14},{8,16},... | collective-permute-start | bytes 147464 | tf_op jit(solution)/shard_map/ppermute | solution.py:787
  78.5 4.8 %collective-permute-start.35 = (bf16[192,128]{1,0:T(8,128)(2,1)S(1)}, bf16[192,128]{1,0:T(8,128)(2,1)S(1)}, u32[]{:S(2)}, u32[]{:S(2)}) collective-permute-start(bf16[192,128]{1,0:T(8,128)(2,1)S(1)} %shard_map.208.refs_0_), channel_id=1, source_target_pairs={{24,0},{26,2},{28,4},{30,6},{16,8},{18,10},{20,12},{22,14},{8,16},... | collective-permute-start | bytes 147464 | tf_op jit(solution)/shard_map/ppermute | solution.py:790
  81.0 3.8 %collective-permute-start.34 = (bf16[192,128]{1,0:T(8,128)(2,1)S(1)}, bf16[192,128]{1,0:T(8,128)(2,1)S(1)}, u32[]{:S(2)}, u32[]{:S(2)}) collective-permute-start(bf16[192,128]{1,0:T(8,128)(2,1)S(1)} %shard_map.208.refs_0_), channel_id=1, source_target_pairs={{16,0},{18,2},{20,4},{22,6},{24,8},{26,10},{28,12},{30,14},{0,16},... | collective-permute-start | bytes 147464 | tf_op jit(solution)/shard_map/ppermute | solution.py:790
  81.1 3.8 %collective-permute-start.33 = (bf16[192,128]{1,0:T(8,128)(2,1)S(1)}, bf16[192,128]{1,0:T(8,128)(2,1)S(1)}, u32[]{:S(2)}, u32[]{:S(2)}) collective-permute-start(bf16[192,128]{1,0:T(8,128)(2,1)S(1)} %shard_map.208.refs_0_), channel_id=1, source_target_pairs={{8,0},{10,2},{12,4},{14,6},{0,8},{2,10},{4,12},{6,14},{24,16},{26,... | collective-permute-start | bytes 147464 | tf_op jit(solution)/shard_map/ppermute | solution.py:790
  84.9 5.6 %collective-permute-start.38 = (bf16[768,128]{1,0:T(8,128)(2,1)S(1)}, bf16[768,128]{1,0:T(8,128)(2,1)S(1)}, u32[]{:S(2)}, u32[]{:S(2)}) collective-permute-start(bf16[768,128]{1,0:T(8,128)(2,1)S(1)} %shard_map.209.refs_0_), channel_id=1, source_target_pairs={{5,0},{4,1},{7,2},{6,3},{1,4},{0,5},{3,6},{2,7},{13,8},{12,9},{15,... | collective-permute-start | bytes 589832 | tf_op jit(solution)/shard_map/ppermute | solution.py:802
  86.1 6.4 %collective-permute-start.37 = (bf16[768,128]{1,0:T(8,128)(2,1)S(1)}, bf16[768,128]{1,0:T(8,128)(2,1)S(1)}, u32[]{:S(2)}, u32[]{:S(2)}) collective-permute-start(bf16[768,128]{1,0:T(8,128)(2,1)S(1)} %shard_map.209.refs_0_), channel_id=1, source_target_pairs={{1,0},{0,1},{3,2},{2,3},{5,4},{4,5},{7,6},{6,7},{9,8},{8,9},{11,10... | collective-permute-start | bytes 589832 | tf_op jit(solution)/shard_map/ppermute | solution.py:802
  87.3 5.2 %collective-permute-start.36 = (bf16[768,128]{1,0:T(8,128)(2,1)S(1)}, bf16[768,128]{1,0:T(8,128)(2,1)S(1)}, u32[]{:S(2)}, u32[]{:S(2)}) collective-permute-start(bf16[768,128]{1,0:T(8,128)(2,1)S(1)} %shard_map.209.refs_0_), channel_id=1, source_target_pairs={{4,0},{5,1},{6,2},{7,3},{0,4},{1,5},{2,6},{3,7},{12,8},{13,9},{14,... | collective-permute-start | bytes 589832 | tf_op jit(solution)/shard_map/ppermute | solution.py:802
  92.6 11.1 %collective-permute-start.39 = (bf16[3072,128]{1,0:T(8,128)(2,1)S(1)}, bf16[3072,128]{1,0:T(8,128)(2,1)S(1)}, u32[]{:S(2)}, u32[]{:S(2)}) collective-permute-start(bf16[3072,128]{1,0:T(8,128)(2,1)S(1)} %shard_map.210.refs_0_), channel_id=1, source_target_pairs={{2,0},{0,2},{6,4},{4,6},{10,8},{8,10},{14,12},{12,14},{18,16},{16,... | collective-permute-start | bytes 2359304 | tf_op jit(solution)/shard_map/ppermute | solution.py:781
  97.8 5.8 %collective-permute-start.40 = (f32[2,512]{1,0:T(2,128)S(1)}, f32[2,512]{1,0:T(2,128)S(1)}, u32[]{:S(2)}, u32[]{:S(2)}) collective-permute-start(f32[2,512]{1,0:T(2,128)S(1)} %shard_map.206.refs_2_), channel_id=1, source_target_pairs={{0,0},{2,2},{10,4},{8,6},{16,8},{18,10},{26,12},{24,14},{28,16},{3... | collective-permute-start | bytes 12296 | tf_op jit(solution)/shard_map/ppermute | solution.py:931
  (21 other events, 128.4 us)

commit v6 on v5

--- a/solution.py
+++ b/solution.py
@@ -18,6 +18,7 @@
 F32 = jnp.float32
 TAPS = 81
 VMEM_MB = 20
+CHUNK = 512
 
 
 def ring_order(count):
@@ -30,24 +31,6 @@
         cores = (0, 1) if place % 2 == 0 else (1, 0)
         order += [z * 4 + y * 2 + core for core in cores]
     return order
-
-
-def spread_first():
-    out = np.zeros((81, 5, 256), np.float32)
-    for tap in range(81):
-        dx, rest = divmod(tap, 27)
-        for dest in range(5):
-            out[tap, dest, rest * ROWS + dest + dx] = 1
-    return out.reshape(81, 5 * 256)
-
-
-def spread_last():
-    out = np.zeros((3, 2, 216, 81), np.float32)
-    for tap in range(81):
-        dx, rest = divmod(tap, 27)
-        for o in range(2):
-            out[dx, o, rest * 8 + o, tap] = 1
-    return out
 
 
 def spread_last_back():
@@ -177,8 +160,8 @@
     return (row == lax.broadcasted_iota(jnp.int32, (n, n), 1)).astype(F32).astype(BF)
 
 
-def pack_ahead_kernel(layer, ready, w_mid, w_first, w_last, biases, lanes, spread_rows, *refs):
-    matrix, first, narrow, columns, taps, rows = refs[-6:]
+def pack_ahead_kernel(layer, ready, w_mid, *refs):
+    matrix, taps = refs[-2:]
     channels = w_mid.shape[1]
     few = channels // 2
     for o in range(few):
@@ -199,15 +182,30 @@
                 matrix[at, wide] = jnp.concatenate([low, high], axis=1).astype(BF)
             else:
                 matrix[at, outer * channels :] = low.astype(BF)
-    first[...] = dot(w_first[layer], lanes[...]).astype(BF)
+
+
+def pack_narrow_kernel(ready, w_first, w_last, biases, *refs):
+    outs, rows = refs[-7:-1], refs[-1]
+    channels = w_first.shape[1]
+    tap = lax.broadcasted_iota(jnp.int32, (TAPS, 256), 0)
+    column = lax.broadcasted_iota(jnp.int32, (TAPS, 256), 1)
+    for dest in range(5):
+        dx = column % ROWS - dest
+        hit = jnp.logical_and(tap == dx * 27 + column // ROWS, jnp.logical_and(dx >= 0, dx <= 2))
+        hit = jnp.logical_and(hit, column < 27 * ROWS).astype(F32).astype(BF)
+        for layer in range(2):
+            outs[3 * layer][:, dest * 256 : (dest + 1) * 256] = dot(w_first[layer], hit).astype(BF)
+    row = lax.broadcasted_iota(jnp.int32, (216, TAPS), 0)
+    tap = lax.broadcasted_iota(jnp.int32, (216, TAPS), 1)
     for dx in range(3):
-        narrow[dx] = sum(
-            dot_nt(spread_rows[(dx * 2 + o) * 216 : (dx * 2 + o + 1) * 216, :TAPS], w_last[layer, o])
-            for o in range(2)
-        ).astype(BF)
-    rows[...] = jnp.zeros_like(rows)
-    rows[0:3, :channels] = biases[3 * layer : 3 * layer + 3, :]
-    columns[...] = rows[...].T
+        hit = tap == dx * 27 + row // 8
+        hits = [jnp.logical_and(hit, row % 8 == o).astype(F32).astype(BF) for o in range(2)]
+        for layer in range(2):
+            outs[3 * layer + 1][dx] = sum(dot_nt(hits[o], w_last[layer, o]) for o in range(2)).astype(BF)
+    for layer in range(2):
+        rows[...] = jnp.zeros_like(rows)
+        rows[0:3, :channels] = biases[3 * layer : 3 * layer + 3, :]
+        outs[3 * layer + 2][...] = rows[...].T
 
 
 def pack_back_kernel(ready, matrix_zero, matrix_one, w_first, w_last, lanes, spread_rows, *refs):
@@ -320,12 +318,7 @@
     if layer == 0:
         (coords, w_first, w_mid, w_last, columns,
          field_out, state, own_out, logdet, first_out, second_out, first, stack) = refs
-        field_out[...] = jnp.zeros_like(field_out)
-        piece = field_out.shape[1] // halves
-        for rel in range(halves):
-            to = pl.multiple_of(lax.rem(coords[1] + rel, halves) * piece, 128)
-            for r, ref in enumerate(windows):
-                field_out[r : r + 1, pl.ds(to, piece)] = ref[:, rel * piece : (rel + 1) * piece]
+        place_windows(windows, 0, field_out)
     else:
         (coords, w_first, w_mid, w_last, columns,
          field_out, state, own_out, logdet, growth_out, first_out, second_out,
@@ -349,10 +342,10 @@
     ready(w_mid)
     for dest in range(3):
         stack_planes(stack, first, channels, lambda dx, dz: (dest + dx, dz - 1))
-        for at in range(0, length, 256):
-            wide = dot(w_mid[...], stack[:, at : at + 256])
+        for at in range(0, length, CHUNK):
+            wide = dot(w_mid[...], stack[:, at : at + CHUNK])
             wide = gather_wide(wide, channels, 1, period)
-            second_out[dest * channels : (dest + 1) * channels, at : at + 256] = jnp.tanh(
+            second_out[dest * channels : (dest + 1) * channels, at : at + CHUNK] = jnp.tanh(
                 wide + bias_mid
             ).astype(BF)
     ready(w_last)
@@ -411,11 +404,11 @@
 def first_gradient(period, mids, first, w_mid, stack, grad_first):
     channels = mids.shape[0] // 3
     stack_planes(stack, mids, channels, lambda dx, dz: (2 - dx, 1 - dz))
-    for at in range(0, stack.shape[1], 256):
-        wide = dot(w_mid[...], stack[:, at : at + 256])
+    for at in range(0, stack.shape[1], CHUNK):
+        wide = dot(w_mid[...], stack[:, at : at + CHUNK])
         wide = gather_wide(wide, channels, -1, period)
-        seen = first[channels : 2 * channels, at : at + 256].astype(F32)
-        grad_first[:, at : at + 256] = (wide * (1.0 - seen * seen)).astype(BF)
+        seen = first[channels : 2 * channels, at : at + CHUNK].astype(F32)
+        grad_first[:, at : at + CHUNK] = (wide * (1.0 - seen * seen)).astype(BF)
 
 
 def first_weights(period, net, grad_first, pick_f):
@@ -713,17 +706,22 @@
     return kernel_call(body, outs, scratch, args, flops)
 
 
-def pack_ahead(layer, params, picks, after=()):
+def pack_ahead(layer, w_mid, after=()):
+    channels = w_mid.shape[1]
+    outs = [shape((9 * channels, 9 * channels), BF)]
+    scratch = [pltpu.VMEM((TAPS * channels // 2, 2 * channels), F32)]
+    body = functools.partial(pack_ahead_kernel, layer)
+    return kernel_call(body, outs, scratch, [w_mid, *after], 1_000_000_000, loose=after)[0]
+
+
+def pack_narrow(params, after):
     channels = params[0].shape[1]
-    outs = [
-        shape((9 * channels, 9 * channels), BF),
-        shape((channels, 5 * 256), BF),
-        shape((3, 216, channels), BF),
-        shape((128, 8)),
-    ]
-    scratch = [pltpu.VMEM((TAPS * channels // 2, 2 * channels), F32), pltpu.VMEM((8, 128), F32)]
-    body = functools.partial(pack_ahead_kernel, layer)
-    return kernel_call(body, outs, scratch, [*params, *picks, *after], 1_000_000_000, loose=after)
+    outs = [shape((channels, 5 * 256), BF), shape((3, 216, channels), BF), shape((128, 8))]
+    scratch = [pltpu.VMEM((8, 128), F32)]
+    got = kernel_call(
+        pack_narrow_kernel, outs * 2, scratch, [*params, *after], 1_000_000_000, loose=after
+    )
+    return got[:3], got[3:]
 
 
 def pack_back(matrices, narrow, picks, after):
@@ -843,42 +841,42 @@
     ]
     back = spread_last_back()
     pad = ((0, 0), (0, 128 - TAPS))
-    picks = [
-        jnp.asarray(spread_first(), BF),
-        jnp.asarray(np.pad(spread_last().reshape(6 * 216, TAPS), pad), BF),
-    ]
     back_picks = [
         jnp.asarray(np.concatenate([back[0], back[1]], axis=1), BF),
         jnp.asarray(np.pad(spread_first_back(), pad), BF),
     ]
     pick_l, pick_f = jnp.asarray(pick_last(), BF), jnp.asarray(pick_first(), BF)
-    packed = [pack_ahead(0, params, picks)]
-
-    def join(ready, *refs):
+    matrices = [pack_ahead(0, params[0])]
+
+    def join(ready, here, *refs):
+        out, held = refs[-2:]
         rows = noise.shape[1] * noise.shape[2]
+        piece = rows * period
         for rel in range(halves):
             for k in range(rows):
-                at = (rel * rows + k) * period
                 y = k % noise.shape[2]
-                refs[-1][:, at : at + period] = refs[rel][0, k // noise.shape[2], y : y + 1, :]
-
-    waits = (packed[0][0],)
+                held[:, k * period : (k + 1) * period] = refs[rel][0, k // noise.shape[2], y : y + 1, :]
+            to = pl.multiple_of(lax.rem(here[1] + rel, halves) * piece, 128)
+            out[:, pl.ds(to, piece)] = held[...]
+
+    waits = (matrices[0],)
     (whole,) = kernel_call(
-        join, [shape((1, noise.size * halves))], [], [*whole, *waits], 1000, loose=waits, bytes_moved=1000
-    )
+        join, [shape((1, noise.size * halves))], [pltpu.VMEM((1, noise.size), F32)],
+        [HERE, *whole, *waits], 1000, loose=waits, bytes_moved=1000,
+    )
+    narrow = pack_narrow(params[1:], (whole,))
 
     def exchange(values):
         return [values if m == 0 else step(values, m) for m in range(-3, 4)]
 
-    order_weights = lambda p: (p[1], p[0], p[2], p[3])
     field0, state, _, logdet0, first0, second0 = forward(
-        period, 0, exchange(whole), coords, order_weights(packed[0]), channels, halves
-    )
-    packed.append(pack_ahead(1, params, picks, (logdet0,)))
+        period, 0, exchange(whole), coords, (narrow[0][0], matrices[0], *narrow[0][1:]), channels, halves
+    )
+    matrices.append(pack_ahead(1, params[0], (logdet0,)))
     field1, state, own, logdet1, growth0, first1, second1 = forward(
-        period, 1, exchange(state), coords, order_weights(packed[1]), channels, halves
-    )
-    back_weights = pack_back([p[0] for p in packed], params[1:3], back_picks, (logdet1,))
+        period, 1, exchange(state), coords, (narrow[1][0], matrices[1], *narrow[1][1:]), channels, halves
+    )
+    back_weights = pack_back(matrices, params[1:3], back_picks, (logdet1,))
     core, cross, scatter, gather, square = permuters(count, halves, depth)
     length = field0.shape[1]
     full = shape((ROWS, length))

time: 107 us -> 103 us (0.963)
  local copies, waits for them, and re-layouts: 5.84 us -> 2.33 us
    unnamed x24 -> x20, local copies, waits for them, and re-layouts: 5.14 us -> 1.64 us
    pallas_call x17 -> x18, Pallas kernels: 28.2 us -> 28.5 us  [kernel_call(): pl.pallas_call(whole, out_shape=tuple(outs), in_specs=[spec(a) for a in a...]
  transfers between devices with their start and end apart: 41 -> 41, of which waited for: 16 -> 17; matrix products, arithmetic and copies ran while one was open for 1% -> 1% of each run, Pallas kernels for 8% -> 9%
where the time goes in v6:
time: 103 us; the launch traced here: 102 us
  starting transfers between devices  48.8 us (47%)
  Pallas kernels  28.5 us (28%)
  waiting for transfers between devices  21.6 us (21%)
  local copies, waits for them, and re-layouts  2.33 us (2%)
  between operations  1.16 us (1%)
    pallas_call x18, Pallas kernels, kernel_call(): pl.pallas_call(whole, out_shape=tuple(outs), in_specs=[spec(a) for a in a...  28.5 us
    ppermute x26, starting transfers between devices, step(): lax.ppermute(values, 'xy', [(order[(p + offset) % count], order[p]) for p...  22.9 us
    ppermute x26, waiting for transfers between devices, step(): lax.ppermute(values, 'xy', [(order[(p + offset) % count], order[p]) for p...  7.56 us
    ppermute x2, starting transfers between devices, per_device(): lax.ppermute(noise, ('xy', 'gz'), [(p * halves + (j + rel) % halves, orde...  6.25 us
    ppermute x2, starting transfers between devices, core(): return lax.ppermute(v, 'xy', xy(lambda a: a ^ 1))  6 us
    ppermute x3, waiting for transfers between devices, square(): out.append(lax.ppermute(v, ('xy', 'gz'), pairs))  4.88 us
    ppermute x3, starting transfers between devices, gather(): lax.ppermute(v, 'xy', xy(lambda a, s=s: a ^ 4 * s))  3.61 us
    ppermute x3, starting transfers between devices, scatter(): lax.ppermute(pieces[s], 'xy', xy(lambda a, s=s: a ^ 4 * s))  3.61 us
  transfers between devices with their start and end apart: 41, of which 17 were waited for; matrix products, arithmetic and copies ran while one was open for 1% of the time, Pallas kernels for 9%

profile of v6, /device:TPU:5, one launch (start us, length us, event | category | flops | bytes accessed | tf_op | source)
XLA Modules:
  0.0 102.3 jit_solution(5695400032086203312)
XLA Ops:
  0.7 2.8 %collective-permute-start.1 = (f32[1,4,4,32]{3,2,1,0:T(4,128)}, f32[1,4,4,32]{3,2,1,0:T(4,128)S(1)}, u32[]{:S(2)}, u32[]{:S(2)}) collective-permute-start(f32[1,4,4,32]{3,2,1,0:T(4,128)} %param.11), channel_id=1, source_target_pairs={{1,0},{0,1},{3,2},{2,3},{5,10},{4,11},{7,8},{6,9},{9,16},{8,17},{1... | collective-permute-start | bytes 6152 | tf_op jit(solution)/shard_map/ppermute | solution.py:825
  3.4 3.5 %collective-permute-start = (f32[1,4,4,32]{3,2,1,0:T(4,128)}, f32[1,4,4,32]{3,2,1,0:T(4,128)S(1)}, u32[]{:S(2)}, u32[]{:S(2)}) collective-permute-start(f32[1,4,4,32]{3,2,1,0:T(4,128)} %param.11), channel_id=1, source_target_pairs={{0,0},{1,1},{2,2},{3,3},{4,10},{5,11},{6,8},{7,9},{8,16},{9,17},{1... | collective-permute-start | bytes 6152 | tf_op jit(solution)/shard_map/ppermute | solution.py:825
  7.6 1.6 %copy-done = bf16[2,81,64,64]{1,3,2,0:T(8,128)(2,1)S(1)} copy-done((bf16[2,81,64,64]{1,3,2,0:T(8,128)(2,1)S(1)}, bf16[2,81,64,64]{1,3,2,0:T(8,128)(2,1)}, u32[]{:S(2)}) %copy-start) | copy-done | bytes 1327128
  9.2 1.6 %shard_map.178.refs_2_.refs_8_.refs_0_ = bf16[576,576]{1,0:T(8,128)(2,1)S(1)} custom-call(bf16[2,64,64,81]{3,2,1,0:T(8,128)(2,1)S(1)} %bitcast.19), custom_call_target="tpu_custom_call" | custom-call | flops 1000000000 | bytes 4000000 | tf_op jit(solution)/shard_map/pallas_call | solution.py:672
  11.2 2.1 %collective-permute-start.6 = (f32[1,1024]{1,0:T(1,128)S(1)}, f32[1,1024]{1,0:T(1,128)S(1)}, u32[]{:S(2)}, u32[]{:S(2)}) collective-permute-start(f32[1,1024]{1,0:T(1,128)S(1)} %shard_map.179.refs_3_), channel_id=1, source_target_pairs={{10,0},{8,2},{16,10},{18,8},{26,16},{24,18},{28,26},{30,24},{22,28... | collective-permute-start | bytes 12296 | tf_op jit(solution)/shard_map/ppermute | solution.py:820
  13.9 1.5 %collective-permute-start.3 = (f32[1,1024]{1,0:T(1,128)S(1)}, f32[1,1024]{1,0:T(1,128)S(1)}, u32[]{:S(2)}, u32[]{:S(2)}) collective-permute-start(f32[1,1024]{1,0:T(1,128)S(1)} %shard_map.179.refs_3_), channel_id=1, source_target_pairs={{6,0},{4,2},{0,10},{2,8},{10,16},{8,18},{16,26},{18,24},{26,28},{2... | collective-permute-start | bytes 12296 | tf_op jit(solution)/shard_map/ppermute | solution.py:820
  17.5 1.8 %collective-permute-done.2.refs_0_ = f32[1,1024]{1,0:T(1,128)S(1)} collective-permute-done((f32[1,1024]{1,0:T(1,128)S(1)}, f32[1,1024]{1,0:T(1,128)S(1)}, u32[]{:S(2)}, u32[]{:S(2)}) %collective-permute-start.2) | collective-permute-done | bytes 4128 | tf_op jit(solution)/shard_map/ppermute | solution.py:820
  19.4 5.0 %shard_map.181 = (f32[8,1024]{1,0:T(8,128)S(1)}, f32[2,1024]{1,0:T(2,128)S(1)}, f32[1,1024]{1,0:T(1,128)}, f32[1,128]{1,0:T(1,128)S(1)}, bf16[192,1024]{1,0:T(8,128)(2,1)S(1)}, /*index=5*/bf16[192,1024]{1,0:T(8,128)(2,1)S(1)}) custom-call(f32[1,1024]{1,0:T(1,128)S(1)} %collective-permute-done.2.refs_0_, f32[1,1024]{1,0:T(1,128)S(1)} %collective-permute-done.3.refs_1_, ...), custom_call_target="tpu_custom_call" | custom-call | flops 2038431744 | bytes 4000000 | tf_op jit(solution)/shard_map/pallas_call | solution.py:672
  24.3 2.0 %collective-permute-start.13 = (f32[2,1024]{1,0:T(2,128)S(1)}, f32[2,1024]{1,0:T(2,128)S(1)}, u32[]{:S(2)}, u32[]{:S(2)}) collective-permute-start(f32[2,1024]{1,0:T(2,128)S(1)} %get-tuple-element.65.refs_3_), channel_id=1, source_target_pairs={{8,0},{16,2},{18,10},{26,8},{24,16},{28,18},{30,26},{22,24},{20,28... | collective-permute-start | bytes 24584 | tf_op jit(solution)/shard_map/ppermute | solution.py:820
  28.7 1.3 %collective-permute-start.8 = (f32[2,1024]{1,0:T(2,128)S(1)}, f32[2,1024]{1,0:T(2,128)S(1)}, u32[]{:S(2)}, u32[]{:S(2)}) collective-permute-start(f32[2,1024]{1,0:T(2,128)S(1)} %get-tuple-element.65.refs_3_), channel_id=1, source_target_pairs={{14,0},{6,2},{4,10},{0,8},{2,16},{10,18},{8,26},{16,24},{18,28},{2... | collective-permute-start | bytes 24584 | tf_op jit(solution)/shard_map/ppermute | solution.py:820
  30.1 1.6 %shard_map.182.refs_8_.refs_1_ = bf16[576,576]{1,0:T(8,128)(2,1)S(1)} custom-call(bf16[2,64,64,81]{3,2,1,0:T(8,128)(2,1)S(1)} %bitcast.20, f32[1,128]{1,0:T(1,128)S(1)} %get-tuple-element.67.refs_1_.refs_7_), custom_call_target="tpu_custom_call" | custom-call | flops 1000000000 | bytes 4000000 | tf_op jit(solution)/shard_map/pallas_call | solution.py:672
  32.8 4.4 %shard_map.183 = (f32[8,1024]{1,0:T(8,128)S(1)}, f32[2,1024]{1,0:T(2,128)S(1)}, f32[1,1024]{1,0:T(1,128)S(1)}, f32[1,128]{1,0:T(1,128)S(1)}, f32[8,1024]{1,0:T(8...) custom-call(f32[2,1024]{1,0:T(2,128)S(1)} %collective-permute-done.8.refs_0_, ...), custom_call_target="tpu_custom_call" | custom-call | flops 2038431744 | bytes 4000000 | tf_op jit(solution)/shard_map/pallas_call | solution.py:672
  39.2 1.6 %collective-permute-start.15 = (f32[2,1024]{1,0:T(2,128)S(1)}, f32[2,1024]{1,0:T(2,128)S(1)}, u32[]{:S(2)}, u32[]{:S(2)}) collective-permute-start(f32[2,1024]{1,0:T(2,128)S(1)} %get-tuple-element.70.refs_3_), channel_id=1, source_target_pairs={{6,0},{4,2},{0,10},{2,8},{10,16},{8,18},{16,26},{18,24},{26,28},{2... | collective-permute-start | bytes 24584 | tf_op jit(solution)/shard_map/ppermute | solution.py:820
  40.8 1.8 %collective-permute-start.14 = (f32[2,1024]{1,0:T(2,128)S(1)}, f32[2,1024]{1,0:T(2,128)S(1)}, u32[]{:S(2)}, u32[]{:S(2)}) collective-permute-start(f32[2,1024]{1,0:T(2,128)S(1)} %get-tuple-element.70.refs_3_), channel_id=1, source_target_pairs={{14,0},{6,2},{4,10},{0,8},{2,16},{10,18},{8,26},{16,24},{18,28},{2... | collective-permute-start | bytes 24584 | tf_op jit(solution)/shard_map/ppermute | solution.py:820
  44.8 2.6 %shard_map.185 = (f32[8,1024]{1,0:T(8,128)S(1)}, f32[3,1024]{1,0:T(4,128)S(1)}, f32[16,64]{1,0:T(8,128)S(1)}, f32[16,1024]{1,0:T(8,128)S(1)}, bf16[192,1024]{1,0...) custom-call(f32[2,1024]{1,0:T(2,128)S(1)} %collective-permute-done.14.refs_0_, f32[2,1024]{1,0:T(2,128)S(1)} %collective-permute-done.15.refs_1_, ...), custom_call_target="tpu_custom_call" | custom-call | flops 679477248 | bytes 4000000 | tf_op jit(solution)/shard_map/pallas_call | solution.py:672
  47.4 1.5 %collective-permute-start.25 = (f32[3,1024]{1,0:T(4,128)S(1)}, f32[3,1024]{1,0:T(4,128)S(1)}, u32[]{:S(2)}, u32[]{:S(2)}) collective-permute-start(f32[3,1024]{1,0:T(4,128)S(1)} %get-tuple-element.78.refs_3_), channel_id=1, source_target_pairs={{8,0},{16,2},{18,10},{26,8},{24,16},{28,18},{30,26},{22,24},{20,28... | collective-permute-start | bytes 36872 | tf_op jit(solution)/shard_map/ppermute | solution.py:820
  51.1 1.6 %collective-permute-start.20 = (f32[3,1024]{1,0:T(4,128)S(1)}, f32[3,1024]{1,0:T(4,128)S(1)}, u32[]{:S(2)}, u32[]{:S(2)}) collective-permute-start(f32[3,1024]{1,0:T(4,128)S(1)} %get-tuple-element.78.refs_3_), channel_id=1, source_target_pairs={{14,0},{6,2},{4,10},{0,8},{2,16},{10,18},{8,26},{16,24},{18,28},{2... | collective-permute-start | bytes 36872 | tf_op jit(solution)/shard_map/ppermute | solution.py:820
  52.7 2.1 %shard_map.186.refs_11_ = bf16[3072,128]{1,0:T(8,128)(2,1)S(1)} custom-call(f32[8,1024]{1,0:T(8,128)S(1)} %get-tuple-element.72.refs_9_.refs_0_, bf16[192,1024]{1,0:T(8,128)(2,1)S(1)} %get-tuple-element.73.refs_10_.refs_1_, bf16[192,1024]{1,0:T(8,128)(2,1)S(1)} %get-tuple-element.74.refs_11_.refs_2_, f32[16,1024]{1,0:T(8,128)S(1)} %get-tuple-element.83.refs_3_, ...), custom_call_target="tpu_custom_call" | custom-call | flops 679477248 | bytes 4000000 | tf_op jit(solution)/shard_map/pallas_call | solution.py:672
  55.3 4.1 %shard_map.187 = (f32[1,1024]{1,0:T(1,128)S(1)}, f32[2,1024]{1,0:T(2,128)S(1)}, f32[1,1024]{1,0:T(1,128)S(1)}, bf16[1536,128]{1,0:T(8,128)(2,1)S(1)}, bf16[1536,128]{1,0:T(8,128)(2,1)S(1)}) custom-call(f32[3,1024]{1,0:T(4,128)S(1)} %collective-permute-done.20.refs_0_, f32[3,1024]{1,0:T(4,128)S(1)} %collective-permute-done.21.refs_1_, ...), custom_call_target="tpu_custom_call" | custom-call | flops 1358954496 | bytes 4000000 | tf_op jit(solution)/shard_map/pallas_call | solution.py:672
  60.2 1.3 %collective-permute-done.26.refs_1_ = bf16[1536,128]{1,0:T(8,128)(2,1)S(1)} collective-permute-done((bf16[1536,128]{1,0:T(8,128)(2,1)S(1)}, bf16[1536,128]{1,0:T(8,128)(2,1)S(1)}, u32[]{:S(2)}, u32[]{:S(2)}) %collective-permute-start.26) | collective-permute-done | bytes 393248 | tf_op jit(solution)/shard_map/ppermute | solution.py:779
  63.7 2.0 %collective-permute-done.29.refs_2_ = f32[1,1024]{1,0:T(1,128)S(1)} collective-permute-done((f32[1,1024]{1,0:T(1,128)S(1)}, f32[1,1024]{1,0:T(1,128)S(1)}, u32[]{:S(2)}, u32[]{:S(2)}) %collective-permute-start.29) | collective-permute-done | bytes 4128 | tf_op jit(solution)/shard_map/ppermute | solution.py:820
  65.7 2.2 %collective-permute-done.27.refs_1_ = bf16[768,128]{1,0:T(8,128)(2,1)S(1)} collective-permute-done((bf16[768,128]{1,0:T(8,128)(2,1)S(1)}, bf16[768,128]{1,0:T(8,128)(2,1)S(1)}, u32[]{:S(2)}, u32[]{:S(2)}) %collective-permute-start.27) | collective-permute-done | bytes 196640 | tf_op jit(solution)/shard_map/ppermute | solution.py:782
  69.3 2.2 %collective-permute-start.32 = (bf16[192,128]{1,0:T(8,128)(2,1)S(1)}, bf16[192,128]{1,0:T(8,128)(2,1)S(1)}, u32[]{:S(2)}, u32[]{:S(2)}) collective-permute-start(bf16[192,128]{1,0:T(8,128)(2,1)S(1)} %get-tuple-element.102), channel_id=1, source_target_pairs={{24,0},{26,2},{28,4},{30,6},{16,8},{18,10},{20,12},{22,14},{8,16},... | collective-permute-start | bytes 147464 | tf_op jit(solution)/shard_map/ppermute | solution.py:785
  72.3 1.8 %collective-permute-done.32.refs_3_ = bf16[192,128]{1,0:T(8,128)(2,1)S(1)} collective-permute-done((bf16[192,128]{1,0:T(8,128)(2,1)S(1)}, bf16[192,128]{1,0:T(8,128)(2,1)S(1)}, u32[]{:S(2)}, u32[]{:S(2)}) %collective-permute-start.32) | collective-permute-done | bytes 49184 | tf_op jit(solution)/shard_map/ppermute | solution.py:785
  74.1 2.7 %collective-permute-start.35 = (bf16[192,128]{1,0:T(8,128)(2,1)S(1)}, bf16[192,128]{1,0:T(8,128)(2,1)S(1)}, u32[]{:S(2)}, u32[]{:S(2)}) collective-permute-start(bf16[192,128]{1,0:T(8,128)(2,1)S(1)} %shard_map.191.refs_0_), channel_id=1, source_target_pairs={{24,0},{26,2},{28,4},{30,6},{16,8},{18,10},{20,12},{22,14},{8,16},... | collective-permute-start | bytes 147464 | tf_op jit(solution)/shard_map/ppermute | solution.py:788
  78.9 1.7 %collective-permute-done.34.refs_2_ = bf16[192,128]{1,0:T(8,128)(2,1)S(1)} collective-permute-done((bf16[192,128]{1,0:T(8,128)(2,1)S(1)}, bf16[192,128]{1,0:T(8,128)(2,1)S(1)}, u32[]{:S(2)}, u32[]{:S(2)}) %collective-permute-start.34) | collective-permute-done | bytes 49184 | tf_op jit(solution)/shard_map/ppermute | solution.py:788
  83.4 2.9 %collective-permute-done.38.refs_3_ = bf16[768,128]{1,0:T(8,128)(2,1)S(1)} collective-permute-done((bf16[768,128]{1,0:T(8,128)(2,1)S(1)}, bf16[768,128]{1,0:T(8,128)(2,1)S(1)}, u32[]{:S(2)}, u32[]{:S(2)}) %collective-permute-start.38) | collective-permute-done | bytes 196640 | tf_op jit(solution)/shard_map/ppermute | solution.py:800
  86.2 1.8 %collective-permute-done.37.refs_2_ = bf16[768,128]{1,0:T(8,128)(2,1)S(1)} collective-permute-done((bf16[768,128]{1,0:T(8,128)(2,1)S(1)}, bf16[768,128]{1,0:T(8,128)(2,1)S(1)}, u32[]{:S(2)}, u32[]{:S(2)}) %collective-permute-start.37) | collective-permute-done | bytes 196640 | tf_op jit(solution)/shard_map/ppermute | solution.py:800
  88.3 5.2 %collective-permute-start.39 = (bf16[3072,128]{1,0:T(8,128)(2,1)S(1)}, bf16[3072,128]{1,0:T(8,128)(2,1)S(1)}, u32[]{:S(2)}, u32[]{:S(2)}) collective-permute-start(bf16[3072,128]{1,0:T(8,128)(2,1)S(1)} %shard_map.193.refs_0_), channel_id=1, source_target_pairs={{2,0},{0,2},{6,4},{4,6},{10,8},{8,10},{14,12},{12,14},{18,16},{16,... | collective-permute-start | bytes 2359304 | tf_op jit(solution)/shard_map/ppermute | solution.py:779
  93.5 3.5 %collective-permute-start.40 = (f32[2,512]{1,0:T(2,128)S(1)}, f32[2,512]{1,0:T(2,128)S(1)}, u32[]{:S(2)}, u32[]{:S(2)}) collective-permute-start(f32[2,512]{1,0:T(2,128)S(1)} %shard_map.189.refs_2_), channel_id=1, source_target_pairs={{0,0},{2,2},{10,4},{8,6},{16,8},{18,10},{26,12},{24,14},{28,16},{3... | collective-permute-start | bytes 12296 | tf_op jit(solution)/shard_map/ppermute | solution.py:929
  97.0 2.2 %shard_map.194 = (f32[2,64,64,81]{3,2,1,0:T(8,128)}, f32[2,2,64,81]{3,2,1,0:T(8,128)}, f32[2,64,81]{2,1,0:T(8,128)}) custom-call(bf16[3072,128]{1,0:T(8,128)(2,1)S(1)} %shard_map.193.refs_0_), custom_call_target="tpu_custom_call" | custom-call | flops 1000000000 | bytes 4000000 | tf_op jit(solution)/shard_map/pallas_call | solution.py:672
  99.3 2.8 %shard_map.195 = (f32[2,64]{1,0:T(2,128)}, f32[2,64]{1,0:T(2,128)}, f32[2,2]{1,0:T(2,128)}, f32[1,1]{1,0:T(1,128)}, f32[1,4,4,32]{3,2,1,0:T(4,128)}, /*index=5*/...) custom-call(bf16[3072,128]{1,0:T(8,128)(2,1)S(1)} %collective-permut, ...), custom_call_target="tpu_custom_call", output_to_operand_aliasing={{6}: (2, {}), {7}: (3, {}), {8}: (4, {})} | custom-call | flops 1000000000 | bytes 4000000 | tf_op jit(solution)/shard_map/pallas_call | solution.py:672
  (92 shorter events, 24.4 us)
Async XLA Ops:
  0.7 10.2 %collective-permute-start.1 = (f32[1,4,4,32]{3,2,1,0:T(4,128)}, f32[1,4,4,32]{3,2,1,0:T(4,128)S(1)}, u32[]{:S(2)}, u32[]{:S(2)}) collective-permute-start(f32[1,4,4,32]{3,2,1,0:T(4,128)} %param.11), channel_id=1, source_target_pairs={{1,0},{0,1},{3,2},{2,3},{5,10},{4,11},{7,8},{6,9},{9,16},{8,17},{1... | collective-permute-start | bytes 6152 | tf_op jit(solution)/shard_map/ppermute | solution.py:825
  3.4 7.4 %collective-permute-start = (f32[1,4,4,32]{3,2,1,0:T(4,128)}, f32[1,4,4,32]{3,2,1,0:T(4,128)S(1)}, u32[]{:S(2)}, u32[]{:S(2)}) collective-permute-start(f32[1,4,4,32]{3,2,1,0:T(4,128)} %param.11), channel_id=1, source_target_pairs={{0,0},{1,1},{2,2},{3,3},{4,10},{5,11},{6,8},{7,9},{8,16},{9,17},{1... | collective-permute-start | bytes 6152 | tf_op jit(solution)/shard_map/ppermute | solution.py:825
  10.9 4.5 %collective-permute-start.7 = (f32[1,1024]{1,0:T(1,128)S(1)}, f32[1,1024]{1,0:T(1,128)S(1)}, u32[]{:S(2)}, u32[]{:S(2)}) collective-permute-start(f32[1,1024]{1,0:T(1,128)S(1)} %shard_map.179.refs_3_), channel_id=1, source_target_pairs={{8,0},{16,2},{18,10},{26,8},{24,16},{28,18},{30,26},{22,24},{20,28... | collective-permute-start | bytes 12296 | tf_op jit(solution)/shard_map/ppermute | solution.py:820
  11.2 5.8 %collective-permute-start.6 = (f32[1,1024]{1,0:T(1,128)S(1)}, f32[1,1024]{1,0:T(1,128)S(1)}, u32[]{:S(2)}, u32[]{:S(2)}) collective-permute-start(f32[1,1024]{1,0:T(1,128)S(1)} %shard_map.179.refs_3_), channel_id=1, source_target_pairs={{10,0},{8,2},{16,10},{18,8},{26,16},{24,18},{28,26},{30,24},{22,28... | collective-permute-start | bytes 12296 | tf_op jit(solution)/shard_map/ppermute | solution.py:820
  15.4 3.9 %collective-permute-start.2 = (f32[1,1024]{1,0:T(1,128)S(1)}, f32[1,1024]{1,0:T(1,128)S(1)}, u32[]{:S(2)}, u32[]{:S(2)}) collective-permute-start(f32[1,1024]{1,0:T(1,128)S(1)} %shard_map.179.refs_3_), channel_id=1, source_target_pairs={{14,0},{6,2},{4,10},{0,8},{2,16},{10,18},{8,26},{16,24},{18,28},{2... | collective-permute-start | bytes 12296 | tf_op jit(solution)/shard_map/ppermute | solution.py:820
  24.3 4.4 %collective-permute-start.13 = (f32[2,1024]{1,0:T(2,128)S(1)}, f32[2,1024]{1,0:T(2,128)S(1)}, u32[]{:S(2)}, u32[]{:S(2)}) collective-permute-start(f32[2,1024]{1,0:T(2,128)S(1)} %get-tuple-element.65.refs_3_), channel_id=1, source_target_pairs={{8,0},{16,2},{18,10},{26,8},{24,16},{28,18},{30,26},{22,24},{20,28... | collective-permute-start | bytes 24584 | tf_op jit(solution)/shard_map/ppermute | solution.py:820
  26.3 5.4 %collective-permute-start.12 = (f32[2,1024]{1,0:T(2,128)S(1)}, f32[2,1024]{1,0:T(2,128)S(1)}, u32[]{:S(2)}, u32[]{:S(2)}) collective-permute-start(f32[2,1024]{1,0:T(2,128)S(1)} %get-tuple-element.65.refs_3_), channel_id=1, source_target_pairs={{10,0},{8,2},{16,10},{18,8},{26,16},{24,18},{28,26},{30,24},{22,28... | collective-permute-start | bytes 24584 | tf_op jit(solution)/shard_map/ppermute | solution.py:820
  26.9 4.9 %collective-permute-start.11 = (f32[2,1024]{1,0:T(2,128)S(1)}, f32[2,1024]{1,0:T(2,128)S(1)}, u32[]{:S(2)}, u32[]{:S(2)}) collective-permute-start(f32[2,1024]{1,0:T(2,128)S(1)} %get-tuple-element.65.refs_3_), channel_id=1, source_target_pairs={{2,0},{10,2},{8,10},{16,8},{18,16},{26,18},{24,26},{28,24},{30,28}... | collective-permute-start | bytes 24584 | tf_op jit(solution)/shard_map/ppermute | solution.py:820
  27.0 4.7 %collective-permute-start.10 = (f32[2,1024]{1,0:T(2,128)S(1)}, f32[2,1024]{1,0:T(2,128)S(1)}, u32[]{:S(2)}, u32[]{:S(2)}) collective-permute-start(f32[2,1024]{1,0:T(2,128)S(1)} %get-tuple-element.65.refs_3_), channel_id=1, source_target_pairs={{4,0},{0,2},{2,10},{10,8},{8,16},{16,18},{18,26},{26,24},{24,28},{... | collective-permute-start | bytes 24584 | tf_op jit(solution)/shard_map/ppermute | solution.py:820
  27.4 4.4 %collective-permute-start.9 = (f32[2,1024]{1,0:T(2,128)S(1)}, f32[2,1024]{1,0:T(2,128)S(1)}, u32[]{:S(2)}, u32[]{:S(2)}) collective-permute-start(f32[2,1024]{1,0:T(2,128)S(1)} %get-tuple-element.65.refs_3_), channel_id=1, source_target_pairs={{6,0},{4,2},{0,10},{2,8},{10,16},{8,18},{16,26},{18,24},{26,28},{2... | collective-permute-start | bytes 24584 | tf_op jit(solution)/shard_map/ppermute | solution.py:820
  28.7 4.1 %collective-permute-start.8 = (f32[2,1024]{1,0:T(2,128)S(1)}, f32[2,1024]{1,0:T(2,128)S(1)}, u32[]{:S(2)}, u32[]{:S(2)}) collective-permute-start(f32[2,1024]{1,0:T(2,128)S(1)} %get-tuple-element.65.refs_3_), channel_id=1, source_target_pairs={{14,0},{6,2},{4,10},{0,8},{2,16},{10,18},{8,26},{16,24},{18,28},{2... | collective-permute-start | bytes 24584 | tf_op jit(solution)/shard_map/ppermute | solution.py:820
  38.5 5.3 %collective-permute-start.18 = (f32[2,1024]{1,0:T(2,128)S(1)}, f32[2,1024]{1,0:T(2,128)S(1)}, u32[]{:S(2)}, u32[]{:S(2)}) collective-permute-start(f32[2,1024]{1,0:T(2,128)S(1)} %get-tuple-element.70.refs_3_), channel_id=1, source_target_pairs={{10,0},{8,2},{16,10},{18,8},{26,16},{24,18},{28,26},{30,24},{22,28... | collective-permute-start | bytes 24584 | tf_op jit(solution)/shard_map/ppermute | solution.py:820
  38.6 5.2 %collective-permute-start.17 = (f32[2,1024]{1,0:T(2,128)S(1)}, f32[2,1024]{1,0:T(2,128)S(1)}, u32[]{:S(2)}, u32[]{:S(2)}) collective-permute-start(f32[2,1024]{1,0:T(2,128)S(1)} %get-tuple-element.70.refs_3_), channel_id=1, source_target_pairs={{2,0},{10,2},{8,10},{16,8},{18,16},{26,18},{24,26},{28,24},{30,28}... | collective-permute-start | bytes 24584 | tf_op jit(solution)/shard_map/ppermute | solution.py:820
  39.2 4.6 %collective-permute-start.16 = (f32[2,1024]{1,0:T(2,128)S(1)}, f32[2,1024]{1,0:T(2,128)S(1)}, u32[]{:S(2)}, u32[]{:S(2)}) collective-permute-start(f32[2,1024]{1,0:T(2,128)S(1)} %get-tuple-element.70.refs_3_), channel_id=1, source_target_pairs={{4,0},{0,2},{2,10},{10,8},{8,16},{16,18},{18,26},{26,24},{24,28},{... | collective-permute-start | bytes 24584 | tf_op jit(solution)/shard_map/ppermute | solution.py:820
  39.2 4.7 %collective-permute-start.15 = (f32[2,1024]{1,0:T(2,128)S(1)}, f32[2,1024]{1,0:T(2,128)S(1)}, u32[]{:S(2)}, u32[]{:S(2)}) collective-permute-start(f32[2,1024]{1,0:T(2,128)S(1)} %get-tuple-element.70.refs_3_), channel_id=1, source_target_pairs={{6,0},{4,2},{0,10},{2,8},{10,16},{8,18},{16,26},{18,24},{26,28},{2... | collective-permute-start | bytes 24584 | tf_op jit(solution)/shard_map/ppermute | solution.py:820
  40.8 4.0 %collective-permute-start.14 = (f32[2,1024]{1,0:T(2,128)S(1)}, f32[2,1024]{1,0:T(2,128)S(1)}, u32[]{:S(2)}, u32[]{:S(2)}) collective-permute-start(f32[2,1024]{1,0:T(2,128)S(1)} %get-tuple-element.70.refs_3_), channel_id=1, source_target_pairs={{14,0},{6,2},{4,10},{0,8},{2,16},{10,18},{8,26},{16,24},{18,28},{2... | collective-permute-start | bytes 24584 | tf_op jit(solution)/shard_map/ppermute | solution.py:820
  48.9 5.9 %collective-permute-start.24 = (f32[3,1024]{1,0:T(4,128)S(1)}, f32[3,1024]{1,0:T(4,128)S(1)}, u32[]{:S(2)}, u32[]{:S(2)}) collective-permute-start(f32[3,1024]{1,0:T(4,128)S(1)} %get-tuple-element.78.refs_3_), channel_id=1, source_target_pairs={{10,0},{8,2},{16,10},{18,8},{26,16},{24,18},{28,26},{30,24},{22,28... | collective-permute-start | bytes 36872 | tf_op jit(solution)/shard_map/ppermute | solution.py:820
  49.0 5.8 %collective-permute-start.23 = (f32[3,1024]{1,0:T(4,128)S(1)}, f32[3,1024]{1,0:T(4,128)S(1)}, u32[]{:S(2)}, u32[]{:S(2)}) collective-permute-start(f32[3,1024]{1,0:T(4,128)S(1)} %get-tuple-element.78.refs_3_), channel_id=1, source_target_pairs={{2,0},{10,2},{8,10},{16,8},{18,16},{26,18},{24,26},{28,24},{30,28}... | collective-permute-start | bytes 36872 | tf_op jit(solution)/shard_map/ppermute | solution.py:820
  49.9 4.9 %collective-permute-start.22 = (f32[3,1024]{1,0:T(4,128)S(1)}, f32[3,1024]{1,0:T(4,128)S(1)}, u32[]{:S(2)}, u32[]{:S(2)}) collective-permute-start(f32[3,1024]{1,0:T(4,128)S(1)} %get-tuple-element.78.refs_3_), channel_id=1, source_target_pairs={{4,0},{0,2},{2,10},{10,8},{8,16},{16,18},{18,26},{26,24},{24,28},{... | collective-permute-start | bytes 36872 | tf_op jit(solution)/shard_map/ppermute | solution.py:820
  49.9 5.0 %collective-permute-start.21 = (f32[3,1024]{1,0:T(4,128)S(1)}, f32[3,1024]{1,0:T(4,128)S(1)}, u32[]{:S(2)}, u32[]{:S(2)}) collective-permute-start(f32[3,1024]{1,0:T(4,128)S(1)} %get-tuple-element.78.refs_3_), channel_id=1, source_target_pairs={{6,0},{4,2},{0,10},{2,8},{10,16},{8,18},{16,26},{18,24},{26,28},{2... | collective-permute-start | bytes 36872 | tf_op jit(solution)/shard_map/ppermute | solution.py:820
  51.1 4.2 %collective-permute-start.20 = (f32[3,1024]{1,0:T(4,128)S(1)}, f32[3,1024]{1,0:T(4,128)S(1)}, u32[]{:S(2)}, u32[]{:S(2)}) collective-permute-start(f32[3,1024]{1,0:T(4,128)S(1)} %get-tuple-element.78.refs_3_), channel_id=1, source_target_pairs={{14,0},{6,2},{4,10},{0,8},{2,16},{10,18},{8,26},{16,24},{18,28},{2... | collective-permute-start | bytes 36872 | tf_op jit(solution)/shard_map/ppermute | solution.py:820
  61.7 6.2 %collective-permute-start.27 = (bf16[768,128]{1,0:T(8,128)(2,1)S(1)}, bf16[768,128]{1,0:T(8,128)(2,1)S(1)}, u32[]{:S(2)}, u32[]{:S(2)}) collective-permute-start(bf16[768,128]{1,0:T(8,128)(2,1)S(1)} %get-tuple-element.95), channel_id=1, source_target_pairs={{4,0},{6,2},{0,4},{2,6},{12,8},{14,10},{8,12},{10,14},{20,16},{22,... | collective-permute-start | bytes 589832 | tf_op jit(solution)/shard_map/ppermute | solution.py:782
  68.4 3.9 %collective-permute-start.31 = (bf16[192,128]{1,0:T(8,128)(2,1)S(1)}, bf16[192,128]{1,0:T(8,128)(2,1)S(1)}, u32[]{:S(2)}, u32[]{:S(2)}) collective-permute-start(bf16[192,128]{1,0:T(8,128)(2,1)S(1)} %get-tuple-element.101), channel_id=1, source_target_pairs={{16,0},{18,2},{20,4},{22,6},{24,8},{26,10},{28,12},{30,14},{0,16},... | collective-permute-start | bytes 147464 | tf_op jit(solution)/shard_map/ppermute | solution.py:785
  69.3 4.7 %collective-permute-start.32 = (bf16[192,128]{1,0:T(8,128)(2,1)S(1)}, bf16[192,128]{1,0:T(8,128)(2,1)S(1)}, u32[]{:S(2)}, u32[]{:S(2)}) collective-permute-start(bf16[192,128]{1,0:T(8,128)(2,1)S(1)} %get-tuple-element.102), channel_id=1, source_target_pairs={{24,0},{26,2},{28,4},{30,6},{16,8},{18,10},{20,12},{22,14},{8,16},... | collective-permute-start | bytes 147464 | tf_op jit(solution)/shard_map/ppermute | solution.py:785
  74.1 4.8 %collective-permute-start.35 = (bf16[192,128]{1,0:T(8,128)(2,1)S(1)}, bf16[192,128]{1,0:T(8,128)(2,1)S(1)}, u32[]{:S(2)}, u32[]{:S(2)}) collective-permute-start(bf16[192,128]{1,0:T(8,128)(2,1)S(1)} %shard_map.191.refs_0_), channel_id=1, source_target_pairs={{24,0},{26,2},{28,4},{30,6},{16,8},{18,10},{20,12},{22,14},{8,16},... | collective-permute-start | bytes 147464 | tf_op jit(solution)/shard_map/ppermute | solution.py:788
  76.8 3.8 %collective-permute-start.34 = (bf16[192,128]{1,0:T(8,128)(2,1)S(1)}, bf16[192,128]{1,0:T(8,128)(2,1)S(1)}, u32[]{:S(2)}, u32[]{:S(2)}) collective-permute-start(bf16[192,128]{1,0:T(8,128)(2,1)S(1)} %shard_map.191.refs_0_), channel_id=1, source_target_pairs={{16,0},{18,2},{20,4},{22,6},{24,8},{26,10},{28,12},{30,14},{0,16},... | collective-permute-start | bytes 147464 | tf_op jit(solution)/shard_map/ppermute | solution.py:788
  76.8 3.8 %collective-permute-start.33 = (bf16[192,128]{1,0:T(8,128)(2,1)S(1)}, bf16[192,128]{1,0:T(8,128)(2,1)S(1)}, u32[]{:S(2)}, u32[]{:S(2)}) collective-permute-start(bf16[192,128]{1,0:T(8,128)(2,1)S(1)} %shard_map.191.refs_0_), channel_id=1, source_target_pairs={{8,0},{10,2},{12,4},{14,6},{0,8},{2,10},{4,12},{6,14},{24,16},{26,... | collective-permute-start | bytes 147464 | tf_op jit(solution)/shard_map/ppermute | solution.py:788
  80.7 5.6 %collective-permute-start.38 = (bf16[768,128]{1,0:T(8,128)(2,1)S(1)}, bf16[768,128]{1,0:T(8,128)(2,1)S(1)}, u32[]{:S(2)}, u32[]{:S(2)}) collective-permute-start(bf16[768,128]{1,0:T(8,128)(2,1)S(1)} %shard_map.192.refs_0_), channel_id=1, source_target_pairs={{5,0},{4,1},{7,2},{6,3},{1,4},{0,5},{3,6},{2,7},{13,8},{12,9},{15,... | collective-permute-start | bytes 589832 | tf_op jit(solution)/shard_map/ppermute | solution.py:800
  81.6 6.4 %collective-permute-start.37 = (bf16[768,128]{1,0:T(8,128)(2,1)S(1)}, bf16[768,128]{1,0:T(8,128)(2,1)S(1)}, u32[]{:S(2)}, u32[]{:S(2)}) collective-permute-start(bf16[768,128]{1,0:T(8,128)(2,1)S(1)} %shard_map.192.refs_0_), channel_id=1, source_target_pairs={{1,0},{0,1},{3,2},{2,3},{5,4},{4,5},{7,6},{6,7},{9,8},{8,9},{11,10... | collective-permute-start | bytes 589832 | tf_op jit(solution)/shard_map/ppermute | solution.py:800
  82.8 5.4 %collective-permute-start.36 = (bf16[768,128]{1,0:T(8,128)(2,1)S(1)}, bf16[768,128]{1,0:T(8,128)(2,1)S(1)}, u32[]{:S(2)}, u32[]{:S(2)}) collective-permute-start(bf16[768,128]{1,0:T(8,128)(2,1)S(1)} %shard_map.192.refs_0_), channel_id=1, source_target_pairs={{4,0},{5,1},{6,2},{7,3},{0,4},{1,5},{2,6},{3,7},{12,8},{13,9},{14,... | collective-permute-start | bytes 589832 | tf_op jit(solution)/shard_map/ppermute | solution.py:800
  88.3 11.0 %collective-permute-start.39 = (bf16[3072,128]{1,0:T(8,128)(2,1)S(1)}, bf16[3072,128]{1,0:T(8,128)(2,1)S(1)}, u32[]{:S(2)}, u32[]{:S(2)}) collective-permute-start(bf16[3072,128]{1,0:T(8,128)(2,1)S(1)} %shard_map.193.refs_0_), channel_id=1, source_target_pairs={{2,0},{0,2},{6,4},{4,6},{10,8},{8,10},{14,12},{12,14},{18,16},{16,... | collective-permute-start | bytes 2359304 | tf_op jit(solution)/shard_map/ppermute | solution.py:779
  93.5 5.8 %collective-permute-start.40 = (f32[2,512]{1,0:T(2,128)S(1)}, f32[2,512]{1,0:T(2,128)S(1)}, u32[]{:S(2)}, u32[]{:S(2)}) collective-permute-start(f32[2,512]{1,0:T(2,128)S(1)} %shard_map.189.refs_2_), channel_id=1, source_target_pairs={{0,0},{2,2},{10,4},{8,6},{16,8},{18,10},{26,12},{24,14},{28,16},{3... | collective-permute-start | bytes 12296 | tf_op jit(solution)/shard_map/ppermute | solution.py:929
  (19 other events, 131.0 us)

commit v7 on v6

--- a/solution.py
+++ b/solution.py
@@ -837,7 +837,6 @@
         w_mid.transpose(0, 2, 3, 1),
         w_first.transpose(0, 2, 3, 1).reshape(2, channels, TAPS),
         w_last.transpose(0, 2, 3, 1),
-        jnp.stack([b_first, b_mid, jnp.pad(b_last, ((0, 0), (0, channels - 2)))], axis=1).reshape(6, channels),
     ]
     back = spread_last_back()
     pad = ((0, 0), (0, 128 - TAPS))
@@ -864,7 +863,9 @@
         join, [shape((1, noise.size * halves))], [pltpu.VMEM((1, noise.size), F32)],
         [HERE, *whole, *waits], 1000, loose=waits, bytes_moved=1000,
     )
-    narrow = pack_narrow(params[1:], (whole,))
+    *bias, whole = lax.optimization_barrier((b_first, b_mid, b_last, whole))
+    bias[2] = jnp.pad(bias[2], ((0, 0), (0, channels - 2)))
+    narrow = pack_narrow([*params[1:3], jnp.stack(bias, axis=1).reshape(6, channels)], (whole,))
 
     def exchange(values):
         return [values if m == 0 else step(values, m) for m in range(-3, 4)]
@@ -924,9 +925,9 @@
     (pieces,) = stage([("split", depth, [stay, crossed])], after=(force,))
     ((total,),) = stage([("sum", 1, [pieces[0], *scatter(pieces)])])
     ((line,),) = stage([("join", 1, [total, *gather(total)])])
-    ((mine,),) = stage([("join", 1, [line, *square(line)])])
+    force = lax.ppermute(force, "xy", [(order[p], p) for p in range(count)])
+    ((mine,),) = stage([("join", 1, [line, *square(line)])], after=(force,))
     other = core(mine)
-    force = lax.ppermute(force, "xy", [(order[p], p) for p in range(count)])
     outs = unpack(False, layout, volume, coords, mine, channels, [])
     g_mid, g_last, g_first, gb_first, gb_mid, gb_last, loss, sample, force = unpack(
         True, layout, volume, coords, other, channels, list(outs), force, noise.shape

time: 103 us -> 100 us (0.971)
  waiting for transfers between devices: 21.6 us -> 16.6 us
  starting transfers between devices: 48.8 us -> 51.3 us
    ppermute x3, waiting for transfers between devices: 4.88 us -> 0.01 us  [square(): out.append(lax.ppermute(v, ('xy', 'gz'), pairs))]
    ppermute x1, starting transfers between devices: 3.51 us -> 8.14 us  [per_device(): force = lax.ppermute(force, 'xy', [(order[p], p) for p in range(count)])]
    ppermute x2, starting transfers between devices: 6 us -> 2.33 us  [core(): return lax.ppermute(v, 'xy', xy(lambda a: a ^ 1))]
    ppermute x26, waiting for transfers between devices: 7.56 us -> 5.98 us  [step(): lax.ppermute(values, 'xy', [(order[(p + offset) % count], order[p]) for p...]
    ppermute x26, starting transfers between devices: 22.9 us -> 24.3 us  [step(): lax.ppermute(values, 'xy', [(order[(p + offset) % count], order[p]) for p...]
    ppermute x1, waiting for transfers between devices: 0.12 us -> 1.28 us  [per_device(): force = lax.ppermute(force, 'xy', [(order[p], p) for p in range(count)])]
  transfers between devices with their start and end apart: 41 -> 41, of which waited for: 17 -> 13; matrix products, arithmetic and copies ran while one was open for 1% -> 0% of each run, Pallas kernels for 9% -> 9%
where the time goes in v7:
time: 100 us; the launch traced here: 99.2 us
  starting transfers between devices  51.3 us (51%)
  Pallas kernels  28.5 us (28%)
  waiting for transfers between devices  16.6 us (17%)
  local copies, waits for them, and re-layouts  1.65 us (2%)
  between operations  1.21 us (1%)
    pallas_call x18, Pallas kernels, kernel_call(): pl.pallas_call(whole, out_shape=tuple(outs), in_specs=[spec(a) for a in a...  28.5 us
    ppermute x26, starting transfers between devices, step(): lax.ppermute(values, 'xy', [(order[(p + offset) % count], order[p]) for p...  24.3 us
    ppermute x1, starting transfers between devices, per_device(): force = lax.ppermute(force, 'xy', [(order[p], p) for p in range(count)])  8.14 us
    ppermute x2, starting transfers between devices, per_device(): lax.ppermute(noise, ('xy', 'gz'), [(p * halves + (j + rel) % halves, orde...  6.25 us
    ppermute x26, waiting for transfers between devices, step(): lax.ppermute(values, 'xy', [(order[(p + offset) % count], order[p]) for p...  5.98 us
    ppermute x3, starting transfers between devices, gather(): lax.ppermute(v, 'xy', xy(lambda a, s=s: a ^ 4 * s))  3.61 us
    ppermute x3, starting transfers between devices, scatter(): lax.ppermute(pieces[s], 'xy', xy(lambda a, s=s: a ^ 4 * s))  3.61 us
    ppermute x3, waiting for transfers between devices, gather(): lax.ppermute(v, 'xy', xy(lambda a, s=s: a ^ 4 * s))  2.91 us
  transfers between devices with their start and end apart: 41, of which 13 were waited for; matrix products, arithmetic and copies ran while one was open for 0% of the time, Pallas kernels for 9%

profile of v7, /device:TPU:5, one launch (start us, length us, event | category | flops | bytes accessed | tf_op | source)
XLA Modules:
  0.0 99.2 jit_solution(9610965050447735950)
XLA Ops:
  0.7 2.8 %collective-permute-start.1 = (f32[1,4,4,32]{3,2,1,0:T(4,128)}, f32[1,4,4,32]{3,2,1,0:T(4,128)S(1)}, u32[]{:S(2)}, u32[]{:S(2)}) collective-permute-start(f32[1,4,4,32]{3,2,1,0:T(4,128)} %param.11), channel_id=1, source_target_pairs={{1,0},{0,1},{3,2},{2,3},{5,10},{4,11},{7,8},{6,9},{9,16},{8,17},{1... | collective-permute-start | bytes 6152 | tf_op jit(solution)/shard_map/ppermute | solution.py:825
  3.4 3.5 %collective-permute-start = (f32[1,4,4,32]{3,2,1,0:T(4,128)}, f32[1,4,4,32]{3,2,1,0:T(4,128)S(1)}, u32[]{:S(2)}, u32[]{:S(2)}) collective-permute-start(f32[1,4,4,32]{3,2,1,0:T(4,128)} %param.11), channel_id=1, source_target_pairs={{0,0},{1,1},{2,2},{3,3},{4,10},{5,11},{6,8},{7,9},{8,16},{9,17},{1... | collective-permute-start | bytes 6152 | tf_op jit(solution)/shard_map/ppermute | solution.py:825
  6.9 1.6 %copy-done = bf16[2,81,64,64]{1,3,2,0:T(8,128)(2,1)S(1)} copy-done((bf16[2,81,64,64]{1,3,2,0:T(8,128)(2,1)S(1)}, bf16[2,81,64,64]{1,3,2,0:T(8,128)(2,1)}, u32[]{:S(2)}) %copy-start) | copy-done | bytes 1327128
  8.5 1.6 %shard_map.178.refs_2_.refs_8_.refs_0_ = bf16[576,576]{1,0:T(8,128)(2,1)S(1)} custom-call(bf16[2,64,64,81]{3,2,1,0:T(8,128)(2,1)S(1)} %bitcast.19), custom_call_target="tpu_custom_call" | custom-call | flops 1000000000 | bytes 4000000 | tf_op jit(solution)/shard_map/pallas_call | solution.py:672
  10.6 2.7 %collective-permute-start.6 = (f32[1,1024]{1,0:T(1,128)S(1)}, f32[1,1024]{1,0:T(1,128)S(1)}, u32[]{:S(2)}, u32[]{:S(2)}) collective-permute-start(f32[1,1024]{1,0:T(1,128)S(1)} %shard_map.179.refs_3_), channel_id=1, source_target_pairs={{10,0},{8,2},{16,10},{18,8},{26,16},{24,18},{28,26},{30,24},{22,28... | collective-permute-start | bytes 12296 | tf_op jit(solution)/shard_map/ppermute | solution.py:820
  13.7 1.6 %collective-permute-start.3 = (f32[1,1024]{1,0:T(1,128)S(1)}, f32[1,1024]{1,0:T(1,128)S(1)}, u32[]{:S(2)}, u32[]{:S(2)}) collective-permute-start(f32[1,1024]{1,0:T(1,128)S(1)} %shard_map.179.refs_3_), channel_id=1, source_target_pairs={{6,0},{4,2},{0,10},{2,8},{10,16},{8,18},{16,26},{18,24},{26,28},{2... | collective-permute-start | bytes 12296 | tf_op jit(solution)/shard_map/ppermute | solution.py:820
  17.0 2.4 %collective-permute-done.2.refs_0_ = f32[1,1024]{1,0:T(1,128)S(1)} collective-permute-done((f32[1,1024]{1,0:T(1,128)S(1)}, f32[1,1024]{1,0:T(1,128)S(1)}, u32[]{:S(2)}, u32[]{:S(2)}) %collective-permute-start.2) | collective-permute-done | bytes 4128 | tf_op jit(solution)/shard_map/ppermute | solution.py:820
  19.4 5.0 %shard_map.181 = (f32[8,1024]{1,0:T(8,128)S(1)}, f32[2,1024]{1,0:T(2,128)S(1)}, f32[1,1024]{1,0:T(1,128)}, f32[1,128]{1,0:T(1,128)S(1)}, bf16[192,1024]{1,0:T(8,128)(2,1)S(1)}, /*index=5*/bf16[192,1024]{1,0:T(8,128)(2,1)S(1)}) custom-call(f32[1,1024]{1,0:T(1,128)S(1)} %collective-permute-done.2.refs_0_, f32[1,1024]{1,0:T(1,128)S(1)} %collective-permute-done.3.refs_1_, ...), custom_call_target="tpu_custom_call" | custom-call | flops 2038431744 | bytes 4000000 | tf_op jit(solution)/shard_map/pallas_call | solution.py:672
  24.4 1.3 %collective-permute-start.13 = (f32[2,1024]{1,0:T(2,128)S(1)}, f32[2,1024]{1,0:T(2,128)S(1)}, u32[]{:S(2)}, u32[]{:S(2)}) collective-permute-start(f32[2,1024]{1,0:T(2,128)S(1)} %get-tuple-element.73.refs_3_), channel_id=1, source_target_pairs={{8,0},{16,2},{18,10},{26,8},{24,16},{28,18},{30,26},{22,24},{20,28... | collective-permute-start | bytes 24584 | tf_op jit(solution)/shard_map/ppermute | solution.py:820
  26.7 1.3 %collective-permute-start.9 = (f32[2,1024]{1,0:T(2,128)S(1)}, f32[2,1024]{1,0:T(2,128)S(1)}, u32[]{:S(2)}, u32[]{:S(2)}) collective-permute-start(f32[2,1024]{1,0:T(2,128)S(1)} %get-tuple-element.73.refs_3_), channel_id=1, source_target_pairs={{6,0},{4,2},{0,10},{2,8},{10,16},{8,18},{16,26},{18,24},{26,28},{2... | collective-permute-start | bytes 24584 | tf_op jit(solution)/shard_map/ppermute | solution.py:820
  28.1 2.0 %collective-permute-start.8 = (f32[2,1024]{1,0:T(2,128)S(1)}, f32[2,1024]{1,0:T(2,128)S(1)}, u32[]{:S(2)}, u32[]{:S(2)}) collective-permute-start(f32[2,1024]{1,0:T(2,128)S(1)} %get-tuple-element.73.refs_3_), channel_id=1, source_target_pairs={{14,0},{6,2},{4,10},{0,8},{2,16},{10,18},{8,26},{16,24},{18,28},{2... | collective-permute-start | bytes 24584 | tf_op jit(solution)/shard_map/ppermute | solution.py:820
  30.1 1.6 %shard_map.182.refs_8_.refs_1_ = bf16[576,576]{1,0:T(8,128)(2,1)S(1)} custom-call(bf16[2,64,64,81]{3,2,1,0:T(8,128)(2,1)S(1)} %bitcast.20, f32[1,128]{1,0:T(1,128)S(1)} %get-tuple-element.75.refs_1_.refs_7_), custom_call_target="tpu_custom_call" | custom-call | flops 1000000000 | bytes 4000000 | tf_op jit(solution)/shard_map/pallas_call | solution.py:672
  32.1 4.4 %shard_map.183 = (f32[8,1024]{1,0:T(8,128)S(1)}, f32[2,1024]{1,0:T(2,128)S(1)}, f32[1,1024]{1,0:T(1,128)S(1)}, f32[1,128]{1,0:T(1,128)S(1)}, f32[8,1024]{1,0:T(8...) custom-call(f32[2,1024]{1,0:T(2,128)S(1)} %collective-permute-done.8.refs_0_, ...), custom_call_target="tpu_custom_call" | custom-call | flops 2038431744 | bytes 4000000 | tf_op jit(solution)/shard_map/pallas_call | solution.py:672
  40.1 2.2 %collective-permute-start.14 = (f32[2,1024]{1,0:T(2,128)S(1)}, f32[2,1024]{1,0:T(2,128)S(1)}, u32[]{:S(2)}, u32[]{:S(2)}) collective-permute-start(f32[2,1024]{1,0:T(2,128)S(1)} %get-tuple-element.78.refs_3_), channel_id=1, source_target_pairs={{14,0},{6,2},{4,10},{0,8},{2,16},{10,18},{8,26},{16,24},{18,28},{2... | collective-permute-start | bytes 24584 | tf_op jit(solution)/shard_map/ppermute | solution.py:820
  44.1 2.6 %shard_map.185 = (f32[8,1024]{1,0:T(8,128)S(1)}, f32[3,1024]{1,0:T(4,128)S(1)}, f32[16,64]{1,0:T(8,128)S(1)}, f32[16,1024]{1,0:T(8,128)S(1)}, bf16[192,1024]{1,0...) custom-call(f32[2,1024]{1,0:T(2,128)S(1)} %collective-permute-done.14.refs_0_, f32[2,1024]{1,0:T(2,128)S(1)} %collective-permute-done.15.refs_1_, ...), custom_call_target="tpu_custom_call" | custom-call | flops 679477248 | bytes 4000000 | tf_op jit(solution)/shard_map/pallas_call | solution.py:672
  46.7 1.4 %collective-permute-start.25 = (f32[3,1024]{1,0:T(4,128)S(1)}, f32[3,1024]{1,0:T(4,128)S(1)}, u32[]{:S(2)}, u32[]{:S(2)}) collective-permute-start(f32[3,1024]{1,0:T(4,128)S(1)} %get-tuple-element.86.refs_3_), channel_id=1, source_target_pairs={{8,0},{16,2},{18,10},{26,8},{24,16},{28,18},{30,26},{22,24},{20,28... | collective-permute-start | bytes 36872 | tf_op jit(solution)/shard_map/ppermute | solution.py:820
  48.3 1.5 %collective-permute-start.23 = (f32[3,1024]{1,0:T(4,128)S(1)}, f32[3,1024]{1,0:T(4,128)S(1)}, u32[]{:S(2)}, u32[]{:S(2)}) collective-permute-start(f32[3,1024]{1,0:T(4,128)S(1)} %get-tuple-element.86.refs_3_), channel_id=1, source_target_pairs={{2,0},{10,2},{8,10},{16,8},{18,16},{26,18},{24,26},{28,24},{30,28}... | collective-permute-start | bytes 36872 | tf_op jit(solution)/shard_map/ppermute | solution.py:820
  50.4 2.2 %collective-permute-start.20 = (f32[3,1024]{1,0:T(4,128)S(1)}, f32[3,1024]{1,0:T(4,128)S(1)}, u32[]{:S(2)}, u32[]{:S(2)}) collective-permute-start(f32[3,1024]{1,0:T(4,128)S(1)} %get-tuple-element.86.refs_3_), channel_id=1, source_target_pairs={{14,0},{6,2},{4,10},{0,8},{2,16},{10,18},{8,26},{16,24},{18,28},{2... | collective-permute-start | bytes 36872 | tf_op jit(solution)/shard_map/ppermute | solution.py:820
  52.6 2.1 %shard_map.186.refs_11_ = bf16[3072,128]{1,0:T(8,128)(2,1)S(1)} custom-call(f32[8,1024]{1,0:T(8,128)S(1)} %get-tuple-element.80.refs_9_.refs_0_, bf16[192,1024]{1,0:T(8,128)(2,1)S(1)} %get-tuple-element.81.refs_10_.refs_1_, bf16[192,1024]{1,0:T(8,128)(2,1)S(1)} %get-tuple-element.82.refs_11_.refs_2_, f32[16,1024]{1,0:T(8,128)S(1)} %get-tuple-element.91.refs_3_, ...), custom_call_target="tpu_custom_call" | custom-call | flops 679477248 | bytes 4000000 | tf_op jit(solution)/shard_map/pallas_call | solution.py:672
  54.7 4.1 %shard_map.187 = (f32[1,1024]{1,0:T(1,128)S(1)}, f32[2,1024]{1,0:T(2,128)S(1)}, f32[1,1024]{1,0:T(1,128)S(1)}, bf16[1536,128]{1,0:T(8,128)(2,1)S(1)}, bf16[1536,128]{1,0:T(8,128)(2,1)S(1)}) custom-call(f32[3,1024]{1,0:T(4,128)S(1)} %collective-permute-done.20.refs_0_, f32[3,1024]{1,0:T(4,128)S(1)} %collective-permute-done.21.refs_1_, ...), custom_call_target="tpu_custom_call" | custom-call | flops 1358954496 | bytes 4000000 | tf_op jit(solution)/shard_map/pallas_call | solution.py:672
  60.1 1.3 %collective-permute-done.26.refs_1_ = bf16[1536,128]{1,0:T(8,128)(2,1)S(1)} collective-permute-done((bf16[1536,128]{1,0:T(8,128)(2,1)S(1)}, bf16[1536,128]{1,0:T(8,128)(2,1)S(1)}, u32[]{:S(2)}, u32[]{:S(2)}) %collective-permute-start.26) | collective-permute-done | bytes 393248 | tf_op jit(solution)/shard_map/ppermute | solution.py:779
  63.7 2.0 %collective-permute-done.29.refs_2_ = f32[1,1024]{1,0:T(1,128)S(1)} collective-permute-done((f32[1,1024]{1,0:T(1,128)S(1)}, f32[1,1024]{1,0:T(1,128)S(1)}, u32[]{:S(2)}, u32[]{:S(2)}) %collective-permute-start.29) | collective-permute-done | bytes 4128 | tf_op jit(solution)/shard_map/ppermute | solution.py:820
  65.7 2.0 %collective-permute-done.27.refs_1_ = bf16[768,128]{1,0:T(8,128)(2,1)S(1)} collective-permute-done((bf16[768,128]{1,0:T(8,128)(2,1)S(1)}, bf16[768,128]{1,0:T(8,128)(2,1)S(1)}, u32[]{:S(2)}, u32[]{:S(2)}) %collective-permute-start.27) | collective-permute-done | bytes 196640 | tf_op jit(solution)/shard_map/ppermute | solution.py:782
  68.1 1.3 %collective-permute-start.31 = (bf16[192,128]{1,0:T(8,128)(2,1)S(1)}, bf16[192,128]{1,0:T(8,128)(2,1)S(1)}, u32[]{:S(2)}, u32[]{:S(2)}) collective-permute-start(bf16[192,128]{1,0:T(8,128)(2,1)S(1)} %get-tuple-element.109), channel_id=1, source_target_pairs={{16,0},{18,2},{20,4},{22,6},{24,8},{26,10},{28,12},{30,14},{0,16},... | collective-permute-start | bytes 147464 | tf_op jit(solution)/shard_map/ppermute | solution.py:785
  69.4 2.0 %collective-permute-start.32 = (bf16[192,128]{1,0:T(8,128)(2,1)S(1)}, bf16[192,128]{1,0:T(8,128)(2,1)S(1)}, u32[]{:S(2)}, u32[]{:S(2)}) collective-permute-start(bf16[192,128]{1,0:T(8,128)(2,1)S(1)} %get-tuple-element.110), channel_id=1, source_target_pairs={{24,0},{26,2},{28,4},{30,6},{16,8},{18,10},{20,12},{22,14},{8,16},... | collective-permute-start | bytes 147464 | tf_op jit(solution)/shard_map/ppermute | solution.py:785
  72.0 2.2 %collective-permute-done.32.refs_3_ = bf16[192,128]{1,0:T(8,128)(2,1)S(1)} collective-permute-done((bf16[192,128]{1,0:T(8,128)(2,1)S(1)}, bf16[192,128]{1,0:T(8,128)(2,1)S(1)}, u32[]{:S(2)}, u32[]{:S(2)}) %collective-permute-start.32) | collective-permute-done | bytes 49184 | tf_op jit(solution)/shard_map/ppermute | solution.py:785
  74.2 2.7 %collective-permute-start.35 = (bf16[192,128]{1,0:T(8,128)(2,1)S(1)}, bf16[192,128]{1,0:T(8,128)(2,1)S(1)}, u32[]{:S(2)}, u32[]{:S(2)}) collective-permute-start(bf16[192,128]{1,0:T(8,128)(2,1)S(1)} %shard_map.191.refs_0_), channel_id=1, source_target_pairs={{24,0},{26,2},{28,4},{30,6},{16,8},{18,10},{20,12},{22,14},{8,16},... | collective-permute-start | bytes 147464 | tf_op jit(solution)/shard_map/ppermute | solution.py:788
  79.0 1.7 %collective-permute-done.34.refs_2_ = bf16[192,128]{1,0:T(8,128)(2,1)S(1)} collective-permute-done((bf16[192,128]{1,0:T(8,128)(2,1)S(1)}, bf16[192,128]{1,0:T(8,128)(2,1)S(1)}, u32[]{:S(2)}, u32[]{:S(2)}) %collective-permute-start.34) | collective-permute-done | bytes 49184 | tf_op jit(solution)/shard_map/ppermute | solution.py:788
  83.4 8.1 %collective-permute-start.39 = (f32[2,512]{1,0:T(2,128)S(1)}, f32[2,512]{1,0:T(2,128)S(1)}, u32[]{:S(2)}, u32[]{:S(2)}) collective-permute-start(f32[2,512]{1,0:T(2,128)S(1)} %shard_map.189.refs_2_), channel_id=1, source_target_pairs={{0,0},{2,2},{10,4},{8,6},{16,8},{18,10},{26,12},{24,14},{28,16},{3... | collective-permute-start | bytes 12296 | tf_op jit(solution)/shard_map/ppermute | solution.py:928
  91.6 1.3 %collective-permute-done.39.refs_4_.refs_1_ = f32[2,512]{1,0:T(2,128)S(1)} collective-permute-done((f32[2,512]{1,0:T(2,128)S(1)}, f32[2,512]{1,0:T(2,128)S(1)}, u32[]{:S(2)}, u32[]{:S(2)}) %collective-permute-start.39) | collective-permute-done | bytes 4128 | tf_op jit(solution)/shard_map/ppermute | solution.py:928
  94.0 2.2 %shard_map.194 = (f32[2,64,64,81]{3,2,1,0:T(8,128)}, f32[2,2,64,81]{3,2,1,0:T(8,128)}, f32[2,64,81]{2,1,0:T(8,128)}) custom-call(bf16[3072,128]{1,0:T(8,128)(2,1)S(1)} %shard_map.193.refs_0_), custom_call_target="tpu_custom_call" | custom-call | flops 1000000000 | bytes 4000000 | tf_op jit(solution)/shard_map/pallas_call | solution.py:672
  96.2 2.8 %shard_map.195 = (f32[2,64]{1,0:T(2,128)}, f32[2,64]{1,0:T(2,128)}, f32[2,2]{1,0:T(2,128)}, f32[1,1]{1,0:T(1,128)}, f32[1,4,4,32]{3,2,1,0:T(4,128)}, /*index=5*/...) custom-call(bf16[3072,128]{1,0:T(8,128)(2,1)S(1)} %collective-permut, ...), custom_call_target="tpu_custom_call", output_to_operand_aliasing={{6}: (2, {}), {7}: (3, {}), {8}: (4, {})} | custom-call | flops 1000000000 | bytes 4000000 | tf_op jit(solution)/shard_map/pallas_call | solution.py:672
  (94 shorter events, 20.5 us)
Async XLA Ops:
  0.7 9.5 %collective-permute-start.1 = (f32[1,4,4,32]{3,2,1,0:T(4,128)}, f32[1,4,4,32]{3,2,1,0:T(4,128)S(1)}, u32[]{:S(2)}, u32[]{:S(2)}) collective-permute-start(f32[1,4,4,32]{3,2,1,0:T(4,128)} %param.11), channel_id=1, source_target_pairs={{1,0},{0,1},{3,2},{2,3},{5,10},{4,11},{7,8},{6,9},{9,16},{8,17},{1... | collective-permute-start | bytes 6152 | tf_op jit(solution)/shard_map/ppermute | solution.py:825
  3.4 7.0 %collective-permute-start = (f32[1,4,4,32]{3,2,1,0:T(4,128)}, f32[1,4,4,32]{3,2,1,0:T(4,128)S(1)}, u32[]{:S(2)}, u32[]{:S(2)}) collective-permute-start(f32[1,4,4,32]{3,2,1,0:T(4,128)} %param.11), channel_id=1, source_target_pairs={{0,0},{1,1},{2,2},{3,3},{4,10},{5,11},{6,8},{7,9},{8,16},{9,17},{1... | collective-permute-start | bytes 6152 | tf_op jit(solution)/shard_map/ppermute | solution.py:825
  10.5 4.9 %collective-permute-start.7 = (f32[1,1024]{1,0:T(1,128)S(1)}, f32[1,1024]{1,0:T(1,128)S(1)}, u32[]{:S(2)}, u32[]{:S(2)}) collective-permute-start(f32[1,1024]{1,0:T(1,128)S(1)} %shard_map.179.refs_3_), channel_id=1, source_target_pairs={{8,0},{16,2},{18,10},{26,8},{24,16},{28,18},{30,26},{22,24},{20,28... | collective-permute-start | bytes 12296 | tf_op jit(solution)/shard_map/ppermute | solution.py:820
  10.6 6.4 %collective-permute-start.6 = (f32[1,1024]{1,0:T(1,128)S(1)}, f32[1,1024]{1,0:T(1,128)S(1)}, u32[]{:S(2)}, u32[]{:S(2)}) collective-permute-start(f32[1,1024]{1,0:T(1,128)S(1)} %shard_map.179.refs_3_), channel_id=1, source_target_pairs={{10,0},{8,2},{16,10},{18,8},{26,16},{24,18},{28,26},{30,24},{22,28... | collective-permute-start | bytes 12296 | tf_op jit(solution)/shard_map/ppermute | solution.py:820
  13.2 3.8 %collective-permute-start.5 = (f32[1,1024]{1,0:T(1,128)S(1)}, f32[1,1024]{1,0:T(1,128)S(1)}, u32[]{:S(2)}, u32[]{:S(2)}) collective-permute-start(f32[1,1024]{1,0:T(1,128)S(1)} %shard_map.179.refs_3_), channel_id=1, source_target_pairs={{2,0},{10,2},{8,10},{16,8},{18,16},{26,18},{24,26},{28,24},{30,28}... | collective-permute-start | bytes 12296 | tf_op jit(solution)/shard_map/ppermute | solution.py:820
  13.2 3.8 %collective-permute-start.4 = (f32[1,1024]{1,0:T(1,128)S(1)}, f32[1,1024]{1,0:T(1,128)S(1)}, u32[]{:S(2)}, u32[]{:S(2)}) collective-permute-start(f32[1,1024]{1,0:T(1,128)S(1)} %shard_map.179.refs_3_), channel_id=1, source_target_pairs={{4,0},{0,2},{2,10},{10,8},{8,16},{16,18},{18,26},{26,24},{24,28},{... | collective-permute-start | bytes 12296 | tf_op jit(solution)/shard_map/ppermute | solution.py:820
  15.4 4.0 %collective-permute-start.2 = (f32[1,1024]{1,0:T(1,128)S(1)}, f32[1,1024]{1,0:T(1,128)S(1)}, u32[]{:S(2)}, u32[]{:S(2)}) collective-permute-start(f32[1,1024]{1,0:T(1,128)S(1)} %shard_map.179.refs_3_), channel_id=1, source_target_pairs={{14,0},{6,2},{4,10},{0,8},{2,16},{10,18},{8,26},{16,24},{18,28},{2... | collective-permute-start | bytes 12296 | tf_op jit(solution)/shard_map/ppermute | solution.py:820
  25.7 6.1 %collective-permute-start.12 = (f32[2,1024]{1,0:T(2,128)S(1)}, f32[2,1024]{1,0:T(2,128)S(1)}, u32[]{:S(2)}, u32[]{:S(2)}) collective-permute-start(f32[2,1024]{1,0:T(2,128)S(1)} %get-tuple-element.73.refs_3_), channel_id=1, source_target_pairs={{10,0},{8,2},{16,10},{18,8},{26,16},{24,18},{28,26},{30,24},{22,28... | collective-permute-start | bytes 24584 | tf_op jit(solution)/shard_map/ppermute | solution.py:820
  26.2 5.5 %collective-permute-start.11 = (f32[2,1024]{1,0:T(2,128)S(1)}, f32[2,1024]{1,0:T(2,128)S(1)}, u32[]{:S(2)}, u32[]{:S(2)}) collective-permute-start(f32[2,1024]{1,0:T(2,128)S(1)} %get-tuple-element.73.refs_3_), channel_id=1, source_target_pairs={{2,0},{10,2},{8,10},{16,8},{18,16},{26,18},{24,26},{28,24},{30,28}... | collective-permute-start | bytes 24584 | tf_op jit(solution)/shard_map/ppermute | solution.py:820
  26.4 5.4 %collective-permute-start.10 = (f32[2,1024]{1,0:T(2,128)S(1)}, f32[2,1024]{1,0:T(2,128)S(1)}, u32[]{:S(2)}, u32[]{:S(2)}) collective-permute-start(f32[2,1024]{1,0:T(2,128)S(1)} %get-tuple-element.73.refs_3_), channel_id=1, source_target_pairs={{4,0},{0,2},{2,10},{10,8},{8,16},{16,18},{18,26},{26,24},{24,28},{... | collective-permute-start | bytes 24584 | tf_op jit(solution)/shard_map/ppermute | solution.py:820
  26.7 5.0 %collective-permute-start.9 = (f32[2,1024]{1,0:T(2,128)S(1)}, f32[2,1024]{1,0:T(2,128)S(1)}, u32[]{:S(2)}, u32[]{:S(2)}) collective-permute-start(f32[2,1024]{1,0:T(2,128)S(1)} %get-tuple-element.73.refs_3_), channel_id=1, source_target_pairs={{6,0},{4,2},{0,10},{2,8},{10,16},{8,18},{16,26},{18,24},{26,28},{2... | collective-permute-start | bytes 24584 | tf_op jit(solution)/shard_map/ppermute | solution.py:820
  28.1 4.0 %collective-permute-start.8 = (f32[2,1024]{1,0:T(2,128)S(1)}, f32[2,1024]{1,0:T(2,128)S(1)}, u32[]{:S(2)}, u32[]{:S(2)}) collective-permute-start(f32[2,1024]{1,0:T(2,128)S(1)} %get-tuple-element.73.refs_3_), channel_id=1, source_target_pairs={{14,0},{6,2},{4,10},{0,8},{2,16},{10,18},{8,26},{16,24},{18,28},{2... | collective-permute-start | bytes 24584 | tf_op jit(solution)/shard_map/ppermute | solution.py:820
  37.8 5.7 %collective-permute-start.18 = (f32[2,1024]{1,0:T(2,128)S(1)}, f32[2,1024]{1,0:T(2,128)S(1)}, u32[]{:S(2)}, u32[]{:S(2)}) collective-permute-start(f32[2,1024]{1,0:T(2,128)S(1)} %get-tuple-element.78.refs_3_), channel_id=1, source_target_pairs={{10,0},{8,2},{16,10},{18,8},{26,16},{24,18},{28,26},{30,24},{22,28... | collective-permute-start | bytes 24584 | tf_op jit(solution)/shard_map/ppermute | solution.py:820
  38.3 5.2 %collective-permute-start.17 = (f32[2,1024]{1,0:T(2,128)S(1)}, f32[2,1024]{1,0:T(2,128)S(1)}, u32[]{:S(2)}, u32[]{:S(2)}) collective-permute-start(f32[2,1024]{1,0:T(2,128)S(1)} %get-tuple-element.78.refs_3_), channel_id=1, source_target_pairs={{2,0},{10,2},{8,10},{16,8},{18,16},{26,18},{24,26},{28,24},{30,28}... | collective-permute-start | bytes 24584 | tf_op jit(solution)/shard_map/ppermute | solution.py:820
  38.8 4.7 %collective-permute-start.16 = (f32[2,1024]{1,0:T(2,128)S(1)}, f32[2,1024]{1,0:T(2,128)S(1)}, u32[]{:S(2)}, u32[]{:S(2)}) collective-permute-start(f32[2,1024]{1,0:T(2,128)S(1)} %get-tuple-element.78.refs_3_), channel_id=1, source_target_pairs={{4,0},{0,2},{2,10},{10,8},{8,16},{16,18},{18,26},{26,24},{24,28},{... | collective-permute-start | bytes 24584 | tf_op jit(solution)/shard_map/ppermute | solution.py:820
  38.8 4.7 %collective-permute-start.15 = (f32[2,1024]{1,0:T(2,128)S(1)}, f32[2,1024]{1,0:T(2,128)S(1)}, u32[]{:S(2)}, u32[]{:S(2)}) collective-permute-start(f32[2,1024]{1,0:T(2,128)S(1)} %get-tuple-element.78.refs_3_), channel_id=1, source_target_pairs={{6,0},{4,2},{0,10},{2,8},{10,16},{8,18},{16,26},{18,24},{26,28},{2... | collective-permute-start | bytes 24584 | tf_op jit(solution)/shard_map/ppermute | solution.py:820
  40.1 4.0 %collective-permute-start.14 = (f32[2,1024]{1,0:T(2,128)S(1)}, f32[2,1024]{1,0:T(2,128)S(1)}, u32[]{:S(2)}, u32[]{:S(2)}) collective-permute-start(f32[2,1024]{1,0:T(2,128)S(1)} %get-tuple-element.78.refs_3_), channel_id=1, source_target_pairs={{14,0},{6,2},{4,10},{0,8},{2,16},{10,18},{8,26},{16,24},{18,28},{2... | collective-permute-start | bytes 24584 | tf_op jit(solution)/shard_map/ppermute | solution.py:820
  48.1 6.6 %collective-permute-start.24 = (f32[3,1024]{1,0:T(4,128)S(1)}, f32[3,1024]{1,0:T(4,128)S(1)}, u32[]{:S(2)}, u32[]{:S(2)}) collective-permute-start(f32[3,1024]{1,0:T(4,128)S(1)} %get-tuple-element.86.refs_3_), channel_id=1, source_target_pairs={{10,0},{8,2},{16,10},{18,8},{26,16},{24,18},{28,26},{30,24},{22,28... | collective-permute-start | bytes 36872 | tf_op jit(solution)/shard_map/ppermute | solution.py:820
  48.3 6.3 %collective-permute-start.23 = (f32[3,1024]{1,0:T(4,128)S(1)}, f32[3,1024]{1,0:T(4,128)S(1)}, u32[]{:S(2)}, u32[]{:S(2)}) collective-permute-start(f32[3,1024]{1,0:T(4,128)S(1)} %get-tuple-element.86.refs_3_), channel_id=1, source_target_pairs={{2,0},{10,2},{8,10},{16,8},{18,16},{26,18},{24,26},{28,24},{30,28}... | collective-permute-start | bytes 36872 | tf_op jit(solution)/shard_map/ppermute | solution.py:820
  49.9 4.8 %collective-permute-start.22 = (f32[3,1024]{1,0:T(4,128)S(1)}, f32[3,1024]{1,0:T(4,128)S(1)}, u32[]{:S(2)}, u32[]{:S(2)}) collective-permute-start(f32[3,1024]{1,0:T(4,128)S(1)} %get-tuple-element.86.refs_3_), channel_id=1, source_target_pairs={{4,0},{0,2},{2,10},{10,8},{8,16},{16,18},{18,26},{26,24},{24,28},{... | collective-permute-start | bytes 36872 | tf_op jit(solution)/shard_map/ppermute | solution.py:820
  49.9 4.8 %collective-permute-start.21 = (f32[3,1024]{1,0:T(4,128)S(1)}, f32[3,1024]{1,0:T(4,128)S(1)}, u32[]{:S(2)}, u32[]{:S(2)}) collective-permute-start(f32[3,1024]{1,0:T(4,128)S(1)} %get-tuple-element.86.refs_3_), channel_id=1, source_target_pairs={{6,0},{4,2},{0,10},{2,8},{10,16},{8,18},{16,26},{18,24},{26,28},{2... | collective-permute-start | bytes 36872 | tf_op jit(solution)/shard_map/ppermute | solution.py:820
  50.4 4.3 %collective-permute-start.20 = (f32[3,1024]{1,0:T(4,128)S(1)}, f32[3,1024]{1,0:T(4,128)S(1)}, u32[]{:S(2)}, u32[]{:S(2)}) collective-permute-start(f32[3,1024]{1,0:T(4,128)S(1)} %get-tuple-element.86.refs_3_), channel_id=1, source_target_pairs={{14,0},{6,2},{4,10},{0,8},{2,16},{10,18},{8,26},{16,24},{18,28},{2... | collective-permute-start | bytes 36872 | tf_op jit(solution)/shard_map/ppermute | solution.py:820
  61.6 6.2 %collective-permute-start.27 = (bf16[768,128]{1,0:T(8,128)(2,1)S(1)}, bf16[768,128]{1,0:T(8,128)(2,1)S(1)}, u32[]{:S(2)}, u32[]{:S(2)}) collective-permute-start(bf16[768,128]{1,0:T(8,128)(2,1)S(1)} %get-tuple-element.103), channel_id=1, source_target_pairs={{4,0},{6,2},{0,4},{2,6},{12,8},{14,10},{8,12},{10,14},{20,16},{22,... | collective-permute-start | bytes 589832 | tf_op jit(solution)/shard_map/ppermute | solution.py:782
  68.1 3.8 %collective-permute-start.31 = (bf16[192,128]{1,0:T(8,128)(2,1)S(1)}, bf16[192,128]{1,0:T(8,128)(2,1)S(1)}, u32[]{:S(2)}, u32[]{:S(2)}) collective-permute-start(bf16[192,128]{1,0:T(8,128)(2,1)S(1)} %get-tuple-element.109), channel_id=1, source_target_pairs={{16,0},{18,2},{20,4},{22,6},{24,8},{26,10},{28,12},{30,14},{0,16},... | collective-permute-start | bytes 147464 | tf_op jit(solution)/shard_map/ppermute | solution.py:785
  69.4 4.7 %collective-permute-start.32 = (bf16[192,128]{1,0:T(8,128)(2,1)S(1)}, bf16[192,128]{1,0:T(8,128)(2,1)S(1)}, u32[]{:S(2)}, u32[]{:S(2)}) collective-permute-start(bf16[192,128]{1,0:T(8,128)(2,1)S(1)} %get-tuple-element.110), channel_id=1, source_target_pairs={{24,0},{26,2},{28,4},{30,6},{16,8},{18,10},{20,12},{22,14},{8,16},... | collective-permute-start | bytes 147464 | tf_op jit(solution)/shard_map/ppermute | solution.py:785
  74.2 4.8 %collective-permute-start.35 = (bf16[192,128]{1,0:T(8,128)(2,1)S(1)}, bf16[192,128]{1,0:T(8,128)(2,1)S(1)}, u32[]{:S(2)}, u32[]{:S(2)}) collective-permute-start(bf16[192,128]{1,0:T(8,128)(2,1)S(1)} %shard_map.191.refs_0_), channel_id=1, source_target_pairs={{24,0},{26,2},{28,4},{30,6},{16,8},{18,10},{20,12},{22,14},{8,16},... | collective-permute-start | bytes 147464 | tf_op jit(solution)/shard_map/ppermute | solution.py:788
  76.9 3.8 %collective-permute-start.34 = (bf16[192,128]{1,0:T(8,128)(2,1)S(1)}, bf16[192,128]{1,0:T(8,128)(2,1)S(1)}, u32[]{:S(2)}, u32[]{:S(2)}) collective-permute-start(bf16[192,128]{1,0:T(8,128)(2,1)S(1)} %shard_map.191.refs_0_), channel_id=1, source_target_pairs={{16,0},{18,2},{20,4},{22,6},{24,8},{26,10},{28,12},{30,14},{0,16},... | collective-permute-start | bytes 147464 | tf_op jit(solution)/shard_map/ppermute | solution.py:788
  76.9 3.8 %collective-permute-start.33 = (bf16[192,128]{1,0:T(8,128)(2,1)S(1)}, bf16[192,128]{1,0:T(8,128)(2,1)S(1)}, u32[]{:S(2)}, u32[]{:S(2)}) collective-permute-start(bf16[192,128]{1,0:T(8,128)(2,1)S(1)} %shard_map.191.refs_0_), channel_id=1, source_target_pairs={{8,0},{10,2},{12,4},{14,6},{0,8},{2,10},{4,12},{6,14},{24,16},{26,... | collective-permute-start | bytes 147464 | tf_op jit(solution)/shard_map/ppermute | solution.py:788
  80.7 12.1 %collective-permute-start.38 = (bf16[768,128]{1,0:T(8,128)(2,1)S(1)}, bf16[768,128]{1,0:T(8,128)(2,1)S(1)}, u32[]{:S(2)}, u32[]{:S(2)}) collective-permute-start(bf16[768,128]{1,0:T(8,128)(2,1)S(1)} %shard_map.192.refs_0_), channel_id=1, source_target_pairs={{5,0},{4,1},{7,2},{6,3},{1,4},{0,5},{3,6},{2,7},{13,8},{12,9},{15,... | collective-permute-start | bytes 589832 | tf_op jit(solution)/shard_map/ppermute | solution.py:800
  81.7 11.1 %collective-permute-start.37 = (bf16[768,128]{1,0:T(8,128)(2,1)S(1)}, bf16[768,128]{1,0:T(8,128)(2,1)S(1)}, u32[]{:S(2)}, u32[]{:S(2)}) collective-permute-start(bf16[768,128]{1,0:T(8,128)(2,1)S(1)} %shard_map.192.refs_0_), channel_id=1, source_target_pairs={{1,0},{0,1},{3,2},{2,3},{5,4},{4,5},{7,6},{6,7},{9,8},{8,9},{11,10... | collective-permute-start | bytes 589832 | tf_op jit(solution)/shard_map/ppermute | solution.py:800
  82.9 10.0 %collective-permute-start.36 = (bf16[768,128]{1,0:T(8,128)(2,1)S(1)}, bf16[768,128]{1,0:T(8,128)(2,1)S(1)}, u32[]{:S(2)}, u32[]{:S(2)}) collective-permute-start(bf16[768,128]{1,0:T(8,128)(2,1)S(1)} %shard_map.192.refs_0_), channel_id=1, source_target_pairs={{4,0},{5,1},{6,2},{7,3},{0,4},{1,5},{2,6},{3,7},{12,8},{13,9},{14,... | collective-permute-start | bytes 589832 | tf_op jit(solution)/shard_map/ppermute | solution.py:800
  83.4 9.4 %collective-permute-start.39 = (f32[2,512]{1,0:T(2,128)S(1)}, f32[2,512]{1,0:T(2,128)S(1)}, u32[]{:S(2)}, u32[]{:S(2)}) collective-permute-start(f32[2,512]{1,0:T(2,128)S(1)} %shard_map.189.refs_2_), channel_id=1, source_target_pairs={{0,0},{2,2},{10,4},{8,6},{16,8},{18,10},{26,12},{24,14},{28,16},{3... | collective-permute-start | bytes 12296 | tf_op jit(solution)/shard_map/ppermute | solution.py:928
  (20 other events, 140.5 us)

commit v8 on v7

--- a/solution.py
+++ b/solution.py
@@ -17,6 +17,7 @@
 BF = jnp.bfloat16
 F32 = jnp.float32
 TAPS = 81
+TAP_ROWS = 88
 VMEM_MB = 20
 CHUNK = 512
 
@@ -709,7 +710,7 @@
 def pack_ahead(layer, w_mid, after=()):
     channels = w_mid.shape[1]
     outs = [shape((9 * channels, 9 * channels), BF)]
-    scratch = [pltpu.VMEM((TAPS * channels // 2, 2 * channels), F32)]
+    scratch = [pltpu.VMEM((TAP_ROWS * channels // 2, 2 * channels), F32)]
     body = functools.partial(pack_ahead_kernel, layer)
     return kernel_call(body, outs, scratch, [w_mid, *after], 1_000_000_000, loose=after)[0]
 
@@ -747,7 +748,7 @@
     ]
     scratch = [
         pltpu.VMEM((2, 2 * halves * depth * chunk, 128), BF),
-        pltpu.VMEM((TAPS * few // 2, 2 * channels), F32),
+        pltpu.VMEM((TAP_ROWS * few // 2, 2 * channels), F32),
         pltpu.VMEM((2, few, channels, TAPS), F32),
         pltpu.VMEM((2, channels, TAPS), F32),
         pltpu.VMEM((2, few, TAPS), F32),

time: 100 us -> 100 us (level)
  no operation moved by 1% of the time
where the time goes in v8:
time: 100 us; the launch traced here: 99.2 us
  starting transfers between devices  51.3 us (51%)
  Pallas kernels  28.5 us (28%)
  waiting for transfers between devices  16.6 us (17%)
  local copies, waits for them, and re-layouts  1.65 us (2%)
  between operations  1.21 us (1%)
    pallas_call x18, Pallas kernels, kernel_call(): pl.pallas_call(whole, out_shape=tuple(outs), in_specs=[spec(a) for a in a...  28.5 us
    ppermute x26, starting transfers between devices, step(): lax.ppermute(values, 'xy', [(order[(p + offset) % count], order[p]) for p...  24.3 us
    ppermute x1, starting transfers between devices, per_device(): force = lax.ppermute(force, 'xy', [(order[p], p) for p in range(count)])  8.14 us
    ppermute x2, starting transfers between devices, per_device(): lax.ppermute(noise, ('xy', 'gz'), [(p * halves + (j + rel) % halves, orde...  6.25 us
    ppermute x26, waiting for transfers between devices, step(): lax.ppermute(values, 'xy', [(order[(p + offset) % count], order[p]) for p...  5.98 us
    ppermute x3, starting transfers between devices, gather(): lax.ppermute(v, 'xy', xy(lambda a, s=s: a ^ 4 * s))  3.61 us
    ppermute x3, starting transfers between devices, scatter(): lax.ppermute(pieces[s], 'xy', xy(lambda a, s=s: a ^ 4 * s))  3.61 us
    ppermute x3, waiting for transfers between devices, gather(): lax.ppermute(v, 'xy', xy(lambda a, s=s: a ^ 4 * s))  2.91 us
  transfers between devices with their start and end apart: 41, of which 13 were waited for; matrix products, arithmetic and copies ran while one was open for 0% of the time, Pallas kernels for 9%

profile of v8, /device:TPU:5, one launch (start us, length us, event | category | flops | bytes accessed | tf_op | source)
XLA Modules:
  0.0 99.2 jit_solution(13979950546010476211)
XLA Ops:
  0.7 2.8 %collective-permute-start.1 = (f32[1,4,4,32]{3,2,1,0:T(4,128)}, f32[1,4,4,32]{3,2,1,0:T(4,128)S(1)}, u32[]{:S(2)}, u32[]{:S(2)}) collective-permute-start(f32[1,4,4,32]{3,2,1,0:T(4,128)} %param.11), channel_id=1, source_target_pairs={{1,0},{0,1},{3,2},{2,3},{5,10},{4,11},{7,8},{6,9},{9,16},{8,17},{1... | collective-permute-start | bytes 6152 | tf_op jit(solution)/shard_map/ppermute | solution.py:826
  3.4 3.5 %collective-permute-start = (f32[1,4,4,32]{3,2,1,0:T(4,128)}, f32[1,4,4,32]{3,2,1,0:T(4,128)S(1)}, u32[]{:S(2)}, u32[]{:S(2)}) collective-permute-start(f32[1,4,4,32]{3,2,1,0:T(4,128)} %param.11), channel_id=1, source_target_pairs={{0,0},{1,1},{2,2},{3,3},{4,10},{5,11},{6,8},{7,9},{8,16},{9,17},{1... | collective-permute-start | bytes 6152 | tf_op jit(solution)/shard_map/ppermute | solution.py:826
  6.9 1.6 %copy-done = bf16[2,81,64,64]{1,3,2,0:T(8,128)(2,1)S(1)} copy-done((bf16[2,81,64,64]{1,3,2,0:T(8,128)(2,1)S(1)}, bf16[2,81,64,64]{1,3,2,0:T(8,128)(2,1)}, u32[]{:S(2)}) %copy-start) | copy-done | bytes 1327128
  8.5 1.6 %shard_map.178.refs_2_.refs_8_.refs_0_ = bf16[576,576]{1,0:T(8,128)(2,1)S(1)} custom-call(bf16[2,64,64,81]{3,2,1,0:T(8,128)(2,1)S(1)} %bitcast.19), custom_call_target="tpu_custom_call" | custom-call | flops 1000000000 | bytes 4000000 | tf_op jit(solution)/shard_map/pallas_call | solution.py:673
  10.6 2.7 %collective-permute-start.6 = (f32[1,1024]{1,0:T(1,128)S(1)}, f32[1,1024]{1,0:T(1,128)S(1)}, u32[]{:S(2)}, u32[]{:S(2)}) collective-permute-start(f32[1,1024]{1,0:T(1,128)S(1)} %shard_map.179.refs_3_), channel_id=1, source_target_pairs={{10,0},{8,2},{16,10},{18,8},{26,16},{24,18},{28,26},{30,24},{22,28... | collective-permute-start | bytes 12296 | tf_op jit(solution)/shard_map/ppermute | solution.py:821
  13.7 1.6 %collective-permute-start.3 = (f32[1,1024]{1,0:T(1,128)S(1)}, f32[1,1024]{1,0:T(1,128)S(1)}, u32[]{:S(2)}, u32[]{:S(2)}) collective-permute-start(f32[1,1024]{1,0:T(1,128)S(1)} %shard_map.179.refs_3_), channel_id=1, source_target_pairs={{6,0},{4,2},{0,10},{2,8},{10,16},{8,18},{16,26},{18,24},{26,28},{2... | collective-permute-start | bytes 12296 | tf_op jit(solution)/shard_map/ppermute | solution.py:821
  17.0 2.4 %collective-permute-done.2.refs_0_ = f32[1,1024]{1,0:T(1,128)S(1)} collective-permute-done((f32[1,1024]{1,0:T(1,128)S(1)}, f32[1,1024]{1,0:T(1,128)S(1)}, u32[]{:S(2)}, u32[]{:S(2)}) %collective-permute-start.2) | collective-permute-done | bytes 4128 | tf_op jit(solution)/shard_map/ppermute | solution.py:821
  19.4 5.0 %shard_map.181 = (f32[8,1024]{1,0:T(8,128)S(1)}, f32[2,1024]{1,0:T(2,128)S(1)}, f32[1,1024]{1,0:T(1,128)}, f32[1,128]{1,0:T(1,128)S(1)}, bf16[192,1024]{1,0:T(8,128)(2,1)S(1)}, /*index=5*/bf16[192,1024]{1,0:T(8,128)(2,1)S(1)}) custom-call(f32[1,1024]{1,0:T(1,128)S(1)} %collective-permute-done.2.refs_0_, f32[1,1024]{1,0:T(1,128)S(1)} %collective-permute-done.3.refs_1_, ...), custom_call_target="tpu_custom_call" | custom-call | flops 2038431744 | bytes 4000000 | tf_op jit(solution)/shard_map/pallas_call | solution.py:673
  24.4 1.3 %collective-permute-start.13 = (f32[2,1024]{1,0:T(2,128)S(1)}, f32[2,1024]{1,0:T(2,128)S(1)}, u32[]{:S(2)}, u32[]{:S(2)}) collective-permute-start(f32[2,1024]{1,0:T(2,128)S(1)} %get-tuple-element.73.refs_3_), channel_id=1, source_target_pairs={{8,0},{16,2},{18,10},{26,8},{24,16},{28,18},{30,26},{22,24},{20,28... | collective-permute-start | bytes 24584 | tf_op jit(solution)/shard_map/ppermute | solution.py:821
  26.7 1.3 %collective-permute-start.9 = (f32[2,1024]{1,0:T(2,128)S(1)}, f32[2,1024]{1,0:T(2,128)S(1)}, u32[]{:S(2)}, u32[]{:S(2)}) collective-permute-start(f32[2,1024]{1,0:T(2,128)S(1)} %get-tuple-element.73.refs_3_), channel_id=1, source_target_pairs={{6,0},{4,2},{0,10},{2,8},{10,16},{8,18},{16,26},{18,24},{26,28},{2... | collective-permute-start | bytes 24584 | tf_op jit(solution)/shard_map/ppermute | solution.py:821
  28.1 2.0 %collective-permute-start.8 = (f32[2,1024]{1,0:T(2,128)S(1)}, f32[2,1024]{1,0:T(2,128)S(1)}, u32[]{:S(2)}, u32[]{:S(2)}) collective-permute-start(f32[2,1024]{1,0:T(2,128)S(1)} %get-tuple-element.73.refs_3_), channel_id=1, source_target_pairs={{14,0},{6,2},{4,10},{0,8},{2,16},{10,18},{8,26},{16,24},{18,28},{2... | collective-permute-start | bytes 24584 | tf_op jit(solution)/shard_map/ppermute | solution.py:821
  30.1 1.6 %shard_map.182.refs_8_.refs_1_ = bf16[576,576]{1,0:T(8,128)(2,1)S(1)} custom-call(bf16[2,64,64,81]{3,2,1,0:T(8,128)(2,1)S(1)} %bitcast.20, f32[1,128]{1,0:T(1,128)S(1)} %get-tuple-element.75.refs_1_.refs_7_), custom_call_target="tpu_custom_call" | custom-call | flops 1000000000 | bytes 4000000 | tf_op jit(solution)/shard_map/pallas_call | solution.py:673
  32.1 4.4 %shard_map.183 = (f32[8,1024]{1,0:T(8,128)S(1)}, f32[2,1024]{1,0:T(2,128)S(1)}, f32[1,1024]{1,0:T(1,128)S(1)}, f32[1,128]{1,0:T(1,128)S(1)}, f32[8,1024]{1,0:T(8...) custom-call(f32[2,1024]{1,0:T(2,128)S(1)} %collective-permute-done.8.refs_0_, ...), custom_call_target="tpu_custom_call" | custom-call | flops 2038431744 | bytes 4000000 | tf_op jit(solution)/shard_map/pallas_call | solution.py:673
  40.1 2.2 %collective-permute-start.14 = (f32[2,1024]{1,0:T(2,128)S(1)}, f32[2,1024]{1,0:T(2,128)S(1)}, u32[]{:S(2)}, u32[]{:S(2)}) collective-permute-start(f32[2,1024]{1,0:T(2,128)S(1)} %get-tuple-element.78.refs_3_), channel_id=1, source_target_pairs={{14,0},{6,2},{4,10},{0,8},{2,16},{10,18},{8,26},{16,24},{18,28},{2... | collective-permute-start | bytes 24584 | tf_op jit(solution)/shard_map/ppermute | solution.py:821
  44.1 2.6 %shard_map.185 = (f32[8,1024]{1,0:T(8,128)S(1)}, f32[3,1024]{1,0:T(4,128)S(1)}, f32[16,64]{1,0:T(8,128)S(1)}, f32[16,1024]{1,0:T(8,128)S(1)}, bf16[192,1024]{1,0...) custom-call(f32[2,1024]{1,0:T(2,128)S(1)} %collective-permute-done.14.refs_0_, f32[2,1024]{1,0:T(2,128)S(1)} %collective-permute-done.15.refs_1_, ...), custom_call_target="tpu_custom_call" | custom-call | flops 679477248 | bytes 4000000 | tf_op jit(solution)/shard_map/pallas_call | solution.py:673
  46.7 1.4 %collective-permute-start.25 = (f32[3,1024]{1,0:T(4,128)S(1)}, f32[3,1024]{1,0:T(4,128)S(1)}, u32[]{:S(2)}, u32[]{:S(2)}) collective-permute-start(f32[3,1024]{1,0:T(4,128)S(1)} %get-tuple-element.86.refs_3_), channel_id=1, source_target_pairs={{8,0},{16,2},{18,10},{26,8},{24,16},{28,18},{30,26},{22,24},{20,28... | collective-permute-start | bytes 36872 | tf_op jit(solution)/shard_map/ppermute | solution.py:821
  48.3 1.5 %collective-permute-start.23 = (f32[3,1024]{1,0:T(4,128)S(1)}, f32[3,1024]{1,0:T(4,128)S(1)}, u32[]{:S(2)}, u32[]{:S(2)}) collective-permute-start(f32[3,1024]{1,0:T(4,128)S(1)} %get-tuple-element.86.refs_3_), channel_id=1, source_target_pairs={{2,0},{10,2},{8,10},{16,8},{18,16},{26,18},{24,26},{28,24},{30,28}... | collective-permute-start | bytes 36872 | tf_op jit(solution)/shard_map/ppermute | solution.py:821
  50.4 2.2 %collective-permute-start.20 = (f32[3,1024]{1,0:T(4,128)S(1)}, f32[3,1024]{1,0:T(4,128)S(1)}, u32[]{:S(2)}, u32[]{:S(2)}) collective-permute-start(f32[3,1024]{1,0:T(4,128)S(1)} %get-tuple-element.86.refs_3_), channel_id=1, source_target_pairs={{14,0},{6,2},{4,10},{0,8},{2,16},{10,18},{8,26},{16,24},{18,28},{2... | collective-permute-start | bytes 36872 | tf_op jit(solution)/shard_map/ppermute | solution.py:821
  52.6 2.1 %shard_map.186.refs_11_ = bf16[3072,128]{1,0:T(8,128)(2,1)S(1)} custom-call(f32[8,1024]{1,0:T(8,128)S(1)} %get-tuple-element.80.refs_9_.refs_0_, bf16[192,1024]{1,0:T(8,128)(2,1)S(1)} %get-tuple-element.81.refs_10_.refs_1_, bf16[192,1024]{1,0:T(8,128)(2,1)S(1)} %get-tuple-element.82.refs_11_.refs_2_, f32[16,1024]{1,0:T(8,128)S(1)} %get-tuple-element.91.refs_3_, ...), custom_call_target="tpu_custom_call" | custom-call | flops 679477248 | bytes 4000000 | tf_op jit(solution)/shard_map/pallas_call | solution.py:673
  54.7 4.1 %shard_map.187 = (f32[1,1024]{1,0:T(1,128)S(1)}, f32[2,1024]{1,0:T(2,128)S(1)}, f32[1,1024]{1,0:T(1,128)S(1)}, bf16[1536,128]{1,0:T(8,128)(2,1)S(1)}, bf16[1536,128]{1,0:T(8,128)(2,1)S(1)}) custom-call(f32[3,1024]{1,0:T(4,128)S(1)} %collective-permute-done.20.refs_0_, f32[3,1024]{1,0:T(4,128)S(1)} %collective-permute-done.21.refs_1_, ...), custom_call_target="tpu_custom_call" | custom-call | flops 1358954496 | bytes 4000000 | tf_op jit(solution)/shard_map/pallas_call | solution.py:673
  60.1 1.3 %collective-permute-done.26.refs_1_ = bf16[1536,128]{1,0:T(8,128)(2,1)S(1)} collective-permute-done((bf16[1536,128]{1,0:T(8,128)(2,1)S(1)}, bf16[1536,128]{1,0:T(8,128)(2,1)S(1)}, u32[]{:S(2)}, u32[]{:S(2)}) %collective-permute-start.26) | collective-permute-done | bytes 393248 | tf_op jit(solution)/shard_map/ppermute | solution.py:780
  63.7 2.0 %collective-permute-done.29.refs_2_ = f32[1,1024]{1,0:T(1,128)S(1)} collective-permute-done((f32[1,1024]{1,0:T(1,128)S(1)}, f32[1,1024]{1,0:T(1,128)S(1)}, u32[]{:S(2)}, u32[]{:S(2)}) %collective-permute-start.29) | collective-permute-done | bytes 4128 | tf_op jit(solution)/shard_map/ppermute | solution.py:821
  65.7 2.0 %collective-permute-done.27.refs_1_ = bf16[768,128]{1,0:T(8,128)(2,1)S(1)} collective-permute-done((bf16[768,128]{1,0:T(8,128)(2,1)S(1)}, bf16[768,128]{1,0:T(8,128)(2,1)S(1)}, u32[]{:S(2)}, u32[]{:S(2)}) %collective-permute-start.27) | collective-permute-done | bytes 196640 | tf_op jit(solution)/shard_map/ppermute | solution.py:783
  68.1 1.3 %collective-permute-start.31 = (bf16[192,128]{1,0:T(8,128)(2,1)S(1)}, bf16[192,128]{1,0:T(8,128)(2,1)S(1)}, u32[]{:S(2)}, u32[]{:S(2)}) collective-permute-start(bf16[192,128]{1,0:T(8,128)(2,1)S(1)} %get-tuple-element.109), channel_id=1, source_target_pairs={{16,0},{18,2},{20,4},{22,6},{24,8},{26,10},{28,12},{30,14},{0,16},... | collective-permute-start | bytes 147464 | tf_op jit(solution)/shard_map/ppermute | solution.py:786
  69.4 2.0 %collective-permute-start.32 = (bf16[192,128]{1,0:T(8,128)(2,1)S(1)}, bf16[192,128]{1,0:T(8,128)(2,1)S(1)}, u32[]{:S(2)}, u32[]{:S(2)}) collective-permute-start(bf16[192,128]{1,0:T(8,128)(2,1)S(1)} %get-tuple-element.110), channel_id=1, source_target_pairs={{24,0},{26,2},{28,4},{30,6},{16,8},{18,10},{20,12},{22,14},{8,16},... | collective-permute-start | bytes 147464 | tf_op jit(solution)/shard_map/ppermute | solution.py:786
  72.0 2.2 %collective-permute-done.32.refs_3_ = bf16[192,128]{1,0:T(8,128)(2,1)S(1)} collective-permute-done((bf16[192,128]{1,0:T(8,128)(2,1)S(1)}, bf16[192,128]{1,0:T(8,128)(2,1)S(1)}, u32[]{:S(2)}, u32[]{:S(2)}) %collective-permute-start.32) | collective-permute-done | bytes 49184 | tf_op jit(solution)/shard_map/ppermute | solution.py:786
  74.2 2.7 %collective-permute-start.35 = (bf16[192,128]{1,0:T(8,128)(2,1)S(1)}, bf16[192,128]{1,0:T(8,128)(2,1)S(1)}, u32[]{:S(2)}, u32[]{:S(2)}) collective-permute-start(bf16[192,128]{1,0:T(8,128)(2,1)S(1)} %shard_map.191.refs_0_), channel_id=1, source_target_pairs={{24,0},{26,2},{28,4},{30,6},{16,8},{18,10},{20,12},{22,14},{8,16},... | collective-permute-start | bytes 147464 | tf_op jit(solution)/shard_map/ppermute | solution.py:789
  79.0 1.7 %collective-permute-done.34.refs_2_ = bf16[192,128]{1,0:T(8,128)(2,1)S(1)} collective-permute-done((bf16[192,128]{1,0:T(8,128)(2,1)S(1)}, bf16[192,128]{1,0:T(8,128)(2,1)S(1)}, u32[]{:S(2)}, u32[]{:S(2)}) %collective-permute-start.34) | collective-permute-done | bytes 49184 | tf_op jit(solution)/shard_map/ppermute | solution.py:789
  83.4 8.1 %collective-permute-start.39 = (f32[2,512]{1,0:T(2,128)S(1)}, f32[2,512]{1,0:T(2,128)S(1)}, u32[]{:S(2)}, u32[]{:S(2)}) collective-permute-start(f32[2,512]{1,0:T(2,128)S(1)} %shard_map.189.refs_2_), channel_id=1, source_target_pairs={{0,0},{2,2},{10,4},{8,6},{16,8},{18,10},{26,12},{24,14},{28,16},{3... | collective-permute-start | bytes 12296 | tf_op jit(solution)/shard_map/ppermute | solution.py:929
  91.6 1.3 %collective-permute-done.39.refs_4_.refs_1_ = f32[2,512]{1,0:T(2,128)S(1)} collective-permute-done((f32[2,512]{1,0:T(2,128)S(1)}, f32[2,512]{1,0:T(2,128)S(1)}, u32[]{:S(2)}, u32[]{:S(2)}) %collective-permute-start.39) | collective-permute-done | bytes 4128 | tf_op jit(solution)/shard_map/ppermute | solution.py:929
  94.0 2.2 %shard_map.194 = (f32[2,64,64,81]{3,2,1,0:T(8,128)}, f32[2,2,64,81]{3,2,1,0:T(8,128)}, f32[2,64,81]{2,1,0:T(8,128)}) custom-call(bf16[3072,128]{1,0:T(8,128)(2,1)S(1)} %shard_map.193.refs_0_), custom_call_target="tpu_custom_call" | custom-call | flops 1000000000 | bytes 4000000 | tf_op jit(solution)/shard_map/pallas_call | solution.py:673
  96.2 2.8 %shard_map.195 = (f32[2,64]{1,0:T(2,128)}, f32[2,64]{1,0:T(2,128)}, f32[2,2]{1,0:T(2,128)}, f32[1,1]{1,0:T(1,128)}, f32[1,4,4,32]{3,2,1,0:T(4,128)}, /*index=5*/...) custom-call(bf16[3072,128]{1,0:T(8,128)(2,1)S(1)} %collective-permut, ...), custom_call_target="tpu_custom_call", output_to_operand_aliasing={{6}: (2, {}), {7}: (3, {}), {8}: (4, {})} | custom-call | flops 1000000000 | bytes 4000000 | tf_op jit(solution)/shard_map/pallas_call | solution.py:673
  (94 shorter events, 20.5 us)
Async XLA Ops:
  0.7 9.5 %collective-permute-start.1 = (f32[1,4,4,32]{3,2,1,0:T(4,128)}, f32[1,4,4,32]{3,2,1,0:T(4,128)S(1)}, u32[]{:S(2)}, u32[]{:S(2)}) collective-permute-start(f32[1,4,4,32]{3,2,1,0:T(4,128)} %param.11), channel_id=1, source_target_pairs={{1,0},{0,1},{3,2},{2,3},{5,10},{4,11},{7,8},{6,9},{9,16},{8,17},{1... | collective-permute-start | bytes 6152 | tf_op jit(solution)/shard_map/ppermute | solution.py:826
  3.4 7.0 %collective-permute-start = (f32[1,4,4,32]{3,2,1,0:T(4,128)}, f32[1,4,4,32]{3,2,1,0:T(4,128)S(1)}, u32[]{:S(2)}, u32[]{:S(2)}) collective-permute-start(f32[1,4,4,32]{3,2,1,0:T(4,128)} %param.11), channel_id=1, source_target_pairs={{0,0},{1,1},{2,2},{3,3},{4,10},{5,11},{6,8},{7,9},{8,16},{9,17},{1... | collective-permute-start | bytes 6152 | tf_op jit(solution)/shard_map/ppermute | solution.py:826
  10.5 4.9 %collective-permute-start.7 = (f32[1,1024]{1,0:T(1,128)S(1)}, f32[1,1024]{1,0:T(1,128)S(1)}, u32[]{:S(2)}, u32[]{:S(2)}) collective-permute-start(f32[1,1024]{1,0:T(1,128)S(1)} %shard_map.179.refs_3_), channel_id=1, source_target_pairs={{8,0},{16,2},{18,10},{26,8},{24,16},{28,18},{30,26},{22,24},{20,28... | collective-permute-start | bytes 12296 | tf_op jit(solution)/shard_map/ppermute | solution.py:821
  10.6 6.4 %collective-permute-start.6 = (f32[1,1024]{1,0:T(1,128)S(1)}, f32[1,1024]{1,0:T(1,128)S(1)}, u32[]{:S(2)}, u32[]{:S(2)}) collective-permute-start(f32[1,1024]{1,0:T(1,128)S(1)} %shard_map.179.refs_3_), channel_id=1, source_target_pairs={{10,0},{8,2},{16,10},{18,8},{26,16},{24,18},{28,26},{30,24},{22,28... | collective-permute-start | bytes 12296 | tf_op jit(solution)/shard_map/ppermute | solution.py:821
  13.2 3.8 %collective-permute-start.5 = (f32[1,1024]{1,0:T(1,128)S(1)}, f32[1,1024]{1,0:T(1,128)S(1)}, u32[]{:S(2)}, u32[]{:S(2)}) collective-permute-start(f32[1,1024]{1,0:T(1,128)S(1)} %shard_map.179.refs_3_), channel_id=1, source_target_pairs={{2,0},{10,2},{8,10},{16,8},{18,16},{26,18},{24,26},{28,24},{30,28}... | collective-permute-start | bytes 12296 | tf_op jit(solution)/shard_map/ppermute | solution.py:821
  13.2 3.8 %collective-permute-start.4 = (f32[1,1024]{1,0:T(1,128)S(1)}, f32[1,1024]{1,0:T(1,128)S(1)}, u32[]{:S(2)}, u32[]{:S(2)}) collective-permute-start(f32[1,1024]{1,0:T(1,128)S(1)} %shard_map.179.refs_3_), channel_id=1, source_target_pairs={{4,0},{0,2},{2,10},{10,8},{8,16},{16,18},{18,26},{26,24},{24,28},{... | collective-permute-start | bytes 12296 | tf_op jit(solution)/shard_map/ppermute | solution.py:821
  15.4 4.0 %collective-permute-start.2 = (f32[1,1024]{1,0:T(1,128)S(1)}, f32[1,1024]{1,0:T(1,128)S(1)}, u32[]{:S(2)}, u32[]{:S(2)}) collective-permute-start(f32[1,1024]{1,0:T(1,128)S(1)} %shard_map.179.refs_3_), channel_id=1, source_target_pairs={{14,0},{6,2},{4,10},{0,8},{2,16},{10,18},{8,26},{16,24},{18,28},{2... | collective-permute-start | bytes 12296 | tf_op jit(solution)/shard_map/ppermute | solution.py:821
  25.7 6.1 %collective-permute-start.12 = (f32[2,1024]{1,0:T(2,128)S(1)}, f32[2,1024]{1,0:T(2,128)S(1)}, u32[]{:S(2)}, u32[]{:S(2)}) collective-permute-start(f32[2,1024]{1,0:T(2,128)S(1)} %get-tuple-element.73.refs_3_), channel_id=1, source_target_pairs={{10,0},{8,2},{16,10},{18,8},{26,16},{24,18},{28,26},{30,24},{22,28... | collective-permute-start | bytes 24584 | tf_op jit(solution)/shard_map/ppermute | solution.py:821
  26.2 5.5 %collective-permute-start.11 = (f32[2,1024]{1,0:T(2,128)S(1)}, f32[2,1024]{1,0:T(2,128)S(1)}, u32[]{:S(2)}, u32[]{:S(2)}) collective-permute-start(f32[2,1024]{1,0:T(2,128)S(1)} %get-tuple-element.73.refs_3_), channel_id=1, source_target_pairs={{2,0},{10,2},{8,10},{16,8},{18,16},{26,18},{24,26},{28,24},{30,28}... | collective-permute-start | bytes 24584 | tf_op jit(solution)/shard_map/ppermute | solution.py:821
  26.4 5.4 %collective-permute-start.10 = (f32[2,1024]{1,0:T(2,128)S(1)}, f32[2,1024]{1,0:T(2,128)S(1)}, u32[]{:S(2)}, u32[]{:S(2)}) collective-permute-start(f32[2,1024]{1,0:T(2,128)S(1)} %get-tuple-element.73.refs_3_), channel_id=1, source_target_pairs={{4,0},{0,2},{2,10},{10,8},{8,16},{16,18},{18,26},{26,24},{24,28},{... | collective-permute-start | bytes 24584 | tf_op jit(solution)/shard_map/ppermute | solution.py:821
  26.7 5.0 %collective-permute-start.9 = (f32[2,1024]{1,0:T(2,128)S(1)}, f32[2,1024]{1,0:T(2,128)S(1)}, u32[]{:S(2)}, u32[]{:S(2)}) collective-permute-start(f32[2,1024]{1,0:T(2,128)S(1)} %get-tuple-element.73.refs_3_), channel_id=1, source_target_pairs={{6,0},{4,2},{0,10},{2,8},{10,16},{8,18},{16,26},{18,24},{26,28},{2... | collective-permute-start | bytes 24584 | tf_op jit(solution)/shard_map/ppermute | solution.py:821
  28.1 4.0 %collective-permute-start.8 = (f32[2,1024]{1,0:T(2,128)S(1)}, f32[2,1024]{1,0:T(2,128)S(1)}, u32[]{:S(2)}, u32[]{:S(2)}) collective-permute-start(f32[2,1024]{1,0:T(2,128)S(1)} %get-tuple-element.73.refs_3_), channel_id=1, source_target_pairs={{14,0},{6,2},{4,10},{0,8},{2,16},{10,18},{8,26},{16,24},{18,28},{2... | collective-permute-start | bytes 24584 | tf_op jit(solution)/shard_map/ppermute | solution.py:821
  37.8 5.7 %collective-permute-start.18 = (f32[2,1024]{1,0:T(2,128)S(1)}, f32[2,1024]{1,0:T(2,128)S(1)}, u32[]{:S(2)}, u32[]{:S(2)}) collective-permute-start(f32[2,1024]{1,0:T(2,128)S(1)} %get-tuple-element.78.refs_3_), channel_id=1, source_target_pairs={{10,0},{8,2},{16,10},{18,8},{26,16},{24,18},{28,26},{30,24},{22,28... | collective-permute-start | bytes 24584 | tf_op jit(solution)/shard_map/ppermute | solution.py:821
  38.3 5.2 %collective-permute-start.17 = (f32[2,1024]{1,0:T(2,128)S(1)}, f32[2,1024]{1,0:T(2,128)S(1)}, u32[]{:S(2)}, u32[]{:S(2)}) collective-permute-start(f32[2,1024]{1,0:T(2,128)S(1)} %get-tuple-element.78.refs_3_), channel_id=1, source_target_pairs={{2,0},{10,2},{8,10},{16,8},{18,16},{26,18},{24,26},{28,24},{30,28}... | collective-permute-start | bytes 24584 | tf_op jit(solution)/shard_map/ppermute | solution.py:821
  38.8 4.7 %collective-permute-start.16 = (f32[2,1024]{1,0:T(2,128)S(1)}, f32[2,1024]{1,0:T(2,128)S(1)}, u32[]{:S(2)}, u32[]{:S(2)}) collective-permute-start(f32[2,1024]{1,0:T(2,128)S(1)} %get-tuple-element.78.refs_3_), channel_id=1, source_target_pairs={{4,0},{0,2},{2,10},{10,8},{8,16},{16,18},{18,26},{26,24},{24,28},{... | collective-permute-start | bytes 24584 | tf_op jit(solution)/shard_map/ppermute | solution.py:821
  38.8 4.7 %collective-permute-start.15 = (f32[2,1024]{1,0:T(2,128)S(1)}, f32[2,1024]{1,0:T(2,128)S(1)}, u32[]{:S(2)}, u32[]{:S(2)}) collective-permute-start(f32[2,1024]{1,0:T(2,128)S(1)} %get-tuple-element.78.refs_3_), channel_id=1, source_target_pairs={{6,0},{4,2},{0,10},{2,8},{10,16},{8,18},{16,26},{18,24},{26,28},{2... | collective-permute-start | bytes 24584 | tf_op jit(solution)/shard_map/ppermute | solution.py:821
  40.1 4.0 %collective-permute-start.14 = (f32[2,1024]{1,0:T(2,128)S(1)}, f32[2,1024]{1,0:T(2,128)S(1)}, u32[]{:S(2)}, u32[]{:S(2)}) collective-permute-start(f32[2,1024]{1,0:T(2,128)S(1)} %get-tuple-element.78.refs_3_), channel_id=1, source_target_pairs={{14,0},{6,2},{4,10},{0,8},{2,16},{10,18},{8,26},{16,24},{18,28},{2... | collective-permute-start | bytes 24584 | tf_op jit(solution)/shard_map/ppermute | solution.py:821
  48.1 6.6 %collective-permute-start.24 = (f32[3,1024]{1,0:T(4,128)S(1)}, f32[3,1024]{1,0:T(4,128)S(1)}, u32[]{:S(2)}, u32[]{:S(2)}) collective-permute-start(f32[3,1024]{1,0:T(4,128)S(1)} %get-tuple-element.86.refs_3_), channel_id=1, source_target_pairs={{10,0},{8,2},{16,10},{18,8},{26,16},{24,18},{28,26},{30,24},{22,28... | collective-permute-start | bytes 36872 | tf_op jit(solution)/shard_map/ppermute | solution.py:821
  48.3 6.3 %collective-permute-start.23 = (f32[3,1024]{1,0:T(4,128)S(1)}, f32[3,1024]{1,0:T(4,128)S(1)}, u32[]{:S(2)}, u32[]{:S(2)}) collective-permute-start(f32[3,1024]{1,0:T(4,128)S(1)} %get-tuple-element.86.refs_3_), channel_id=1, source_target_pairs={{2,0},{10,2},{8,10},{16,8},{18,16},{26,18},{24,26},{28,24},{30,28}... | collective-permute-start | bytes 36872 | tf_op jit(solution)/shard_map/ppermute | solution.py:821
  49.9 4.8 %collective-permute-start.22 = (f32[3,1024]{1,0:T(4,128)S(1)}, f32[3,1024]{1,0:T(4,128)S(1)}, u32[]{:S(2)}, u32[]{:S(2)}) collective-permute-start(f32[3,1024]{1,0:T(4,128)S(1)} %get-tuple-element.86.refs_3_), channel_id=1, source_target_pairs={{4,0},{0,2},{2,10},{10,8},{8,16},{16,18},{18,26},{26,24},{24,28},{... | collective-permute-start | bytes 36872 | tf_op jit(solution)/shard_map/ppermute | solution.py:821
  49.9 4.8 %collective-permute-start.21 = (f32[3,1024]{1,0:T(4,128)S(1)}, f32[3,1024]{1,0:T(4,128)S(1)}, u32[]{:S(2)}, u32[]{:S(2)}) collective-permute-start(f32[3,1024]{1,0:T(4,128)S(1)} %get-tuple-element.86.refs_3_), channel_id=1, source_target_pairs={{6,0},{4,2},{0,10},{2,8},{10,16},{8,18},{16,26},{18,24},{26,28},{2... | collective-permute-start | bytes 36872 | tf_op jit(solution)/shard_map/ppermute | solution.py:821
  50.4 4.3 %collective-permute-start.20 = (f32[3,1024]{1,0:T(4,128)S(1)}, f32[3,1024]{1,0:T(4,128)S(1)}, u32[]{:S(2)}, u32[]{:S(2)}) collective-permute-start(f32[3,1024]{1,0:T(4,128)S(1)} %get-tuple-element.86.refs_3_), channel_id=1, source_target_pairs={{14,0},{6,2},{4,10},{0,8},{2,16},{10,18},{8,26},{16,24},{18,28},{2... | collective-permute-start | bytes 36872 | tf_op jit(solution)/shard_map/ppermute | solution.py:821
  61.6 6.2 %collective-permute-start.27 = (bf16[768,128]{1,0:T(8,128)(2,1)S(1)}, bf16[768,128]{1,0:T(8,128)(2,1)S(1)}, u32[]{:S(2)}, u32[]{:S(2)}) collective-permute-start(bf16[768,128]{1,0:T(8,128)(2,1)S(1)} %get-tuple-element.103), channel_id=1, source_target_pairs={{4,0},{6,2},{0,4},{2,6},{12,8},{14,10},{8,12},{10,14},{20,16},{22,... | collective-permute-start | bytes 589832 | tf_op jit(solution)/shard_map/ppermute | solution.py:783
  68.1 3.8 %collective-permute-start.31 = (bf16[192,128]{1,0:T(8,128)(2,1)S(1)}, bf16[192,128]{1,0:T(8,128)(2,1)S(1)}, u32[]{:S(2)}, u32[]{:S(2)}) collective-permute-start(bf16[192,128]{1,0:T(8,128)(2,1)S(1)} %get-tuple-element.109), channel_id=1, source_target_pairs={{16,0},{18,2},{20,4},{22,6},{24,8},{26,10},{28,12},{30,14},{0,16},... | collective-permute-start | bytes 147464 | tf_op jit(solution)/shard_map/ppermute | solution.py:786
  69.4 4.7 %collective-permute-start.32 = (bf16[192,128]{1,0:T(8,128)(2,1)S(1)}, bf16[192,128]{1,0:T(8,128)(2,1)S(1)}, u32[]{:S(2)}, u32[]{:S(2)}) collective-permute-start(bf16[192,128]{1,0:T(8,128)(2,1)S(1)} %get-tuple-element.110), channel_id=1, source_target_pairs={{24,0},{26,2},{28,4},{30,6},{16,8},{18,10},{20,12},{22,14},{8,16},... | collective-permute-start | bytes 147464 | tf_op jit(solution)/shard_map/ppermute | solution.py:786
  74.2 4.8 %collective-permute-start.35 = (bf16[192,128]{1,0:T(8,128)(2,1)S(1)}, bf16[192,128]{1,0:T(8,128)(2,1)S(1)}, u32[]{:S(2)}, u32[]{:S(2)}) collective-permute-start(bf16[192,128]{1,0:T(8,128)(2,1)S(1)} %shard_map.191.refs_0_), channel_id=1, source_target_pairs={{24,0},{26,2},{28,4},{30,6},{16,8},{18,10},{20,12},{22,14},{8,16},... | collective-permute-start | bytes 147464 | tf_op jit(solution)/shard_map/ppermute | solution.py:789
  76.9 3.8 %collective-permute-start.34 = (bf16[192,128]{1,0:T(8,128)(2,1)S(1)}, bf16[192,128]{1,0:T(8,128)(2,1)S(1)}, u32[]{:S(2)}, u32[]{:S(2)}) collective-permute-start(bf16[192,128]{1,0:T(8,128)(2,1)S(1)} %shard_map.191.refs_0_), channel_id=1, source_target_pairs={{16,0},{18,2},{20,4},{22,6},{24,8},{26,10},{28,12},{30,14},{0,16},... | collective-permute-start | bytes 147464 | tf_op jit(solution)/shard_map/ppermute | solution.py:789
  76.9 3.8 %collective-permute-start.33 = (bf16[192,128]{1,0:T(8,128)(2,1)S(1)}, bf16[192,128]{1,0:T(8,128)(2,1)S(1)}, u32[]{:S(2)}, u32[]{:S(2)}) collective-permute-start(bf16[192,128]{1,0:T(8,128)(2,1)S(1)} %shard_map.191.refs_0_), channel_id=1, source_target_pairs={{8,0},{10,2},{12,4},{14,6},{0,8},{2,10},{4,12},{6,14},{24,16},{26,... | collective-permute-start | bytes 147464 | tf_op jit(solution)/shard_map/ppermute | solution.py:789
  80.7 12.1 %collective-permute-start.38 = (bf16[768,128]{1,0:T(8,128)(2,1)S(1)}, bf16[768,128]{1,0:T(8,128)(2,1)S(1)}, u32[]{:S(2)}, u32[]{:S(2)}) collective-permute-start(bf16[768,128]{1,0:T(8,128)(2,1)S(1)} %shard_map.192.refs_0_), channel_id=1, source_target_pairs={{5,0},{4,1},{7,2},{6,3},{1,4},{0,5},{3,6},{2,7},{13,8},{12,9},{15,... | collective-permute-start | bytes 589832 | tf_op jit(solution)/shard_map/ppermute | solution.py:801
  81.7 11.1 %collective-permute-start.37 = (bf16[768,128]{1,0:T(8,128)(2,1)S(1)}, bf16[768,128]{1,0:T(8,128)(2,1)S(1)}, u32[]{:S(2)}, u32[]{:S(2)}) collective-permute-start(bf16[768,128]{1,0:T(8,128)(2,1)S(1)} %shard_map.192.refs_0_), channel_id=1, source_target_pairs={{1,0},{0,1},{3,2},{2,3},{5,4},{4,5},{7,6},{6,7},{9,8},{8,9},{11,10... | collective-permute-start | bytes 589832 | tf_op jit(solution)/shard_map/ppermute | solution.py:801
  82.9 10.0 %collective-permute-start.36 = (bf16[768,128]{1,0:T(8,128)(2,1)S(1)}, bf16[768,128]{1,0:T(8,128)(2,1)S(1)}, u32[]{:S(2)}, u32[]{:S(2)}) collective-permute-start(bf16[768,128]{1,0:T(8,128)(2,1)S(1)} %shard_map.192.refs_0_), channel_id=1, source_target_pairs={{4,0},{5,1},{6,2},{7,3},{0,4},{1,5},{2,6},{3,7},{12,8},{13,9},{14,... | collective-permute-start | bytes 589832 | tf_op jit(solution)/shard_map/ppermute | solution.py:801
  83.4 9.4 %collective-permute-start.39 = (f32[2,512]{1,0:T(2,128)S(1)}, f32[2,512]{1,0:T(2,128)S(1)}, u32[]{:S(2)}, u32[]{:S(2)}) collective-permute-start(f32[2,512]{1,0:T(2,128)S(1)} %shard_map.189.refs_2_), channel_id=1, source_target_pairs={{0,0},{2,2},{10,4},{8,6},{16,8},{18,10},{26,12},{24,14},{28,16},{3... | collective-permute-start | bytes 12296 | tf_op jit(solution)/shard_map/ppermute | solution.py:929
  (20 other events, 140.5 us)
